TPU v7x, 32 devices: a whole 2x2x4 slice. The times are simulated.
32 devices in a mesh: mem: 16 (over z, y, x), rows: 2 (over core).
Axes of the slice: x: 2, y: 2, z: 4, core: 2. Of those that a mesh axis runs over, the one named last changes fastest.
Arguments:
- sample_collection: float32 [256, 2, 16, 128], P('mem', None, 'rows'), may hold values from -6 to 6
- obs_values: float32 [2, 16, 128], P(None, 'rows', 'mem'), may hold values from -6 to 6
- obs_inverse_variance: float32 [2, 16, 128], P(None, 'rows', 'mem'), may hold values from 0.5 to 4
- obs_mask: int32 [2, 16, 128], P(None, 'rows', 'mem'), may hold values 0 or 1
Outputs:
- cycled: float32 [256, 2, 16, 128], P('mem', None, 'rows')
All inputs are finite; a program needn't handle non-finite values. No bound on the sum of `obs_mask` on one device may be relied on, other than what follows from the above.
Results may differ from a plain program's by a relative error of at most 0.0051.
Values may be sent and summed in bfloat16 or wider, within the bound.
No kernel may reach another device: no remote copies, remote signals or barrier semaphores. Data moves between devices by JAX's collectives and lax.ppermute only.
A program may use at most 64 MiB of HBM per device.

v0:
```python
import jax
import jax.numpy as jnp
from jax import lax
from jax.sharding import PartitionSpec as P

PATCH = 8
RADIUS = 4
FSTEPS = 4
SCHULZ_STEPS = 3


CADV = 0.05


def with_halo(shard, sides, width):
    for axis, dim in sides:
        count, length = (lax.axis_size(axis), shard.shape[dim])
        up = [(i, (i + 1) % count) for i in range(count)]
        down = [(j, i) for i, j in up]
        last = lax.slice_in_dim(shard, length - width, length, axis=dim)
        initial = lax.slice_in_dim(shard, 0, width, axis=dim)
        before = lax.ppermute(last, axis, up)
        after = lax.ppermute(initial, axis, down)
        shard = jnp.concatenate([before, shard, after], axis=dim)
    return shard


def advance_rows(extended):
    u_field = extended[:, 0]
    v_field = extended[:, 1]

    def tendency(field):
        along_x = jnp.roll(field, -1, -1) - jnp.roll(field, 1, -1)
        along_y = field[:, 2:] - field[:, :-2]
        return field[:, 1:-1] - CADV * (
            u_field[:, 1:-1] * along_x[:, 1:-1] + v_field[:, 1:-1] * along_y
        )

    return jnp.stack([tendency(u_field), tendency(v_field)], 1)


def predicted_prior(dynamics_fields):
    extended = with_halo(dynamics_fields, (("rows", 2),), FSTEPS)
    for step in range(FSTEPS):
        extended = advance_rows(extended)
    dynamics_fields = extended
    return dynamics_fields


def owner_layout(fields):
    local_members, fields_count, band_rows, complete_width = fields.shape
    owning_patches = lax.axis_size("mem")
    col_width = complete_width // owning_patches
    split = fields.reshape(local_members, fields_count, band_rows, owning_patches, col_width)
    split = jnp.transpose(split, (0, 3, 1, 2, 4))
    return split.reshape(local_members, owning_patches, fields_count * band_rows * col_width)


def taper_table():
    index = jnp.arange(2 * PATCH)
    dist = jnp.maximum(jnp.maximum(RADIUS - index, index - (RADIUS + PATCH - 1)), 0)
    far = jnp.maximum(dist[:, None], dist[None, :]).astype(jnp.float32)
    return 1.0 - far / (RADIUS + 1.0)


def analyse(dev_ext, obs_ext, mean):
    high = lax.Precision.HIGHEST
    members = dev_ext.shape[-1]
    col_width = dev_ext.shape[2] - 2 * RADIUS
    count = col_width // PATCH
    taper = taper_table()[None, :, :]
    factor = obs_ext[..., 0].astype(jnp.float32) * taper
    weighted = (dev_ext.astype(jnp.float32) * factor[..., None]).astype(jnp.bfloat16)
    weighted_list = [weighted.reshape(-1, members)]
    region_list = [dev_ext.reshape(-1, members)]
    innov_list = [obs_ext[..., 1].reshape(-1)]
    inner = dev_ext[:, RADIUS : RADIUS + PATCH, RADIUS : RADIUS + PATCH, :]
    interior_pieces = [inner.reshape(-1, members)]
    weighted_all = jnp.stack(weighted_list)
    region_all = jnp.stack(region_list)
    innovation_combined = jnp.stack(innov_list)
    interior_combined = jnp.stack(interior_pieces)
    gram = jnp.einsum("pqk,pql->pkl", weighted_all, region_all, preferred_element_type=jnp.float32)
    projected = jnp.einsum(
        "pqk,pq->pk",
        weighted_all.astype(jnp.float32),
        innovation_combined.astype(jnp.float32),
        precision=high,
    )
    eye = jnp.eye(members, dtype=jnp.float32)
    system = (members - 1.0) * eye + gram
    scale = jnp.sqrt(jnp.sum(system * system, axis=(1, 2)))[:, None, None]
    iter_y = system / scale
    iter_z = jnp.broadcast_to(eye, system.shape)
    for step in range(SCHULZ_STEPS):
        middle = 1.5 * eye - 0.5 * jnp.matmul(iter_z, iter_y, precision=high)
        iter_y = jnp.matmul(iter_y, middle, precision=high)
        iter_z = jnp.matmul(middle, iter_z, precision=high)
    root = iter_z / jnp.sqrt(scale)
    half_way = jnp.einsum("pkl,pl->pk", root, projected, precision=high)
    shift = jnp.einsum("pkl,pl->pk", root, half_way, precision=high)
    ensemble_transform = (jnp.sqrt(members - 1.0) * root + shift[:, :, None]).astype(jnp.bfloat16)
    increment = jnp.einsum(
        "vhf,vfa->vha", interior_combined, ensemble_transform, preferred_element_type=jnp.float32
    )
    increment = increment.reshape(count, 2, PATCH, PATCH, members)
    increment = jnp.transpose(increment, (1, 2, 0, 3, 4)).reshape(2, PATCH, col_width, members)
    return mean[..., None] + increment


def local(sample_collection, obs_values, obs_inverse_variance, obs_mask):
    leading_output = predicted_prior(sample_collection)
    local_members, fields_count, band_rows, complete_width = leading_output.shape
    col_width = obs_values.shape[2]
    owning_patches = lax.axis_size("mem")
    members = local_members * owning_patches
    sending = owner_layout(leading_output)
    gathered = lax.all_to_all(sending, "mem", split_axis=1, concat_axis=0, tiled=True)
    gathered = gathered.reshape(members, -1)
    mean_flat = jnp.sum(gathered, 0) / members
    deviation_flat = (gathered - mean_flat).astype(jnp.bfloat16)
    mean = mean_flat.reshape(fields_count, band_rows, col_width)
    deviation = jnp.transpose(deviation_flat).reshape(fields_count, band_rows, col_width, members)
    member_weight = (obs_mask.astype(jnp.float32) * obs_inverse_variance).astype(jnp.bfloat16)
    innovation = (obs_values - mean).astype(jnp.bfloat16)
    obs_pair = jnp.stack([member_weight, innovation], -1)
    dev_ext, obs_ext = (
        with_halo(deviation, (("rows", 1), ("mem", 2)), RADIUS),
        with_halo(obs_pair, (("rows", 1), ("mem", 2)), RADIUS),
    )
    updated_estimate = analyse(dev_ext, obs_ext, mean)
    returning = jnp.transpose(updated_estimate.reshape(-1, members)).reshape(members, 1, -1)
    output_result = lax.all_to_all(returning, "mem", split_axis=0, concat_axis=1, tiled=True)
    output_result = output_result.reshape(
        local_members, owning_patches, fields_count, band_rows, col_width
    )
    output_result = jnp.transpose(output_result, (0, 2, 3, 1, 4)).reshape(
        local_members, fields_count, band_rows, complete_width
    )
    return predicted_prior(output_result)


def solution(mesh):
    return jax.shard_map(
        local,
        mesh=mesh,
        in_specs=(
            P("mem", None, "rows", None),
            P(None, "rows", "mem"),
            P(None, "rows", "mem"),
            P(None, "rows", "mem"),
        ),
        out_specs=P("mem", None, "rows", None),
        check_vma=False,
    )
```

profile of v0, /device:TPU:0, one launch (start us, length us, event | category | flops | bytes accessed | tf_op | source)
XLA Modules:
  0.0 68.3 jit_solution(17926856079104959010)
XLA Ops:
  0.0 1.1 %fusion.126 = (f32[16,2,4,128]{3,2,1,0:T(4,128)S(1)}, f32[16,2,4,128]{3,2,1,0:T(4,128)S(1)}) fusion(f32[16,2,8,128]{3,2,1,0:T(8,128)} %param.4), kind=kLoop, calls=%fused_computation.209 | loop fusion | bytes 262144 | tf_op jit(solution)/shard_map/slice | solution.py:20
  1.1 0.5 collective-permute-start
  1.7 0.8 %collective-permute-done = f32[16,2,4,128]{3,2,1,0:T(4,128)S(1)} collective-permute-done((f32[16,2,4,128]{3,2,1,0:T(4,128)S(1)}, f32[16,2,4,128]{3,2,1,0:T(4,128)S(1)}, u32[]{:S(2)}, u32[]{:S(2)}) %collective-permute-start) | collective-permute-done | bytes 65568 | tf_op jit(solution)/shard_map/ppermute | solution.py:22
  5.8 0.9 %copy.216 = f32[16,16,2,8,8]{1,4,3,2,0:T(8,128)S(1)} copy(f32[16,16,2,8,8]{0,4,1,3,2:T(8,128)S(1)} %maximum_bitcast_fusion) | data formatting | bytes 262144 | tf_op jit(solution)/shard_map/transpose | solution.py:55
  6.7 1.0 %copy.217 = f32[16,16,128]{2,0,1:T(8,128)} copy(f32[16,16,128]{1,2,0:T(8,128)S(1)} %bitcast.86) | data formatting | bytes 262144 | tf_op jit(solution)/shard_map/reshape | solution.py:56
  7.7 8.1 %all-to-all-start = ((f32[16,16,128]{2,0,1:T(8,128)}), f32[16,16,128]{2,0,1:T(8,128)S(1)}, u32[]{:S(2)}, u32[]{:S(2)}) async-start(f32[16,16,128]{2,0,1:T(8,128)} %copy.217), calls=%async_computation | async-start | bytes 262144 | tf_op jit(solution)/shard_map/all_to_all | solution.py:118
  15.9 0.6 copy-done.1
  16.6 7.2 %all-to-all-done = f32[16,16,128]{2,0,1:T(8,128)S(1)} async-done(((f32[16,16,128]{2,0,1:T(8,128)}), f32[16,16,128]{2,0,1:T(8,128)S(1)}, u32[]{:S(2)}, u32[]{:S(2)}) %all-to-all-start) | async-done | bytes 131104 | tf_op jit(solution)/shard_map/all_to_all | solution.py:118
  24.0 0.6 copy-done.3
  24.7 0.5 collective-permute-start.7
  25.3 0.5 collective-permute-done.6
  26.1 1.1 %collective-permute-start.8 = (bf16[2,16,4,2]{2,1,0,3:T(8,128)(2,1)S(1)}, bf16[2,16,4,2]{2,1,0,3:T(8,128)(2,1)S(1)}, u32[]{:S(2)}, u32[]{:S(2)}) collective-permute-start(bf16[2,16,4,2]{2,1,0,3:T(8,128)(2,1)S(1)} %get-tuple-element.97), channel_id=1, source_target_pairs={{0,2},{2,4},{4,6},{6,8},{8,10},{10,12},{12,14},{14,16},{16,18},{18... | collective-permute-start | bytes 1544 | tf_op jit(solution)/shard_map/ppermute | solution.py:22
  27.2 4.5 %collective-permute-start.9 = (bf16[2,16,4,2]{2,1,0,3:T(8,128)(2,1)S(1)}, bf16[2,16,4,2]{2,1,0,3:T(8,128)(2,1)S(1)}, u32[]{:S(2)}, u32[]{:S(2)}) collective-permute-start(bf16[2,16,4,2]{2,1,0,3:T(8,128)(2,1)S(1)} %get-tuple-element.98), channel_id=1, source_target_pairs={{2,0},{4,2},{6,4},{8,6},{10,8},{12,10},{14,12},{16,14},{18,16},{20... | collective-permute-start | bytes 1544 | tf_op jit(solution)/shard_map/ppermute | solution.py:23
  31.7 0.5 collective-permute-start.3
  32.2 1.2 %collective-permute-done.8 = bf16[2,16,4,2]{2,1,0,3:T(8,128)(2,1)S(1)} collective-permute-done((bf16[2,16,4,2]{2,1,0,3:T(8,128)(2,1)S(1)}, bf16[2,16,4,2]{2,1,0,3:T(8,128)(2,1)S(1)}, u32[]{:S(2)}, u32[]{:S(2)}) %collective-permute-start.8) | collective-permute-done | bytes 544 | tf_op jit(solution)/shard_map/ppermute | solution.py:22
  33.7 5.8 %collective-permute-start.5 = (bf16[2,16,4,256]{3,2,1,0:T(4,128)(2,1)S(1)}, bf16[2,16,4,256]{3,2,1,0:T(4,128)(2,1)S(1)}, u32[]{:S(2)}, u32[]{:S(2)}) collective-permute-start(bf16[2,16,4,256]{3,2,1,0:T(4,128)(2,1)S(1)} %get-tuple-element.36), channel_id=1, source_target_pairs={{2,0},{4,2},{6,4},{8,6},{10,8},{12,10},{14,12},{16,14},{18,16},{20... | collective-permute-start | bytes 196616 | tf_op jit(solution)/shard_map/ppermute | solution.py:23
  39.5 2.1 %collective-permute-done.4 = bf16[2,16,4,256]{3,2,1,0:T(4,128)(2,1)S(1)} collective-permute-done((bf16[2,16,4,256]{3,2,1,0:T(4,128)(2,1)S(1)}, bf16[2,16,4,256]{3,2,1,0:T(4,128)(2,1)S(1)}, u32[]{:S(2)}, u32[]{:S(2)}) %collective-permute-start.4) | collective-permute-done | bytes 65568 | tf_op jit(solution)/shard_map/ppermute | solution.py:22
  41.6 1.1 %multiply_reduce_fusion = (f32[]{:T(128)}, f32[256,256]{1,0:T(8,128)S(1)}) fusion(bf16[2,16,4,256]{3,2,1,0:T(4,128)(2,1)S(1)} %collective-permute-done.5, bf16[2,4,8,256]{3,2,1,0:T(8,128)(2,1)S(1)} %collective-permute-done.3, bf16[2,8,8,256]{3,2,1,0:T(8,128)(2,1)S(1)} %bitcast.93, bf16[2,4,8,256]{3,2,1,0:T(8,128)(2,1)S(1)} %collective-permute-done.2, ...), kind=kOutput, calls=%fused_computation.18 | convolution fusion | flops 70320128 | bytes 526340 | tf_op jit(solution)/shard_map/pqk,pql->pkl/dot_general | solution.py:83
  45.9 0.4 fusion
  47.7 14.7 %all_to_all.30 = f32[256,1,128]{2,1,0:T(1,128)S(1)} all-to-all(f32[256,1,128]{2,1,0:T(1,128)S(1)} %bitcast.99), channel_id=1, replica_groups=mesh['mem'=16,'rows'=2] {'mem'}, dimensions={0} | all-to-all | bytes 262144 | tf_op jit(solution)/shard_map/all_to_all | solution.py:133
  62.7 0.7 %copy.221 = f32[16,2,8,16,8]{0,4,3,2,1:T(8,128)S(1)} copy(f32[16,2,8,16,8]{3,4,2,1,0:T(8,128)S(1)} %bitcast.87) | data formatting | bytes 262144 | tf_op jit(solution)/shard_map/transpose | solution.py:137
  63.8 0.5 collective-permute-start.11
  64.3 0.7 %collective-permute-done.10 = f32[16,2,4,128]{3,0,2,1:T(8,128)S(1)} collective-permute-done((f32[16,2,4,128]{3,0,2,1:T(8,128)S(1)}, f32[16,2,4,128]{3,0,2,1:T(8,128)S(1)}, u32[]{:S(2)}, u32[]{:S(2)}) %collective-permute-start.10) | collective-permute-done | bytes 65568 | tf_op jit(solution)/shard_map/ppermute | solution.py:22
  67.6 0.7 pad_maximum_fusion.4
  (103 shorter events, 11.1 us)
Async XLA Ops:
  0.0 2.9 %copy-start = (f32[16,2,8,128]{3,2,1,0:T(8,128)S(1)}, f32[16,2,8,128]{3,2,1,0:T(8,128)}, u32[]{:S(2)}) copy-start(f32[16,2,8,128]{3,2,1,0:T(8,128)} %param.4) | copy-start | bytes 393220
  1.1 1.4 %collective-permute-start = (f32[16,2,4,128]{3,2,1,0:T(4,128)S(1)}, f32[16,2,4,128]{3,2,1,0:T(4,128)S(1)}, u32[]{:S(2)}, u32[]{:S(2)}) collective-permute-start(f32[16,2,4,128]{3,2,1,0:T(4,128)S(1)} %get-tuple-element.45), channel_id=1, source_target_pairs={{0,1},{1,0},{2,3},{3,2},{4,5},{5,4},{6,7},{7,6},{8,9},{9,8},{10,11... | collective-permute-start | bytes 196616 | tf_op jit(solution)/shard_map/ppermute | solution.py:22
  1.6 1.3 %collective-permute-start.1 = (f32[16,2,4,128]{3,2,1,0:T(4,128)S(1)}, f32[16,2,4,128]{3,2,1,0:T(4,128)S(1)}, u32[]{:S(2)}, u32[]{:S(2)}) collective-permute-start(f32[16,2,4,128]{3,2,1,0:T(4,128)S(1)} %get-tuple-element.46), channel_id=1, source_target_pairs={{1,0},{0,1},{3,2},{2,3},{5,4},{4,5},{7,6},{6,7},{9,8},{8,9},{11,10... | collective-permute-start | bytes 196616 | tf_op jit(solution)/shard_map/ppermute | solution.py:23
  7.7 8.2 %copy-start.2 = (s32[2,8,8]{2,1,0:T(8,128)S(1)}, s32[2,8,8]{2,1,0:T(8,128)}, u32[]{:S(2)}) copy-start(s32[2,8,8]{2,1,0:T(8,128)} %param.7) | copy-start | bytes 1540
  7.7 16.1 %all-to-all-start = ((f32[16,16,128]{2,0,1:T(8,128)}), f32[16,16,128]{2,0,1:T(8,128)S(1)}, u32[]{:S(2)}, u32[]{:S(2)}) async-start(f32[16,16,128]{2,0,1:T(8,128)} %copy.217), calls=%async_computation | async-start | bytes 262144 | tf_op jit(solution)/shard_map/all_to_all | solution.py:118
  15.9 0.7 %copy-start.1 = (f32[2,8,8]{2,1,0:T(8,128)S(1)}, f32[2,8,8]{2,1,0:T(8,128)}, u32[]{:S(2)}) copy-start(f32[2,8,8]{2,1,0:T(8,128)} %param.6) | copy-start | bytes 1540
  23.9 0.7 %copy-start.3 = (f32[2,8,8]{2,1,0:T(8,128)S(1)}, f32[2,8,8]{2,1,0:T(8,128)}, u32[]{:S(2)}) copy-start(f32[2,8,8]{2,1,0:T(8,128)} %param.5) | copy-start | bytes 1540
  24.6 1.2 %collective-permute-start.6 = (bf16[2,4,8,2]{2,1,0,3:T(4,128)(2,1)S(1)}, bf16[2,4,8,2]{2,1,0,3:T(4,128)(2,1)S(1)}, u32[]{:S(2)}, u32[]{:S(2)}) collective-permute-start(bf16[2,4,8,2]{2,1,0,3:T(4,128)(2,1)S(1)} %get-tuple-element.99), channel_id=1, source_target_pairs={{0,1},{1,0},{2,3},{3,2},{4,5},{5,4},{6,7},{7,6},{8,9},{9,8},{10,11... | collective-permute-start | bytes 776 | tf_op jit(solution)/shard_map/ppermute | solution.py:22
  24.7 1.3 %collective-permute-start.7 = (bf16[2,4,8,2]{2,1,0,3:T(4,128)(2,1)S(1)}, bf16[2,4,8,2]{2,1,0,3:T(4,128)(2,1)S(1)}, u32[]{:S(2)}, u32[]{:S(2)}) collective-permute-start(bf16[2,4,8,2]{2,1,0,3:T(4,128)(2,1)S(1)} %get-tuple-element.100), channel_id=1, source_target_pairs={{1,0},{0,1},{3,2},{2,3},{5,4},{4,5},{7,6},{6,7},{9,8},{8,9},{11,10... | collective-permute-start | bytes 776 | tf_op jit(solution)/shard_map/ppermute | solution.py:23
  26.1 7.3 %collective-permute-start.8 = (bf16[2,16,4,2]{2,1,0,3:T(8,128)(2,1)S(1)}, bf16[2,16,4,2]{2,1,0,3:T(8,128)(2,1)S(1)}, u32[]{:S(2)}, u32[]{:S(2)}) collective-permute-start(bf16[2,16,4,2]{2,1,0,3:T(8,128)(2,1)S(1)} %get-tuple-element.97), channel_id=1, source_target_pairs={{0,2},{2,4},{4,6},{6,8},{8,10},{10,12},{12,14},{14,16},{16,18},{18... | collective-permute-start | bytes 1544 | tf_op jit(solution)/shard_map/ppermute | solution.py:22
  27.2 6.2 %collective-permute-start.9 = (bf16[2,16,4,2]{2,1,0,3:T(8,128)(2,1)S(1)}, bf16[2,16,4,2]{2,1,0,3:T(8,128)(2,1)S(1)}, u32[]{:S(2)}, u32[]{:S(2)}) collective-permute-start(bf16[2,16,4,2]{2,1,0,3:T(8,128)(2,1)S(1)} %get-tuple-element.98), channel_id=1, source_target_pairs={{2,0},{4,2},{6,4},{8,6},{10,8},{12,10},{14,12},{16,14},{18,16},{20... | collective-permute-start | bytes 1544 | tf_op jit(solution)/shard_map/ppermute | solution.py:23
  31.7 1.8 %collective-permute-start.2 = (bf16[2,4,8,256]{3,2,1,0:T(8,128)(2,1)S(1)}, bf16[2,4,8,256]{3,2,1,0:T(8,128)(2,1)S(1)}, u32[]{:S(2)}, u32[]{:S(2)}) collective-permute-start(bf16[2,4,8,256]{3,2,1,0:T(8,128)(2,1)S(1)} %get-tuple-element.95), channel_id=1, source_target_pairs={{0,1},{1,0},{2,3},{3,2},{4,5},{5,4},{6,7},{7,6},{8,9},{9,8},{10,11... | collective-permute-start | bytes 98312 | tf_op jit(solution)/shard_map/ppermute | solution.py:22
  31.7 1.8 %collective-permute-start.3 = (bf16[2,4,8,256]{3,2,1,0:T(8,128)(2,1)S(1)}, bf16[2,4,8,256]{3,2,1,0:T(8,128)(2,1)S(1)}, u32[]{:S(2)}, u32[]{:S(2)}) collective-permute-start(bf16[2,4,8,256]{3,2,1,0:T(8,128)(2,1)S(1)} %get-tuple-element.96), channel_id=1, source_target_pairs={{1,0},{0,1},{3,2},{2,3},{5,4},{4,5},{7,6},{6,7},{9,8},{8,9},{11,10... | collective-permute-start | bytes 98312 | tf_op jit(solution)/shard_map/ppermute | solution.py:23
  33.6 8.0 %collective-permute-start.4 = (bf16[2,16,4,256]{3,2,1,0:T(4,128)(2,1)S(1)}, bf16[2,16,4,256]{3,2,1,0:T(4,128)(2,1)S(1)}, u32[]{:S(2)}, u32[]{:S(2)}) collective-permute-start(bf16[2,16,4,256]{3,2,1,0:T(4,128)(2,1)S(1)} %get-tuple-element.35), channel_id=1, source_target_pairs={{0,2},{2,4},{4,6},{6,8},{8,10},{10,12},{12,14},{14,16},{16,18},{18... | collective-permute-start | bytes 196616 | tf_op jit(solution)/shard_map/ppermute | solution.py:22
  33.7 8.0 %collective-permute-start.5 = (bf16[2,16,4,256]{3,2,1,0:T(4,128)(2,1)S(1)}, bf16[2,16,4,256]{3,2,1,0:T(4,128)(2,1)S(1)}, u32[]{:S(2)}, u32[]{:S(2)}) collective-permute-start(bf16[2,16,4,256]{3,2,1,0:T(4,128)(2,1)S(1)} %get-tuple-element.36), channel_id=1, source_target_pairs={{2,0},{4,2},{6,4},{8,6},{10,8},{12,10},{14,12},{16,14},{18,16},{20... | collective-permute-start | bytes 196616 | tf_op jit(solution)/shard_map/ppermute | solution.py:23
  63.8 1.3 %collective-permute-start.10 = (f32[16,2,4,128]{3,0,2,1:T(8,128)S(1)}, f32[16,2,4,128]{3,0,2,1:T(8,128)S(1)}, u32[]{:S(2)}, u32[]{:S(2)}) collective-permute-start(f32[16,2,4,128]{3,0,2,1:T(8,128)S(1)} %get-tuple-element.33), channel_id=1, source_target_pairs={{0,1},{1,0},{2,3},{3,2},{4,5},{5,4},{6,7},{7,6},{8,9},{9,8},{10,11... | collective-permute-start | bytes 196616 | tf_op jit(solution)/shard_map/ppermute | solution.py:22
  63.8 1.4 %collective-permute-start.11 = (f32[16,2,4,128]{3,0,2,1:T(8,128)S(1)}, f32[16,2,4,128]{3,0,2,1:T(8,128)S(1)}, u32[]{:S(2)}, u32[]{:S(2)}) collective-permute-start(f32[16,2,4,128]{3,0,2,1:T(8,128)S(1)} %get-tuple-element.34), channel_id=1, source_target_pairs={{1,0},{0,1},{3,2},{2,3},{5,4},{4,5},{7,6},{6,7},{9,8},{8,9},{11,10... | collective-permute-start | bytes 196616 | tf_op jit(solution)/shard_map/ppermute | solution.py:23
where the time goes:
time: 68.7 us; the launch traced here: 68.3 us
  starting transfers between devices  21.8 us (32%)
  blocking collectives  14.7 us (21%)
  waiting for transfers between devices  13.3 us (19%)
  local copies, waits for them, and re-layouts  9.48 us (14%)
  matrix products  4.99 us (7%)
  other arithmetic  2.7 us (4%)
  between operations  1.3 us (2%)
    all_to_all x1, blocking collectives, local(): lax.all_to_all(returning, 'mem', split_axis=0, concat_axis=1, tiled=True)  14.7 us
    ppermute x6, starting transfers between devices, with_halo(): after = lax.ppermute(initial, axis, down)  11.9 us
    all_to_all x1, starting transfers between devices, local(): lax.all_to_all(sending, 'mem', split_axis=1, concat_axis=0, tiled=True)  8.15 us
    all_to_all x1, waiting for transfers between devices, local(): lax.all_to_all(sending, 'mem', split_axis=1, concat_axis=0, tiled=True)  7.25 us
    ppermute x6, waiting for transfers between devices, with_halo(): before = lax.ppermute(last, axis, up)  5.37 us
    slice x32, local copies, waits for them, and re-layouts, tendency(): along_x = jnp.roll(field, -1, -1) - jnp.roll(field, 1, -1)  2.84 us
    ppermute x6, starting transfers between devices, with_halo(): before = lax.ppermute(last, axis, up)  1.81 us
  transfers between devices with their start and end apart: 13, of which 9 were waited for; matrix products, arithmetic and copies ran while one was open for 1% of the time, Pallas kernels for 0%

commit v1 on v0

v1 whole, which is shorter than its diff:
```python
import functools

import jax
import jax.numpy as jnp
from jax import lax
from jax.experimental import pallas as pl
from jax.experimental.pallas import tpu as pltpu
from jax.sharding import PartitionSpec as P

PATCH = 8
RADIUS = 4
FSTEPS = 4
CADV = 0.05

LOCAL = 16
FIELDS = 2
BAND = 8
WIDTH = 128
REGION = PATCH + 2 * RADIUS
HALF = FIELDS * (BAND // 2) * REGION
BLOCKS = 2 * FIELDS * (BAND // 2)

BF = jnp.bfloat16
F32 = jnp.float32


def forecast_rows(u_rows, v_rows):
    for _ in range(FSTEPS):
        new_u, new_v = [], []
        for i in range(1, len(u_rows) - 1):
            cu, cv = CADV * u_rows[i], CADV * v_rows[i]
            for rows, new in ((u_rows, new_u), (v_rows, new_v)):
                along_x = pltpu.roll(rows[i], WIDTH - 1, 1) - pltpu.roll(rows[i], 1, 1)
                along_y = rows[i + 1] - rows[i - 1]
                new.append(rows[i] - (cu * along_x + cv * along_y))
        u_rows, v_rows = new_u, new_v
    return u_rows, v_rows


def swap_blocks(parts, size):
    count = len(parts)
    lane = lax.broadcasted_iota(jnp.int32, parts[0].shape, 1) // size
    stride = 1
    while stride < count:
        upper = (lane & stride) != 0
        new = list(parts)
        for j in range(count):
            if j & stride == 0:
                a, b = parts[j], parts[j + stride]
                new[j] = jnp.where(upper, pltpu.roll(b, stride * size, 1), a)
                new[j + stride] = jnp.where(upper, b, pltpu.roll(a, WIDTH - stride * size, 1))
        parts = new
        stride *= 2
    return parts


def pack_kernel(x_ref, near_ref, obs_ref, out_ref):
    stride = FIELDS * BAND

    def row(ref, field, index):
        return ref[pl.ds(field * BAND + index, LOCAL, stride=stride), :]

    fields = []
    for field in range(FIELDS):
        before = [row(near_ref, field, r) for r in range(BAND - FSTEPS, BAND)]
        own = [row(x_ref, field, r) for r in range(BAND)]
        after = [row(near_ref, field, r) for r in range(FSTEPS)]
        fields.append(before + own + after)
    done = forecast_rows(*fields)
    stacked = []
    for half in range(2):
        for field in range(FIELDS):
            for r in range(BAND // 2):
                value = done[field][half * (BAND // 2) + r]
                mean = jnp.sum(value, 0, keepdims=True) * (1.0 / LOCAL)
                high = mean.astype(BF).astype(F32)
                low = mean - high
                index = lax.broadcasted_iota(jnp.int32, (8, WIDTH), 0)
                tail = jnp.where(index == 0, high, jnp.where(index == 1, low, 0.0))
                stacked += [value - mean, tail]
    rows = jnp.concatenate(stacked, 0).astype(BF)
    column = lax.broadcasted_iota(jnp.int32, (WIDTH, 2 * WIDTH), 0)
    lane = lax.broadcasted_iota(jnp.int32, (WIDTH, 2 * WIDTH), 1)
    wanted = ((lane // REGION) * PATCH + lane % REGION + (WIDTH - RADIUS)) % WIDTH
    widen = (column == wanted).astype(F32).astype(BF)
    wide = jnp.dot(rows, widen, preferred_element_type=F32)
    height = LOCAL + 8
    for side in range(2):
        tails = [[], []]
        for half in range(2):
            parts = [
                wide[(half * 8 + j) * height : (half * 8 + j + 1) * height, side * WIDTH : (side + 1) * WIDTH]
                for j in range(8)
            ]
            parts = swap_blocks(parts, REGION)
            for i in range(8):
                out_ref[side * 8 + i, :, half * WIDTH : (half + 1) * WIDTH] = parts[i][:LOCAL].astype(BF)
                tails[half].append(parts[i][LOCAL:])
        for i in range(8):
            tail = jnp.concatenate([tails[0][i], tails[1][i]], 0) + obs_ref[...]
            out_ref[side * 8 + i, :, 2 * WIDTH :] = tail.astype(BF)


def halves_of(ref, me, count):
    tails = [ref[s, :, 2 * WIDTH :].astype(F32) for s in range(count)]
    lane = lax.broadcasted_iota(jnp.int32, (16, WIDTH), 1) % REGION
    left = ref[lax.rem(me + count - 1, count), :, 2 * WIDTH :].astype(F32)
    own = ref[me, :, 2 * WIDTH :].astype(F32)
    right = ref[lax.rem(me + 1, count), :, 2 * WIDTH :].astype(F32)
    seen = jnp.where(
        lane < RADIUS,
        pltpu.roll(left, WIDTH - (PATCH - RADIUS), 1),
        jnp.where(lane < RADIUS + PATCH, pltpu.roll(own, RADIUS, 1), pltpu.roll(right, RADIUS + PATCH, 1)),
    )
    result = []
    for half in range(2):
        base = half * 8
        means = [t[base : base + 1] + t[base + 1 : base + 2] for t in tails]
        mean = functools.reduce(jnp.add, means) * (1.0 / count)
        deviation = jnp.concatenate(
            [
                (ref[s, :, half * WIDTH : (half + 1) * WIDTH].astype(F32) + (means[s] - mean)).astype(BF)
                for s in range(count)
            ],
            0,
        )
        weight = seen[base + 2 : base + 3]
        obs = seen[base + 3 : base + 4] + seen[base + 4 : base + 5] + seen[base + 5 : base + 6]
        innovation = (obs - mean).astype(BF).astype(F32)
        result.append((deviation, mean, weight, innovation))
    return result


def analysis_kernel(me_ref, own_ref, near_ref, out_ref):
    count = own_ref.shape[0]
    members = count * LOCAL
    me = me_ref[0]
    own = halves_of(own_ref, me, count)
    near = halves_of(near_ref, me, count)
    lane = lax.broadcasted_iota(jnp.int32, (1, WIDTH), 1)
    region_column = lane % REGION
    half_row = (lane // REGION) % (BAND // 2)
    column_distance = jnp.maximum(
        jnp.maximum(RADIUS - region_column, region_column - (RADIUS + PATCH - 1)), 0
    )
    row_distances = (0 * lane, 0 * lane, half_row + 1, RADIUS - half_row)
    weighted, deviation, innovation = [], [], []
    for (dev, _, weight, inno), row_distance in zip(own + near, row_distances):
        far = jnp.maximum(row_distance, column_distance).astype(F32)
        factor = weight * (1.0 - far / (RADIUS + 1.0))
        weighted.append((dev.astype(F32) * factor).astype(BF))
        deviation.append(dev)
        innovation.append(jnp.broadcast_to(inno, (16, WIDTH)).astype(BF))
    weighted = jnp.concatenate(weighted, 1)
    inner = jnp.concatenate(deviation[:2], 1)
    rows = jnp.concatenate([jnp.concatenate(deviation, 1), jnp.concatenate(innovation, 1)], 0)
    both = lax.dot_general(rows, weighted, (((1,), (1,)), ((), ())), preferred_element_type=F32)
    row = lax.broadcasted_iota(jnp.int32, (members, members), 0)
    col = lax.broadcasted_iota(jnp.int32, (members, members), 1)
    system = both[:members] + jnp.where(row == col, members - 1.0, 0.0)
    line = both[members:]
    scale = jnp.sqrt(jnp.sum(system * system))
    y0 = system * (1.0 / scale)

    def mul(a, b):
        return jnp.dot(a.astype(BF), b.astype(BF), preferred_element_type=F32)

    y0b = y0.astype(BF)
    inner_f = inner.astype(F32)
    x1 = 1.5 * inner_f - 0.5 * mul(y0b, inner)
    line1 = 1.5 * line - 0.5 * mul(line, y0b)
    y1 = 1.5 * y0 - 0.5 * mul(y0b, y0b)
    p1 = 1.5 * y1 - 0.5 * mul(y1, y0b)
    p1b = p1.astype(BF)
    x2 = 1.5 * x1 - 0.5 * mul(p1b, x1)
    line2 = 1.5 * line1 - 0.5 * mul(line1, p1b)
    q1 = 1.5 * p1 - 0.5 * mul(p1b, p1b)
    p2 = 1.5 * q1 - 0.5 * mul(q1, p1b)
    p2b = p2.astype(BF)
    x3 = 1.5 * x2 - 0.5 * mul(p2b, x2)
    line3 = 1.5 * line2 - 0.5 * mul(line2, p2b)
    inverse = 1.0 / jnp.sqrt(scale)
    x3 = x3 * inverse
    line3 = line3 * inverse
    xh = x3.astype(BF)
    xl = (x3 - xh.astype(F32)).astype(BF)
    lh = line3.astype(BF)
    ll = (line3 - lh.astype(F32)).astype(BF)
    shift = mul(lh, xh) + (mul(ll, xh) + mul(lh, xl))
    mean = jnp.concatenate([own[0][1], own[1][1]], 1)
    root = jnp.sqrt(jnp.full((1, 1), members - 1.0, F32))
    result = (root * x3 + (shift[:1] + mean)).astype(BF)
    lane = lax.broadcasted_iota(jnp.int32, (2 * WIDTH, WIDTH), 0)
    target = lax.broadcasted_iota(jnp.int32, (2 * WIDTH, WIDTH), 1)
    narrow = (lane == (target // PATCH) * REGION + RADIUS + target % PATCH).astype(F32).astype(BF)
    result = jnp.dot(result, narrow, preferred_element_type=F32).astype(BF)
    for s in range(count):
        out_ref[s] = result[s * LOCAL : (s + 1) * LOCAL]


def unpack_kernel(own_ref, near_ref, out_ref):
    count = own_ref.shape[0]

    def rows_of(ref):
        parts = swap_blocks([ref[p].astype(F32) for p in range(count)], PATCH)
        half = BAND // 2
        return [
            [parts[h * FIELDS * half + field * half + r] for h in range(2) for r in range(half)]
            for field in range(FIELDS)
        ]

    own, near = rows_of(own_ref), rows_of(near_ref)
    fields = [n[BAND - FSTEPS :] + o + n[:FSTEPS] for o, n in zip(own, near)]
    done = forecast_rows(*fields)
    for field in range(FIELDS):
        for r in range(BAND):
            out_ref[pl.ds(field * BAND + r, LOCAL, stride=FIELDS * BAND), :] = done[field][r]


def from_next(value):
    count = lax.axis_size("rows")
    return lax.ppermute(value, "rows", [((i + 1) % count, i) for i in range(count)])


def from_previous(value):
    count = lax.axis_size("rows")
    return lax.ppermute(value, "rows", [(i, (i + 1) % count) for i in range(count)])


def near_rows(value, join):
    if lax.axis_size("rows") == 2:
        return from_next(value)
    return join(from_next(value), from_previous(value))


def join_grid(after, before):
    return jnp.concatenate([after[:, :, : BAND // 2], before[:, :, BAND // 2 :]], 2)


def join_region(after, before):
    tail = jnp.concatenate([after[:, :8, 2 * WIDTH :], before[:, 8:, 2 * WIDTH :]], 1)
    return jnp.concatenate([after[..., :WIDTH], before[..., WIDTH : 2 * WIDTH], tail], 2)


def join_inner(after, before):
    return jnp.concatenate([after[..., : WIDTH // 2], before[..., WIDTH // 2 :]], 2)


def vmem(count):
    return [pl.BlockSpec(memory_space=pltpu.VMEM)] * count


def observation_rows(obs_values, obs_inverse_variance, obs_mask):
    weight = (obs_mask.astype(F32) * obs_inverse_variance).astype(BF).astype(F32)
    high = obs_values.astype(BF).astype(F32)
    rest = obs_values - high
    middle = rest.astype(BF).astype(F32)
    low = rest - middle
    rows = jnp.stack([weight, high, middle, low], 0)
    rows = rows.reshape(4, FIELDS, 2, BAND // 2, PATCH)
    rows = jnp.transpose(rows, (2, 0, 1, 3, 4))
    rows = jnp.pad(rows, ((0, 0), (2, 2), (0, 0), (0, 0), (0, REGION - PATCH)))
    return rows.reshape(16, WIDTH)


def local(sample_collection, obs_values, obs_inverse_variance, obs_mask):
    count = lax.axis_size("mem")
    shape = sample_collection.shape
    assert shape == (LOCAL, FIELDS, BAND, WIDTH) and count * PATCH == WIDTH
    near = near_rows(sample_collection, join_grid)
    obs = observation_rows(obs_values, obs_inverse_variance, obs_mask)
    sending = pl.pallas_call(
        pack_kernel,
        out_shape=jax.ShapeDtypeStruct((count, LOCAL, 3 * WIDTH), BF),
        in_specs=vmem(3),
        out_specs=vmem(1)[0],
        name="forecast_pack",
    )(sample_collection.reshape(-1, WIDTH), near.reshape(-1, WIDTH), obs)
    region = lax.all_to_all(sending, "mem", split_axis=0, concat_axis=0, tiled=True)
    region_near = near_rows(region, join_region)
    me = lax.axis_index("mem").astype(jnp.int32).reshape(1)
    returning = pl.pallas_call(
        analysis_kernel,
        out_shape=jax.ShapeDtypeStruct((count, LOCAL, WIDTH), BF),
        in_specs=[pl.BlockSpec(memory_space=pltpu.SMEM)] + vmem(2),
        out_specs=vmem(1)[0],
        name="analysis",
    )(me, region, region_near)
    inner = lax.all_to_all(returning, "mem", split_axis=0, concat_axis=0, tiled=True)
    inner_near = near_rows(inner, join_inner)
    cycled = pl.pallas_call(
        unpack_kernel,
        out_shape=jax.ShapeDtypeStruct((LOCAL * FIELDS * BAND, WIDTH), F32),
        in_specs=vmem(2),
        out_specs=vmem(1)[0],
        name="unpack_forecast",
    )(inner, inner_near)
    return cycled.reshape(shape)


def solution(mesh):
    return jax.shard_map(
        local,
        mesh=mesh,
        in_specs=(
            P("mem", None, "rows", None),
            P(None, "rows", "mem"),
            P(None, "rows", "mem"),
            P(None, "rows", "mem"),
        ),
        out_specs=P("mem", None, "rows", None),
        check_vma=False,
    )
```

time: 68.7 us -> 43.4 us (0.63)
  starting transfers between devices: 21.8 us -> 0.46 us
  blocking collectives: 14.7 us -> 28.2 us
  waiting for transfers between devices: 13.3 us -> 2.69 us
  Pallas kernels: 0 us -> 8.16 us
  local copies, waits for them, and re-layouts: 9.48 us -> 2.67 us
  matrix products: 4.99 us -> 0 us
  other arithmetic: 2.7 us -> 0.8 us
  between operations: 1.3 us -> 0.05 us
    all_to_all x1 -> x2, blocking collectives: 14.7 us -> 28.2 us  [the longest x1 17.2 us: local(): lax.all_to_all(sending, 'mem', split_axis=0, concat_axis=0, tiled=True)]
    ppermute x12 -> x3, starting transfers between devices: 13.7 us -> 0.46 us  [from_next(): lax.ppermute(value, 'rows', [((i + 1) % count, i) for i in range(count)])]
    pallas_call x0 -> x3, Pallas kernels: none -> 8.16 us  [the longest x1 3.44 us: local(): pl.pallas_call(analysis_kernel, out_shape=jax.ShapeDtypeStruct((count, LO...]
    all_to_all x1 -> x0, starting transfers between devices: 8.15 us -> none  [local(): lax.all_to_all(sending, 'mem', split_axis=1, concat_axis=0, tiled=True)]
    all_to_all x1 -> x0, waiting for transfers between devices: 7.25 us -> none  [local(): lax.all_to_all(sending, 'mem', split_axis=1, concat_axis=0, tiled=True)]
    dot_general x13 -> x0, matrix products: 4.99 us -> none  [the longest x3 1.08 us: analyse(): middle = 1.5 * eye - 0.5 * jnp.matmul(iter_z, iter_y, precision=high)]
    slice x39 -> x0, local copies, waits for them, and re-layouts: 4.08 us -> none  [the longest x32 2.84 us: tendency(): along_x = jnp.roll(field, -1, -1) - jnp.roll(field, 1, -1)]
    ppermute x12 -> x3, waiting for transfers between devices: 6.05 us -> 2.69 us  [from_next(): lax.ppermute(value, 'rows', [((i + 1) % count, i) for i in range(count)])]
  transfers between devices with their start and end apart: 13 -> 3, of which waited for: 9 -> 2; matrix products, arithmetic and copies ran while one was open for 1% -> 4% of each run, Pallas kernels for 0% -> 0%
where the time goes in v1:
time: 43.4 us; the launch traced here: 43 us
  blocking collectives  28.2 us (65%)
  Pallas kernels  8.16 us (19%)
  waiting for transfers between devices  2.69 us (6%)
  local copies, waits for them, and re-layouts  2.67 us (6%)
  other arithmetic  0.8 us (2%)
  starting transfers between devices  0.46 us (1%)
    all_to_all x1, blocking collectives, local(): lax.all_to_all(sending, 'mem', split_axis=0, concat_axis=0, tiled=True)  17.2 us
    all_to_all x1, blocking collectives, local(): lax.all_to_all(returning, 'mem', split_axis=0, concat_axis=0, tiled=True)  11 us
    pallas_call x1, Pallas kernels, local(): pl.pallas_call(analysis_kernel, out_shape=jax.ShapeDtypeStruct((count, LO...  3.44 us
    ppermute x3, waiting for transfers between devices, from_next(): lax.ppermute(value, 'rows', [((i + 1) % count, i) for i in range(count)])  2.69 us
    pallas_call x1, Pallas kernels, local(): pl.pallas_call(pack_kernel, out_shape=jax.ShapeDtypeStruct((count, LOCAL,...  2.47 us
    pallas_call x1, Pallas kernels, local(): pl.pallas_call(unpack_kernel, out_shape=jax.ShapeDtypeStruct((LOCAL * FIE...  2.24 us
    unnamed x15, local copies, waits for them, and re-layouts  1.96 us
  transfers between devices with their start and end apart: 3, of which 2 were waited for; matrix products, arithmetic and copies ran while one was open for 4% of the time, Pallas kernels for 0%

profile of v1, /device:TPU:0, one launch (start us, length us, event | category | flops | bytes accessed | tf_op | source)
XLA Modules:
  0.0 43.0 jit_solution(8639491225817626627)
XLA Ops:
  0.0 0.0 copy-start.5
  0.0 0.5 %collective-permute-start = (f32[16,2,8,128]{3,2,1,0:T(8,128)}, f32[16,2,8,128]{3,2,1,0:T(8,128)S(1)}, u32[]{:S(2)}, u32[]{:S(2)}) collective-permute-start(f32[16,2,8,128]{3,2,1,0:T(8,128)} %param.4), channel_id=1, source_target_pairs={{1,0},{0,1},{3,2},{2,3},{5,4},{4,5},{7,6},{6,7},{9,8},{8,9},{11,10... | collective-permute-start | bytes 393224 | tf_op jit(solution)/shard_map/ppermute | solution.py:222
  0.5 0.8 %convert_convert_fusion.1 = (f32[2,8,8]{2,1,0:T(8,128)S(1)}, f32[2,8,8]{2,1,0:T(8,128)S(1)}, f32[2,8,8]{2,1,0:T(8,128)S(1)}) fusion(f32[2,8,8]{2,1,0:T(8,128)} %param.5), kind=kLoop, calls=%fused_computation.4 | loop fusion | flops 768 | bytes 2048 | tf_op jit(solution)/shard_map/convert_element_type | solution.py:255
  1.2 0.0 copy-done.6
  1.2 0.0 copy-done.5
  1.3 0.7 %reshape.28.obs_ref = f32[16,128]{1,0:T(8,128)} reshape(f32[2,8,2,4,16]{4,3,2,1,0:T(4,128)S(1)} %pad.4.clone) | data formatting | bytes 16384 | tf_op jit(solution)/shard_map/reshape | solution.py:263
  2.0 0.0 collective-permute-done
  2.0 0.0 copy-start.3
  2.0 0.7 %copy-done.3 = f32[16,2,8,128]{3,2,1,0:T(8,128)} copy-done((f32[16,2,8,128]{3,2,1,0:T(8,128)}, f32[16,2,8,128]{3,2,1,0:T(8,128)S(1)}, u32[]{:S(2)}) %copy-start.3) | copy-done | bytes 131096
  2.7 2.5 %forecast_pack.1 = bf16[16,16,384]{2,1,0:T(8,128)(2,1)} custom-call(f32[256,128]{1,0:T(8,128)} %bitcast.11, f32[256,128]{1,0:T(8,128)} %bitcast.12, f32[16,128]{1,0:T(8,128)} %reshape.28.obs_ref), custom_call_target="tpu_custom_call" | custom-call | tf_op jit(solution)/shard_map/forecast_pack/pallas_call | solution.py:272
  5.2 17.2 %all_to_all.10.own_ref = bf16[16,16,384]{2,1,0:T(8,128)(2,1)S(1)} all-to-all(bf16[16,16,384]{2,1,0:T(8,128)(2,1)} %forecast_pack.1), channel_id=1, replica_groups=mesh['mem'=16,'rows'=2] {'mem'}, dimensions={0} | all-to-all | bytes 393216 | tf_op jit(solution)/shard_map/all_to_all | solution.py:279
  22.3 0.0 copy-start
  22.3 0.0 collective-permute-start.1
  22.3 1.4 %collective-permute-done.1.near_ref = bf16[16,16,384]{2,1,0:T(8,128)(2,1)S(1)} collective-permute-done((bf16[16,16,384]{2,1,0:T(8,128)(2,1)S(1)}, bf16[16,16,384]{2,1,0:T(8,128)(2,1)S(1)}, u32[]{:S(2)}, u32[]{:S(2)}) %collective-permute-start.1) | collective-permute-done | bytes 196640 | tf_op jit(solution)/shard_map/ppermute | solution.py:222
  23.8 0.0 copy-start.2
  23.8 0.0 copy-done
  23.8 0.7 %copy-done.2 = bf16[16,16,384]{2,1,0:T(8,128)(2,1)} copy-done((bf16[16,16,384]{2,1,0:T(8,128)(2,1)}, bf16[16,16,384]{2,1,0:T(8,128)(2,1)S(1)}, u32[]{:S(2)}) %copy-start.2) | copy-done | bytes 196632
  24.4 3.4 %analysis.1 = bf16[16,16,128]{2,1,0:T(8,128)(2,1)} custom-call(s32[1]{0:T(128)} %bitcast.me_ref, bf16[16,16,384]{2,1,0:T(8,128)(2,1)} %copy-done, bf16[16,16,384]{2,1,0:T(8,128)(2,1)} %copy-done.2), custom_call_target="tpu_custom_call" | custom-call | tf_op jit(solution)/shard_map/analysis/pallas_call | solution.py:282
  27.9 11.0 %all_to_all.11.own_ref = bf16[16,16,128]{2,1,0:T(8,128)(2,1)S(1)} all-to-all(bf16[16,16,128]{2,1,0:T(8,128)(2,1)} %analysis.1), channel_id=1, replica_groups=mesh['mem'=16,'rows'=2] {'mem'}, dimensions={0} | all-to-all | bytes 131072 | tf_op jit(solution)/shard_map/all_to_all | solution.py:289
  38.9 0.0 collective-permute-start.2
  38.9 1.3 %collective-permute-done.2.near_ref = bf16[16,16,128]{2,1,0:T(8,128)(2,1)S(1)} collective-permute-done((bf16[16,16,128]{2,1,0:T(8,128)(2,1)S(1)}, bf16[16,16,128]{2,1,0:T(8,128)(2,1)S(1)}, u32[]{:S(2)}, u32[]{:S(2)}) %collective-permute-start.2) | collective-permute-done | bytes 65568 | tf_op jit(solution)/shard_map/ppermute | solution.py:222
  40.1 0.0 copy-done.1
  40.1 0.6 %copy-done.4 = bf16[16,16,128]{2,1,0:T(8,128)(2,1)} copy-done((bf16[16,16,128]{2,1,0:T(8,128)(2,1)}, bf16[16,16,128]{2,1,0:T(8,128)(2,1)S(1)}, u32[]{:S(2)}) %copy-start.4) | copy-done | bytes 65560
  40.8 2.2 %unpack_forecast.1 = f32[256,128]{1,0:T(8,128)} custom-call(bf16[16,16,128]{2,1,0:T(8,128)(2,1)} %copy-done.1, bf16[16,16,128]{2,1,0:T(8,128)(2,1)} %copy-done.4), custom_call_target="tpu_custom_call" | custom-call | tf_op jit(solution)/shard_map/unpack_forecast/pallas_call | solution.py:291
  (8 shorter events, 0.0 us)
Async XLA Ops:
  0.0 1.2 %copy-start.6 = (s32[2,8,8]{2,1,0:T(8,128)S(1)}, s32[2,8,8]{2,1,0:T(8,128)}, u32[]{:S(2)}) copy-start(s32[2,8,8]{2,1,0:T(8,128)} %param.7) | copy-start | bytes 1540
  0.0 1.2 %copy-start.5 = (f32[2,8,8]{2,1,0:T(8,128)S(1)}, f32[2,8,8]{2,1,0:T(8,128)}, u32[]{:S(2)}) copy-start(f32[2,8,8]{2,1,0:T(8,128)} %param.6) | copy-start | bytes 1540
  0.0 2.0 %collective-permute-start = (f32[16,2,8,128]{3,2,1,0:T(8,128)}, f32[16,2,8,128]{3,2,1,0:T(8,128)S(1)}, u32[]{:S(2)}, u32[]{:S(2)}) collective-permute-start(f32[16,2,8,128]{3,2,1,0:T(8,128)} %param.4), channel_id=1, source_target_pairs={{1,0},{0,1},{3,2},{2,3},{5,4},{4,5},{7,6},{6,7},{9,8},{8,9},{11,10... | collective-permute-start | bytes 393224 | tf_op jit(solution)/shard_map/ppermute | solution.py:222
  2.0 0.7 %copy-start.3 = (f32[16,2,8,128]{3,2,1,0:T(8,128)}, f32[16,2,8,128]{3,2,1,0:T(8,128)S(1)}, u32[]{:S(2)}) copy-start(f32[16,2,8,128]{3,2,1,0:T(8,128)S(1)} %collective-permute-done) | copy-start | bytes 393220
  22.3 1.4 %copy-start = (bf16[16,16,384]{2,1,0:T(8,128)(2,1)}, bf16[16,16,384]{2,1,0:T(8,128)(2,1)S(1)}, u32[]{:S(2)}) copy-start(bf16[16,16,384]{2,1,0:T(8,128)(2,1)S(1)} %all_to_all.10.own_ref) | copy-start | bytes 589828
  22.3 1.4 %collective-permute-start.1 = (bf16[16,16,384]{2,1,0:T(8,128)(2,1)S(1)}, bf16[16,16,384]{2,1,0:T(8,128)(2,1)S(1)}, u32[]{:S(2)}, u32[]{:S(2)}) collective-permute-start(bf16[16,16,384]{2,1,0:T(8,128)(2,1)S(1)} %all_to_all.10.own_ref), channel_id=1, source_target_pairs={{1,0},{0,1},{3,2},{2,3},{5,4},{4,5},{7,6},{6,7},{9,8},{8,9},{11,10... | collective-permute-start | bytes 589832 | tf_op jit(solution)/shard_map/ppermute | solution.py:222
  23.8 0.7 %copy-start.2 = (bf16[16,16,384]{2,1,0:T(8,128)(2,1)}, bf16[16,16,384]{2,1,0:T(8,128)(2,1)S(1)}, u32[]{:S(2)}) copy-start(bf16[16,16,384]{2,1,0:T(8,128)(2,1)S(1)} %collective-permute-done.1.near_ref) | copy-start | bytes 589828
  38.9 1.3 %copy-start.1 = (bf16[16,16,128]{2,1,0:T(8,128)(2,1)}, bf16[16,16,128]{2,1,0:T(8,128)(2,1)S(1)}, u32[]{:S(2)}) copy-start(bf16[16,16,128]{2,1,0:T(8,128)(2,1)S(1)} %all_to_all.11.own_ref) | copy-start | bytes 196612
  38.9 1.3 %collective-permute-start.2 = (bf16[16,16,128]{2,1,0:T(8,128)(2,1)S(1)}, bf16[16,16,128]{2,1,0:T(8,128)(2,1)S(1)}, u32[]{:S(2)}, u32[]{:S(2)}) collective-permute-start(bf16[16,16,128]{2,1,0:T(8,128)(2,1)S(1)} %all_to_all.11.own_ref), channel_id=1, source_target_pairs={{1,0},{0,1},{3,2},{2,3},{5,4},{4,5},{7,6},{6,7},{9,8},{8,9},{11,10... | collective-permute-start | bytes 196616 | tf_op jit(solution)/shard_map/ppermute | solution.py:222
  40.1 0.6 %copy-start.4 = (bf16[16,16,128]{2,1,0:T(8,128)(2,1)}, bf16[16,16,128]{2,1,0:T(8,128)(2,1)S(1)}, u32[]{:S(2)}) copy-start(bf16[16,16,128]{2,1,0:T(8,128)(2,1)S(1)} %collective-permute-done.2.near_ref) | copy-start | bytes 196612

commit v2 on v1

--- a/solution.py
+++ b/solution.py
@@ -17,8 +17,7 @@
 BAND = 8
 WIDTH = 128
 REGION = PATCH + 2 * RADIUS
-HALF = FIELDS * (BAND // 2) * REGION
-BLOCKS = 2 * FIELDS * (BAND // 2)
+GROUP = 4
 
 BF = jnp.bfloat16
 F32 = jnp.float32
@@ -54,7 +53,36 @@
     return parts
 
 
-def pack_kernel(x_ref, near_ref, obs_ref, out_ref):
+def xor_blocks(me, high, low):
+    return ((me // GROUP) ^ high) * GROUP + ((me % GROUP) ^ low)
+
+
+def observation_rows(values_ref, inverse_ref, mask_ref):
+    points = FIELDS * BAND
+    weight = (mask_ref[...].astype(F32) * inverse_ref[...]).astype(BF).astype(F32).reshape(points, PATCH)
+    values = values_ref[...].reshape(points, PATCH)
+    high = values.astype(BF).astype(F32)
+    middle = (values - high).astype(BF).astype(F32)
+    low = values - high - middle
+    rows = jnp.concatenate([weight, high, middle, low], 0).astype(BF)
+    source = lax.broadcasted_iota(jnp.int32, (PATCH, WIDTH), 0)
+    lane = lax.broadcasted_iota(jnp.int32, (PATCH, WIDTH), 1)
+    spread = (lane % PATCH == source).astype(F32).astype(BF)
+    wide = jnp.dot(rows, spread, preferred_element_type=F32)
+    row = lax.broadcasted_iota(jnp.int32, wide.shape, 0)
+    lane = lax.broadcasted_iota(jnp.int32, wide.shape, 1)
+    part, field, y = row // points, (row % points) // BAND, row % BAND
+    place = (field * (BAND // 2) + y % (BAND // 2)) * 2 + part % 2
+    wide = jnp.where(lane // PATCH == place, wide, 0.0).astype(BF)
+    target = lax.broadcasted_iota(jnp.int32, (8, 4 * points), 0)
+    row = lax.broadcasted_iota(jnp.int32, (8, 4 * points), 1)
+    wanted = ((row % BAND) // (BAND // 2)) * 4 + 2 + row // (2 * points)
+    gather = (target == wanted).astype(F32).astype(BF)
+    return jnp.dot(gather, wide, preferred_element_type=F32)
+
+
+def pack_kernel(me_ref, x_ref, near_ref, values_ref, inverse_ref, mask_ref, *refs):
+    outs, blocks = refs[:GROUP], refs[GROUP]
     stride = FIELDS * BAND
 
     def row(ref, field, index):
@@ -68,6 +96,7 @@
         fields.append(before + own + after)
     done = forecast_rows(*fields)
     stacked = []
+    index = lax.broadcasted_iota(jnp.int32, (8, WIDTH), 0)
     for half in range(2):
         for field in range(FIELDS):
             for r in range(BAND // 2):
@@ -75,8 +104,7 @@
                 mean = jnp.sum(value, 0, keepdims=True) * (1.0 / LOCAL)
                 high = mean.astype(BF).astype(F32)
                 low = mean - high
-                index = lax.broadcasted_iota(jnp.int32, (8, WIDTH), 0)
-                tail = jnp.where(index == 0, high, jnp.where(index == 1, low, 0.0))
+                tail = jnp.where(index == 4 * half, high, jnp.where(index == 4 * half + 1, low, 0.0))
                 stacked += [value - mean, tail]
     rows = jnp.concatenate(stacked, 0).astype(BF)
     column = lax.broadcasted_iota(jnp.int32, (WIDTH, 2 * WIDTH), 0)
@@ -85,8 +113,9 @@
     widen = (column == wanted).astype(F32).astype(BF)
     wide = jnp.dot(rows, widen, preferred_element_type=F32)
     height = LOCAL + 8
+    obs = observation_rows(values_ref, inverse_ref, mask_ref)
     for side in range(2):
-        tails = [[], []]
+        tails = [obs] * 8
         for half in range(2):
             parts = [
                 wide[(half * 8 + j) * height : (half * 8 + j + 1) * height, side * WIDTH : (side + 1) * WIDTH]
@@ -94,49 +123,82 @@
             ]
             parts = swap_blocks(parts, REGION)
             for i in range(8):
-                out_ref[side * 8 + i, :, half * WIDTH : (half + 1) * WIDTH] = parts[i][:LOCAL].astype(BF)
-                tails[half].append(parts[i][LOCAL:])
+                for eight in range(2):
+                    blocks[side * 8 + i, half * 2 + eight] = parts[i][eight * 8 : eight * 8 + 8].astype(BF)
+                tails[i] = tails[i] + parts[i][LOCAL:]
         for i in range(8):
-            tail = jnp.concatenate([tails[0][i], tails[1][i]], 0) + obs_ref[...]
-            out_ref[side * 8 + i, :, 2 * WIDTH :] = tail.astype(BF)
-
-
-def halves_of(ref, me, count):
-    tails = [ref[s, :, 2 * WIDTH :].astype(F32) for s in range(count)]
-    lane = lax.broadcasted_iota(jnp.int32, (16, WIDTH), 1) % REGION
-    left = ref[lax.rem(me + count - 1, count), :, 2 * WIDTH :].astype(F32)
-    own = ref[me, :, 2 * WIDTH :].astype(F32)
-    right = ref[lax.rem(me + 1, count), :, 2 * WIDTH :].astype(F32)
-    seen = jnp.where(
-        lane < RADIUS,
-        pltpu.roll(left, WIDTH - (PATCH - RADIUS), 1),
-        jnp.where(lane < RADIUS + PATCH, pltpu.roll(own, RADIUS, 1), pltpu.roll(right, RADIUS + PATCH, 1)),
-    )
+            blocks[side * 8 + i, 4] = tails[i].astype(BF)
+    low = me_ref[0] % GROUP
+    for k in range(GROUP):
+        for high in range(GROUP):
+            outs[k][high] = blocks[high * GROUP + (low ^ k)]
+
+
+def regroup_region_kernel(me_ref, *refs):
+    ins, outs = refs[:GROUP], refs[GROUP:]
+    high = me_ref[0] // GROUP
+    for j in range(GROUP):
+        for k in range(GROUP):
+            outs[j][k] = ins[k][high ^ j]
+
+
+def regroup_inner_kernel(*refs):
+    ins, outs = refs[:GROUP], refs[GROUP:]
+    for k in range(GROUP):
+        for j in range(GROUP):
+            outs[k][j] = ins[j][k]
+
+
+def halves_of(refs, tail_ref, me):
+    count = GROUP * GROUP
+    blocks = [(refs[j], k) for j in range(GROUP) for k in range(GROUP)]
+    tails = [ref[k, 4].astype(F32) for ref, k in blocks]
+    for s in range(count):
+        tail_ref[s] = tails[s]
+
+    def tail_of(device):
+        return tail_ref[xor_blocks(me, device // GROUP, device % GROUP)]
+
+    lane = lax.broadcasted_iota(jnp.int32, (8, WIDTH), 1) % REGION
+    left = tail_of(lax.rem(me + count - 1, count))
+    own = tails[0]
+    right = tail_of(lax.rem(me + 1, count))
+
+    def seen(offset):
+        return jnp.where(
+            lane < RADIUS,
+            pltpu.roll(left, (WIDTH + RADIUS - PATCH - offset) % WIDTH, 1),
+            jnp.where(
+                lane < RADIUS + PATCH,
+                pltpu.roll(own, (WIDTH + RADIUS - offset) % WIDTH, 1),
+                pltpu.roll(right, (WIDTH + RADIUS + PATCH - offset) % WIDTH, 1),
+            ),
+        )
+
+    first, second = seen(0), seen(PATCH)
     result = []
     for half in range(2):
-        base = half * 8
+        base = half * 4
         means = [t[base : base + 1] + t[base + 1 : base + 2] for t in tails]
         mean = functools.reduce(jnp.add, means) * (1.0 / count)
-        deviation = jnp.concatenate(
-            [
-                (ref[s, :, half * WIDTH : (half + 1) * WIDTH].astype(F32) + (means[s] - mean)).astype(BF)
-                for s in range(count)
-            ],
-            0,
-        )
-        weight = seen[base + 2 : base + 3]
-        obs = seen[base + 3 : base + 4] + seen[base + 4 : base + 5] + seen[base + 5 : base + 6]
+        deviation = []
+        for (ref, k), own_mean in zip(blocks, means):
+            value = jnp.concatenate([ref[k, half * 2 + eight].astype(F32) for eight in range(2)], 0)
+            deviation.append((value + (own_mean - mean)).astype(BF))
+        weight = first[base + 2 : base + 3]
+        obs = second[base + 2 : base + 3] + first[base + 3 : base + 4] + second[base + 3 : base + 4]
         innovation = (obs - mean).astype(BF).astype(F32)
-        result.append((deviation, mean, weight, innovation))
+        result.append((jnp.concatenate(deviation, 0), mean, weight, innovation))
     return result
 
 
-def analysis_kernel(me_ref, own_ref, near_ref, out_ref):
-    count = own_ref.shape[0]
-    members = count * LOCAL
+def analysis_kernel(me_ref, *refs):
+    own_refs, near_refs, outs = refs[:GROUP], refs[GROUP : 2 * GROUP], refs[2 * GROUP : 3 * GROUP]
+    tail_ref, near_tail_ref = refs[3 * GROUP :]
+    members = GROUP * GROUP * LOCAL
     me = me_ref[0]
-    own = halves_of(own_ref, me, count)
-    near = halves_of(near_ref, me, count)
+    own = halves_of(own_refs, tail_ref, me)
+    near = halves_of(near_refs, near_tail_ref, me)
     lane = lax.broadcasted_iota(jnp.int32, (1, WIDTH), 1)
     region_column = lane % REGION
     half_row = (lane // REGION) % (BAND // 2)
@@ -194,22 +256,28 @@
     target = lax.broadcasted_iota(jnp.int32, (2 * WIDTH, WIDTH), 1)
     narrow = (lane == (target // PATCH) * REGION + RADIUS + target % PATCH).astype(F32).astype(BF)
     result = jnp.dot(result, narrow, preferred_element_type=F32).astype(BF)
-    for s in range(count):
-        out_ref[s] = result[s * LOCAL : (s + 1) * LOCAL]
-
-
-def unpack_kernel(own_ref, near_ref, out_ref):
-    count = own_ref.shape[0]
-
-    def rows_of(ref):
-        parts = swap_blocks([ref[p].astype(F32) for p in range(count)], PATCH)
+    for j in range(GROUP):
+        for k in range(GROUP):
+            start = (j * GROUP + k) * LOCAL
+            outs[j][k] = result[start : start + LOCAL]
+
+
+def unpack_kernel(me_ref, *refs):
+    own_refs, near_refs, out_ref = refs[:GROUP], refs[GROUP : 2 * GROUP], refs[2 * GROUP]
+    me = me_ref[0]
+
+    def rows_of(ins, blocks):
+        for k in range(GROUP):
+            for j in range(GROUP):
+                blocks[xor_blocks(me, j, k)] = ins[k][j].astype(F32)
+        parts = swap_blocks([blocks[p] for p in range(GROUP * GROUP)], PATCH)
         half = BAND // 2
         return [
             [parts[h * FIELDS * half + field * half + r] for h in range(2) for r in range(half)]
             for field in range(FIELDS)
         ]
 
-    own, near = rows_of(own_ref), rows_of(near_ref)
+    own, near = rows_of(own_refs, refs[2 * GROUP + 1]), rows_of(near_refs, refs[2 * GROUP + 2])
     fields = [n[BAND - FSTEPS :] + o + n[:FSTEPS] for o, n in zip(own, near)]
     done = forecast_rows(*fields)
     for field in range(FIELDS):
@@ -238,63 +306,79 @@
 
 
 def join_region(after, before):
-    tail = jnp.concatenate([after[:, :8, 2 * WIDTH :], before[:, 8:, 2 * WIDTH :]], 1)
-    return jnp.concatenate([after[..., :WIDTH], before[..., WIDTH : 2 * WIDTH], tail], 2)
+    tail = jnp.concatenate([after[:, 4:, :4], before[:, 4:, 4:]], 2)
+    return jnp.concatenate([after[:, :2], before[:, 2:4], tail], 1)
 
 
 def join_inner(after, before):
     return jnp.concatenate([after[..., : WIDTH // 2], before[..., WIDTH // 2 :]], 2)
 
 
-def vmem(count):
-    return [pl.BlockSpec(memory_space=pltpu.VMEM)] * count
-
-
-def observation_rows(obs_values, obs_inverse_variance, obs_mask):
-    weight = (obs_mask.astype(F32) * obs_inverse_variance).astype(BF).astype(F32)
-    high = obs_values.astype(BF).astype(F32)
-    rest = obs_values - high
-    middle = rest.astype(BF).astype(F32)
-    low = rest - middle
-    rows = jnp.stack([weight, high, middle, low], 0)
-    rows = rows.reshape(4, FIELDS, 2, BAND // 2, PATCH)
-    rows = jnp.transpose(rows, (2, 0, 1, 3, 4))
-    rows = jnp.pad(rows, ((0, 0), (2, 2), (0, 0), (0, 0), (0, REGION - PATCH)))
-    return rows.reshape(16, WIDTH)
+def from_partner(value, distance):
+    return lax.ppermute(value, "mem", [(i, i ^ distance) for i in range(lax.axis_size("mem"))])
+
+
+def exchange(values, unit):
+    return [values[0]] + [from_partner(values[k], k * unit) for k in range(1, GROUP)]
+
+
+def call(kernel, name, out_shape, *args, scratch=()):
+    spaces = [pltpu.SMEM if arg.shape == (1,) else pltpu.VMEM for arg in args]
+    return pl.pallas_call(
+        kernel,
+        out_shape=out_shape,
+        in_specs=[pl.BlockSpec(memory_space=space) for space in spaces],
+        out_specs=jax.tree.map(lambda _: pl.BlockSpec(memory_space=pltpu.VMEM), out_shape),
+        scratch_shapes=scratch,
+        compiler_params=pltpu.CompilerParams(vmem_limit_bytes=16 * 2**20),
+        name=name,
+    )(*args)
 
 
 def local(sample_collection, obs_values, obs_inverse_variance, obs_mask):
     count = lax.axis_size("mem")
     shape = sample_collection.shape
-    assert shape == (LOCAL, FIELDS, BAND, WIDTH) and count * PATCH == WIDTH
+    assert shape == (LOCAL, FIELDS, BAND, WIDTH) and count * PATCH == WIDTH and count == GROUP * GROUP
+    me = lax.axis_index("mem").astype(jnp.int32).reshape(1)
     near = near_rows(sample_collection, join_grid)
-    obs = observation_rows(obs_values, obs_inverse_variance, obs_mask)
-    sending = pl.pallas_call(
+    region_shape = [jax.ShapeDtypeStruct((GROUP, 5, 8, WIDTH), BF)] * GROUP
+    inner_shape = [jax.ShapeDtypeStruct((GROUP, LOCAL, WIDTH), BF)] * GROUP
+    sending = call(
         pack_kernel,
-        out_shape=jax.ShapeDtypeStruct((count, LOCAL, 3 * WIDTH), BF),
-        in_specs=vmem(3),
-        out_specs=vmem(1)[0],
-        name="forecast_pack",
-    )(sample_collection.reshape(-1, WIDTH), near.reshape(-1, WIDTH), obs)
-    region = lax.all_to_all(sending, "mem", split_axis=0, concat_axis=0, tiled=True)
-    region_near = near_rows(region, join_region)
-    me = lax.axis_index("mem").astype(jnp.int32).reshape(1)
-    returning = pl.pallas_call(
+        "forecast_pack",
+        region_shape,
+        me,
+        sample_collection.reshape(-1, WIDTH),
+        near.reshape(-1, WIDTH),
+        obs_values,
+        obs_inverse_variance,
+        obs_mask,
+        scratch=[pltpu.VMEM((count, 5, 8, WIDTH), BF)],
+    )
+    sending = call(regroup_region_kernel, "regroup_region", region_shape, me, *exchange(sending, 1))
+    region = exchange(sending, GROUP)
+    region_near = [near_rows(value, join_region) for value in region]
+    returning = call(
         analysis_kernel,
-        out_shape=jax.ShapeDtypeStruct((count, LOCAL, WIDTH), BF),
-        in_specs=[pl.BlockSpec(memory_space=pltpu.SMEM)] + vmem(2),
-        out_specs=vmem(1)[0],
-        name="analysis",
-    )(me, region, region_near)
-    inner = lax.all_to_all(returning, "mem", split_axis=0, concat_axis=0, tiled=True)
-    inner_near = near_rows(inner, join_inner)
-    cycled = pl.pallas_call(
+        "analysis",
+        inner_shape,
+        me,
+        *region,
+        *region_near,
+        scratch=[pltpu.VMEM((count, 8, WIDTH), F32)] * 2,
+    )
+    returning = call(regroup_inner_kernel, "regroup_inner", inner_shape, *exchange(returning, GROUP))
+    inner = exchange(returning, 1)
+    inner_near = [near_rows(value, join_inner) for value in inner]
+    cycled = call(
         unpack_kernel,
-        out_shape=jax.ShapeDtypeStruct((LOCAL * FIELDS * BAND, WIDTH), F32),
-        in_specs=vmem(2),
-        out_specs=vmem(1)[0],
-        name="unpack_forecast",
-    )(inner, inner_near)
+        "unpack_forecast",
+        jax.ShapeDtypeStruct((LOCAL * FIELDS * BAND, WIDTH), F32),
+        me,
+        *inner,
+        *inner_near,
+        scratch=[pltpu.VMEM((count, LOCAL, WIDTH), F32)] * 2,
+    )
     return cycled.reshape(shape)
 
 

time: 43.4 us -> 42.5 us (0.979)
  blocking collectives: 28.2 us -> 0 us
  starting transfers between devices: 0.46 us -> 18.1 us
  waiting for transfers between devices: 2.69 us -> 17.6 us
  Pallas kernels: 8.16 us -> 4.26 us
  other arithmetic: 0.8 us -> 0 us
    all_to_all x2 -> x0, blocking collectives: 28.2 us -> none  [the longest x1 17.2 us: local(): lax.all_to_all(sending, 'mem', split_axis=0, concat_axis=0, tiled=True)]
    ppermute x0 -> x12, starting transfers between devices: none -> 16.8 us  [from_partner(): lax.ppermute(value, 'mem', [(i, i ^ distance) for i in range(lax.axis_siz...]
    ppermute x0 -> x12, waiting for transfers between devices: none -> 14 us  [from_partner(): lax.ppermute(value, 'mem', [(i, i ^ distance) for i in range(lax.axis_siz...]
    pallas_call x3 -> x5, Pallas kernels: 8.16 us -> 4.26 us  [call(): pl.pallas_call(kernel, out_shape=out_shape, in_specs=[pl.BlockSpec(memory...]
    ppermute x3 -> x9, waiting for transfers between devices: 2.69 us -> 3.57 us  [from_next(): lax.ppermute(value, 'rows', [((i + 1) % count, i) for i in range(count)])]
    ppermute x3 -> x9, starting transfers between devices: 0.46 us -> 1.24 us  [from_next(): lax.ppermute(value, 'rows', [((i + 1) % count, i) for i in range(count)])]
    convert_element_type x2 -> x0, other arithmetic: 0.78 us -> none  [the longest x1 0.78 us: observation_rows(): high = obs_values.astype(BF).astype(F32)]
    reshape x1 -> x0, local copies, waits for them, and re-layouts: 0.7 us -> none  [observation_rows(): return rows.reshape(16, WIDTH)]
  transfers between devices with their start and end apart: 3 -> 21, of which waited for: 2 -> 13; matrix products, arithmetic and copies ran while one was open for 4% -> 0% of each run, Pallas kernels for 0% -> 0%
where the time goes in v2:
time: 42.5 us; the launch traced here: 42.3 us
  starting transfers between devices  18.1 us (43%)
  waiting for transfers between devices  17.6 us (41%)
  Pallas kernels  4.26 us (10%)
  local copies, waits for them, and re-layouts  2.3 us (5%)
    ppermute x12, starting transfers between devices, from_partner(): lax.ppermute(value, 'mem', [(i, i ^ distance) for i in range(lax.axis_siz...  16.8 us
    ppermute x12, waiting for transfers between devices, from_partner(): lax.ppermute(value, 'mem', [(i, i ^ distance) for i in range(lax.axis_siz...  14 us
    pallas_call x5, Pallas kernels, call(): pl.pallas_call(kernel, out_shape=out_shape, in_specs=[pl.BlockSpec(memory...  4.26 us
    ppermute x9, waiting for transfers between devices, from_next(): lax.ppermute(value, 'rows', [((i + 1) % count, i) for i in range(count)])  3.57 us
    unnamed x8, local copies, waits for them, and re-layouts  2.3 us
    ppermute x9, starting transfers between devices, from_next(): lax.ppermute(value, 'rows', [((i + 1) % count, i) for i in range(count)])  1.24 us
  transfers between devices with their start and end apart: 21, of which 13 were waited for; matrix products, arithmetic and copies ran while one was open for 0% of the time, Pallas kernels for 0%

profile of v2, /device:TPU:0, one launch (start us, length us, event | category | flops | bytes accessed | tf_op | source)
XLA Modules:
  0.0 42.3 jit_solution(17787286829031561400)
XLA Ops:
  0.5 1.2 %collective-permute-done = f32[16,2,8,128]{3,2,1,0:T(8,128)S(1)} collective-permute-done((f32[16,2,8,128]{3,2,1,0:T(8,128)}, f32[16,2,8,128]{3,2,1,0:T(8,128)S(1)}, u32[]{:S(2)}, u32[]{:S(2)}) %collective-permute-start) | collective-permute-done | bytes 131104 | tf_op jit(solution)/shard_map/ppermute | solution.py:290
  1.7 0.9 %copy-done = f32[16,2,8,128]{3,2,1,0:T(8,128)S(1)} copy-done((f32[16,2,8,128]{3,2,1,0:T(8,128)S(1)}, f32[16,2,8,128]{3,2,1,0:T(8,128)}, u32[]{:S(2)}) %copy-start) | copy-done | bytes 131096
  2.6 0.7 %copy-done.2 = f32[2,8,8]{2,1,0:T(8,128)S(1)} copy-done((f32[2,8,8]{2,1,0:T(8,128)S(1)}, f32[2,8,8]{2,1,0:T(8,128)}, u32[]{:S(2)}) %copy-start.2) | copy-done | bytes 536
  3.3 0.7 %copy-done.3 = s32[2,8,8]{2,1,0:T(8,128)S(1)} copy-done((s32[2,8,8]{2,1,0:T(8,128)S(1)}, s32[2,8,8]{2,1,0:T(8,128)}, u32[]{:S(2)}) %copy-start.3) | copy-done | bytes 536
  4.0 0.8 %forecast_pack.1 = (bf16[4,5,8,128]{3,2,1,0:T(8,128)(2,1)S(1)}, bf16[4,5,8,128]{3,2,1,0:T(8,128)(2,1)S(1)}, bf16[4,5,8,128]{3,2,1,0:T(8,128)(2,1)S(1)}, bf16[4,5,8,128]{3,2,1,0:T(8,128)(2,1)S(1)}) custom-call(s32[1]{0:T(128)} %bitcast.me_ref, f32[256,128]{1,0:T(8,128)S(1)} %bitcast.4, f32[256,128]{1,0:T(8,128)S(1)} %bitcast.5, f32[2,8,8]{2,1,0:T(8,128)S(1)} %copy-done.1, ...), custom_call_target="tpu_custom_call" | custom-call | tf_op jit(solution)/shard_map/forecast_pack/pallas_call | solution.py:327
  4.8 2.9 %collective-permute-start.1 = (bf16[4,5,8,128]{3,2,1,0:T(8,128)(2,1)S(1)}, bf16[4,5,8,128]{3,2,1,0:T(8,128)(2,1)S(1)}, u32[]{:S(2)}, u32[]{:S(2)}) collective-permute-start(bf16[4,5,8,128]{3,2,1,0:T(8,128)(2,1)S(1)} %get-tuple-element.22), channel_id=1, source_target_pairs={{0,2},{2,0},{4,6},{6,4},{8,10},{10,8},{12,14},{14,12},{16,18},{18,... | collective-permute-start | bytes 122888 | tf_op jit(solution)/shard_map/ppermute | solution.py:318
  7.7 1.5 %collective-permute-start.2 = (bf16[4,5,8,128]{3,2,1,0:T(8,128)(2,1)S(1)}, bf16[4,5,8,128]{3,2,1,0:T(8,128)(2,1)S(1)}, u32[]{:S(2)}, u32[]{:S(2)}) collective-permute-start(bf16[4,5,8,128]{3,2,1,0:T(8,128)(2,1)S(1)} %get-tuple-element.23), channel_id=1, source_target_pairs={{0,4},{2,6},{4,0},{6,2},{8,12},{10,14},{12,8},{14,10},{16,20},{18,... | collective-permute-start | bytes 122888 | tf_op jit(solution)/shard_map/ppermute | solution.py:318
  9.7 2.0 %collective-permute-done.2.refs_2_ = bf16[4,5,8,128]{3,2,1,0:T(8,128)(2,1)S(1)} collective-permute-done((bf16[4,5,8,128]{3,2,1,0:T(8,128)(2,1)S(1)}, bf16[4,5,8,128]{3,2,1,0:T(8,128)(2,1)S(1)}, u32[]{:S(2)}, u32[]{:S(2)}) %collective-permute-start.2) | collective-permute-done | bytes 40992 | tf_op jit(solution)/shard_map/ppermute | solution.py:318
  11.7 2.4 %collective-permute-done.3.refs_3_ = bf16[4,5,8,128]{3,2,1,0:T(8,128)(2,1)S(1)} collective-permute-done((bf16[4,5,8,128]{3,2,1,0:T(8,128)(2,1)S(1)}, bf16[4,5,8,128]{3,2,1,0:T(8,128)(2,1)S(1)}, u32[]{:S(2)}, u32[]{:S(2)}) %collective-permute-start.3) | collective-permute-done | bytes 40992 | tf_op jit(solution)/shard_map/ppermute | solution.py:318
  14.2 1.6 %collective-permute-start.4 = (bf16[4,5,8,128]{3,2,1,0:T(8,128)(2,1)S(1)}, bf16[4,5,8,128]{3,2,1,0:T(8,128)(2,1)S(1)}, u32[]{:S(2)}, u32[]{:S(2)}) collective-permute-start(bf16[4,5,8,128]{3,2,1,0:T(8,128)(2,1)S(1)} %get-tuple-element.26), channel_id=1, source_target_pairs={{0,8},{2,10},{4,12},{6,14},{8,0},{10,2},{12,4},{14,6},{16,24},{18,... | collective-permute-start | bytes 122888 | tf_op jit(solution)/shard_map/ppermute | solution.py:318
  15.8 2.6 %collective-permute-start.5 = (bf16[4,5,8,128]{3,2,1,0:T(8,128)(2,1)S(1)}, bf16[4,5,8,128]{3,2,1,0:T(8,128)(2,1)S(1)}, u32[]{:S(2)}, u32[]{:S(2)}) collective-permute-start(bf16[4,5,8,128]{3,2,1,0:T(8,128)(2,1)S(1)} %get-tuple-element.27), channel_id=1, source_target_pairs={{0,16},{2,18},{4,20},{6,22},{8,24},{10,26},{12,28},{14,30},{16,0},... | collective-permute-start | bytes 122888 | tf_op jit(solution)/shard_map/ppermute | solution.py:318
  18.6 0.5 %collective-permute-start.8 = (bf16[4,5,8,128]{3,2,1,0:T(8,128)(2,1)S(1)}, bf16[4,5,8,128]{3,2,1,0:T(8,128)(2,1)S(1)}, u32[]{:S(2)}, u32[]{:S(2)}) collective-permute-start(bf16[4,5,8,128]{3,2,1,0:T(8,128)(2,1)S(1)} %collective-permute-done.4.refs_1_), channel_id=1, source_target_pairs={{1,0},{0,1},{3,2},{2,3},{5,4},{4,5},{7,6},{6,7},{9,8},{8,9},{11,10... | collective-permute-start | bytes 122888 | tf_op jit(solution)/shard_map/ppermute | solution.py:290
  19.1 2.4 %collective-permute-done.5.refs_2_ = bf16[4,5,8,128]{3,2,1,0:T(8,128)(2,1)S(1)} collective-permute-done((bf16[4,5,8,128]{3,2,1,0:T(8,128)(2,1)S(1)}, bf16[4,5,8,128]{3,2,1,0:T(8,128)(2,1)S(1)}, u32[]{:S(2)}, u32[]{:S(2)}) %collective-permute-start.5) | collective-permute-done | bytes 40992 | tf_op jit(solution)/shard_map/ppermute | solution.py:318
  21.6 2.6 %collective-permute-done.6.refs_3_ = bf16[4,5,8,128]{3,2,1,0:T(8,128)(2,1)S(1)} collective-permute-done((bf16[4,5,8,128]{3,2,1,0:T(8,128)(2,1)S(1)}, bf16[4,5,8,128]{3,2,1,0:T(8,128)(2,1)S(1)}, u32[]{:S(2)}, u32[]{:S(2)}) %collective-permute-start.6) | collective-permute-done | bytes 40992 | tf_op jit(solution)/shard_map/ppermute | solution.py:318
  24.2 1.2 %collective-permute-done.10.refs_7_ = bf16[4,5,8,128]{3,2,1,0:T(8,128)(2,1)S(1)} collective-permute-done((bf16[4,5,8,128]{3,2,1,0:T(8,128)(2,1)S(1)}, bf16[4,5,8,128]{3,2,1,0:T(8,128)(2,1)S(1)}, u32[]{:S(2)}, u32[]{:S(2)}) %collective-permute-start.10) | collective-permute-done | bytes 40992 | tf_op jit(solution)/shard_map/ppermute | solution.py:290
  25.4 1.8 %analysis.1 = (bf16[4,16,128]{2,1,0:T(8,128)(2,1)S(1)}, bf16[4,16,128]{2,1,0:T(8,128)(2,1)S(1)}, bf16[4,16,128]{2,1,0:T(8,128)(2,1)S(1)}, bf16[4,16,128]{2,1,0:T(8,128)(2,1)S(1)}) custom-call(s32[1]{0:T(128)} %bitcast.me_ref, bf16[4,5,8,128]{3,2,1,0:T(8,128)(2,1)S(1)} %get-tuple-element.25.refs_0_, ...), custom_call_target="tpu_custom_call" | custom-call | tf_op jit(solution)/shard_map/analysis/pallas_call | solution.py:327
  27.3 1.0 %collective-permute-start.12 = (bf16[4,16,128]{2,1,0:T(8,128)(2,1)S(1)}, bf16[4,16,128]{2,1,0:T(8,128)(2,1)S(1)}, u32[]{:S(2)}, u32[]{:S(2)}) collective-permute-start(bf16[4,16,128]{2,1,0:T(8,128)(2,1)S(1)} %get-tuple-element.31), channel_id=1, source_target_pairs={{0,16},{2,18},{4,20},{6,22},{8,24},{10,26},{12,28},{14,30},{16,0},... | collective-permute-start | bytes 49160 | tf_op jit(solution)/shard_map/ppermute | solution.py:318
  28.3 3.4 %collective-permute-start.13 = (bf16[4,16,128]{2,1,0:T(8,128)(2,1)S(1)}, bf16[4,16,128]{2,1,0:T(8,128)(2,1)S(1)}, u32[]{:S(2)}, u32[]{:S(2)}) collective-permute-start(bf16[4,16,128]{2,1,0:T(8,128)(2,1)S(1)} %get-tuple-element.32), channel_id=1, source_target_pairs={{0,24},{2,26},{4,28},{6,30},{8,16},{10,18},{12,20},{14,22},{16,8},... | collective-permute-start | bytes 49160 | tf_op jit(solution)/shard_map/ppermute | solution.py:318
  32.0 1.8 %collective-permute-done.13.refs_3_ = bf16[4,16,128]{2,1,0:T(8,128)(2,1)S(1)} collective-permute-done((bf16[4,16,128]{2,1,0:T(8,128)(2,1)S(1)}, bf16[4,16,128]{2,1,0:T(8,128)(2,1)S(1)}, u32[]{:S(2)}, u32[]{:S(2)}) %collective-permute-start.13) | collective-permute-done | bytes 16416 | tf_op jit(solution)/shard_map/ppermute | solution.py:318
  33.8 0.5 %collective-permute-start.14 = (bf16[4,16,128]{2,1,0:T(8,128)(2,1)S(1)}, bf16[4,16,128]{2,1,0:T(8,128)(2,1)S(1)}, u32[]{:S(2)}, u32[]{:S(2)}) collective-permute-start(bf16[4,16,128]{2,1,0:T(8,128)(2,1)S(1)} %get-tuple-element.34), channel_id=1, source_target_pairs={{0,2},{2,0},{4,6},{6,4},{8,10},{10,8},{12,14},{14,12},{16,18},{18,... | collective-permute-start | bytes 49160 | tf_op jit(solution)/shard_map/ppermute | solution.py:318
  34.9 2.5 %collective-permute-start.16 = (bf16[4,16,128]{2,1,0:T(8,128)(2,1)S(1)}, bf16[4,16,128]{2,1,0:T(8,128)(2,1)S(1)}, u32[]{:S(2)}, u32[]{:S(2)}) collective-permute-start(bf16[4,16,128]{2,1,0:T(8,128)(2,1)S(1)} %get-tuple-element.36), channel_id=1, source_target_pairs={{0,6},{2,4},{4,2},{6,0},{8,14},{10,12},{12,10},{14,8},{16,22},{18,... | collective-permute-start | bytes 49160 | tf_op jit(solution)/shard_map/ppermute | solution.py:318
  38.1 1.4 %collective-permute-done.16.refs_3_ = bf16[4,16,128]{2,1,0:T(8,128)(2,1)S(1)} collective-permute-done((bf16[4,16,128]{2,1,0:T(8,128)(2,1)S(1)}, bf16[4,16,128]{2,1,0:T(8,128)(2,1)S(1)}, u32[]{:S(2)}, u32[]{:S(2)}) %collective-permute-start.16) | collective-permute-done | bytes 16416 | tf_op jit(solution)/shard_map/ppermute | solution.py:318
  39.5 1.2 %collective-permute-done.20.refs_7_ = bf16[4,16,128]{2,1,0:T(8,128)(2,1)S(1)} collective-permute-done((bf16[4,16,128]{2,1,0:T(8,128)(2,1)S(1)}, bf16[4,16,128]{2,1,0:T(8,128)(2,1)S(1)}, u32[]{:S(2)}, u32[]{:S(2)}) %collective-permute-start.20) | collective-permute-done | bytes 16416 | tf_op jit(solution)/shard_map/ppermute | solution.py:290
  40.7 1.6 %unpack_forecast.1 = f32[256,128]{1,0:T(8,128)} custom-call(s32[1]{0:T(128)} %bitcast.me_ref, bf16[4,16,128]{2,1,0:T(8,128)(2,1)S(1)} %get-tuple-element.33.refs_0_, bf16[4,16,128]{2,1,0:T(8,128)(2,1)S(1)} %collective-permute-done.14.refs_1_, bf16[4,16,128]{2,1,0:T(8,128)(2,1)S(1)} %collective-permute-done.15.refs_2_, ...), custom_call_target="tpu_custom_call" | custom-call | tf_op jit(solution)/shard_map/unpack_forecast/pallas_call | solution.py:327
  (31 shorter events, 2.9 us)
Async XLA Ops:
  0.0 1.7 %copy-start.1 = (f32[2,8,8]{2,1,0:T(8,128)S(1)}, f32[2,8,8]{2,1,0:T(8,128)}, u32[]{:S(2)}) copy-start(f32[2,8,8]{2,1,0:T(8,128)} %values_ref.1) | copy-start | bytes 1540
  0.0 1.6 %collective-permute-start = (f32[16,2,8,128]{3,2,1,0:T(8,128)}, f32[16,2,8,128]{3,2,1,0:T(8,128)S(1)}, u32[]{:S(2)}, u32[]{:S(2)}) collective-permute-start(f32[16,2,8,128]{3,2,1,0:T(8,128)} %param.4), channel_id=1, source_target_pairs={{1,0},{0,1},{3,2},{2,3},{5,4},{4,5},{7,6},{6,7},{9,8},{8,9},{11,10... | collective-permute-start | bytes 393224 | tf_op jit(solution)/shard_map/ppermute | solution.py:290
  1.7 0.9 %copy-start = (f32[16,2,8,128]{3,2,1,0:T(8,128)S(1)}, f32[16,2,8,128]{3,2,1,0:T(8,128)}, u32[]{:S(2)}) copy-start(f32[16,2,8,128]{3,2,1,0:T(8,128)} %param.4) | copy-start | bytes 393220
  2.6 0.7 %copy-start.2 = (f32[2,8,8]{2,1,0:T(8,128)S(1)}, f32[2,8,8]{2,1,0:T(8,128)}, u32[]{:S(2)}) copy-start(f32[2,8,8]{2,1,0:T(8,128)} %inverse_ref.1) | copy-start | bytes 1540
  4.8 4.9 %collective-permute-start.1 = (bf16[4,5,8,128]{3,2,1,0:T(8,128)(2,1)S(1)}, bf16[4,5,8,128]{3,2,1,0:T(8,128)(2,1)S(1)}, u32[]{:S(2)}, u32[]{:S(2)}) collective-permute-start(bf16[4,5,8,128]{3,2,1,0:T(8,128)(2,1)S(1)} %get-tuple-element.22), channel_id=1, source_target_pairs={{0,2},{2,0},{4,6},{6,4},{8,10},{10,8},{12,14},{14,12},{16,18},{18,... | collective-permute-start | bytes 122888 | tf_op jit(solution)/shard_map/ppermute | solution.py:318
  7.7 4.0 %collective-permute-start.2 = (bf16[4,5,8,128]{3,2,1,0:T(8,128)(2,1)S(1)}, bf16[4,5,8,128]{3,2,1,0:T(8,128)(2,1)S(1)}, u32[]{:S(2)}, u32[]{:S(2)}) collective-permute-start(bf16[4,5,8,128]{3,2,1,0:T(8,128)(2,1)S(1)} %get-tuple-element.23), channel_id=1, source_target_pairs={{0,4},{2,6},{4,0},{6,2},{8,12},{10,14},{12,8},{14,10},{16,20},{18,... | collective-permute-start | bytes 122888 | tf_op jit(solution)/shard_map/ppermute | solution.py:318
  9.2 4.9 %collective-permute-start.3 = (bf16[4,5,8,128]{3,2,1,0:T(8,128)(2,1)S(1)}, bf16[4,5,8,128]{3,2,1,0:T(8,128)(2,1)S(1)}, u32[]{:S(2)}, u32[]{:S(2)}) collective-permute-start(bf16[4,5,8,128]{3,2,1,0:T(8,128)(2,1)S(1)} %get-tuple-element.24), channel_id=1, source_target_pairs={{0,6},{2,4},{4,2},{6,0},{8,14},{10,12},{12,10},{14,8},{16,22},{18,... | collective-permute-start | bytes 122888 | tf_op jit(solution)/shard_map/ppermute | solution.py:318
  14.2 4.5 %collective-permute-start.4 = (bf16[4,5,8,128]{3,2,1,0:T(8,128)(2,1)S(1)}, bf16[4,5,8,128]{3,2,1,0:T(8,128)(2,1)S(1)}, u32[]{:S(2)}, u32[]{:S(2)}) collective-permute-start(bf16[4,5,8,128]{3,2,1,0:T(8,128)(2,1)S(1)} %get-tuple-element.26), channel_id=1, source_target_pairs={{0,8},{2,10},{4,12},{6,14},{8,0},{10,2},{12,4},{14,6},{16,24},{18,... | collective-permute-start | bytes 122888 | tf_op jit(solution)/shard_map/ppermute | solution.py:318
  15.8 5.8 %collective-permute-start.5 = (bf16[4,5,8,128]{3,2,1,0:T(8,128)(2,1)S(1)}, bf16[4,5,8,128]{3,2,1,0:T(8,128)(2,1)S(1)}, u32[]{:S(2)}, u32[]{:S(2)}) collective-permute-start(bf16[4,5,8,128]{3,2,1,0:T(8,128)(2,1)S(1)} %get-tuple-element.27), channel_id=1, source_target_pairs={{0,16},{2,18},{4,20},{6,22},{8,24},{10,26},{12,28},{14,30},{16,0},... | collective-permute-start | bytes 122888 | tf_op jit(solution)/shard_map/ppermute | solution.py:318
  18.4 5.8 %collective-permute-start.6 = (bf16[4,5,8,128]{3,2,1,0:T(8,128)(2,1)S(1)}, bf16[4,5,8,128]{3,2,1,0:T(8,128)(2,1)S(1)}, u32[]{:S(2)}, u32[]{:S(2)}) collective-permute-start(bf16[4,5,8,128]{3,2,1,0:T(8,128)(2,1)S(1)} %get-tuple-element.28), channel_id=1, source_target_pairs={{0,24},{2,26},{4,28},{6,30},{8,16},{10,18},{12,20},{14,22},{16,8},... | collective-permute-start | bytes 122888 | tf_op jit(solution)/shard_map/ppermute | solution.py:318
  18.6 5.6 %collective-permute-start.7 = (bf16[4,5,8,128]{3,2,1,0:T(8,128)(2,1)S(1)}, bf16[4,5,8,128]{3,2,1,0:T(8,128)(2,1)S(1)}, u32[]{:S(2)}, u32[]{:S(2)}) collective-permute-start(bf16[4,5,8,128]{3,2,1,0:T(8,128)(2,1)S(1)} %get-tuple-element.25.refs_0_), channel_id=1, source_target_pairs={{1,0},{0,1},{3,2},{2,3},{5,4},{4,5},{7,6},{6,7},{9,8},{8,9},{11,10... | collective-permute-start | bytes 122888 | tf_op jit(solution)/shard_map/ppermute | solution.py:290
  18.6 5.6 %collective-permute-start.8 = (bf16[4,5,8,128]{3,2,1,0:T(8,128)(2,1)S(1)}, bf16[4,5,8,128]{3,2,1,0:T(8,128)(2,1)S(1)}, u32[]{:S(2)}, u32[]{:S(2)}) collective-permute-start(bf16[4,5,8,128]{3,2,1,0:T(8,128)(2,1)S(1)} %collective-permute-done.4.refs_1_), channel_id=1, source_target_pairs={{1,0},{0,1},{3,2},{2,3},{5,4},{4,5},{7,6},{6,7},{9,8},{8,9},{11,10... | collective-permute-start | bytes 122888 | tf_op jit(solution)/shard_map/ppermute | solution.py:290
  21.6 2.6 %collective-permute-start.9 = (bf16[4,5,8,128]{3,2,1,0:T(8,128)(2,1)S(1)}, bf16[4,5,8,128]{3,2,1,0:T(8,128)(2,1)S(1)}, u32[]{:S(2)}, u32[]{:S(2)}) collective-permute-start(bf16[4,5,8,128]{3,2,1,0:T(8,128)(2,1)S(1)} %collective-permute-done.5.refs_2_), channel_id=1, source_target_pairs={{1,0},{0,1},{3,2},{2,3},{5,4},{4,5},{7,6},{6,7},{9,8},{8,9},{11,10... | collective-permute-start | bytes 122888 | tf_op jit(solution)/shard_map/ppermute | solution.py:290
  24.2 1.2 %collective-permute-start.10 = (bf16[4,5,8,128]{3,2,1,0:T(8,128)(2,1)S(1)}, bf16[4,5,8,128]{3,2,1,0:T(8,128)(2,1)S(1)}, u32[]{:S(2)}, u32[]{:S(2)}) collective-permute-start(bf16[4,5,8,128]{3,2,1,0:T(8,128)(2,1)S(1)} %collective-permute-done.6.refs_3_), channel_id=1, source_target_pairs={{1,0},{0,1},{3,2},{2,3},{5,4},{4,5},{7,6},{6,7},{9,8},{8,9},{11,10... | collective-permute-start | bytes 122888 | tf_op jit(solution)/shard_map/ppermute | solution.py:290
  27.2 4.5 %collective-permute-start.11 = (bf16[4,16,128]{2,1,0:T(8,128)(2,1)S(1)}, bf16[4,16,128]{2,1,0:T(8,128)(2,1)S(1)}, u32[]{:S(2)}, u32[]{:S(2)}) collective-permute-start(bf16[4,16,128]{2,1,0:T(8,128)(2,1)S(1)} %get-tuple-element.30), channel_id=1, source_target_pairs={{0,8},{2,10},{4,12},{6,14},{8,0},{10,2},{12,4},{14,6},{16,24},{18,... | collective-permute-start | bytes 49160 | tf_op jit(solution)/shard_map/ppermute | solution.py:318
  27.3 4.7 %collective-permute-start.12 = (bf16[4,16,128]{2,1,0:T(8,128)(2,1)S(1)}, bf16[4,16,128]{2,1,0:T(8,128)(2,1)S(1)}, u32[]{:S(2)}, u32[]{:S(2)}) collective-permute-start(bf16[4,16,128]{2,1,0:T(8,128)(2,1)S(1)} %get-tuple-element.31), channel_id=1, source_target_pairs={{0,16},{2,18},{4,20},{6,22},{8,24},{10,26},{12,28},{14,30},{16,0},... | collective-permute-start | bytes 49160 | tf_op jit(solution)/shard_map/ppermute | solution.py:318
  28.3 5.5 %collective-permute-start.13 = (bf16[4,16,128]{2,1,0:T(8,128)(2,1)S(1)}, bf16[4,16,128]{2,1,0:T(8,128)(2,1)S(1)}, u32[]{:S(2)}, u32[]{:S(2)}) collective-permute-start(bf16[4,16,128]{2,1,0:T(8,128)(2,1)S(1)} %get-tuple-element.32), channel_id=1, source_target_pairs={{0,24},{2,26},{4,28},{6,30},{8,16},{10,18},{12,20},{14,22},{16,8},... | collective-permute-start | bytes 49160 | tf_op jit(solution)/shard_map/ppermute | solution.py:318
  33.8 3.7 %collective-permute-start.14 = (bf16[4,16,128]{2,1,0:T(8,128)(2,1)S(1)}, bf16[4,16,128]{2,1,0:T(8,128)(2,1)S(1)}, u32[]{:S(2)}, u32[]{:S(2)}) collective-permute-start(bf16[4,16,128]{2,1,0:T(8,128)(2,1)S(1)} %get-tuple-element.34), channel_id=1, source_target_pairs={{0,2},{2,0},{4,6},{6,4},{8,10},{10,8},{12,14},{14,12},{16,18},{18,... | collective-permute-start | bytes 49160 | tf_op jit(solution)/shard_map/ppermute | solution.py:318
  34.4 3.7 %collective-permute-start.15 = (bf16[4,16,128]{2,1,0:T(8,128)(2,1)S(1)}, bf16[4,16,128]{2,1,0:T(8,128)(2,1)S(1)}, u32[]{:S(2)}, u32[]{:S(2)}) collective-permute-start(bf16[4,16,128]{2,1,0:T(8,128)(2,1)S(1)} %get-tuple-element.35), channel_id=1, source_target_pairs={{0,4},{2,6},{4,0},{6,2},{8,12},{10,14},{12,8},{14,10},{16,20},{18,... | collective-permute-start | bytes 49160 | tf_op jit(solution)/shard_map/ppermute | solution.py:318
  34.9 4.6 %collective-permute-start.16 = (bf16[4,16,128]{2,1,0:T(8,128)(2,1)S(1)}, bf16[4,16,128]{2,1,0:T(8,128)(2,1)S(1)}, u32[]{:S(2)}, u32[]{:S(2)}) collective-permute-start(bf16[4,16,128]{2,1,0:T(8,128)(2,1)S(1)} %get-tuple-element.36), channel_id=1, source_target_pairs={{0,6},{2,4},{4,2},{6,0},{8,14},{10,12},{12,10},{14,8},{16,22},{18,... | collective-permute-start | bytes 49160 | tf_op jit(solution)/shard_map/ppermute | solution.py:318
  37.3 2.2 %collective-permute-start.17 = (bf16[4,16,128]{2,1,0:T(8,128)(2,1)S(1)}, bf16[4,16,128]{2,1,0:T(8,128)(2,1)S(1)}, u32[]{:S(2)}, u32[]{:S(2)}) collective-permute-start(bf16[4,16,128]{2,1,0:T(8,128)(2,1)S(1)} %get-tuple-element.33.refs_0_), channel_id=1, source_target_pairs={{1,0},{0,1},{3,2},{2,3},{5,4},{4,5},{7,6},{6,7},{9,8},{8,9},{11,10... | collective-permute-start | bytes 49160 | tf_op jit(solution)/shard_map/ppermute | solution.py:290
  37.6 1.9 %collective-permute-start.18 = (bf16[4,16,128]{2,1,0:T(8,128)(2,1)S(1)}, bf16[4,16,128]{2,1,0:T(8,128)(2,1)S(1)}, u32[]{:S(2)}, u32[]{:S(2)}) collective-permute-start(bf16[4,16,128]{2,1,0:T(8,128)(2,1)S(1)} %collective-permute-done.14.refs_1_), channel_id=1, source_target_pairs={{1,0},{0,1},{3,2},{2,3},{5,4},{4,5},{7,6},{6,7},{9,8},{8,9},{11,10... | collective-permute-start | bytes 49160 | tf_op jit(solution)/shard_map/ppermute | solution.py:290
  38.1 1.4 %collective-permute-start.19 = (bf16[4,16,128]{2,1,0:T(8,128)(2,1)S(1)}, bf16[4,16,128]{2,1,0:T(8,128)(2,1)S(1)}, u32[]{:S(2)}, u32[]{:S(2)}) collective-permute-start(bf16[4,16,128]{2,1,0:T(8,128)(2,1)S(1)} %collective-permute-done.15.refs_2_), channel_id=1, source_target_pairs={{1,0},{0,1},{3,2},{2,3},{5,4},{4,5},{7,6},{6,7},{9,8},{8,9},{11,10... | collective-permute-start | bytes 49160 | tf_op jit(solution)/shard_map/ppermute | solution.py:290
  39.5 1.2 %collective-permute-start.20 = (bf16[4,16,128]{2,1,0:T(8,128)(2,1)S(1)}, bf16[4,16,128]{2,1,0:T(8,128)(2,1)S(1)}, u32[]{:S(2)}, u32[]{:S(2)}) collective-permute-start(bf16[4,16,128]{2,1,0:T(8,128)(2,1)S(1)} %collective-permute-done.16.refs_3_), channel_id=1, source_target_pairs={{1,0},{0,1},{3,2},{2,3},{5,4},{4,5},{7,6},{6,7},{9,8},{8,9},{11,10... | collective-permute-start | bytes 49160 | tf_op jit(solution)/shard_map/ppermute | solution.py:290
  (1 other events, 0.7 us)

commit v3 on v2

--- a/solution.py
+++ b/solution.py
@@ -51,10 +51,6 @@
         parts = new
         stride *= 2
     return parts
-
-
-def xor_blocks(me, high, low):
-    return ((me // GROUP) ^ high) * GROUP + ((me % GROUP) ^ low)
 
 
 def observation_rows(values_ref, inverse_ref, mask_ref):
@@ -81,18 +77,30 @@
     return jnp.dot(gather, wide, preferred_element_type=F32)
 
 
-def pack_kernel(me_ref, x_ref, near_ref, values_ref, inverse_ref, mask_ref, *refs):
-    outs, blocks = refs[:GROUP], refs[GROUP]
-    stride = FIELDS * BAND
-
-    def row(ref, field, index):
-        return ref[pl.ds(field * BAND + index, LOCAL, stride=stride), :]
+def prepare_kernel(*refs):
+    sources, rows_ref, obs_ref, held, sems = refs[:4], refs[4], refs[5], refs[6:10], refs[10]
+    points = FIELDS * BAND
+    copies = [pltpu.make_async_copy(a, b, sems.at[i]) for i, (a, b) in enumerate(zip(sources, held))]
+    for copy in copies:
+        copy.start()
+    for copy in copies:
+        copy.wait()
+    for i in range(points):
+        rows_ref[i] = held[0][pl.ds(i, LOCAL, stride=points), :]
+    obs_ref[...] = observation_rows(*held[1:])
+
+
+def pack_kernel(rows_ref, near_ref, obs_ref, out_ref):
+    points = FIELDS * BAND
+
+    def near(field, index):
+        return near_ref[pl.ds(field * BAND + index, LOCAL, stride=points), :]
 
     fields = []
     for field in range(FIELDS):
-        before = [row(near_ref, field, r) for r in range(BAND - FSTEPS, BAND)]
-        own = [row(x_ref, field, r) for r in range(BAND)]
-        after = [row(near_ref, field, r) for r in range(FSTEPS)]
+        before = [near(field, r) for r in range(BAND - FSTEPS, BAND)]
+        own = [rows_ref[field * BAND + r] for r in range(BAND)]
+        after = [near(field, r) for r in range(FSTEPS)]
         fields.append(before + own + after)
     done = forecast_rows(*fields)
     stacked = []
@@ -113,7 +121,7 @@
     widen = (column == wanted).astype(F32).astype(BF)
     wide = jnp.dot(rows, widen, preferred_element_type=F32)
     height = LOCAL + 8
-    obs = observation_rows(values_ref, inverse_ref, mask_ref)
+    obs = obs_ref[...]
     for side in range(2):
         tails = [obs] * 8
         for half in range(2):
@@ -124,44 +132,28 @@
             parts = swap_blocks(parts, REGION)
             for i in range(8):
                 for eight in range(2):
-                    blocks[side * 8 + i, half * 2 + eight] = parts[i][eight * 8 : eight * 8 + 8].astype(BF)
+                    out_ref[i % GROUP, side * 2 + i // GROUP, half * 2 + eight] = parts[i][eight * 8 : eight * 8 + 8].astype(BF)
                 tails[i] = tails[i] + parts[i][LOCAL:]
         for i in range(8):
-            blocks[side * 8 + i, 4] = tails[i].astype(BF)
-    low = me_ref[0] % GROUP
-    for k in range(GROUP):
-        for high in range(GROUP):
-            outs[k][high] = blocks[high * GROUP + (low ^ k)]
-
-
-def regroup_region_kernel(me_ref, *refs):
-    ins, outs = refs[:GROUP], refs[GROUP:]
-    high = me_ref[0] // GROUP
-    for j in range(GROUP):
-        for k in range(GROUP):
-            outs[j][k] = ins[k][high ^ j]
-
-
-def regroup_inner_kernel(*refs):
-    ins, outs = refs[:GROUP], refs[GROUP:]
-    for k in range(GROUP):
+            out_ref[i % GROUP, side * 2 + i // GROUP, 4] = tails[i].astype(BF)
+
+
+def regroup_kernel(in_ref, out_ref):
+    for i in range(GROUP):
         for j in range(GROUP):
-            outs[k][j] = ins[j][k]
-
-
-def halves_of(refs, tail_ref, me):
+            out_ref[j, i] = in_ref[i, j]
+
+
+def halves_of(ref, me):
     count = GROUP * GROUP
-    blocks = [(refs[j], k) for j in range(GROUP) for k in range(GROUP)]
-    tails = [ref[k, 4].astype(F32) for ref, k in blocks]
-    for s in range(count):
-        tail_ref[s] = tails[s]
+    tails = [ref[s // GROUP, s % GROUP, 4].astype(F32) for s in range(count)]
 
     def tail_of(device):
-        return tail_ref[xor_blocks(me, device // GROUP, device % GROUP)]
+        return ref[device // GROUP, device % GROUP, 4].astype(F32)
 
     lane = lax.broadcasted_iota(jnp.int32, (8, WIDTH), 1) % REGION
     left = tail_of(lax.rem(me + count - 1, count))
-    own = tails[0]
+    own = tail_of(me)
     right = tail_of(lax.rem(me + 1, count))
 
     def seen(offset):
@@ -182,8 +174,9 @@
         means = [t[base : base + 1] + t[base + 1 : base + 2] for t in tails]
         mean = functools.reduce(jnp.add, means) * (1.0 / count)
         deviation = []
-        for (ref, k), own_mean in zip(blocks, means):
-            value = jnp.concatenate([ref[k, half * 2 + eight].astype(F32) for eight in range(2)], 0)
+        for s, own_mean in enumerate(means):
+            block = ref.at[s // GROUP, s % GROUP]
+            value = jnp.concatenate([block[half * 2 + eight].astype(F32) for eight in range(2)], 0)
             deviation.append((value + (own_mean - mean)).astype(BF))
         weight = first[base + 2 : base + 3]
         obs = second[base + 2 : base + 3] + first[base + 3 : base + 4] + second[base + 3 : base + 4]
@@ -192,13 +185,11 @@
     return result
 
 
-def analysis_kernel(me_ref, *refs):
-    own_refs, near_refs, outs = refs[:GROUP], refs[GROUP : 2 * GROUP], refs[2 * GROUP : 3 * GROUP]
-    tail_ref, near_tail_ref = refs[3 * GROUP :]
+def analysis_kernel(me_ref, own_ref, near_ref, out_ref):
     members = GROUP * GROUP * LOCAL
     me = me_ref[0]
-    own = halves_of(own_refs, tail_ref, me)
-    near = halves_of(near_refs, near_tail_ref, me)
+    own = halves_of(own_ref, me)
+    near = halves_of(near_ref, me)
     lane = lax.broadcasted_iota(jnp.int32, (1, WIDTH), 1)
     region_column = lane % REGION
     half_row = (lane // REGION) % (BAND // 2)
@@ -259,25 +250,20 @@
     for j in range(GROUP):
         for k in range(GROUP):
             start = (j * GROUP + k) * LOCAL
-            outs[j][k] = result[start : start + LOCAL]
-
-
-def unpack_kernel(me_ref, *refs):
-    own_refs, near_refs, out_ref = refs[:GROUP], refs[GROUP : 2 * GROUP], refs[2 * GROUP]
-    me = me_ref[0]
-
-    def rows_of(ins, blocks):
-        for k in range(GROUP):
-            for j in range(GROUP):
-                blocks[xor_blocks(me, j, k)] = ins[k][j].astype(F32)
-        parts = swap_blocks([blocks[p] for p in range(GROUP * GROUP)], PATCH)
+            out_ref[j, k] = result[start : start + LOCAL]
+
+
+def unpack_kernel(own_ref, near_ref, out_ref):
+    def rows_of(ref):
+        blocks = [ref[p % GROUP, p // GROUP].astype(F32) for p in range(GROUP * GROUP)]
+        parts = swap_blocks(blocks, PATCH)
         half = BAND // 2
         return [
             [parts[h * FIELDS * half + field * half + r] for h in range(2) for r in range(half)]
             for field in range(FIELDS)
         ]
 
-    own, near = rows_of(own_refs, refs[2 * GROUP + 1]), rows_of(near_refs, refs[2 * GROUP + 2])
+    own, near = rows_of(own_ref), rows_of(near_ref)
     fields = [n[BAND - FSTEPS :] + o + n[:FSTEPS] for o, n in zip(own, near)]
     done = forecast_rows(*fields)
     for field in range(FIELDS):
@@ -306,24 +292,22 @@
 
 
 def join_region(after, before):
-    tail = jnp.concatenate([after[:, 4:, :4], before[:, 4:, 4:]], 2)
-    return jnp.concatenate([after[:, :2], before[:, 2:4], tail], 1)
+    tail = jnp.concatenate([after[:, :, 4:, :4], before[:, :, 4:, 4:]], 3)
+    return jnp.concatenate([after[:, :, :2], before[:, :, 2:4], tail], 2)
 
 
 def join_inner(after, before):
-    return jnp.concatenate([after[..., : WIDTH // 2], before[..., WIDTH // 2 :]], 2)
-
-
-def from_partner(value, distance):
-    return lax.ppermute(value, "mem", [(i, i ^ distance) for i in range(lax.axis_size("mem"))])
-
-
-def exchange(values, unit):
-    return [values[0]] + [from_partner(values[k], k * unit) for k in range(1, GROUP)]
-
-
-def call(kernel, name, out_shape, *args, scratch=()):
-    spaces = [pltpu.SMEM if arg.shape == (1,) else pltpu.VMEM for arg in args]
+    return jnp.concatenate([after[..., : WIDTH // 2], before[..., WIDTH // 2 :]], 3)
+
+
+def exchange(value, low):
+    places = range(GROUP)
+    groups = [[(i * GROUP + j) if low else (j * GROUP + i) for j in places] for i in places]
+    return lax.all_to_all(value, "mem", split_axis=0, concat_axis=0, axis_index_groups=groups, tiled=True)
+
+
+def call(kernel, name, out_shape, *args, space=pltpu.VMEM, scratch=()):
+    spaces = [pltpu.SMEM if arg.shape == (1,) else space for arg in args]
     return pl.pallas_call(
         kernel,
         out_shape=out_shape,
@@ -341,43 +325,29 @@
     assert shape == (LOCAL, FIELDS, BAND, WIDTH) and count * PATCH == WIDTH and count == GROUP * GROUP
     me = lax.axis_index("mem").astype(jnp.int32).reshape(1)
     near = near_rows(sample_collection, join_grid)
-    region_shape = [jax.ShapeDtypeStruct((GROUP, 5, 8, WIDTH), BF)] * GROUP
-    inner_shape = [jax.ShapeDtypeStruct((GROUP, LOCAL, WIDTH), BF)] * GROUP
-    sending = call(
-        pack_kernel,
-        "forecast_pack",
-        region_shape,
-        me,
-        sample_collection.reshape(-1, WIDTH),
-        near.reshape(-1, WIDTH),
-        obs_values,
-        obs_inverse_variance,
-        obs_mask,
-        scratch=[pltpu.VMEM((count, 5, 8, WIDTH), BF)],
+    sources = (sample_collection.reshape(-1, WIDTH), obs_values, obs_inverse_variance, obs_mask)
+    rows, obs = call(
+        prepare_kernel,
+        "prepare",
+        [jax.ShapeDtypeStruct((FIELDS * BAND, LOCAL, WIDTH), F32), jax.ShapeDtypeStruct((8, WIDTH), F32)],
+        *sources,
+        space=pltpu.HBM,
+        scratch=[pltpu.VMEM(x.shape, x.dtype) for x in sources] + [pltpu.SemaphoreType.DMA((len(sources),))],
     )
-    sending = call(regroup_region_kernel, "regroup_region", region_shape, me, *exchange(sending, 1))
-    region = exchange(sending, GROUP)
-    region_near = [near_rows(value, join_region) for value in region]
-    returning = call(
-        analysis_kernel,
-        "analysis",
-        inner_shape,
-        me,
-        *region,
-        *region_near,
-        scratch=[pltpu.VMEM((count, 8, WIDTH), F32)] * 2,
-    )
-    returning = call(regroup_inner_kernel, "regroup_inner", inner_shape, *exchange(returning, GROUP))
-    inner = exchange(returning, 1)
-    inner_near = [near_rows(value, join_inner) for value in inner]
+    region_shape = jax.ShapeDtypeStruct((GROUP, GROUP, 5, 8, WIDTH), BF)
+    inner_shape = jax.ShapeDtypeStruct((GROUP, GROUP, LOCAL, WIDTH), BF)
+    sending = call(pack_kernel, "forecast_pack", region_shape, rows, near.reshape(-1, WIDTH), obs)
+    region = exchange(call(regroup_kernel, "regroup_region", region_shape, exchange(sending, True)), False)
+    region_near = near_rows(region, join_region)
+    returning = call(analysis_kernel, "analysis", inner_shape, me, region, region_near)
+    inner = exchange(call(regroup_kernel, "regroup_inner", inner_shape, exchange(returning, False)), True)
+    inner_near = near_rows(inner, join_inner)
     cycled = call(
         unpack_kernel,
         "unpack_forecast",
         jax.ShapeDtypeStruct((LOCAL * FIELDS * BAND, WIDTH), F32),
-        me,
-        *inner,
-        *inner_near,
-        scratch=[pltpu.VMEM((count, LOCAL, WIDTH), F32)] * 2,
+        inner,
+        inner_near,
     )
     return cycled.reshape(shape)
 

time: 42.5 us -> 47.9 us (1.13)
  blocking collectives: 0 us -> 36.8 us
  starting transfers between devices: 18.1 us -> 0.46 us
  waiting for transfers between devices: 17.6 us -> 2.65 us
  local copies, waits for them, and re-layouts: 2.3 us -> 2.99 us
    all_to_all x0 -> x4, blocking collectives: none -> 36.8 us  [exchange(): lax.all_to_all(value, 'mem', split_axis=0, concat_axis=0, axis_index_grou...]
    ppermute x12 -> x0, starting transfers between devices: 16.8 us -> none  [from_partner(): lax.ppermute(value, 'mem', [(i, i ^ distance) for i in range(lax.axis_siz...]
    ppermute x12 -> x0, waiting for transfers between devices: 14 us -> none  [from_partner(): lax.ppermute(value, 'mem', [(i, i ^ distance) for i in range(lax.axis_siz...]
    ppermute x9 -> x3, waiting for transfers between devices: 3.57 us -> 2.65 us  [from_next(): lax.ppermute(value, 'rows', [((i + 1) % count, i) for i in range(count)])]
    ppermute x9 -> x3, starting transfers between devices: 1.24 us -> 0.46 us  [from_next(): lax.ppermute(value, 'rows', [((i + 1) % count, i) for i in range(count)])]
    unnamed x8, local copies, waits for them, and re-layouts: 2.3 us -> 2.99 us
    pallas_call x5 -> x6, Pallas kernels: 4.26 us -> 4.52 us  [call(): pl.pallas_call(kernel, out_shape=out_shape, in_specs=[pl.BlockSpec(memory...]
  transfers between devices with their start and end apart: 21 -> 3, of which waited for: 13 -> 2; matrix products, arithmetic and copies ran while one was open for 0% -> 0% of each run, Pallas kernels for 0% -> 1%
where the time goes in v3:
time: 47.9 us; the launch traced here: 47.5 us
  blocking collectives  36.8 us (77%)
  Pallas kernels  4.52 us (9%)
  local copies, waits for them, and re-layouts  2.99 us (6%)
  waiting for transfers between devices  2.65 us (6%)
    all_to_all x4, blocking collectives, exchange(): lax.all_to_all(value, 'mem', split_axis=0, concat_axis=0, axis_index_grou...  36.8 us
    pallas_call x6, Pallas kernels, call(): pl.pallas_call(kernel, out_shape=out_shape, in_specs=[pl.BlockSpec(memory...  4.52 us
    unnamed x8, local copies, waits for them, and re-layouts  2.99 us
    ppermute x3, waiting for transfers between devices, from_next(): lax.ppermute(value, 'rows', [((i + 1) % count, i) for i in range(count)])  2.65 us
  transfers between devices with their start and end apart: 3, of which 2 were waited for; matrix products, arithmetic and copies ran while one was open for 0% of the time, Pallas kernels for 1%

profile of v3, /device:TPU:0, one launch (start us, length us, event | category | flops | bytes accessed | tf_op | source)
XLA Modules:
  0.0 47.5 jit_solution(11092485330913724265)
XLA Ops:
  0.0 0.5 collective-permute-start
  0.5 0.0 copy-start
  0.5 0.9 %copy-done = f32[16,2,8,128]{3,2,1,0:T(8,128)S(1)} copy-done((f32[16,2,8,128]{3,2,1,0:T(8,128)S(1)}, f32[16,2,8,128]{3,2,1,0:T(8,128)}, u32[]{:S(2)}) %copy-start) | copy-done | bytes 131096
  1.4 0.0 copy-start.1
  1.4 0.7 %copy-done.1 = f32[2,8,8]{2,1,0:T(8,128)S(1)} copy-done((f32[2,8,8]{2,1,0:T(8,128)S(1)}, f32[2,8,8]{2,1,0:T(8,128)}, u32[]{:S(2)}) %copy-start.1) | copy-done | bytes 536
  2.1 0.0 copy-start.2
  2.1 0.7 %copy-done.2 = f32[2,8,8]{2,1,0:T(8,128)S(1)} copy-done((f32[2,8,8]{2,1,0:T(8,128)S(1)}, f32[2,8,8]{2,1,0:T(8,128)}, u32[]{:S(2)}) %copy-start.2) | copy-done | bytes 536
  2.8 0.0 copy-start.3
  2.8 0.7 %copy-done.3 = s32[2,8,8]{2,1,0:T(8,128)S(1)} copy-done((s32[2,8,8]{2,1,0:T(8,128)S(1)}, s32[2,8,8]{2,1,0:T(8,128)}, u32[]{:S(2)}) %copy-start.3) | copy-done | bytes 536
  3.5 0.5 %prepare.1 = (f32[16,16,128]{2,1,0:T(8,128)S(1)}, f32[8,128]{1,0:T(8,128)S(1)}) custom-call(f32[256,128]{1,0:T(8,128)S(1)} %bitcast.4, f32[2,8,8]{2,1,0:T(8,128)S(1)} %copy-done.1, f32[2,8,8]{2,1,0:T(8,128)S(1)} %copy-done.2, s32[2,8,8]{2,1,0:T(8,128)S(1)} %copy-done.3), custom_call_target="tpu_custom_call" | custom-call | tf_op jit(solution)/shard_map/prepare/pallas_call | solution.py:311
  3.9 0.0 collective-permute-done
  4.0 0.8 %forecast_pack.1 = bf16[4,4,5,8,128]{4,3,2,1,0:T(8,128)(2,1)S(1)} custom-call(f32[16,16,128]{2,1,0:T(8,128)S(1)} %get-tuple-element.7.rows_ref, f32[256,128]{1,0:T(8,128)S(1)} %bitcast.5, f32[8,128]{1,0:T(8,128)S(1)} %get-tuple-element.8.obs_ref), custom_call_target="tpu_custom_call" | custom-call | tf_op jit(solution)/shard_map/forecast_pack/pallas_call | solution.py:311
  4.8 10.1 %all_to_all.20.in_ref = bf16[4,4,5,8,128]{4,3,2,1,0:T(8,128)(2,1)S(1)} all-to-all(bf16[4,4,5,8,128]{4,3,2,1,0:T(8,128)(2,1)S(1)} %forecast_pack.1), channel_id=1, replica_groups={{0,2,4,6},{8,10,12,14},{16,18,20,22},{24,26,28,30},{1,3,5,7},{9,11,13,1..., dimensions={0} | all-to-all | bytes 327680 | tf_op jit(solution)/shard_map/all_to_all | solution.py:306
  14.9 11.4 %all_to_all.21.own_ref = bf16[4,4,5,8,128]{4,3,2,1,0:T(8,128)(2,1)S(1)} all-to-all(bf16[4,4,5,8,128]{4,3,2,1,0:T(8,128)(2,1)S(1)} %regroup_region.1), channel_id=1, replica_groups={{0,8,16,24},{2,10,18,26},{4,12,20,28},{6,14,22,30},{1,9,17,25},{3,11,19..., dimensions={0} | all-to-all | bytes 327680 | tf_op jit(solution)/shard_map/all_to_all | solution.py:306
  26.3 0.0 collective-permute-start.1
  26.3 1.4 %collective-permute-done.1.near_ref = bf16[4,4,5,8,128]{4,3,2,1,0:T(8,128)(2,1)S(1)} collective-permute-done((bf16[4,4,5,8,128]{4,3,2,1,0:T(8,128)(2,1)S(1)}, bf16[4,4,5,8,128]{4,3,2,1,0:T(8,128)(2,1)S(1)}, u32[]{:S(2)}, u32[]{:S(2)}) %collective-permute-start.1) | collective-permute-done | bytes 163872 | tf_op jit(solution)/shard_map/ppermute | solution.py:276
  27.7 1.8 %analysis.1 = bf16[4,4,16,128]{3,2,1,0:T(8,128)(2,1)S(1)} custom-call(s32[1]{0:T(128)} %bitcast.me_ref, bf16[4,4,5,8,128]{4,3,2,1,0:T(8,128)(2,1)S(1)} %all_to_all.21.own_ref, bf16[4,4,5,8,128]{4,3,2,1,0:T(8,128)(2,1)S(1)} %collective-permute-done.1.near_ref), custom_call_target="tpu_custom_call" | custom-call | tf_op jit(solution)/shard_map/analysis/pallas_call | solution.py:311
  29.5 8.1 %all_to_all.22.in_ref = bf16[4,4,16,128]{3,2,1,0:T(8,128)(2,1)S(1)} all-to-all(bf16[4,4,16,128]{3,2,1,0:T(8,128)(2,1)S(1)} %analysis.1), channel_id=1, replica_groups={{0,8,16,24},{2,10,18,26},{4,12,20,28},{6,14,22,30},{1,9,17,25},{3,11,19..., dimensions={0} | all-to-all | bytes 131072 | tf_op jit(solution)/shard_map/all_to_all | solution.py:306
  37.6 7.2 %all_to_all.23.own_ref = bf16[4,4,16,128]{3,2,1,0:T(8,128)(2,1)S(1)} all-to-all(bf16[4,4,16,128]{3,2,1,0:T(8,128)(2,1)S(1)} %regroup_inner.1), channel_id=1, replica_groups={{0,2,4,6},{8,10,12,14},{16,18,20,22},{24,26,28,30},{1,3,5,7},{9,11,13,1..., dimensions={0} | all-to-all | bytes 131072 | tf_op jit(solution)/shard_map/all_to_all | solution.py:306
  44.8 0.0 collective-permute-start.2
  44.8 1.3 %collective-permute-done.2.near_ref = bf16[4,4,16,128]{3,2,1,0:T(8,128)(2,1)S(1)} collective-permute-done((bf16[4,4,16,128]{3,2,1,0:T(8,128)(2,1)S(1)}, bf16[4,4,16,128]{3,2,1,0:T(8,128)(2,1)S(1)}, u32[]{:S(2)}, u32[]{:S(2)}) %collective-permute-start.2) | collective-permute-done | bytes 65568 | tf_op jit(solution)/shard_map/ppermute | solution.py:276
  46.1 1.4 %unpack_forecast.1 = f32[256,128]{1,0:T(8,128)} custom-call(bf16[4,4,16,128]{3,2,1,0:T(8,128)(2,1)S(1)} %all_to_all.23.own_ref, bf16[4,4,16,128]{3,2,1,0:T(8,128)(2,1)S(1)} %collective-permute-done.2.near_ref), custom_call_target="tpu_custom_call" | custom-call | tf_op jit(solution)/shard_map/unpack_forecast/pallas_call | solution.py:311
  (2 shorter events, 0.0 us)
Async XLA Ops:
  0.0 3.9 %collective-permute-start = (f32[16,2,8,128]{3,2,1,0:T(8,128)}, f32[16,2,8,128]{3,2,1,0:T(8,128)S(1)}, u32[]{:S(2)}, u32[]{:S(2)}) collective-permute-start(f32[16,2,8,128]{3,2,1,0:T(8,128)} %param.4), channel_id=1, source_target_pairs={{1,0},{0,1},{3,2},{2,3},{5,4},{4,5},{7,6},{6,7},{9,8},{8,9},{11,10... | collective-permute-start | bytes 393224 | tf_op jit(solution)/shard_map/ppermute | solution.py:276
  0.5 0.9 %copy-start = (f32[16,2,8,128]{3,2,1,0:T(8,128)S(1)}, f32[16,2,8,128]{3,2,1,0:T(8,128)}, u32[]{:S(2)}) copy-start(f32[16,2,8,128]{3,2,1,0:T(8,128)} %param.4) | copy-start | bytes 393220
  1.4 0.7 %copy-start.1 = (f32[2,8,8]{2,1,0:T(8,128)S(1)}, f32[2,8,8]{2,1,0:T(8,128)}, u32[]{:S(2)}) copy-start(f32[2,8,8]{2,1,0:T(8,128)} %refs_1_.1) | copy-start | bytes 1540
  2.1 0.7 %copy-start.2 = (f32[2,8,8]{2,1,0:T(8,128)S(1)}, f32[2,8,8]{2,1,0:T(8,128)}, u32[]{:S(2)}) copy-start(f32[2,8,8]{2,1,0:T(8,128)} %refs_2_.1) | copy-start | bytes 1540
  2.8 0.7 %copy-start.3 = (s32[2,8,8]{2,1,0:T(8,128)S(1)}, s32[2,8,8]{2,1,0:T(8,128)}, u32[]{:S(2)}) copy-start(s32[2,8,8]{2,1,0:T(8,128)} %refs_3_.1) | copy-start | bytes 1540
  26.3 1.4 %collective-permute-start.1 = (bf16[4,4,5,8,128]{4,3,2,1,0:T(8,128)(2,1)S(1)}, bf16[4,4,5,8,128]{4,3,2,1,0:T(8,128)(2,1)S(1)}, u32[]{:S(2)}, u32[]{:S(2)}) collective-permute-start(bf16[4,4,5,8,128]{4,3,2,1,0:T(8,128)(2,1)S(1)} %all_to_all.21.own_ref), channel_id=1, source_target_pairs={{1,0},{0,1},{3,2},{2,3},{5,4},{4,5},{7,6},{6,7},{9,8},{8,9},{11,10... | collective-permute-start | bytes 491528 | tf_op jit(solution)/shard_map/ppermute | solution.py:276
  44.8 1.3 %collective-permute-start.2 = (bf16[4,4,16,128]{3,2,1,0:T(8,128)(2,1)S(1)}, bf16[4,4,16,128]{3,2,1,0:T(8,128)(2,1)S(1)}, u32[]{:S(2)}, u32[]{:S(2)}) collective-permute-start(bf16[4,4,16,128]{3,2,1,0:T(8,128)(2,1)S(1)} %all_to_all.23.own_ref), channel_id=1, source_target_pairs={{1,0},{0,1},{3,2},{2,3},{5,4},{4,5},{7,6},{6,7},{9,8},{8,9},{11,10... | collective-permute-start | bytes 196616 | tf_op jit(solution)/shard_map/ppermute | solution.py:276

commit v4 on v3

--- a/solution.py
+++ b/solution.py
@@ -17,7 +17,6 @@
 BAND = 8
 WIDTH = 128
 REGION = PATCH + 2 * RADIUS
-GROUP = 4
 
 BF = jnp.bfloat16
 F32 = jnp.float32
@@ -53,10 +52,10 @@
     return parts
 
 
-def observation_rows(values_ref, inverse_ref, mask_ref):
+def observation_rows(stack_ref):
     points = FIELDS * BAND
-    weight = (mask_ref[...].astype(F32) * inverse_ref[...]).astype(BF).astype(F32).reshape(points, PATCH)
-    values = values_ref[...].reshape(points, PATCH)
+    values, inverse, mask = (stack_ref[i].reshape(points, PATCH) for i in range(3))
+    weight = (mask * inverse).astype(BF).astype(F32)
     high = values.astype(BF).astype(F32)
     middle = (values - high).astype(BF).astype(F32)
     low = values - high - middle
@@ -77,20 +76,7 @@
     return jnp.dot(gather, wide, preferred_element_type=F32)
 
 
-def prepare_kernel(*refs):
-    sources, rows_ref, obs_ref, held, sems = refs[:4], refs[4], refs[5], refs[6:10], refs[10]
-    points = FIELDS * BAND
-    copies = [pltpu.make_async_copy(a, b, sems.at[i]) for i, (a, b) in enumerate(zip(sources, held))]
-    for copy in copies:
-        copy.start()
-    for copy in copies:
-        copy.wait()
-    for i in range(points):
-        rows_ref[i] = held[0][pl.ds(i, LOCAL, stride=points), :]
-    obs_ref[...] = observation_rows(*held[1:])
-
-
-def pack_kernel(rows_ref, near_ref, obs_ref, out_ref):
+def pack_kernel(rows_ref, near_ref, stack_ref, out_ref):
     points = FIELDS * BAND
 
     def near(field, index):
@@ -121,7 +107,7 @@
     widen = (column == wanted).astype(F32).astype(BF)
     wide = jnp.dot(rows, widen, preferred_element_type=F32)
     height = LOCAL + 8
-    obs = obs_ref[...]
+    obs = observation_rows(stack_ref)
     for side in range(2):
         tails = [obs] * 8
         for half in range(2):
@@ -132,24 +118,18 @@
             parts = swap_blocks(parts, REGION)
             for i in range(8):
                 for eight in range(2):
-                    out_ref[i % GROUP, side * 2 + i // GROUP, half * 2 + eight] = parts[i][eight * 8 : eight * 8 + 8].astype(BF)
+                    out_ref[side * 8 + i, half * 2 + eight] = parts[i][eight * 8 : eight * 8 + 8].astype(BF)
                 tails[i] = tails[i] + parts[i][LOCAL:]
         for i in range(8):
-            out_ref[i % GROUP, side * 2 + i // GROUP, 4] = tails[i].astype(BF)
-
-
-def regroup_kernel(in_ref, out_ref):
-    for i in range(GROUP):
-        for j in range(GROUP):
-            out_ref[j, i] = in_ref[i, j]
+            out_ref[side * 8 + i, 4] = tails[i].astype(BF)
 
 
 def halves_of(ref, me):
-    count = GROUP * GROUP
-    tails = [ref[s // GROUP, s % GROUP, 4].astype(F32) for s in range(count)]
+    count = ref.shape[0]
+    tails = [ref[s, 4].astype(F32) for s in range(count)]
 
     def tail_of(device):
-        return ref[device // GROUP, device % GROUP, 4].astype(F32)
+        return ref[device, 4].astype(F32)
 
     lane = lax.broadcasted_iota(jnp.int32, (8, WIDTH), 1) % REGION
     left = tail_of(lax.rem(me + count - 1, count))
@@ -175,8 +155,7 @@
         mean = functools.reduce(jnp.add, means) * (1.0 / count)
         deviation = []
         for s, own_mean in enumerate(means):
-            block = ref.at[s // GROUP, s % GROUP]
-            value = jnp.concatenate([block[half * 2 + eight].astype(F32) for eight in range(2)], 0)
+            value = jnp.concatenate([ref[s, half * 2 + eight].astype(F32) for eight in range(2)], 0)
             deviation.append((value + (own_mean - mean)).astype(BF))
         weight = first[base + 2 : base + 3]
         obs = second[base + 2 : base + 3] + first[base + 3 : base + 4] + second[base + 3 : base + 4]
@@ -186,7 +165,8 @@
 
 
 def analysis_kernel(me_ref, own_ref, near_ref, out_ref):
-    members = GROUP * GROUP * LOCAL
+    count = own_ref.shape[0]
+    members = count * LOCAL
     me = me_ref[0]
     own = halves_of(own_ref, me)
     near = halves_of(near_ref, me)
@@ -247,16 +227,13 @@
     target = lax.broadcasted_iota(jnp.int32, (2 * WIDTH, WIDTH), 1)
     narrow = (lane == (target // PATCH) * REGION + RADIUS + target % PATCH).astype(F32).astype(BF)
     result = jnp.dot(result, narrow, preferred_element_type=F32).astype(BF)
-    for j in range(GROUP):
-        for k in range(GROUP):
-            start = (j * GROUP + k) * LOCAL
-            out_ref[j, k] = result[start : start + LOCAL]
+    for s in range(count):
+        out_ref[s] = result[s * LOCAL : (s + 1) * LOCAL]
 
 
 def unpack_kernel(own_ref, near_ref, out_ref):
     def rows_of(ref):
-        blocks = [ref[p % GROUP, p // GROUP].astype(F32) for p in range(GROUP * GROUP)]
-        parts = swap_blocks(blocks, PATCH)
+        parts = swap_blocks([ref[p].astype(F32) for p in range(ref.shape[0])], PATCH)
         half = BAND // 2
         return [
             [parts[h * FIELDS * half + field * half + r] for h in range(2) for r in range(half)]
@@ -292,28 +269,25 @@
 
 
 def join_region(after, before):
-    tail = jnp.concatenate([after[:, :, 4:, :4], before[:, :, 4:, 4:]], 3)
-    return jnp.concatenate([after[:, :, :2], before[:, :, 2:4], tail], 2)
+    tail = jnp.concatenate([after[:, 4:, :4], before[:, 4:, 4:]], 2)
+    return jnp.concatenate([after[:, :2], before[:, 2:4], tail], 1)
 
 
 def join_inner(after, before):
-    return jnp.concatenate([after[..., : WIDTH // 2], before[..., WIDTH // 2 :]], 3)
-
-
-def exchange(value, low):
-    places = range(GROUP)
-    groups = [[(i * GROUP + j) if low else (j * GROUP + i) for j in places] for i in places]
-    return lax.all_to_all(value, "mem", split_axis=0, concat_axis=0, axis_index_groups=groups, tiled=True)
-
-
-def call(kernel, name, out_shape, *args, space=pltpu.VMEM, scratch=()):
-    spaces = [pltpu.SMEM if arg.shape == (1,) else space for arg in args]
+    return jnp.concatenate([after[..., : WIDTH // 2], before[..., WIDTH // 2 :]], 2)
+
+
+def exchange(value):
+    return lax.all_to_all(value, "mem", split_axis=0, concat_axis=0, tiled=True)
+
+
+def call(kernel, name, out_shape, *args):
+    spaces = [pltpu.SMEM if arg.shape == (1,) else pltpu.VMEM for arg in args]
     return pl.pallas_call(
         kernel,
         out_shape=out_shape,
         in_specs=[pl.BlockSpec(memory_space=space) for space in spaces],
         out_specs=jax.tree.map(lambda _: pl.BlockSpec(memory_space=pltpu.VMEM), out_shape),
-        scratch_shapes=scratch,
         compiler_params=pltpu.CompilerParams(vmem_limit_bytes=16 * 2**20),
         name=name,
     )(*args)
@@ -322,25 +296,16 @@
 def local(sample_collection, obs_values, obs_inverse_variance, obs_mask):
     count = lax.axis_size("mem")
     shape = sample_collection.shape
-    assert shape == (LOCAL, FIELDS, BAND, WIDTH) and count * PATCH == WIDTH and count == GROUP * GROUP
+    assert shape == (LOCAL, FIELDS, BAND, WIDTH) and count * PATCH == WIDTH
     me = lax.axis_index("mem").astype(jnp.int32).reshape(1)
     near = near_rows(sample_collection, join_grid)
-    sources = (sample_collection.reshape(-1, WIDTH), obs_values, obs_inverse_variance, obs_mask)
-    rows, obs = call(
-        prepare_kernel,
-        "prepare",
-        [jax.ShapeDtypeStruct((FIELDS * BAND, LOCAL, WIDTH), F32), jax.ShapeDtypeStruct((8, WIDTH), F32)],
-        *sources,
-        space=pltpu.HBM,
-        scratch=[pltpu.VMEM(x.shape, x.dtype) for x in sources] + [pltpu.SemaphoreType.DMA((len(sources),))],
-    )
-    region_shape = jax.ShapeDtypeStruct((GROUP, GROUP, 5, 8, WIDTH), BF)
-    inner_shape = jax.ShapeDtypeStruct((GROUP, GROUP, LOCAL, WIDTH), BF)
-    sending = call(pack_kernel, "forecast_pack", region_shape, rows, near.reshape(-1, WIDTH), obs)
-    region = exchange(call(regroup_kernel, "regroup_region", region_shape, exchange(sending, True)), False)
+    rows = jnp.transpose(sample_collection.reshape(LOCAL, FIELDS * BAND, WIDTH), (1, 0, 2))
+    stack = jnp.stack([obs_values, obs_inverse_variance, obs_mask.astype(F32)])
+    region_shape = jax.ShapeDtypeStruct((count, 5, 8, WIDTH), BF)
+    inner_shape = jax.ShapeDtypeStruct((count, LOCAL, WIDTH), BF)
+    region = exchange(call(pack_kernel, "forecast_pack", region_shape, rows, near.reshape(-1, WIDTH), stack))
     region_near = near_rows(region, join_region)
-    returning = call(analysis_kernel, "analysis", inner_shape, me, region, region_near)
-    inner = exchange(call(regroup_kernel, "regroup_inner", inner_shape, exchange(returning, False)), True)
+    inner = exchange(call(analysis_kernel, "analysis", inner_shape, me, region, region_near))
     inner_near = near_rows(inner, join_inner)
     cycled = call(
         unpack_kernel,

time: 47.9 us -> 36.1 us (0.75)
  blocking collectives: 36.8 us -> 27 us
  local copies, waits for them, and re-layouts: 2.99 us -> 0.98 us
  other arithmetic: 0 us -> 0.7 us
  Pallas kernels: 4.52 us -> 4 us
    all_to_all x4 -> x2, blocking collectives: 36.8 us -> 27 us  [exchange(): return lax.all_to_all(value, 'mem', split_axis=0, concat_axis=0, tiled=True)]
    unnamed x8 -> x5, local copies, waits for them, and re-layouts: 2.99 us -> 0.98 us
    another operation x0 -> x2, other arithmetic: none -> 0.7 us  [local(): stack = jnp.stack([obs_values, obs_inverse_variance, obs_mask.astype(F32)])]
    pallas_call x6 -> x3, Pallas kernels: 4.52 us -> 4 us  [call(): pl.pallas_call(kernel, out_shape=out_shape, in_specs=[pl.BlockSpec(memory...]
  transfers between devices with their start and end apart: 3 -> 3, of which waited for: 2 -> 2; matrix products, arithmetic and copies ran while one was open for 0% -> 5% of each run, Pallas kernels for 1% -> 0%
where the time goes in v4:
time: 36.1 us; the launch traced here: 35.8 us
  blocking collectives  27 us (75%)
  Pallas kernels  4 us (11%)
  waiting for transfers between devices  2.65 us (7%)
  local copies, waits for them, and re-layouts  0.98 us (3%)
  other arithmetic  0.7 us (2%)
  starting transfers between devices  0.46 us (1%)
    all_to_all x2, blocking collectives, exchange(): return lax.all_to_all(value, 'mem', split_axis=0, concat_axis=0, tiled=True)  27 us
    pallas_call x3, Pallas kernels, call(): pl.pallas_call(kernel, out_shape=out_shape, in_specs=[pl.BlockSpec(memory...  4 us
    ppermute x3, waiting for transfers between devices, from_next(): lax.ppermute(value, 'rows', [((i + 1) % count, i) for i in range(count)])  2.65 us
    unnamed x5, local copies, waits for them, and re-layouts  0.98 us
  transfers between devices with their start and end apart: 3, of which 2 were waited for; matrix products, arithmetic and copies ran while one was open for 5% of the time, Pallas kernels for 0%

profile of v4, /device:TPU:0, one launch (start us, length us, event | category | flops | bytes accessed | tf_op | source)
XLA Modules:
  0.0 35.8 jit_solution(17724517394052814243)
XLA Ops:
  0.0 0.5 %collective-permute-start = (f32[16,2,8,128]{3,2,1,0:T(8,128)}, f32[16,2,8,128]{3,2,1,0:T(8,128)S(1)}, u32[]{:S(2)}, u32[]{:S(2)}) collective-permute-start(f32[16,2,8,128]{3,2,1,0:T(8,128)} %param.4), channel_id=1, source_target_pairs={{1,0},{0,1},{3,2},{2,3},{5,4},{4,5},{7,6},{6,7},{9,8},{8,9},{11,10... | collective-permute-start | bytes 393224 | tf_op jit(solution)/shard_map/ppermute | solution.py:253
  0.5 0.7 %convert_bitcast_fusion = f32[1,2,8,8]{3,2,1,0:T(8,128)S(1)} fusion(s32[2,8,8]{2,1,0:T(8,128)} %param.7), kind=kLoop, calls=%fused_computation.1 | loop fusion | flops 128 | bytes 1024 | tf_op jit(solution)/shard_map/stack | solution.py:303
  1.2 0.0 copy-start
  1.2 0.0 copy-start.1
  1.2 1.0 %copy.5 = f32[16,2,8,128]{3,0,2,1:T(8,128)S(1)} copy(f32[16,2,8,128]{3,2,1,0:T(8,128)} %param.4) | data formatting | bytes 262144 | tf_op args[0]
  2.1 0.0 copy-done
  2.1 0.0 copy-done.1
  2.2 0.0 collective-permute-done
  2.2 0.8 %forecast_pack.1 = bf16[16,5,8,128]{3,2,1,0:T(8,128)(2,1)S(1)} custom-call(f32[16,16,128]{2,1,0:T(8,128)S(1)} %bitcast.10, f32[256,128]{1,0:T(8,128)S(1)} %bitcast.11, f32[3,2,8,8]{3,2,1,0:T(8,128)S(1)} %pad_maximum_fusion.stack_ref), custom_call_target="tpu_custom_call" | custom-call | tf_op jit(solution)/shard_map/forecast_pack/pallas_call | solution.py:286
  3.0 16.2 %all_to_all.10.own_ref = bf16[16,5,8,128]{3,2,1,0:T(8,128)(2,1)S(1)} all-to-all(bf16[16,5,8,128]{3,2,1,0:T(8,128)(2,1)S(1)} %forecast_pack.1), channel_id=1, replica_groups=mesh['mem'=16,'rows'=2] {'mem'}, dimensions={0} | all-to-all | bytes 327680 | tf_op jit(solution)/shard_map/all_to_all | solution.py:281
  19.2 0.0 collective-permute-start.1
  19.2 1.4 %collective-permute-done.1.near_ref = bf16[16,5,8,128]{3,2,1,0:T(8,128)(2,1)S(1)} collective-permute-done((bf16[16,5,8,128]{3,2,1,0:T(8,128)(2,1)S(1)}, bf16[16,5,8,128]{3,2,1,0:T(8,128)(2,1)S(1)}, u32[]{:S(2)}, u32[]{:S(2)}) %collective-permute-start.1) | collective-permute-done | bytes 163872 | tf_op jit(solution)/shard_map/ppermute | solution.py:253
  20.6 1.8 %analysis.1 = bf16[16,16,128]{2,1,0:T(8,128)(2,1)S(1)} custom-call(s32[1]{0:T(128)} %bitcast.me_ref, bf16[16,5,8,128]{3,2,1,0:T(8,128)(2,1)S(1)} %all_to_all.10.own_ref, bf16[16,5,8,128]{3,2,1,0:T(8,128)(2,1)S(1)} %collective-permute-done.1.near_ref), custom_call_target="tpu_custom_call" | custom-call | tf_op jit(solution)/shard_map/analysis/pallas_call | solution.py:286
  22.4 10.8 %all_to_all.11.own_ref = bf16[16,16,128]{2,1,0:T(8,128)(2,1)S(1)} all-to-all(bf16[16,16,128]{2,1,0:T(8,128)(2,1)S(1)} %analysis.1), channel_id=1, replica_groups=mesh['mem'=16,'rows'=2] {'mem'}, dimensions={0} | all-to-all | bytes 131072 | tf_op jit(solution)/shard_map/all_to_all | solution.py:281
  33.2 0.0 collective-permute-start.2
  33.2 1.3 %collective-permute-done.2.near_ref = bf16[16,16,128]{2,1,0:T(8,128)(2,1)S(1)} collective-permute-done((bf16[16,16,128]{2,1,0:T(8,128)(2,1)S(1)}, bf16[16,16,128]{2,1,0:T(8,128)(2,1)S(1)}, u32[]{:S(2)}, u32[]{:S(2)}) %collective-permute-start.2) | collective-permute-done | bytes 65568 | tf_op jit(solution)/shard_map/ppermute | solution.py:253
  34.4 1.4 %unpack_forecast.1 = f32[256,128]{1,0:T(8,128)} custom-call(bf16[16,16,128]{2,1,0:T(8,128)(2,1)S(1)} %all_to_all.11.own_ref, bf16[16,16,128]{2,1,0:T(8,128)(2,1)S(1)} %collective-permute-done.2.near_ref), custom_call_target="tpu_custom_call" | custom-call | tf_op jit(solution)/shard_map/unpack_forecast/pallas_call | solution.py:286
  (1 shorter events, 0.0 us)
Async XLA Ops:
  0.0 2.2 %collective-permute-start = (f32[16,2,8,128]{3,2,1,0:T(8,128)}, f32[16,2,8,128]{3,2,1,0:T(8,128)S(1)}, u32[]{:S(2)}, u32[]{:S(2)}) collective-permute-start(f32[16,2,8,128]{3,2,1,0:T(8,128)} %param.4), channel_id=1, source_target_pairs={{1,0},{0,1},{3,2},{2,3},{5,4},{4,5},{7,6},{6,7},{9,8},{8,9},{11,10... | collective-permute-start | bytes 393224 | tf_op jit(solution)/shard_map/ppermute | solution.py:253
  1.2 1.0 %copy-start = (f32[2,8,8]{2,1,0:T(8,128)S(1)}, f32[2,8,8]{2,1,0:T(8,128)}, u32[]{:S(2)}) copy-start(f32[2,8,8]{2,1,0:T(8,128)} %param.6) | copy-start | bytes 1540
  1.2 1.0 %copy-start.1 = (f32[2,8,8]{2,1,0:T(8,128)S(1)}, f32[2,8,8]{2,1,0:T(8,128)}, u32[]{:S(2)}) copy-start(f32[2,8,8]{2,1,0:T(8,128)} %param.5) | copy-start | bytes 1540
  19.2 1.4 %collective-permute-start.1 = (bf16[16,5,8,128]{3,2,1,0:T(8,128)(2,1)S(1)}, bf16[16,5,8,128]{3,2,1,0:T(8,128)(2,1)S(1)}, u32[]{:S(2)}, u32[]{:S(2)}) collective-permute-start(bf16[16,5,8,128]{3,2,1,0:T(8,128)(2,1)S(1)} %all_to_all.10.own_ref), channel_id=1, source_target_pairs={{1,0},{0,1},{3,2},{2,3},{5,4},{4,5},{7,6},{6,7},{9,8},{8,9},{11,10... | collective-permute-start | bytes 491528 | tf_op jit(solution)/shard_map/ppermute | solution.py:253
  33.2 1.3 %collective-permute-start.2 = (bf16[16,16,128]{2,1,0:T(8,128)(2,1)S(1)}, bf16[16,16,128]{2,1,0:T(8,128)(2,1)S(1)}, u32[]{:S(2)}, u32[]{:S(2)}) collective-permute-start(bf16[16,16,128]{2,1,0:T(8,128)(2,1)S(1)} %all_to_all.11.own_ref), channel_id=1, source_target_pairs={{1,0},{0,1},{3,2},{2,3},{5,4},{4,5},{7,6},{6,7},{9,8},{8,9},{11,10... | collective-permute-start | bytes 196616 | tf_op jit(solution)/shard_map/ppermute | solution.py:253

commit v5 on v4

--- a/solution.py
+++ b/solution.py
@@ -52,10 +52,10 @@
     return parts
 
 
-def observation_rows(stack_ref):
+def observation_rows(values_ref, inverse_ref, mask_ref):
     points = FIELDS * BAND
-    values, inverse, mask = (stack_ref[i].reshape(points, PATCH) for i in range(3))
-    weight = (mask * inverse).astype(BF).astype(F32)
+    weight = (mask_ref[...].astype(F32) * inverse_ref[...]).astype(BF).astype(F32).reshape(points, PATCH)
+    values = values_ref[...].reshape(points, PATCH)
     high = values.astype(BF).astype(F32)
     middle = (values - high).astype(BF).astype(F32)
     low = values - high - middle
@@ -76,7 +76,7 @@
     return jnp.dot(gather, wide, preferred_element_type=F32)
 
 
-def pack_kernel(rows_ref, near_ref, stack_ref, out_ref):
+def pack_kernel(rows_ref, near_ref, values_ref, inverse_ref, mask_ref, out_ref):
     points = FIELDS * BAND
 
     def near(field, index):
@@ -89,39 +89,33 @@
         after = [near(field, r) for r in range(FSTEPS)]
         fields.append(before + own + after)
     done = forecast_rows(*fields)
-    stacked = []
+    half_rows = BAND // 2
     index = lax.broadcasted_iota(jnp.int32, (8, WIDTH), 0)
+    values, means = [], [jnp.zeros((8, WIDTH), F32)] * (FIELDS * half_rows)
     for half in range(2):
-        for field in range(FIELDS):
-            for r in range(BAND // 2):
-                value = done[field][half * (BAND // 2) + r]
-                mean = jnp.sum(value, 0, keepdims=True) * (1.0 / LOCAL)
-                high = mean.astype(BF).astype(F32)
-                low = mean - high
-                tail = jnp.where(index == 4 * half, high, jnp.where(index == 4 * half + 1, low, 0.0))
-                stacked += [value - mean, tail]
-    rows = jnp.concatenate(stacked, 0).astype(BF)
-    column = lax.broadcasted_iota(jnp.int32, (WIDTH, 2 * WIDTH), 0)
-    lane = lax.broadcasted_iota(jnp.int32, (WIDTH, 2 * WIDTH), 1)
-    wanted = ((lane // REGION) * PATCH + lane % REGION + (WIDTH - RADIUS)) % WIDTH
-    widen = (column == wanted).astype(F32).astype(BF)
-    wide = jnp.dot(rows, widen, preferred_element_type=F32)
-    height = LOCAL + 8
-    obs = observation_rows(stack_ref)
-    for side in range(2):
-        tails = [obs] * 8
+        for j in range(FIELDS * half_rows):
+            value = done[j // half_rows][half * half_rows + j % half_rows]
+            mean = jnp.sum(value, 0, keepdims=True) * (1.0 / LOCAL)
+            high = mean.astype(BF).astype(F32)
+            means[j] = jnp.where(index == 4 * half, high, jnp.where(index == 4 * half + 1, mean - high, means[j]))
+            values.append(value - mean)
+    obs = observation_rows(values_ref, inverse_ref, mask_ref)
+    is_mean = index & 2 == 0
+    means = [
+        jnp.where(is_mean, pltpu.roll(m, RADIUS, 1), pltpu.roll(pltpu.roll(m, WIDTH + RADIUS - PATCH, 1), 2, 0))
+        for m in means
+    ]
+    means = swap_blocks(means, REGION)
+    for parity in range(2):
+        for i in range(8):
+            mean = pltpu.roll(means[i], 6, 0) if parity else means[i]
+            out_ref[2 * i + parity, 4] = jnp.where(is_mean, mean, obs).astype(BF)
         for half in range(2):
-            parts = [
-                wide[(half * 8 + j) * height : (half * 8 + j + 1) * height, side * WIDTH : (side + 1) * WIDTH]
-                for j in range(8)
-            ]
-            parts = swap_blocks(parts, REGION)
+            shift = (WIDTH + RADIUS - parity * PATCH) % WIDTH
+            parts = swap_blocks([pltpu.roll(v, shift, 1) for v in values[half * 8 : half * 8 + 8]], REGION)
             for i in range(8):
                 for eight in range(2):
-                    out_ref[side * 8 + i, half * 2 + eight] = parts[i][eight * 8 : eight * 8 + 8].astype(BF)
-                tails[i] = tails[i] + parts[i][LOCAL:]
-        for i in range(8):
-            out_ref[side * 8 + i, 4] = tails[i].astype(BF)
+                    out_ref[2 * i + parity, half * 2 + eight] = parts[i][eight * 8 : eight * 8 + 8].astype(BF)
 
 
 def halves_of(ref, me):
@@ -164,88 +158,114 @@
     return result
 
 
-def analysis_kernel(me_ref, own_ref, near_ref, out_ref):
-    count = own_ref.shape[0]
-    members = count * LOCAL
-    me = me_ref[0]
-    own = halves_of(own_ref, me)
-    near = halves_of(near_ref, me)
+def half_sums(halves, row_distances):
     lane = lax.broadcasted_iota(jnp.int32, (1, WIDTH), 1)
     region_column = lane % REGION
     half_row = (lane // REGION) % (BAND // 2)
     column_distance = jnp.maximum(
         jnp.maximum(RADIUS - region_column, region_column - (RADIUS + PATCH - 1)), 0
     )
-    row_distances = (0 * lane, 0 * lane, half_row + 1, RADIUS - half_row)
     weighted, deviation, innovation = [], [], []
-    for (dev, _, weight, inno), row_distance in zip(own + near, row_distances):
-        far = jnp.maximum(row_distance, column_distance).astype(F32)
+    for (dev, _, weight, inno), row_distance in zip(halves, row_distances):
+        far = jnp.maximum(row_distance(half_row), column_distance).astype(F32)
         factor = weight * (1.0 - far / (RADIUS + 1.0))
         weighted.append((dev.astype(F32) * factor).astype(BF))
         deviation.append(dev)
         innovation.append(jnp.broadcast_to(inno, (16, WIDTH)).astype(BF))
+    deviation = jnp.concatenate(deviation, 1)
+    rows = jnp.concatenate([deviation, jnp.concatenate(innovation, 1)], 0)
     weighted = jnp.concatenate(weighted, 1)
-    inner = jnp.concatenate(deviation[:2], 1)
-    rows = jnp.concatenate([jnp.concatenate(deviation, 1), jnp.concatenate(innovation, 1)], 0)
-    both = lax.dot_general(rows, weighted, (((1,), (1,)), ((), ())), preferred_element_type=F32)
+    return deviation, lax.dot_general(rows, weighted, (((1,), (1,)), ((), ())), preferred_element_type=F32)
+
+
+def own_kernel(me_ref, own_ref, inner_ref, sums_ref, mean_ref):
+    halves = halves_of(own_ref, me_ref[0])
+    deviation, sums_ref[...] = half_sums(halves, [jnp.zeros_like] * 2)
+    lane = lax.broadcasted_iota(jnp.int32, (2 * WIDTH, WIDTH), 0)
+    target = lax.broadcasted_iota(jnp.int32, (2 * WIDTH, WIDTH), 1)
+    narrow = (lane == (target // PATCH) * REGION + RADIUS + target % PATCH).astype(F32).astype(BF)
+    inner_ref[...] = jnp.dot(deviation, narrow, preferred_element_type=F32).astype(BF)
+    mean = jnp.broadcast_to(jnp.concatenate([halves[0][1], halves[1][1]], 1), (16, 2 * WIDTH))
+    high = mean.astype(BF)
+    middle = (mean - high.astype(F32)).astype(BF)
+    low = (mean - high.astype(F32) - middle.astype(F32)).astype(BF)
+    parts = jnp.dot(jnp.concatenate([high, middle, low], 0), narrow, preferred_element_type=F32)
+    mean_ref[...] = parts[:8] + (parts[16:24] + parts[32:40])
+
+
+def analysis_kernel(me_ref, near_ref, inner_ref, sums_ref, mean_ref, out_ref):
+    count = near_ref.shape[0]
+    members = count * LOCAL
+    halves = halves_of(near_ref, me_ref[0])
+    both = sums_ref[...] + half_sums(halves, [lambda r: r + 1, lambda r: RADIUS - r])[1]
     row = lax.broadcasted_iota(jnp.int32, (members, members), 0)
     col = lax.broadcasted_iota(jnp.int32, (members, members), 1)
     system = both[:members] + jnp.where(row == col, members - 1.0, 0.0)
-    line = both[members:]
-    scale = jnp.sqrt(jnp.sum(system * system))
-    y0 = system * (1.0 / scale)
-
     def mul(a, b):
         return jnp.dot(a.astype(BF), b.astype(BF), preferred_element_type=F32)
 
-    y0b = y0.astype(BF)
-    inner_f = inner.astype(F32)
-    x1 = 1.5 * inner_f - 0.5 * mul(y0b, inner)
-    line1 = 1.5 * line - 0.5 * mul(line, y0b)
-    y1 = 1.5 * y0 - 0.5 * mul(y0b, y0b)
-    p1 = 1.5 * y1 - 0.5 * mul(y1, y0b)
+    def with_line(a, line):
+        return jnp.concatenate([a.astype(BF), line.astype(BF)], 0)
+
+    inner, line = inner_ref[...], both[members:]
+    system_b = system.astype(BF)
+    first = mul(with_line(system_b, line), system_b)
+    system_x = mul(system_b, inner)
+    scale = jnp.sqrt(jnp.sum(system * system))
+    inverse = 1.0 / scale
+    x1 = 1.5 * inner.astype(F32) - (0.5 * inverse) * system_x
+    line1 = 1.5 * line - (0.5 * inverse) * first[members:]
+    y1 = inverse * (1.5 * system - (0.5 * inverse) * first[:members])
+    p1 = 1.5 * y1 - (0.5 * inverse) * mul(y1, system_b)
     p1b = p1.astype(BF)
+    second = mul(with_line(p1b, line1), p1b)
     x2 = 1.5 * x1 - 0.5 * mul(p1b, x1)
-    line2 = 1.5 * line1 - 0.5 * mul(line1, p1b)
-    q1 = 1.5 * p1 - 0.5 * mul(p1b, p1b)
+    line2 = 1.5 * line1 - 0.5 * second[members:]
+    q1 = 1.5 * p1 - 0.5 * second[:members]
     p2 = 1.5 * q1 - 0.5 * mul(q1, p1b)
     p2b = p2.astype(BF)
-    x3 = 1.5 * x2 - 0.5 * mul(p2b, x2)
-    line3 = 1.5 * line2 - 0.5 * mul(line2, p2b)
-    inverse = 1.0 / jnp.sqrt(scale)
-    x3 = x3 * inverse
-    line3 = line3 * inverse
-    xh = x3.astype(BF)
-    xl = (x3 - xh.astype(F32)).astype(BF)
-    lh = line3.astype(BF)
-    ll = (line3 - lh.astype(F32)).astype(BF)
-    shift = mul(lh, xh) + (mul(ll, xh) + mul(lh, xl))
-    mean = jnp.concatenate([own[0][1], own[1][1]], 1)
+    factor = 1.0 / jnp.sqrt(scale)
+    x3 = (1.5 * x2 - 0.5 * mul(p2b, x2)) * factor
+    line3 = (1.5 * line2 - 0.5 * mul(line2, p2b)) * factor
+    line_b = line3.astype(BF)
+    lines = with_line(line_b, line3 - line_b.astype(F32))
+    shift = mul(lines, x3)
+    shift = shift[:1] + shift[16:17]
     root = jnp.sqrt(jnp.full((1, 1), members - 1.0, F32))
-    result = (root * x3 + (shift[:1] + mean)).astype(BF)
-    lane = lax.broadcasted_iota(jnp.int32, (2 * WIDTH, WIDTH), 0)
-    target = lax.broadcasted_iota(jnp.int32, (2 * WIDTH, WIDTH), 1)
-    narrow = (lane == (target // PATCH) * REGION + RADIUS + target % PATCH).astype(F32).astype(BF)
-    result = jnp.dot(result, narrow, preferred_element_type=F32).astype(BF)
+    result = (root * x3 + (shift + mean_ref[:1])).astype(BF)
     for s in range(count):
-        out_ref[s] = result[s * LOCAL : (s + 1) * LOCAL]
-
-
-def unpack_kernel(own_ref, near_ref, out_ref):
-    def rows_of(ref):
-        parts = swap_blocks([ref[p].astype(F32) for p in range(ref.shape[0])], PATCH)
+        for eight in range(2):
+            out_ref[s, eight] = result[s * LOCAL + eight * 8 : s * LOCAL + eight * 8 + 8]
+
+
+def unpacked(ref, eight):
+    return swap_blocks([ref[p, eight].astype(F32) for p in range(ref.shape[0])], PATCH)
+
+
+def unpack_kernel(in_ref, out_ref):
+    @pl.loop(0, 2)
+    def _(eight):
+        for i, row in enumerate(unpacked(in_ref, eight)):
+            out_ref[eight, i] = row
+
+
+def forecast_kernel(own_ref, near_ref, out_ref):
+    def by_field(rows):
         half = BAND // 2
         return [
-            [parts[h * FIELDS * half + field * half + r] for h in range(2) for r in range(half)]
+            [rows[h * FIELDS * half + field * half + r] for h in range(2) for r in range(half)]
             for field in range(FIELDS)
         ]
 
-    own, near = rows_of(own_ref), rows_of(near_ref)
-    fields = [n[BAND - FSTEPS :] + o + n[:FSTEPS] for o, n in zip(own, near)]
-    done = forecast_rows(*fields)
-    for field in range(FIELDS):
-        for r in range(BAND):
-            out_ref[pl.ds(field * BAND + r, LOCAL, stride=FIELDS * BAND), :] = done[field][r]
+    @pl.loop(0, 2)
+    def _(eight):
+        own, near = by_field(own_ref.at[eight]), by_field(unpacked(near_ref, eight))
+        fields = [n[BAND - FSTEPS :] + o + n[:FSTEPS] for o, n in zip(own, near)]
+        done = forecast_rows(*fields)
+        points = FIELDS * BAND
+        for field in range(FIELDS):
+            for r in range(BAND):
+                out_ref[pl.ds(eight * 8 * points + field * BAND + r, 8, stride=points), :] = done[field][r]
 
 
 def from_next(value):
@@ -274,21 +294,23 @@
 
 
 def join_inner(after, before):
-    return jnp.concatenate([after[..., : WIDTH // 2], before[..., WIDTH // 2 :]], 2)
+    return jnp.concatenate([after[..., : WIDTH // 2], before[..., WIDTH // 2 :]], 3)
 
 
 def exchange(value):
     return lax.all_to_all(value, "mem", split_axis=0, concat_axis=0, tiled=True)
 
 
-def call(kernel, name, out_shape, *args):
+def call(kernel, name, out_shape, *args, flops=0):
     spaces = [pltpu.SMEM if arg.shape == (1,) else pltpu.VMEM for arg in args]
+    moved = sum(x.size * x.dtype.itemsize for x in [*args, *jax.tree.leaves(out_shape)])
     return pl.pallas_call(
         kernel,
         out_shape=out_shape,
         in_specs=[pl.BlockSpec(memory_space=space) for space in spaces],
         out_specs=jax.tree.map(lambda _: pl.BlockSpec(memory_space=pltpu.VMEM), out_shape),
         compiler_params=pltpu.CompilerParams(vmem_limit_bytes=16 * 2**20),
+        cost_estimate=pl.CostEstimate(flops=flops, bytes_accessed=moved, transcendentals=0),
         name=name,
     )(*args)
 
@@ -300,20 +322,25 @@
     me = lax.axis_index("mem").astype(jnp.int32).reshape(1)
     near = near_rows(sample_collection, join_grid)
     rows = jnp.transpose(sample_collection.reshape(LOCAL, FIELDS * BAND, WIDTH), (1, 0, 2))
-    stack = jnp.stack([obs_values, obs_inverse_variance, obs_mask.astype(F32)])
     region_shape = jax.ShapeDtypeStruct((count, 5, 8, WIDTH), BF)
-    inner_shape = jax.ShapeDtypeStruct((count, LOCAL, WIDTH), BF)
-    region = exchange(call(pack_kernel, "forecast_pack", region_shape, rows, near.reshape(-1, WIDTH), stack))
+    inner_shape = jax.ShapeDtypeStruct((count, 2, 8, WIDTH), BF)
+    observations = (obs_values, obs_inverse_variance, obs_mask)
+    region = exchange(call(pack_kernel, "forecast_pack", region_shape, rows, near.reshape(-1, WIDTH), *observations))
+    members, points = count * LOCAL, 2 * WIDTH
+    own_shapes = [
+        jax.ShapeDtypeStruct((members, WIDTH), BF),
+        jax.ShapeDtypeStruct((members + 16, members), F32),
+        jax.ShapeDtypeStruct((8, WIDTH), F32),
+    ]
+    flops = 2 * members * members * points
     region_near = near_rows(region, join_region)
-    inner = exchange(call(analysis_kernel, "analysis", inner_shape, me, region, region_near))
+    own = call(own_kernel, "own_half", own_shapes, me, region, flops=flops)
+    inner = exchange(call(analysis_kernel, "analysis", inner_shape, me, region_near, *own, flops=8 * flops))
     inner_near = near_rows(inner, join_inner)
-    cycled = call(
-        unpack_kernel,
-        "unpack_forecast",
-        jax.ShapeDtypeStruct((LOCAL * FIELDS * BAND, WIDTH), F32),
-        inner,
-        inner_near,
-    )
+    rows_shape = jax.ShapeDtypeStruct((2, FIELDS * BAND, 8, WIDTH), F32)
+    inner = call(unpack_kernel, "unpack_own", rows_shape, inner)
+    out_shape = jax.ShapeDtypeStruct((LOCAL * FIELDS * BAND, WIDTH), F32)
+    cycled = call(forecast_kernel, "unpack_forecast", out_shape, inner, inner_near)
     return cycled.reshape(shape)
 
 

time: 36.1 us -> 35.7 us (0.989)
  Pallas kernels: 4 us -> 5.14 us
  waiting for transfers between devices: 2.65 us -> 1.92 us
  other arithmetic: 0.7 us -> 0 us
    pallas_call x3 -> x5, Pallas kernels: 4 us -> 5.14 us  [call(): pl.pallas_call(kernel, out_shape=out_shape, in_specs=[pl.BlockSpec(memory...]
    ppermute x3, waiting for transfers between devices: 2.65 us -> 1.92 us  [from_next(): lax.ppermute(value, 'rows', [((i + 1) % count, i) for i in range(count)])]
    another operation x2 -> x0, other arithmetic: 0.7 us -> none  [local(): stack = jnp.stack([obs_values, obs_inverse_variance, obs_mask.astype(F32)])]
    unnamed x5 -> x7, local copies, waits for them, and re-layouts: 0.98 us -> 1 us
  transfers between devices with their start and end apart: 3 -> 3, of which waited for: 2 -> 3; matrix products, arithmetic and copies ran while one was open for 5% -> 3% of each run, Pallas kernels for 0% -> 3%
where the time goes in v5:
time: 35.7 us; the launch traced here: 35.5 us
  blocking collectives  27 us (76%)
  Pallas kernels  5.14 us (14%)
  waiting for transfers between devices  1.92 us (5%)
  local copies, waits for them, and re-layouts  1 us (3%)
  starting transfers between devices  0.46 us (1%)
    all_to_all x2, blocking collectives, exchange(): return lax.all_to_all(value, 'mem', split_axis=0, concat_axis=0, tiled=True)  27 us
    pallas_call x5, Pallas kernels, call(): pl.pallas_call(kernel, out_shape=out_shape, in_specs=[pl.BlockSpec(memory...  5.14 us
    ppermute x3, waiting for transfers between devices, from_next(): lax.ppermute(value, 'rows', [((i + 1) % count, i) for i in range(count)])  1.92 us
    unnamed x7, local copies, waits for them, and re-layouts  1 us
  transfers between devices with their start and end apart: 3, of which 3 were waited for; matrix products, arithmetic and copies ran while one was open for 3% of the time, Pallas kernels for 3%

profile of v5, /device:TPU:0, one launch (start us, length us, event | category | flops | bytes accessed | tf_op | source)
XLA Modules:
  0.0 35.5 jit_solution(11385613575091887899)
XLA Ops:
  0.0 0.5 %collective-permute-start = (f32[16,2,8,128]{3,2,1,0:T(8,128)}, f32[16,2,8,128]{3,2,1,0:T(8,128)S(1)}, u32[]{:S(2)}, u32[]{:S(2)}) collective-permute-start(f32[16,2,8,128]{3,2,1,0:T(8,128)} %param.4), channel_id=1, source_target_pairs={{1,0},{0,1},{3,2},{2,3},{5,4},{4,5},{7,6},{6,7},{9,8},{8,9},{11,10... | collective-permute-start | bytes 393224 | tf_op jit(solution)/shard_map/ppermute | solution.py:273
  0.5 0.0 copy-start
  0.5 0.0 copy-start.1
  0.5 0.0 copy-start.2
  0.5 1.0 %copy.5 = f32[16,2,8,128]{3,0,2,1:T(8,128)S(1)} copy(f32[16,2,8,128]{3,2,1,0:T(8,128)} %param.4) | data formatting | bytes 262144 | tf_op args[0]
  1.5 0.2 collective-permute-done
  1.7 0.0 copy-done
  1.7 0.0 copy-done.1
  1.7 0.0 copy-done.2
  1.7 1.1 %forecast_pack.1 = bf16[16,5,8,128]{3,2,1,0:T(8,128)(2,1)S(1)} custom-call(f32[16,16,128]{2,1,0:T(8,128)S(1)} %bitcast.6, f32[256,128]{1,0:T(8,128)S(1)} %bitcast.7, f32[2,8,8]{2,1,0:T(8,128)S(1)} %copy-done, f32[2,8,8]{2,1,0:T(8,128)S(1)} %copy-done.1, s32[2,8,8]{2,1,0:T(8,128)S(1)} %copy-done.2), custom_call_target="tpu_custom_call" | custom-call | bytes 427520 | tf_op jit(solution)/shard_map/forecast_pack/pallas_call | solution.py:307
  2.7 16.2 %all_to_all.10.own_ref = bf16[16,5,8,128]{3,2,1,0:T(8,128)(2,1)S(1)} all-to-all(bf16[16,5,8,128]{3,2,1,0:T(8,128)(2,1)S(1)} %forecast_pack.1), channel_id=1, replica_groups=mesh['mem'=16,'rows'=2] {'mem'}, dimensions={0} | all-to-all | bytes 327680 | tf_op jit(solution)/shard_map/all_to_all | solution.py:301
  18.9 0.0 collective-permute-start.1
  18.9 0.3 own_half.1
  19.2 1.1 %collective-permute-done.1.near_ref = bf16[16,5,8,128]{3,2,1,0:T(8,128)(2,1)S(1)} collective-permute-done((bf16[16,5,8,128]{3,2,1,0:T(8,128)(2,1)S(1)}, bf16[16,5,8,128]{3,2,1,0:T(8,128)(2,1)S(1)}, u32[]{:S(2)}, u32[]{:S(2)}) %collective-permute-start.1) | collective-permute-done | bytes 163872 | tf_op jit(solution)/shard_map/ppermute | solution.py:273
  20.3 1.3 %analysis.1 = bf16[16,2,8,128]{3,2,1,0:T(8,128)(2,1)S(1)} custom-call(s32[1]{0:T(128)} %bitcast.me_ref, bf16[16,5,8,128]{3,2,1,0:T(8,128)(2,1)S(1)} %collective-permute-done.1.near_ref, bf16[256,128]{1,0:T(8,128)(2,1)S(1)} %get-tuple-element.8.inner_ref, f32[272,256]{1,0:T(8,128)S(1)} %get-tuple-element.9.sums_ref, f32[8,128]{1,0:T(8,128)S(1)} %get-tuple-element.10.mean_ref), custom_call_target="tpu_custom_call" | custom-call | flops 268435456 | bytes 577540 | tf_op jit(solution)/shard_map/analysis/pallas_call | solution.py:307
  21.6 10.8 %all_to_all.11.in_ref = bf16[16,2,8,128]{3,2,1,0:T(8,128)(2,1)S(1)} all-to-all(bf16[16,2,8,128]{3,2,1,0:T(8,128)(2,1)S(1)} %analysis.1), channel_id=1, replica_groups=mesh['mem'=16,'rows'=2] {'mem'}, dimensions={0} | all-to-all | bytes 131072 | tf_op jit(solution)/shard_map/all_to_all | solution.py:301
  32.4 0.0 collective-permute-start.2
  32.4 0.6 %unpack_own.1.own_ref = f32[2,16,8,128]{3,2,1,0:T(8,128)S(1)} custom-call(bf16[16,2,8,128]{3,2,1,0:T(8,128)(2,1)S(1)} %all_to_all.11.in_ref), custom_call_target="tpu_custom_call" | custom-call | bytes 196608 | tf_op jit(solution)/shard_map/unpack_own/pallas_call | solution.py:307
  33.0 0.7 %collective-permute-done.2.near_ref = bf16[16,2,8,128]{3,2,1,0:T(8,128)(2,1)S(1)} collective-permute-done((bf16[16,2,8,128]{3,2,1,0:T(8,128)(2,1)S(1)}, bf16[16,2,8,128]{3,2,1,0:T(8,128)(2,1)S(1)}, u32[]{:S(2)}, u32[]{:S(2)}) %collective-permute-start.2) | collective-permute-done | bytes 65568 | tf_op jit(solution)/shard_map/ppermute | solution.py:273
  33.7 1.8 %unpack_forecast.1 = f32[256,128]{1,0:T(8,128)} custom-call(f32[2,16,8,128]{3,2,1,0:T(8,128)S(1)} %unpack_own.1.own_ref, bf16[16,2,8,128]{3,2,1,0:T(8,128)(2,1)S(1)} %collective-permute-done.2.near_ref), custom_call_target="tpu_custom_call" | custom-call | bytes 327680 | tf_op jit(solution)/shard_map/unpack_forecast/pallas_call | solution.py:307
Async XLA Ops:
  0.0 1.6 %collective-permute-start = (f32[16,2,8,128]{3,2,1,0:T(8,128)}, f32[16,2,8,128]{3,2,1,0:T(8,128)S(1)}, u32[]{:S(2)}, u32[]{:S(2)}) collective-permute-start(f32[16,2,8,128]{3,2,1,0:T(8,128)} %param.4), channel_id=1, source_target_pairs={{1,0},{0,1},{3,2},{2,3},{5,4},{4,5},{7,6},{6,7},{9,8},{8,9},{11,10... | collective-permute-start | bytes 393224 | tf_op jit(solution)/shard_map/ppermute | solution.py:273
  0.5 1.2 %copy-start = (f32[2,8,8]{2,1,0:T(8,128)S(1)}, f32[2,8,8]{2,1,0:T(8,128)}, u32[]{:S(2)}) copy-start(f32[2,8,8]{2,1,0:T(8,128)} %values_ref.1) | copy-start | bytes 1540
  0.5 1.2 %copy-start.1 = (f32[2,8,8]{2,1,0:T(8,128)S(1)}, f32[2,8,8]{2,1,0:T(8,128)}, u32[]{:S(2)}) copy-start(f32[2,8,8]{2,1,0:T(8,128)} %inverse_ref.1) | copy-start | bytes 1540
  0.5 1.2 %copy-start.2 = (s32[2,8,8]{2,1,0:T(8,128)S(1)}, s32[2,8,8]{2,1,0:T(8,128)}, u32[]{:S(2)}) copy-start(s32[2,8,8]{2,1,0:T(8,128)} %mask_ref.1) | copy-start | bytes 1540
  18.9 1.4 %collective-permute-start.1 = (bf16[16,5,8,128]{3,2,1,0:T(8,128)(2,1)S(1)}, bf16[16,5,8,128]{3,2,1,0:T(8,128)(2,1)S(1)}, u32[]{:S(2)}, u32[]{:S(2)}) collective-permute-start(bf16[16,5,8,128]{3,2,1,0:T(8,128)(2,1)S(1)} %all_to_all.10.own_ref), channel_id=1, source_target_pairs={{1,0},{0,1},{3,2},{2,3},{5,4},{4,5},{7,6},{6,7},{9,8},{8,9},{11,10... | collective-permute-start | bytes 491528 | tf_op jit(solution)/shard_map/ppermute | solution.py:273
  32.4 1.3 %collective-permute-start.2 = (bf16[16,2,8,128]{3,2,1,0:T(8,128)(2,1)S(1)}, bf16[16,2,8,128]{3,2,1,0:T(8,128)(2,1)S(1)}, u32[]{:S(2)}, u32[]{:S(2)}) collective-permute-start(bf16[16,2,8,128]{3,2,1,0:T(8,128)(2,1)S(1)} %all_to_all.11.in_ref), channel_id=1, source_target_pairs={{1,0},{0,1},{3,2},{2,3},{5,4},{4,5},{7,6},{6,7},{9,8},{8,9},{11,10... | collective-permute-start | bytes 196616 | tf_op jit(solution)/shard_map/ppermute | solution.py:273

commit v6 on v5

--- a/solution.py
+++ b/solution.py
@@ -99,31 +99,40 @@
             high = mean.astype(BF).astype(F32)
             means[j] = jnp.where(index == 4 * half, high, jnp.where(index == 4 * half + 1, mean - high, means[j]))
             values.append(value - mean)
+    rows = jnp.concatenate(values + means, 0).astype(BF)
+    column = lax.broadcasted_iota(jnp.int32, (WIDTH, 2 * WIDTH), 0)
+    lane = lax.broadcasted_iota(jnp.int32, (WIDTH, 2 * WIDTH), 1)
+    wanted = ((lane // REGION) * PATCH + lane % REGION + (WIDTH - RADIUS)) % WIDTH
+    widen = (column == wanted).astype(F32).astype(BF)
+    wide = jnp.dot(rows, widen, preferred_element_type=F32)
     obs = observation_rows(values_ref, inverse_ref, mask_ref)
+    start = len(values) * LOCAL
     is_mean = index & 2 == 0
-    means = [
-        jnp.where(is_mean, pltpu.roll(m, RADIUS, 1), pltpu.roll(pltpu.roll(m, WIDTH + RADIUS - PATCH, 1), 2, 0))
-        for m in means
-    ]
+    means = []
+    for j in range(8):
+        part = wide[start + j * 8 : start + j * 8 + 8]
+        means.append(jnp.where(is_mean, part[:, :WIDTH], pltpu.roll(part[:, WIDTH:], 2, 0)))
     means = swap_blocks(means, REGION)
-    for parity in range(2):
+    for side in range(2):
+        for half in range(2):
+            parts = [
+                wide[(half * 8 + j) * LOCAL : (half * 8 + j + 1) * LOCAL, side * WIDTH : (side + 1) * WIDTH].astype(BF)
+                for j in range(8)
+            ]
+            parts = swap_blocks(parts, REGION)
+            for i in range(8):
+                out_ref[side * 8 + i, half * LOCAL : (half + 1) * LOCAL] = parts[i]
         for i in range(8):
-            mean = pltpu.roll(means[i], 6, 0) if parity else means[i]
-            out_ref[2 * i + parity, 4] = jnp.where(is_mean, mean, obs).astype(BF)
-        for half in range(2):
-            shift = (WIDTH + RADIUS - parity * PATCH) % WIDTH
-            parts = swap_blocks([pltpu.roll(v, shift, 1) for v in values[half * 8 : half * 8 + 8]], REGION)
-            for i in range(8):
-                for eight in range(2):
-                    out_ref[2 * i + parity, half * 2 + eight] = parts[i][eight * 8 : eight * 8 + 8].astype(BF)
+            mean = means[i] if side == 0 else pltpu.roll(means[i], 6, 0)
+            out_ref[side * 8 + i, 2 * LOCAL :] = jnp.where(is_mean, mean, obs).astype(BF)
 
 
 def halves_of(ref, me):
     count = ref.shape[0]
-    tails = [ref[s, 4].astype(F32) for s in range(count)]
+    tails = [ref[s, 2 * LOCAL :].astype(F32) for s in range(count)]
 
     def tail_of(device):
-        return ref[device, 4].astype(F32)
+        return ref[device, 2 * LOCAL :].astype(F32)
 
     lane = lax.broadcasted_iota(jnp.int32, (8, WIDTH), 1) % REGION
     left = tail_of(lax.rem(me + count - 1, count))
@@ -149,7 +158,7 @@
         mean = functools.reduce(jnp.add, means) * (1.0 / count)
         deviation = []
         for s, own_mean in enumerate(means):
-            value = jnp.concatenate([ref[s, half * 2 + eight].astype(F32) for eight in range(2)], 0)
+            value = ref[s, half * LOCAL : (half + 1) * LOCAL].astype(F32)
             deviation.append((value + (own_mean - mean)).astype(BF))
         weight = first[base + 2 : base + 3]
         obs = second[base + 2 : base + 3] + first[base + 3 : base + 4] + second[base + 3 : base + 4]
@@ -234,19 +243,16 @@
     root = jnp.sqrt(jnp.full((1, 1), members - 1.0, F32))
     result = (root * x3 + (shift + mean_ref[:1])).astype(BF)
     for s in range(count):
-        for eight in range(2):
-            out_ref[s, eight] = result[s * LOCAL + eight * 8 : s * LOCAL + eight * 8 + 8]
-
-
-def unpacked(ref, eight):
-    return swap_blocks([ref[p, eight].astype(F32) for p in range(ref.shape[0])], PATCH)
+        out_ref[s] = result[s * LOCAL : (s + 1) * LOCAL]
+
+
+def unpacked(ref):
+    return [row.astype(F32) for row in swap_blocks([ref[p] for p in range(ref.shape[0])], PATCH)]
 
 
 def unpack_kernel(in_ref, out_ref):
-    @pl.loop(0, 2)
-    def _(eight):
-        for i, row in enumerate(unpacked(in_ref, eight)):
-            out_ref[eight, i] = row
+    for i, row in enumerate(unpacked(in_ref)):
+        out_ref[i] = row
 
 
 def forecast_kernel(own_ref, near_ref, out_ref):
@@ -257,15 +263,12 @@
             for field in range(FIELDS)
         ]
 
-    @pl.loop(0, 2)
-    def _(eight):
-        own, near = by_field(own_ref.at[eight]), by_field(unpacked(near_ref, eight))
-        fields = [n[BAND - FSTEPS :] + o + n[:FSTEPS] for o, n in zip(own, near)]
-        done = forecast_rows(*fields)
-        points = FIELDS * BAND
-        for field in range(FIELDS):
-            for r in range(BAND):
-                out_ref[pl.ds(eight * 8 * points + field * BAND + r, 8, stride=points), :] = done[field][r]
+    own, near = by_field(own_ref), by_field(unpacked(near_ref))
+    fields = [n[BAND - FSTEPS :] + o + n[:FSTEPS] for o, n in zip(own, near)]
+    done = forecast_rows(*fields)
+    for field in range(FIELDS):
+        for r in range(BAND):
+            out_ref[pl.ds(field * BAND + r, LOCAL, stride=FIELDS * BAND), :] = done[field][r]
 
 
 def from_next(value):
@@ -289,12 +292,13 @@
 
 
 def join_region(after, before):
-    tail = jnp.concatenate([after[:, 4:, :4], before[:, 4:, 4:]], 2)
-    return jnp.concatenate([after[:, :2], before[:, 2:4], tail], 1)
+    after, before = (x.reshape(x.shape[0], -1, 4, WIDTH) for x in (after, before))
+    near = jnp.concatenate([after[:, :4], before[:, 4:8], after[:, 8:9], before[:, 9:]], 1)
+    return near.reshape(near.shape[0], -1, WIDTH)
 
 
 def join_inner(after, before):
-    return jnp.concatenate([after[..., : WIDTH // 2], before[..., WIDTH // 2 :]], 3)
+    return jnp.concatenate([after[..., : WIDTH // 2], before[..., WIDTH // 2 :]], 2)
 
 
 def exchange(value):
@@ -322,8 +326,8 @@
     me = lax.axis_index("mem").astype(jnp.int32).reshape(1)
     near = near_rows(sample_collection, join_grid)
     rows = jnp.transpose(sample_collection.reshape(LOCAL, FIELDS * BAND, WIDTH), (1, 0, 2))
-    region_shape = jax.ShapeDtypeStruct((count, 5, 8, WIDTH), BF)
-    inner_shape = jax.ShapeDtypeStruct((count, 2, 8, WIDTH), BF)
+    region_shape = jax.ShapeDtypeStruct((count, 2 * LOCAL + 8, WIDTH), BF)
+    inner_shape = jax.ShapeDtypeStruct((count, LOCAL, WIDTH), BF)
     observations = (obs_values, obs_inverse_variance, obs_mask)
     region = exchange(call(pack_kernel, "forecast_pack", region_shape, rows, near.reshape(-1, WIDTH), *observations))
     members, points = count * LOCAL, 2 * WIDTH
@@ -337,7 +341,7 @@
     own = call(own_kernel, "own_half", own_shapes, me, region, flops=flops)
     inner = exchange(call(analysis_kernel, "analysis", inner_shape, me, region_near, *own, flops=8 * flops))
     inner_near = near_rows(inner, join_inner)
-    rows_shape = jax.ShapeDtypeStruct((2, FIELDS * BAND, 8, WIDTH), F32)
+    rows_shape = jax.ShapeDtypeStruct((FIELDS * BAND, LOCAL, WIDTH), F32)
     inner = call(unpack_kernel, "unpack_own", rows_shape, inner)
     out_shape = jax.ShapeDtypeStruct((LOCAL * FIELDS * BAND, WIDTH), F32)
     cycled = call(forecast_kernel, "unpack_forecast", out_shape, inner, inner_near)

time: 35.7 us -> 34.9 us (0.978)
  Pallas kernels: 5.14 us -> 4.06 us
    pallas_call x5, Pallas kernels: 5.14 us -> 4.06 us  [call(): pl.pallas_call(kernel, out_shape=out_shape, in_specs=[pl.BlockSpec(memory...]
  transfers between devices with their start and end apart: 3 -> 3, of which waited for: 3 -> 3; matrix products, arithmetic and copies ran while one was open for 3% -> 3% of each run, Pallas kernels for 3% -> 2%
where the time goes in v6:
time: 34.9 us; the launch traced here: 34.7 us
  blocking collectives  27 us (77%)
  Pallas kernels  4.06 us (12%)
  waiting for transfers between devices  2.19 us (6%)
  local copies, waits for them, and re-layouts  1 us (3%)
  starting transfers between devices  0.46 us (1%)
    all_to_all x2, blocking collectives, exchange(): return lax.all_to_all(value, 'mem', split_axis=0, concat_axis=0, tiled=True)  27 us
    pallas_call x5, Pallas kernels, call(): pl.pallas_call(kernel, out_shape=out_shape, in_specs=[pl.BlockSpec(memory...  4.06 us
    ppermute x3, waiting for transfers between devices, from_next(): lax.ppermute(value, 'rows', [((i + 1) % count, i) for i in range(count)])  2.19 us
    unnamed x7, local copies, waits for them, and re-layouts  1 us
  transfers between devices with their start and end apart: 3, of which 3 were waited for; matrix products, arithmetic and copies ran while one was open for 3% of the time, Pallas kernels for 2%

profile of v6, /device:TPU:0, one launch (start us, length us, event | category | flops | bytes accessed | tf_op | source)
XLA Modules:
  0.0 34.7 jit_solution(7590555102410317866)
XLA Ops:
  0.0 0.5 %collective-permute-start = (f32[16,2,8,128]{3,2,1,0:T(8,128)}, f32[16,2,8,128]{3,2,1,0:T(8,128)S(1)}, u32[]{:S(2)}, u32[]{:S(2)}) collective-permute-start(f32[16,2,8,128]{3,2,1,0:T(8,128)} %param.4), channel_id=1, source_target_pairs={{1,0},{0,1},{3,2},{2,3},{5,4},{4,5},{7,6},{6,7},{9,8},{8,9},{11,10... | collective-permute-start | bytes 393224 | tf_op jit(solution)/shard_map/ppermute | solution.py:276
  0.5 0.0 copy-start
  0.5 0.0 copy-start.1
  0.5 0.0 copy-start.2
  0.5 1.0 %copy.5 = f32[16,2,8,128]{3,0,2,1:T(8,128)S(1)} copy(f32[16,2,8,128]{3,2,1,0:T(8,128)} %param.4) | data formatting | bytes 262144 | tf_op args[0]
  1.5 0.2 collective-permute-done
  1.7 0.0 copy-done
  1.7 0.0 copy-done.1
  1.7 0.0 copy-done.2
  1.7 0.8 %forecast_pack.1 = bf16[16,40,128]{2,1,0:T(8,128)(2,1)S(1)} custom-call(f32[16,16,128]{2,1,0:T(8,128)S(1)} %bitcast.6, f32[256,128]{1,0:T(8,128)S(1)} %bitcast.7, f32[2,8,8]{2,1,0:T(8,128)S(1)} %copy-done, f32[2,8,8]{2,1,0:T(8,128)S(1)} %copy-done.1, s32[2,8,8]{2,1,0:T(8,128)S(1)} %copy-done.2), custom_call_target="tpu_custom_call" | custom-call | bytes 427520 | tf_op jit(solution)/shard_map/forecast_pack/pallas_call | solution.py:311
  2.5 16.2 %all_to_all.10.own_ref = bf16[16,40,128]{2,1,0:T(8,128)(2,1)S(1)} all-to-all(bf16[16,40,128]{2,1,0:T(8,128)(2,1)S(1)} %forecast_pack.1), channel_id=1, replica_groups=mesh['mem'=16,'rows'=2] {'mem'}, dimensions={0} | all-to-all | bytes 327680 | tf_op jit(solution)/shard_map/all_to_all | solution.py:305
  18.7 0.0 collective-permute-start.1
  18.7 0.3 own_half.1
  19.0 1.1 %collective-permute-done.1.near_ref = bf16[16,40,128]{2,1,0:T(8,128)(2,1)S(1)} collective-permute-done((bf16[16,40,128]{2,1,0:T(8,128)(2,1)S(1)}, bf16[16,40,128]{2,1,0:T(8,128)(2,1)S(1)}, u32[]{:S(2)}, u32[]{:S(2)}) %collective-permute-start.1) | collective-permute-done | bytes 163872 | tf_op jit(solution)/shard_map/ppermute | solution.py:276
  20.1 1.3 %analysis.1 = bf16[16,16,128]{2,1,0:T(8,128)(2,1)S(1)} custom-call(s32[1]{0:T(128)} %bitcast.me_ref, bf16[16,40,128]{2,1,0:T(8,128)(2,1)S(1)} %collective-permute-done.1.near_ref, bf16[256,128]{1,0:T(8,128)(2,1)S(1)} %get-tuple-element.8.inner_ref, f32[272,256]{1,0:T(8,128)S(1)} %get-tuple-element.9.sums_ref, f32[8,128]{1,0:T(8,128)S(1)} %get-tuple-element.10.mean_ref), custom_call_target="tpu_custom_call" | custom-call | flops 268435456 | bytes 577540 | tf_op jit(solution)/shard_map/analysis/pallas_call | solution.py:311
  21.4 10.8 %all_to_all.11.in_ref = bf16[16,16,128]{2,1,0:T(8,128)(2,1)S(1)} all-to-all(bf16[16,16,128]{2,1,0:T(8,128)(2,1)S(1)} %analysis.1), channel_id=1, replica_groups=mesh['mem'=16,'rows'=2] {'mem'}, dimensions={0} | all-to-all | bytes 131072 | tf_op jit(solution)/shard_map/all_to_all | solution.py:305
  32.2 0.0 collective-permute-start.2
  32.2 0.3 unpack_own.1.own_ref
  32.5 0.9 %collective-permute-done.2.near_ref = bf16[16,16,128]{2,1,0:T(8,128)(2,1)S(1)} collective-permute-done((bf16[16,16,128]{2,1,0:T(8,128)(2,1)S(1)}, bf16[16,16,128]{2,1,0:T(8,128)(2,1)S(1)}, u32[]{:S(2)}, u32[]{:S(2)}) %collective-permute-start.2) | collective-permute-done | bytes 65568 | tf_op jit(solution)/shard_map/ppermute | solution.py:276
  33.5 1.3 %unpack_forecast.1 = f32[256,128]{1,0:T(8,128)} custom-call(f32[16,16,128]{2,1,0:T(8,128)S(1)} %unpack_own.1.own_ref, bf16[16,16,128]{2,1,0:T(8,128)(2,1)S(1)} %collective-permute-done.2.near_ref), custom_call_target="tpu_custom_call" | custom-call | bytes 327680 | tf_op jit(solution)/shard_map/unpack_forecast/pallas_call | solution.py:311
Async XLA Ops:
  0.0 1.6 %collective-permute-start = (f32[16,2,8,128]{3,2,1,0:T(8,128)}, f32[16,2,8,128]{3,2,1,0:T(8,128)S(1)}, u32[]{:S(2)}, u32[]{:S(2)}) collective-permute-start(f32[16,2,8,128]{3,2,1,0:T(8,128)} %param.4), channel_id=1, source_target_pairs={{1,0},{0,1},{3,2},{2,3},{5,4},{4,5},{7,6},{6,7},{9,8},{8,9},{11,10... | collective-permute-start | bytes 393224 | tf_op jit(solution)/shard_map/ppermute | solution.py:276
  0.5 1.2 %copy-start = (f32[2,8,8]{2,1,0:T(8,128)S(1)}, f32[2,8,8]{2,1,0:T(8,128)}, u32[]{:S(2)}) copy-start(f32[2,8,8]{2,1,0:T(8,128)} %values_ref.1) | copy-start | bytes 1540
  0.5 1.2 %copy-start.1 = (f32[2,8,8]{2,1,0:T(8,128)S(1)}, f32[2,8,8]{2,1,0:T(8,128)}, u32[]{:S(2)}) copy-start(f32[2,8,8]{2,1,0:T(8,128)} %inverse_ref.1) | copy-start | bytes 1540
  0.5 1.2 %copy-start.2 = (s32[2,8,8]{2,1,0:T(8,128)S(1)}, s32[2,8,8]{2,1,0:T(8,128)}, u32[]{:S(2)}) copy-start(s32[2,8,8]{2,1,0:T(8,128)} %mask_ref.1) | copy-start | bytes 1540
  18.7 1.4 %collective-permute-start.1 = (bf16[16,40,128]{2,1,0:T(8,128)(2,1)S(1)}, bf16[16,40,128]{2,1,0:T(8,128)(2,1)S(1)}, u32[]{:S(2)}, u32[]{:S(2)}) collective-permute-start(bf16[16,40,128]{2,1,0:T(8,128)(2,1)S(1)} %all_to_all.10.own_ref), channel_id=1, source_target_pairs={{1,0},{0,1},{3,2},{2,3},{5,4},{4,5},{7,6},{6,7},{9,8},{8,9},{11,10... | collective-permute-start | bytes 491528 | tf_op jit(solution)/shard_map/ppermute | solution.py:276
  32.2 1.3 %collective-permute-start.2 = (bf16[16,16,128]{2,1,0:T(8,128)(2,1)S(1)}, bf16[16,16,128]{2,1,0:T(8,128)(2,1)S(1)}, u32[]{:S(2)}, u32[]{:S(2)}) collective-permute-start(bf16[16,16,128]{2,1,0:T(8,128)(2,1)S(1)} %all_to_all.11.in_ref), channel_id=1, source_target_pairs={{1,0},{0,1},{3,2},{2,3},{5,4},{4,5},{7,6},{6,7},{9,8},{8,9},{11,10... | collective-permute-start | bytes 196616 | tf_op jit(solution)/shard_map/ppermute | solution.py:276

commit v7 on v6

--- a/solution.py
+++ b/solution.py
@@ -37,18 +37,22 @@
 
 def swap_blocks(parts, size):
     count = len(parts)
-    lane = lax.broadcasted_iota(jnp.int32, parts[0].shape, 1) // size
+    block = lax.broadcasted_iota(jnp.int32, parts[0].shape, 1) // size
     stride = 1
     while stride < count:
-        upper = (lane & stride) != 0
-        new = list(parts)
+        base = min(4, count // stride)
+        here = [(block // stride) % base == digit for digit in range(base)]
+        new = []
         for j in range(count):
-            if j & stride == 0:
-                a, b = parts[j], parts[j + stride]
-                new[j] = jnp.where(upper, pltpu.roll(b, stride * size, 1), a)
-                new[j + stride] = jnp.where(upper, b, pltpu.roll(a, WIDTH - stride * size, 1))
+            own = (j // stride) % base
+            value = parts[j]
+            for digit in range(base):
+                if digit != own:
+                    move = (digit - own) * stride
+                    value = jnp.where(here[digit], pltpu.roll(parts[j + move], (move * size) % WIDTH, 1), value)
+            new.append(value)
         parts = new
-        stride *= 2
+        stride *= base
     return parts
 
 
@@ -108,12 +112,10 @@
     obs = observation_rows(values_ref, inverse_ref, mask_ref)
     start = len(values) * LOCAL
     is_mean = index & 2 == 0
-    means = []
-    for j in range(8):
-        part = wide[start + j * 8 : start + j * 8 + 8]
-        means.append(jnp.where(is_mean, part[:, :WIDTH], pltpu.roll(part[:, WIDTH:], 2, 0)))
-    means = swap_blocks(means, REGION)
     for side in range(2):
+        means = [wide[start + j * 8 : start + j * 8 + 8, side * WIDTH : (side + 1) * WIDTH] for j in range(8)]
+        for i, mean in enumerate(swap_blocks(means, REGION)):
+            out_ref[side * 8 + i, 2 * LOCAL :] = jnp.where(is_mean, mean, obs).astype(BF)
         for half in range(2):
             parts = [
                 wide[(half * 8 + j) * LOCAL : (half * 8 + j + 1) * LOCAL, side * WIDTH : (side + 1) * WIDTH].astype(BF)
@@ -122,9 +124,6 @@
             parts = swap_blocks(parts, REGION)
             for i in range(8):
                 out_ref[side * 8 + i, half * LOCAL : (half + 1) * LOCAL] = parts[i]
-        for i in range(8):
-            mean = means[i] if side == 0 else pltpu.roll(means[i], 6, 0)
-            out_ref[side * 8 + i, 2 * LOCAL :] = jnp.where(is_mean, mean, obs).astype(BF)
 
 
 def halves_of(ref, me):

time: 34.9 us -> 35 us (level)
  no operation moved by 1% of the time
where the time goes in v7:
time: 35 us; the launch traced here: 34.7 us
  blocking collectives  27 us (77%)
  Pallas kernels  4 us (11%)
  waiting for transfers between devices  2.28 us (7%)
  local copies, waits for them, and re-layouts  1 us (3%)
  starting transfers between devices  0.46 us (1%)
    all_to_all x2, blocking collectives, exchange(): return lax.all_to_all(value, 'mem', split_axis=0, concat_axis=0, tiled=True)  27 us
    pallas_call x5, Pallas kernels, call(): pl.pallas_call(kernel, out_shape=out_shape, in_specs=[pl.BlockSpec(memory...  4 us
    ppermute x3, waiting for transfers between devices, from_next(): lax.ppermute(value, 'rows', [((i + 1) % count, i) for i in range(count)])  2.28 us
    unnamed x7, local copies, waits for them, and re-layouts  1 us
  transfers between devices with their start and end apart: 3, of which 3 were waited for; matrix products, arithmetic and copies ran while one was open for 3% of the time, Pallas kernels for 2%

profile of v7, /device:TPU:0, one launch (start us, length us, event | category | flops | bytes accessed | tf_op | source)
XLA Modules:
  0.0 34.7 jit_solution(1360239027121342671)
XLA Ops:
  0.0 0.5 %collective-permute-start = (f32[16,2,8,128]{3,2,1,0:T(8,128)}, f32[16,2,8,128]{3,2,1,0:T(8,128)S(1)}, u32[]{:S(2)}, u32[]{:S(2)}) collective-permute-start(f32[16,2,8,128]{3,2,1,0:T(8,128)} %param.4), channel_id=1, source_target_pairs={{1,0},{0,1},{3,2},{2,3},{5,4},{4,5},{7,6},{6,7},{9,8},{8,9},{11,10... | collective-permute-start | bytes 393224 | tf_op jit(solution)/shard_map/ppermute | solution.py:275
  0.5 0.0 copy-start
  0.5 0.0 copy-start.1
  0.5 0.0 copy-start.2
  0.5 1.0 %copy.5 = f32[16,2,8,128]{3,0,2,1:T(8,128)S(1)} copy(f32[16,2,8,128]{3,2,1,0:T(8,128)} %param.4) | data formatting | bytes 262144 | tf_op args[0]
  1.5 0.2 collective-permute-done
  1.7 0.0 copy-done
  1.7 0.0 copy-done.1
  1.7 0.0 copy-done.2
  1.7 0.9 %forecast_pack.1 = bf16[16,40,128]{2,1,0:T(8,128)(2,1)S(1)} custom-call(f32[16,16,128]{2,1,0:T(8,128)S(1)} %bitcast.6, f32[256,128]{1,0:T(8,128)S(1)} %bitcast.7, f32[2,8,8]{2,1,0:T(8,128)S(1)} %copy-done, f32[2,8,8]{2,1,0:T(8,128)S(1)} %copy-done.1, s32[2,8,8]{2,1,0:T(8,128)S(1)} %copy-done.2), custom_call_target="tpu_custom_call" | custom-call | bytes 427520 | tf_op jit(solution)/shard_map/forecast_pack/pallas_call | solution.py:310
  2.5 16.2 %all_to_all.10.own_ref = bf16[16,40,128]{2,1,0:T(8,128)(2,1)S(1)} all-to-all(bf16[16,40,128]{2,1,0:T(8,128)(2,1)S(1)} %forecast_pack.1), channel_id=1, replica_groups=mesh['mem'=16,'rows'=2] {'mem'}, dimensions={0} | all-to-all | bytes 327680 | tf_op jit(solution)/shard_map/all_to_all | solution.py:304
  18.7 0.0 collective-permute-start.1
  18.7 0.3 own_half.1
  19.0 1.1 %collective-permute-done.1.near_ref = bf16[16,40,128]{2,1,0:T(8,128)(2,1)S(1)} collective-permute-done((bf16[16,40,128]{2,1,0:T(8,128)(2,1)S(1)}, bf16[16,40,128]{2,1,0:T(8,128)(2,1)S(1)}, u32[]{:S(2)}, u32[]{:S(2)}) %collective-permute-start.1) | collective-permute-done | bytes 163872 | tf_op jit(solution)/shard_map/ppermute | solution.py:275
  20.1 1.3 %analysis.1 = bf16[16,16,128]{2,1,0:T(8,128)(2,1)S(1)} custom-call(s32[1]{0:T(128)} %bitcast.me_ref, bf16[16,40,128]{2,1,0:T(8,128)(2,1)S(1)} %collective-permute-done.1.near_ref, bf16[256,128]{1,0:T(8,128)(2,1)S(1)} %get-tuple-element.8.inner_ref, f32[272,256]{1,0:T(8,128)S(1)} %get-tuple-element.9.sums_ref, f32[8,128]{1,0:T(8,128)S(1)} %get-tuple-element.10.mean_ref), custom_call_target="tpu_custom_call" | custom-call | flops 268435456 | bytes 577540 | tf_op jit(solution)/shard_map/analysis/pallas_call | solution.py:310
  21.4 10.8 %all_to_all.11.in_ref = bf16[16,16,128]{2,1,0:T(8,128)(2,1)S(1)} all-to-all(bf16[16,16,128]{2,1,0:T(8,128)(2,1)S(1)} %analysis.1), channel_id=1, replica_groups=mesh['mem'=16,'rows'=2] {'mem'}, dimensions={0} | all-to-all | bytes 131072 | tf_op jit(solution)/shard_map/all_to_all | solution.py:304
  32.2 0.0 collective-permute-start.2
  32.2 0.2 unpack_own.1.own_ref
  32.5 1.0 %collective-permute-done.2.near_ref = bf16[16,16,128]{2,1,0:T(8,128)(2,1)S(1)} collective-permute-done((bf16[16,16,128]{2,1,0:T(8,128)(2,1)S(1)}, bf16[16,16,128]{2,1,0:T(8,128)(2,1)S(1)}, u32[]{:S(2)}, u32[]{:S(2)}) %collective-permute-start.2) | collective-permute-done | bytes 65568 | tf_op jit(solution)/shard_map/ppermute | solution.py:275
  33.5 1.3 %unpack_forecast.1 = f32[256,128]{1,0:T(8,128)} custom-call(f32[16,16,128]{2,1,0:T(8,128)S(1)} %unpack_own.1.own_ref, bf16[16,16,128]{2,1,0:T(8,128)(2,1)S(1)} %collective-permute-done.2.near_ref), custom_call_target="tpu_custom_call" | custom-call | bytes 327680 | tf_op jit(solution)/shard_map/unpack_forecast/pallas_call | solution.py:310
Async XLA Ops:
  0.0 1.6 %collective-permute-start = (f32[16,2,8,128]{3,2,1,0:T(8,128)}, f32[16,2,8,128]{3,2,1,0:T(8,128)S(1)}, u32[]{:S(2)}, u32[]{:S(2)}) collective-permute-start(f32[16,2,8,128]{3,2,1,0:T(8,128)} %param.4), channel_id=1, source_target_pairs={{1,0},{0,1},{3,2},{2,3},{5,4},{4,5},{7,6},{6,7},{9,8},{8,9},{11,10... | collective-permute-start | bytes 393224 | tf_op jit(solution)/shard_map/ppermute | solution.py:275
  0.5 1.2 %copy-start = (f32[2,8,8]{2,1,0:T(8,128)S(1)}, f32[2,8,8]{2,1,0:T(8,128)}, u32[]{:S(2)}) copy-start(f32[2,8,8]{2,1,0:T(8,128)} %values_ref.1) | copy-start | bytes 1540
  0.5 1.2 %copy-start.1 = (f32[2,8,8]{2,1,0:T(8,128)S(1)}, f32[2,8,8]{2,1,0:T(8,128)}, u32[]{:S(2)}) copy-start(f32[2,8,8]{2,1,0:T(8,128)} %inverse_ref.1) | copy-start | bytes 1540
  0.5 1.2 %copy-start.2 = (s32[2,8,8]{2,1,0:T(8,128)S(1)}, s32[2,8,8]{2,1,0:T(8,128)}, u32[]{:S(2)}) copy-start(s32[2,8,8]{2,1,0:T(8,128)} %mask_ref.1) | copy-start | bytes 1540
  18.7 1.4 %collective-permute-start.1 = (bf16[16,40,128]{2,1,0:T(8,128)(2,1)S(1)}, bf16[16,40,128]{2,1,0:T(8,128)(2,1)S(1)}, u32[]{:S(2)}, u32[]{:S(2)}) collective-permute-start(bf16[16,40,128]{2,1,0:T(8,128)(2,1)S(1)} %all_to_all.10.own_ref), channel_id=1, source_target_pairs={{1,0},{0,1},{3,2},{2,3},{5,4},{4,5},{7,6},{6,7},{9,8},{8,9},{11,10... | collective-permute-start | bytes 491528 | tf_op jit(solution)/shard_map/ppermute | solution.py:275
  32.2 1.3 %collective-permute-start.2 = (bf16[16,16,128]{2,1,0:T(8,128)(2,1)S(1)}, bf16[16,16,128]{2,1,0:T(8,128)(2,1)S(1)}, u32[]{:S(2)}, u32[]{:S(2)}) collective-permute-start(bf16[16,16,128]{2,1,0:T(8,128)(2,1)S(1)} %all_to_all.11.in_ref), channel_id=1, source_target_pairs={{1,0},{0,1},{3,2},{2,3},{5,4},{4,5},{7,6},{6,7},{9,8},{8,9},{11,10... | collective-permute-start | bytes 196616 | tf_op jit(solution)/shard_map/ppermute | solution.py:275

commit v8 on v6

--- a/solution.py
+++ b/solution.py
@@ -89,6 +89,7 @@
         after = [near(field, r) for r in range(FSTEPS)]
         fields.append(before + own + after)
     done = forecast_rows(*fields)
+    last = out_ref.shape[0] - 1
     half_rows = BAND // 2
     index = lax.broadcasted_iota(jnp.int32, (8, WIDTH), 0)
     values, means = [], [jnp.zeros((8, WIDTH), F32)] * (FIELDS * half_rows)
@@ -121,10 +122,10 @@
             ]
             parts = swap_blocks(parts, REGION)
             for i in range(8):
-                out_ref[side * 8 + i, half * LOCAL : (half + 1) * LOCAL] = parts[i]
+                out_ref[last - side * 8 - i, half * LOCAL : (half + 1) * LOCAL] = parts[i]
         for i in range(8):
             mean = means[i] if side == 0 else pltpu.roll(means[i], 6, 0)
-            out_ref[side * 8 + i, 2 * LOCAL :] = jnp.where(is_mean, mean, obs).astype(BF)
+            out_ref[last - side * 8 - i, 2 * LOCAL :] = jnp.where(is_mean, mean, obs).astype(BF)
 
 
 def halves_of(ref, me):
@@ -132,7 +133,7 @@
     tails = [ref[s, 2 * LOCAL :].astype(F32) for s in range(count)]
 
     def tail_of(device):
-        return ref[device, 2 * LOCAL :].astype(F32)
+        return ref[count - 1 - device, 2 * LOCAL :].astype(F32)
 
     lane = lax.broadcasted_iota(jnp.int32, (8, WIDTH), 1) % REGION
     left = tail_of(lax.rem(me + count - 1, count))
@@ -247,7 +248,7 @@
 
 
 def unpacked(ref):
-    return [row.astype(F32) for row in swap_blocks([ref[p] for p in range(ref.shape[0])], PATCH)]
+    return [row.astype(F32) for row in swap_blocks([ref[p] for p in reversed(range(ref.shape[0]))], PATCH)]
 
 
 def unpack_kernel(in_ref, out_ref):
@@ -302,7 +303,8 @@
 
 
 def exchange(value):
-    return lax.all_to_all(value, "mem", split_axis=0, concat_axis=0, tiled=True)
+    group = [list(reversed(range(lax.axis_size("mem"))))]
+    return lax.all_to_all(value, "mem", split_axis=0, concat_axis=0, axis_index_groups=group, tiled=True)
 
 
 def call(kernel, name, out_shape, *args, flops=0):

time: 34.9 us -> 31.9 us (0.914)
  blocking collectives: 27 us -> 23.9 us
    all_to_all x2, blocking collectives: 27 us -> 23.9 us  [exchange(): lax.all_to_all(value, 'mem', split_axis=0, concat_axis=0, axis_index_grou...]
where the time goes in v8:
time: 31.9 us; the launch traced here: 31.7 us
  blocking collectives  23.9 us (75%)
  Pallas kernels  4.07 us (13%)
  waiting for transfers between devices  2.19 us (7%)
  local copies, waits for them, and re-layouts  1 us (3%)
  starting transfers between devices  0.46 us (1%)
    all_to_all x2, blocking collectives, exchange(): lax.all_to_all(value, 'mem', split_axis=0, concat_axis=0, axis_index_grou...  23.9 us
    pallas_call x5, Pallas kernels, call(): pl.pallas_call(kernel, out_shape=out_shape, in_specs=[pl.BlockSpec(memory...  4.07 us
    ppermute x3, waiting for transfers between devices, from_next(): lax.ppermute(value, 'rows', [((i + 1) % count, i) for i in range(count)])  2.19 us
    unnamed x7, local copies, waits for them, and re-layouts  1 us
  transfers between devices with their start and end apart: 3, of which 3 were waited for; matrix products, arithmetic and copies ran while one was open for 3% of the time, Pallas kernels for 2%

profile of v8, /device:TPU:0, one launch (start us, length us, event | category | flops | bytes accessed | tf_op | source)
XLA Modules:
  0.0 31.7 jit_solution(5019035802305239849)
XLA Ops:
  0.0 0.5 %collective-permute-start = (f32[16,2,8,128]{3,2,1,0:T(8,128)}, f32[16,2,8,128]{3,2,1,0:T(8,128)S(1)}, u32[]{:S(2)}, u32[]{:S(2)}) collective-permute-start(f32[16,2,8,128]{3,2,1,0:T(8,128)} %param.4), channel_id=1, source_target_pairs={{1,0},{0,1},{3,2},{2,3},{5,4},{4,5},{7,6},{6,7},{9,8},{8,9},{11,10... | collective-permute-start | bytes 393224 | tf_op jit(solution)/shard_map/ppermute | solution.py:277
  0.5 0.0 copy-start
  0.5 0.0 copy-start.1
  0.5 0.0 copy-start.2
  0.5 1.0 %copy.5 = f32[16,2,8,128]{3,0,2,1:T(8,128)S(1)} copy(f32[16,2,8,128]{3,2,1,0:T(8,128)} %param.4) | data formatting | bytes 262144 | tf_op args[0]
  1.5 0.2 collective-permute-done
  1.7 0.0 copy-done
  1.7 0.0 copy-done.1
  1.7 0.0 copy-done.2
  1.7 0.8 %forecast_pack.1 = bf16[16,40,128]{2,1,0:T(8,128)(2,1)S(1)} custom-call(f32[16,16,128]{2,1,0:T(8,128)S(1)} %bitcast.6, f32[256,128]{1,0:T(8,128)S(1)} %bitcast.7, f32[2,8,8]{2,1,0:T(8,128)S(1)} %copy-done, f32[2,8,8]{2,1,0:T(8,128)S(1)} %copy-done.1, s32[2,8,8]{2,1,0:T(8,128)S(1)} %copy-done.2), custom_call_target="tpu_custom_call" | custom-call | bytes 427520 | tf_op jit(solution)/shard_map/forecast_pack/pallas_call | solution.py:313
  2.5 14.3 %all_to_all.10.own_ref = bf16[16,40,128]{2,1,0:T(8,128)(2,1)S(1)} all-to-all(bf16[16,40,128]{2,1,0:T(8,128)(2,1)S(1)} %forecast_pack.1), channel_id=1, replica_groups={{30,28,26,24,22,20,18,16,14,12,10,8,6,4,2,0},{31,29,27,25,23,21,19,17,1..., dimensions={0} | all-to-all | bytes 327680 | tf_op jit(solution)/shard_map/all_to_all | solution.py:307
  16.8 0.0 collective-permute-start.1
  16.8 0.3 %own_half.1 = (bf16[256,128]{1,0:T(8,128)(2,1)S(1)}, f32[272,256]{1,0:T(8,128)S(1)}, f32[8,128]{1,0:T(8,128)S(1)}) custom-call(s32[1]{0:T(128)} %bitcast.me_ref, bf16[16,40,128]{2,1,0:T(8,128)(2,1)S(1)} %all_to_all.10.own_ref), custom_call_target="tpu_custom_call" | custom-call | flops 33554432 | bytes 512004 | tf_op jit(solution)/shard_map/own_half/pallas_call | solution.py:313
  17.1 1.1 %collective-permute-done.1.near_ref = bf16[16,40,128]{2,1,0:T(8,128)(2,1)S(1)} collective-permute-done((bf16[16,40,128]{2,1,0:T(8,128)(2,1)S(1)}, bf16[16,40,128]{2,1,0:T(8,128)(2,1)S(1)}, u32[]{:S(2)}, u32[]{:S(2)}) %collective-permute-start.1) | collective-permute-done | bytes 163872 | tf_op jit(solution)/shard_map/ppermute | solution.py:277
  18.2 1.3 %analysis.1 = bf16[16,16,128]{2,1,0:T(8,128)(2,1)S(1)} custom-call(s32[1]{0:T(128)} %bitcast.me_ref, bf16[16,40,128]{2,1,0:T(8,128)(2,1)S(1)} %collective-permute-done.1.near_ref, bf16[256,128]{1,0:T(8,128)(2,1)S(1)} %get-tuple-element.8.inner_ref, f32[272,256]{1,0:T(8,128)S(1)} %get-tuple-element.9.sums_ref, f32[8,128]{1,0:T(8,128)S(1)} %get-tuple-element.10.mean_ref), custom_call_target="tpu_custom_call" | custom-call | flops 268435456 | bytes 577540 | tf_op jit(solution)/shard_map/analysis/pallas_call | solution.py:313
  19.5 9.7 %all_to_all.11.in_ref = bf16[16,16,128]{2,1,0:T(8,128)(2,1)S(1)} all-to-all(bf16[16,16,128]{2,1,0:T(8,128)(2,1)S(1)} %analysis.1), channel_id=1, replica_groups={{30,28,26,24,22,20,18,16,14,12,10,8,6,4,2,0},{31,29,27,25,23,21,19,17,1..., dimensions={0} | all-to-all | bytes 131072 | tf_op jit(solution)/shard_map/all_to_all | solution.py:307
  29.2 0.0 collective-permute-start.2
  29.2 0.3 unpack_own.1.own_ref
  29.5 0.9 %collective-permute-done.2.near_ref = bf16[16,16,128]{2,1,0:T(8,128)(2,1)S(1)} collective-permute-done((bf16[16,16,128]{2,1,0:T(8,128)(2,1)S(1)}, bf16[16,16,128]{2,1,0:T(8,128)(2,1)S(1)}, u32[]{:S(2)}, u32[]{:S(2)}) %collective-permute-start.2) | collective-permute-done | bytes 65568 | tf_op jit(solution)/shard_map/ppermute | solution.py:277
  30.4 1.3 %unpack_forecast.1 = f32[256,128]{1,0:T(8,128)} custom-call(f32[16,16,128]{2,1,0:T(8,128)S(1)} %unpack_own.1.own_ref, bf16[16,16,128]{2,1,0:T(8,128)(2,1)S(1)} %collective-permute-done.2.near_ref), custom_call_target="tpu_custom_call" | custom-call | bytes 327680 | tf_op jit(solution)/shard_map/unpack_forecast/pallas_call | solution.py:313
Async XLA Ops:
  0.0 1.6 %collective-permute-start = (f32[16,2,8,128]{3,2,1,0:T(8,128)}, f32[16,2,8,128]{3,2,1,0:T(8,128)S(1)}, u32[]{:S(2)}, u32[]{:S(2)}) collective-permute-start(f32[16,2,8,128]{3,2,1,0:T(8,128)} %param.4), channel_id=1, source_target_pairs={{1,0},{0,1},{3,2},{2,3},{5,4},{4,5},{7,6},{6,7},{9,8},{8,9},{11,10... | collective-permute-start | bytes 393224 | tf_op jit(solution)/shard_map/ppermute | solution.py:277
  0.5 1.2 %copy-start = (f32[2,8,8]{2,1,0:T(8,128)S(1)}, f32[2,8,8]{2,1,0:T(8,128)}, u32[]{:S(2)}) copy-start(f32[2,8,8]{2,1,0:T(8,128)} %values_ref.1) | copy-start | bytes 1540
  0.5 1.2 %copy-start.1 = (f32[2,8,8]{2,1,0:T(8,128)S(1)}, f32[2,8,8]{2,1,0:T(8,128)}, u32[]{:S(2)}) copy-start(f32[2,8,8]{2,1,0:T(8,128)} %inverse_ref.1) | copy-start | bytes 1540
  0.5 1.2 %copy-start.2 = (s32[2,8,8]{2,1,0:T(8,128)S(1)}, s32[2,8,8]{2,1,0:T(8,128)}, u32[]{:S(2)}) copy-start(s32[2,8,8]{2,1,0:T(8,128)} %mask_ref.1) | copy-start | bytes 1540
  16.8 1.4 %collective-permute-start.1 = (bf16[16,40,128]{2,1,0:T(8,128)(2,1)S(1)}, bf16[16,40,128]{2,1,0:T(8,128)(2,1)S(1)}, u32[]{:S(2)}, u32[]{:S(2)}) collective-permute-start(bf16[16,40,128]{2,1,0:T(8,128)(2,1)S(1)} %all_to_all.10.own_ref), channel_id=1, source_target_pairs={{1,0},{0,1},{3,2},{2,3},{5,4},{4,5},{7,6},{6,7},{9,8},{8,9},{11,10... | collective-permute-start | bytes 491528 | tf_op jit(solution)/shard_map/ppermute | solution.py:277
  29.2 1.3 %collective-permute-start.2 = (bf16[16,16,128]{2,1,0:T(8,128)(2,1)S(1)}, bf16[16,16,128]{2,1,0:T(8,128)(2,1)S(1)}, u32[]{:S(2)}, u32[]{:S(2)}) collective-permute-start(bf16[16,16,128]{2,1,0:T(8,128)(2,1)S(1)} %all_to_all.11.in_ref), channel_id=1, source_target_pairs={{1,0},{0,1},{3,2},{2,3},{5,4},{4,5},{7,6},{6,7},{9,8},{8,9},{11,10... | collective-permute-start | bytes 196616 | tf_op jit(solution)/shard_map/ppermute | solution.py:277

commit v9 on v8

--- a/solution.py
+++ b/solution.py
@@ -16,10 +16,16 @@
 FIELDS = 2
 BAND = 8
 WIDTH = 128
+PLACES = WIDTH // PATCH
 REGION = PATCH + 2 * RADIUS
 
 BF = jnp.bfloat16
 F32 = jnp.float32
+
+
+def position(place):
+    low, high = place & 3, place >> 2
+    return PLACES - 1 - (low * 4 + (high & 1) * 2 + (high >> 1))
 
 
 def forecast_rows(u_rows, v_rows):
@@ -89,7 +95,6 @@
         after = [near(field, r) for r in range(FSTEPS)]
         fields.append(before + own + after)
     done = forecast_rows(*fields)
-    last = out_ref.shape[0] - 1
     half_rows = BAND // 2
     index = lax.broadcasted_iota(jnp.int32, (8, WIDTH), 0)
     values, means = [], [jnp.zeros((8, WIDTH), F32)] * (FIELDS * half_rows)
@@ -122,10 +127,10 @@
             ]
             parts = swap_blocks(parts, REGION)
             for i in range(8):
-                out_ref[last - side * 8 - i, half * LOCAL : (half + 1) * LOCAL] = parts[i]
+                out_ref[position(side * 8 + i), half * LOCAL : (half + 1) * LOCAL] = parts[i]
         for i in range(8):
             mean = means[i] if side == 0 else pltpu.roll(means[i], 6, 0)
-            out_ref[last - side * 8 - i, 2 * LOCAL :] = jnp.where(is_mean, mean, obs).astype(BF)
+            out_ref[position(side * 8 + i), 2 * LOCAL :] = jnp.where(is_mean, mean, obs).astype(BF)
 
 
 def halves_of(ref, me):
@@ -133,7 +138,7 @@
     tails = [ref[s, 2 * LOCAL :].astype(F32) for s in range(count)]
 
     def tail_of(device):
-        return ref[count - 1 - device, 2 * LOCAL :].astype(F32)
+        return ref[position(device), 2 * LOCAL :].astype(F32)
 
     lane = lax.broadcasted_iota(jnp.int32, (8, WIDTH), 1) % REGION
     left = tail_of(lax.rem(me + count - 1, count))
@@ -248,7 +253,7 @@
 
 
 def unpacked(ref):
-    return [row.astype(F32) for row in swap_blocks([ref[p] for p in reversed(range(ref.shape[0]))], PATCH)]
+    return [row.astype(F32) for row in swap_blocks([ref[position(p)] for p in range(ref.shape[0])], PATCH)]
 
 
 def unpack_kernel(in_ref, out_ref):
@@ -303,7 +308,7 @@
 
 
 def exchange(value):
-    group = [list(reversed(range(lax.axis_size("mem"))))]
+    group = [sorted(range(lax.axis_size("mem")), key=position)]
     return lax.all_to_all(value, "mem", split_axis=0, concat_axis=0, axis_index_groups=group, tiled=True)
 
 
@@ -324,7 +329,7 @@
 def local(sample_collection, obs_values, obs_inverse_variance, obs_mask):
     count = lax.axis_size("mem")
     shape = sample_collection.shape
-    assert shape == (LOCAL, FIELDS, BAND, WIDTH) and count * PATCH == WIDTH
+    assert shape == (LOCAL, FIELDS, BAND, WIDTH) and count == PLACES
     me = lax.axis_index("mem").astype(jnp.int32).reshape(1)
     near = near_rows(sample_collection, join_grid)
     rows = jnp.transpose(sample_collection.reshape(LOCAL, FIELDS * BAND, WIDTH), (1, 0, 2))

time: 31.9 us -> 31.7 us (level)
  no operation moved by 1% of the time
where the time goes in v9:
time: 31.7 us; the launch traced here: 31.5 us
  blocking collectives  23.7 us (75%)
  Pallas kernels  4.08 us (13%)
  waiting for transfers between devices  2.19 us (7%)
  local copies, waits for them, and re-layouts  1 us (3%)
  starting transfers between devices  0.46 us (1%)
    all_to_all x2, blocking collectives, exchange(): lax.all_to_all(value, 'mem', split_axis=0, concat_axis=0, axis_index_grou...  23.7 us
    pallas_call x5, Pallas kernels, call(): pl.pallas_call(kernel, out_shape=out_shape, in_specs=[pl.BlockSpec(memory...  4.08 us
    ppermute x3, waiting for transfers between devices, from_next(): lax.ppermute(value, 'rows', [((i + 1) % count, i) for i in range(count)])  2.19 us
    unnamed x7, local copies, waits for them, and re-layouts  1 us
  transfers between devices with their start and end apart: 3, of which 3 were waited for; matrix products, arithmetic and copies ran while one was open for 3% of the time, Pallas kernels for 2%

profile of v9, /device:TPU:0, one launch (start us, length us, event | category | flops | bytes accessed | tf_op | source)
XLA Modules:
  0.0 31.5 jit_solution(12538159369466842791)
XLA Ops:
  0.0 0.5 %collective-permute-start = (f32[16,2,8,128]{3,2,1,0:T(8,128)}, f32[16,2,8,128]{3,2,1,0:T(8,128)S(1)}, u32[]{:S(2)}, u32[]{:S(2)}) collective-permute-start(f32[16,2,8,128]{3,2,1,0:T(8,128)} %param.4), channel_id=1, source_target_pairs={{1,0},{0,1},{3,2},{2,3},{5,4},{4,5},{7,6},{6,7},{9,8},{8,9},{11,10... | collective-permute-start | bytes 393224 | tf_op jit(solution)/shard_map/ppermute | solution.py:282
  0.5 0.0 copy-start
  0.5 0.0 copy-start.1
  0.5 0.0 copy-start.2
  0.5 1.0 %copy.5 = f32[16,2,8,128]{3,0,2,1:T(8,128)S(1)} copy(f32[16,2,8,128]{3,2,1,0:T(8,128)} %param.4) | data formatting | bytes 262144 | tf_op args[0]
  1.5 0.2 collective-permute-done
  1.7 0.0 copy-done
  1.7 0.0 copy-done.1
  1.7 0.0 copy-done.2
  1.7 0.8 %forecast_pack.1 = bf16[16,40,128]{2,1,0:T(8,128)(2,1)S(1)} custom-call(f32[16,16,128]{2,1,0:T(8,128)S(1)} %bitcast.6, f32[256,128]{1,0:T(8,128)S(1)} %bitcast.7, f32[2,8,8]{2,1,0:T(8,128)S(1)} %copy-done, f32[2,8,8]{2,1,0:T(8,128)S(1)} %copy-done.1, s32[2,8,8]{2,1,0:T(8,128)S(1)} %copy-done.2), custom_call_target="tpu_custom_call" | custom-call | bytes 427520 | tf_op jit(solution)/shard_map/forecast_pack/pallas_call | solution.py:318
  2.5 14.1 %all_to_all.10.own_ref = bf16[16,40,128]{2,1,0:T(8,128)(2,1)S(1)} all-to-all(bf16[16,40,128]{2,1,0:T(8,128)(2,1)S(1)} %forecast_pack.1), channel_id=1, replica_groups={{30,14,22,6,28,12,20,4,26,10,18,2,24,8,16,0},{31,15,23,7,29,13,21,5,27,..., dimensions={0} | all-to-all | bytes 327680 | tf_op jit(solution)/shard_map/all_to_all | solution.py:312
  16.7 0.0 collective-permute-start.1
  16.7 0.3 %own_half.1 = (bf16[256,128]{1,0:T(8,128)(2,1)S(1)}, f32[272,256]{1,0:T(8,128)S(1)}, f32[8,128]{1,0:T(8,128)S(1)}) custom-call(s32[1]{0:T(128)} %bitcast.me_ref, bf16[16,40,128]{2,1,0:T(8,128)(2,1)S(1)} %all_to_all.10.own_ref), custom_call_target="tpu_custom_call" | custom-call | flops 33554432 | bytes 512004 | tf_op jit(solution)/shard_map/own_half/pallas_call | solution.py:318
  17.0 1.1 %collective-permute-done.1.near_ref = bf16[16,40,128]{2,1,0:T(8,128)(2,1)S(1)} collective-permute-done((bf16[16,40,128]{2,1,0:T(8,128)(2,1)S(1)}, bf16[16,40,128]{2,1,0:T(8,128)(2,1)S(1)}, u32[]{:S(2)}, u32[]{:S(2)}) %collective-permute-start.1) | collective-permute-done | bytes 163872 | tf_op jit(solution)/shard_map/ppermute | solution.py:282
  18.0 1.3 %analysis.1 = bf16[16,16,128]{2,1,0:T(8,128)(2,1)S(1)} custom-call(s32[1]{0:T(128)} %bitcast.me_ref, bf16[16,40,128]{2,1,0:T(8,128)(2,1)S(1)} %collective-permute-done.1.near_ref, bf16[256,128]{1,0:T(8,128)(2,1)S(1)} %get-tuple-element.8.inner_ref, f32[272,256]{1,0:T(8,128)S(1)} %get-tuple-element.9.sums_ref, f32[8,128]{1,0:T(8,128)S(1)} %get-tuple-element.10.mean_ref), custom_call_target="tpu_custom_call" | custom-call | flops 268435456 | bytes 577540 | tf_op jit(solution)/shard_map/analysis/pallas_call | solution.py:318
  19.4 9.6 %all_to_all.11.in_ref = bf16[16,16,128]{2,1,0:T(8,128)(2,1)S(1)} all-to-all(bf16[16,16,128]{2,1,0:T(8,128)(2,1)S(1)} %analysis.1), channel_id=1, replica_groups={{30,14,22,6,28,12,20,4,26,10,18,2,24,8,16,0},{31,15,23,7,29,13,21,5,27,..., dimensions={0} | all-to-all | bytes 131072 | tf_op jit(solution)/shard_map/all_to_all | solution.py:312
  29.0 0.0 collective-permute-start.2
  29.0 0.3 unpack_own.1.own_ref
  29.3 0.9 %collective-permute-done.2.near_ref = bf16[16,16,128]{2,1,0:T(8,128)(2,1)S(1)} collective-permute-done((bf16[16,16,128]{2,1,0:T(8,128)(2,1)S(1)}, bf16[16,16,128]{2,1,0:T(8,128)(2,1)S(1)}, u32[]{:S(2)}, u32[]{:S(2)}) %collective-permute-start.2) | collective-permute-done | bytes 65568 | tf_op jit(solution)/shard_map/ppermute | solution.py:282
  30.2 1.3 %unpack_forecast.1 = f32[256,128]{1,0:T(8,128)} custom-call(f32[16,16,128]{2,1,0:T(8,128)S(1)} %unpack_own.1.own_ref, bf16[16,16,128]{2,1,0:T(8,128)(2,1)S(1)} %collective-permute-done.2.near_ref), custom_call_target="tpu_custom_call" | custom-call | bytes 327680 | tf_op jit(solution)/shard_map/unpack_forecast/pallas_call | solution.py:318
Async XLA Ops:
  0.0 1.6 %collective-permute-start = (f32[16,2,8,128]{3,2,1,0:T(8,128)}, f32[16,2,8,128]{3,2,1,0:T(8,128)S(1)}, u32[]{:S(2)}, u32[]{:S(2)}) collective-permute-start(f32[16,2,8,128]{3,2,1,0:T(8,128)} %param.4), channel_id=1, source_target_pairs={{1,0},{0,1},{3,2},{2,3},{5,4},{4,5},{7,6},{6,7},{9,8},{8,9},{11,10... | collective-permute-start | bytes 393224 | tf_op jit(solution)/shard_map/ppermute | solution.py:282
  0.5 1.2 %copy-start = (f32[2,8,8]{2,1,0:T(8,128)S(1)}, f32[2,8,8]{2,1,0:T(8,128)}, u32[]{:S(2)}) copy-start(f32[2,8,8]{2,1,0:T(8,128)} %values_ref.1) | copy-start | bytes 1540
  0.5 1.2 %copy-start.1 = (f32[2,8,8]{2,1,0:T(8,128)S(1)}, f32[2,8,8]{2,1,0:T(8,128)}, u32[]{:S(2)}) copy-start(f32[2,8,8]{2,1,0:T(8,128)} %inverse_ref.1) | copy-start | bytes 1540
  0.5 1.2 %copy-start.2 = (s32[2,8,8]{2,1,0:T(8,128)S(1)}, s32[2,8,8]{2,1,0:T(8,128)}, u32[]{:S(2)}) copy-start(s32[2,8,8]{2,1,0:T(8,128)} %mask_ref.1) | copy-start | bytes 1540
  16.7 1.4 %collective-permute-start.1 = (bf16[16,40,128]{2,1,0:T(8,128)(2,1)S(1)}, bf16[16,40,128]{2,1,0:T(8,128)(2,1)S(1)}, u32[]{:S(2)}, u32[]{:S(2)}) collective-permute-start(bf16[16,40,128]{2,1,0:T(8,128)(2,1)S(1)} %all_to_all.10.own_ref), channel_id=1, source_target_pairs={{1,0},{0,1},{3,2},{2,3},{5,4},{4,5},{7,6},{6,7},{9,8},{8,9},{11,10... | collective-permute-start | bytes 491528 | tf_op jit(solution)/shard_map/ppermute | solution.py:282
  29.0 1.3 %collective-permute-start.2 = (bf16[16,16,128]{2,1,0:T(8,128)(2,1)S(1)}, bf16[16,16,128]{2,1,0:T(8,128)(2,1)S(1)}, u32[]{:S(2)}, u32[]{:S(2)}) collective-permute-start(bf16[16,16,128]{2,1,0:T(8,128)(2,1)S(1)} %all_to_all.11.in_ref), channel_id=1, source_target_pairs={{1,0},{0,1},{3,2},{2,3},{5,4},{4,5},{7,6},{6,7},{9,8},{8,9},{11,10... | collective-permute-start | bytes 196616 | tf_op jit(solution)/shard_map/ppermute | solution.py:282

commit v10 on v9

--- a/solution.py
+++ b/solution.py
@@ -308,8 +308,10 @@
 
 
 def exchange(value):
-    group = [sorted(range(lax.axis_size("mem")), key=position)]
-    return lax.all_to_all(value, "mem", split_axis=0, concat_axis=0, axis_index_groups=group, tiled=True)
+    bands = lax.axis_size("rows")
+    places = sorted(range(lax.axis_size("mem")), key=position)
+    groups = [[place * bands + band for place in places] for band in reversed(range(bands))]
+    return lax.all_to_all(value, ("mem", "rows"), split_axis=0, concat_axis=0, axis_index_groups=groups, tiled=True)
 
 
 def call(kernel, name, out_shape, *args, flops=0):

time: 31.7 us -> 31.7 us (level)
  no operation moved by 1% of the time
where the time goes in v10:
time: 31.7 us; the launch traced here: 31.5 us
  blocking collectives  23.7 us (75%)
  Pallas kernels  4.08 us (13%)
  waiting for transfers between devices  2.19 us (7%)
  local copies, waits for them, and re-layouts  1 us (3%)
  starting transfers between devices  0.46 us (1%)
    all_to_all x2, blocking collectives, exchange(): lax.all_to_all(value, ('mem', 'rows'), split_axis=0, concat_axis=0, axis_...  23.7 us
    pallas_call x5, Pallas kernels, call(): pl.pallas_call(kernel, out_shape=out_shape, in_specs=[pl.BlockSpec(memory...  4.08 us
    ppermute x3, waiting for transfers between devices, from_next(): lax.ppermute(value, 'rows', [((i + 1) % count, i) for i in range(count)])  2.19 us
    unnamed x7, local copies, waits for them, and re-layouts  1 us
  transfers between devices with their start and end apart: 3, of which 3 were waited for; matrix products, arithmetic and copies ran while one was open for 3% of the time, Pallas kernels for 2%

profile of v10, /device:TPU:0, one launch (start us, length us, event | category | flops | bytes accessed | tf_op | source)
XLA Modules:
  0.0 31.5 jit_solution(2549368966942873027)
XLA Ops:
  0.0 0.5 %collective-permute-start = (f32[16,2,8,128]{3,2,1,0:T(8,128)}, f32[16,2,8,128]{3,2,1,0:T(8,128)S(1)}, u32[]{:S(2)}, u32[]{:S(2)}) collective-permute-start(f32[16,2,8,128]{3,2,1,0:T(8,128)} %param.4), channel_id=1, source_target_pairs={{1,0},{0,1},{3,2},{2,3},{5,4},{4,5},{7,6},{6,7},{9,8},{8,9},{11,10... | collective-permute-start | bytes 393224 | tf_op jit(solution)/shard_map/ppermute | solution.py:282
  0.5 0.0 copy-start
  0.5 0.0 copy-start.1
  0.5 0.0 copy-start.2
  0.5 1.0 %copy.5 = f32[16,2,8,128]{3,0,2,1:T(8,128)S(1)} copy(f32[16,2,8,128]{3,2,1,0:T(8,128)} %param.4) | data formatting | bytes 262144 | tf_op args[0]
  1.5 0.2 collective-permute-done
  1.7 0.0 copy-done
  1.7 0.0 copy-done.1
  1.7 0.0 copy-done.2
  1.7 0.8 %forecast_pack.1 = bf16[16,40,128]{2,1,0:T(8,128)(2,1)S(1)} custom-call(f32[16,16,128]{2,1,0:T(8,128)S(1)} %bitcast.6, f32[256,128]{1,0:T(8,128)S(1)} %bitcast.7, f32[2,8,8]{2,1,0:T(8,128)S(1)} %copy-done, f32[2,8,8]{2,1,0:T(8,128)S(1)} %copy-done.1, s32[2,8,8]{2,1,0:T(8,128)S(1)} %copy-done.2), custom_call_target="tpu_custom_call" | custom-call | bytes 427520 | tf_op jit(solution)/shard_map/forecast_pack/pallas_call | solution.py:320
  2.5 14.1 %all_to_all.10.own_ref = bf16[16,40,128]{2,1,0:T(8,128)(2,1)S(1)} all-to-all(bf16[16,40,128]{2,1,0:T(8,128)(2,1)S(1)} %forecast_pack.1), channel_id=1, replica_groups={{31,15,23,7,29,13,21,5,27,11,19,3,25,9,17,1},{30,14,22,6,28,12,20,4,26,..., dimensions={0} | all-to-all | bytes 327680 | tf_op jit(solution)/shard_map/all_to_all | solution.py:314
  16.7 0.0 collective-permute-start.1
  16.7 0.3 %own_half.1 = (bf16[256,128]{1,0:T(8,128)(2,1)S(1)}, f32[272,256]{1,0:T(8,128)S(1)}, f32[8,128]{1,0:T(8,128)S(1)}) custom-call(s32[1]{0:T(128)} %bitcast.me_ref, bf16[16,40,128]{2,1,0:T(8,128)(2,1)S(1)} %all_to_all.10.own_ref), custom_call_target="tpu_custom_call" | custom-call | flops 33554432 | bytes 512004 | tf_op jit(solution)/shard_map/own_half/pallas_call | solution.py:320
  17.0 1.1 %collective-permute-done.1.near_ref = bf16[16,40,128]{2,1,0:T(8,128)(2,1)S(1)} collective-permute-done((bf16[16,40,128]{2,1,0:T(8,128)(2,1)S(1)}, bf16[16,40,128]{2,1,0:T(8,128)(2,1)S(1)}, u32[]{:S(2)}, u32[]{:S(2)}) %collective-permute-start.1) | collective-permute-done | bytes 163872 | tf_op jit(solution)/shard_map/ppermute | solution.py:282
  18.0 1.3 %analysis.1 = bf16[16,16,128]{2,1,0:T(8,128)(2,1)S(1)} custom-call(s32[1]{0:T(128)} %bitcast.me_ref, bf16[16,40,128]{2,1,0:T(8,128)(2,1)S(1)} %collective-permute-done.1.near_ref, bf16[256,128]{1,0:T(8,128)(2,1)S(1)} %get-tuple-element.8.inner_ref, f32[272,256]{1,0:T(8,128)S(1)} %get-tuple-element.9.sums_ref, f32[8,128]{1,0:T(8,128)S(1)} %get-tuple-element.10.mean_ref), custom_call_target="tpu_custom_call" | custom-call | flops 268435456 | bytes 577540 | tf_op jit(solution)/shard_map/analysis/pallas_call | solution.py:320
  19.4 9.6 %all_to_all.11.in_ref = bf16[16,16,128]{2,1,0:T(8,128)(2,1)S(1)} all-to-all(bf16[16,16,128]{2,1,0:T(8,128)(2,1)S(1)} %analysis.1), channel_id=1, replica_groups={{31,15,23,7,29,13,21,5,27,11,19,3,25,9,17,1},{30,14,22,6,28,12,20,4,26,..., dimensions={0} | all-to-all | bytes 131072 | tf_op jit(solution)/shard_map/all_to_all | solution.py:314
  29.0 0.0 collective-permute-start.2
  29.0 0.3 unpack_own.1.own_ref
  29.3 0.9 %collective-permute-done.2.near_ref = bf16[16,16,128]{2,1,0:T(8,128)(2,1)S(1)} collective-permute-done((bf16[16,16,128]{2,1,0:T(8,128)(2,1)S(1)}, bf16[16,16,128]{2,1,0:T(8,128)(2,1)S(1)}, u32[]{:S(2)}, u32[]{:S(2)}) %collective-permute-start.2) | collective-permute-done | bytes 65568 | tf_op jit(solution)/shard_map/ppermute | solution.py:282
  30.2 1.3 %unpack_forecast.1 = f32[256,128]{1,0:T(8,128)} custom-call(f32[16,16,128]{2,1,0:T(8,128)S(1)} %unpack_own.1.own_ref, bf16[16,16,128]{2,1,0:T(8,128)(2,1)S(1)} %collective-permute-done.2.near_ref), custom_call_target="tpu_custom_call" | custom-call | bytes 327680 | tf_op jit(solution)/shard_map/unpack_forecast/pallas_call | solution.py:320
Async XLA Ops:
  0.0 1.6 %collective-permute-start = (f32[16,2,8,128]{3,2,1,0:T(8,128)}, f32[16,2,8,128]{3,2,1,0:T(8,128)S(1)}, u32[]{:S(2)}, u32[]{:S(2)}) collective-permute-start(f32[16,2,8,128]{3,2,1,0:T(8,128)} %param.4), channel_id=1, source_target_pairs={{1,0},{0,1},{3,2},{2,3},{5,4},{4,5},{7,6},{6,7},{9,8},{8,9},{11,10... | collective-permute-start | bytes 393224 | tf_op jit(solution)/shard_map/ppermute | solution.py:282
  0.5 1.2 %copy-start = (f32[2,8,8]{2,1,0:T(8,128)S(1)}, f32[2,8,8]{2,1,0:T(8,128)}, u32[]{:S(2)}) copy-start(f32[2,8,8]{2,1,0:T(8,128)} %values_ref.1) | copy-start | bytes 1540
  0.5 1.2 %copy-start.1 = (f32[2,8,8]{2,1,0:T(8,128)S(1)}, f32[2,8,8]{2,1,0:T(8,128)}, u32[]{:S(2)}) copy-start(f32[2,8,8]{2,1,0:T(8,128)} %inverse_ref.1) | copy-start | bytes 1540
  0.5 1.2 %copy-start.2 = (s32[2,8,8]{2,1,0:T(8,128)S(1)}, s32[2,8,8]{2,1,0:T(8,128)}, u32[]{:S(2)}) copy-start(s32[2,8,8]{2,1,0:T(8,128)} %mask_ref.1) | copy-start | bytes 1540
  16.7 1.4 %collective-permute-start.1 = (bf16[16,40,128]{2,1,0:T(8,128)(2,1)S(1)}, bf16[16,40,128]{2,1,0:T(8,128)(2,1)S(1)}, u32[]{:S(2)}, u32[]{:S(2)}) collective-permute-start(bf16[16,40,128]{2,1,0:T(8,128)(2,1)S(1)} %all_to_all.10.own_ref), channel_id=1, source_target_pairs={{1,0},{0,1},{3,2},{2,3},{5,4},{4,5},{7,6},{6,7},{9,8},{8,9},{11,10... | collective-permute-start | bytes 491528 | tf_op jit(solution)/shard_map/ppermute | solution.py:282
  29.0 1.3 %collective-permute-start.2 = (bf16[16,16,128]{2,1,0:T(8,128)(2,1)S(1)}, bf16[16,16,128]{2,1,0:T(8,128)(2,1)S(1)}, u32[]{:S(2)}, u32[]{:S(2)}) collective-permute-start(bf16[16,16,128]{2,1,0:T(8,128)(2,1)S(1)} %all_to_all.11.in_ref), channel_id=1, source_target_pairs={{1,0},{0,1},{3,2},{2,3},{5,4},{4,5},{7,6},{6,7},{9,8},{8,9},{11,10... | collective-permute-start | bytes 196616 | tf_op jit(solution)/shard_map/ppermute | solution.py:282

commit v11 on v9

--- a/solution.py
+++ b/solution.py
@@ -173,95 +173,108 @@
     return result
 
 
-def half_sums(halves, row_distances):
+def half_sums(halves, distances):
     lane = lax.broadcasted_iota(jnp.int32, (1, WIDTH), 1)
     region_column = lane % REGION
     half_row = (lane // REGION) % (BAND // 2)
     column_distance = jnp.maximum(
         jnp.maximum(RADIUS - region_column, region_column - (RADIUS + PATCH - 1)), 0
     )
-    weighted, deviation, innovation = [], [], []
-    for (dev, _, weight, inno), row_distance in zip(halves, row_distances):
-        far = jnp.maximum(row_distance(half_row), column_distance).astype(F32)
-        factor = weight * (1.0 - far / (RADIUS + 1.0))
-        weighted.append((dev.astype(F32) * factor).astype(BF))
-        deviation.append(dev)
-        innovation.append(jnp.broadcast_to(inno, (16, WIDTH)).astype(BF))
-    deviation = jnp.concatenate(deviation, 1)
-    rows = jnp.concatenate([deviation, jnp.concatenate(innovation, 1)], 0)
-    weighted = jnp.concatenate(weighted, 1)
+    deviation = jnp.concatenate([dev for dev, _, _, _ in halves], 1)
+    innovation = jnp.concatenate([jnp.broadcast_to(inno, (16, WIDTH)) for _, _, _, inno in halves], 1)
+    rows = jnp.concatenate([deviation, innovation.astype(BF)], 0)
+    weighted = []
+    for row_distances in distances:
+        parts = []
+        for (dev, _, weight, _), row_distance in zip(halves, row_distances):
+            far = jnp.maximum(row_distance(half_row), column_distance).astype(F32)
+            factor = weight * (1.0 - far / (RADIUS + 1.0))
+            parts.append((dev.astype(F32) * factor).astype(BF))
+        weighted.append(jnp.concatenate(parts, 1))
+    weighted = jnp.concatenate(weighted, 0)
     return deviation, lax.dot_general(rows, weighted, (((1,), (1,)), ((), ())), preferred_element_type=F32)
 
 
-def own_kernel(me_ref, own_ref, inner_ref, sums_ref, mean_ref):
-    halves = halves_of(own_ref, me_ref[0])
-    deviation, sums_ref[...] = half_sums(halves, [jnp.zeros_like] * 2)
+INSIDE = (jnp.zeros_like, jnp.zeros_like)
+OUTSIDE = (lambda r: r + 1, lambda r: RADIUS - r)
+
+
+def interior(halves, deviation):
     lane = lax.broadcasted_iota(jnp.int32, (2 * WIDTH, WIDTH), 0)
     target = lax.broadcasted_iota(jnp.int32, (2 * WIDTH, WIDTH), 1)
     narrow = (lane == (target // PATCH) * REGION + RADIUS + target % PATCH).astype(F32).astype(BF)
-    inner_ref[...] = jnp.dot(deviation, narrow, preferred_element_type=F32).astype(BF)
+    inner = jnp.dot(deviation, narrow, preferred_element_type=F32).astype(BF)
     mean = jnp.broadcast_to(jnp.concatenate([halves[0][1], halves[1][1]], 1), (16, 2 * WIDTH))
     high = mean.astype(BF)
     middle = (mean - high.astype(F32)).astype(BF)
     low = (mean - high.astype(F32) - middle.astype(F32)).astype(BF)
     parts = jnp.dot(jnp.concatenate([high, middle, low], 0), narrow, preferred_element_type=F32)
-    mean_ref[...] = parts[:8] + (parts[16:24] + parts[32:40])
-
-
-def analysis_kernel(me_ref, near_ref, inner_ref, sums_ref, mean_ref, out_ref):
+    return inner, parts[:8] + (parts[16:24] + parts[32:40])
+
+
+def own_kernel(patches, me_ref, own_ref, inner_ref, sums_ref, mean_ref):
+    halves = halves_of(own_ref, me_ref[0])
+    deviation, sums_ref[...] = half_sums(halves, (INSIDE, OUTSIDE)[:patches])
+    inner_ref[...], mean_ref[...] = interior(halves, deviation)
+
+
+def analysis_kernel(patches, me_ref, near_ref, inner_ref, sums_ref, mean_ref, out_ref):
     count = near_ref.shape[0]
     members = count * LOCAL
     halves = halves_of(near_ref, me_ref[0])
-    both = sums_ref[...] + half_sums(halves, [lambda r: r + 1, lambda r: RADIUS - r])[1]
+    deviation, sums = half_sums(halves, (OUTSIDE, INSIDE)[:patches])
+    both = sums_ref[...] + sums
+    each = range(patches)
+    inner, mean = [inner_ref[...]], [mean_ref[...]]
+    if patches == 2:
+        near_inner, near_mean = interior(halves, deviation)
+        inner.append(near_inner)
+        mean.append(near_mean)
     row = lax.broadcasted_iota(jnp.int32, (members, members), 0)
     col = lax.broadcasted_iota(jnp.int32, (members, members), 1)
-    system = both[:members] + jnp.where(row == col, members - 1.0, 0.0)
+    diagonal = jnp.where(row == col, members - 1.0, 0.0)
+
     def mul(a, b):
         return jnp.dot(a.astype(BF), b.astype(BF), preferred_element_type=F32)
 
     def with_line(a, line):
         return jnp.concatenate([a.astype(BF), line.astype(BF)], 0)
 
-    inner, line = inner_ref[...], both[members:]
-    system_b = system.astype(BF)
-    first = mul(with_line(system_b, line), system_b)
-    system_x = mul(system_b, inner)
-    scale = jnp.sqrt(jnp.sum(system * system))
-    inverse = 1.0 / scale
-    x1 = 1.5 * inner.astype(F32) - (0.5 * inverse) * system_x
-    line1 = 1.5 * line - (0.5 * inverse) * first[members:]
-    y1 = inverse * (1.5 * system - (0.5 * inverse) * first[:members])
-    p1 = 1.5 * y1 - (0.5 * inverse) * mul(y1, system_b)
-    p1b = p1.astype(BF)
-    second = mul(with_line(p1b, line1), p1b)
-    x2 = 1.5 * x1 - 0.5 * mul(p1b, x1)
-    line2 = 1.5 * line1 - 0.5 * second[members:]
-    q1 = 1.5 * p1 - 0.5 * second[:members]
-    p2 = 1.5 * q1 - 0.5 * mul(q1, p1b)
-    p2b = p2.astype(BF)
-    factor = 1.0 / jnp.sqrt(scale)
-    x3 = (1.5 * x2 - 0.5 * mul(p2b, x2)) * factor
-    line3 = (1.5 * line2 - 0.5 * mul(line2, p2b)) * factor
-    line_b = line3.astype(BF)
-    lines = with_line(line_b, line3 - line_b.astype(F32))
-    shift = mul(lines, x3)
-    shift = shift[:1] + shift[16:17]
+    system = [both[:members, i * members : (i + 1) * members] + diagonal for i in each]
+    line = [both[members:, i * members : (i + 1) * members] for i in each]
+    system_b = [system[i].astype(BF) for i in each]
+    first = [mul(with_line(system_b[i], line[i]), system_b[i]) for i in each]
+    system_x = [mul(system_b[i], inner[i]) for i in each]
+    scale = [jnp.sqrt(jnp.sum(system[i] * system[i])) for i in each]
+    inverse = [1.0 / scale[i] for i in each]
+    x1 = [1.5 * inner[i].astype(F32) - (0.5 * inverse[i]) * system_x[i] for i in each]
+    line1 = [1.5 * line[i] - (0.5 * inverse[i]) * first[i][members:] for i in each]
+    y1 = [inverse[i] * (1.5 * system[i] - (0.5 * inverse[i]) * first[i][:members]) for i in each]
+    p1 = [1.5 * y1[i] - (0.5 * inverse[i]) * mul(y1[i], system_b[i]) for i in each]
+    p1b = [p1[i].astype(BF) for i in each]
+    second = [mul(with_line(p1b[i], line1[i]), p1b[i]) for i in each]
+    x2 = [1.5 * x1[i] - 0.5 * mul(p1b[i], x1[i]) for i in each]
+    line2 = [1.5 * line1[i] - 0.5 * second[i][members:] for i in each]
+    q1 = [1.5 * p1[i] - 0.5 * second[i][:members] for i in each]
+    p2b = [(1.5 * q1[i] - 0.5 * mul(q1[i], p1b[i])).astype(BF) for i in each]
+    factor = [1.0 / jnp.sqrt(scale[i]) for i in each]
+    x3 = [(1.5 * x2[i] - 0.5 * mul(p2b[i], x2[i])) * factor[i] for i in each]
+    line3 = [(1.5 * line2[i] - 0.5 * mul(line2[i], p2b[i])) * factor[i] for i in each]
+    line_b = [line3[i].astype(BF) for i in each]
+    shift = [mul(with_line(line_b[i], line3[i] - line_b[i].astype(F32)), x3[i]) for i in each]
     root = jnp.sqrt(jnp.full((1, 1), members - 1.0, F32))
-    result = (root * x3 + (shift + mean_ref[:1])).astype(BF)
-    for s in range(count):
-        out_ref[s] = result[s * LOCAL : (s + 1) * LOCAL]
-
-
-def unpacked(ref):
-    return [row.astype(F32) for row in swap_blocks([ref[position(p)] for p in range(ref.shape[0])], PATCH)]
-
-
-def unpack_kernel(in_ref, out_ref):
-    for i, row in enumerate(unpacked(in_ref)):
-        out_ref[i] = row
-
-
-def forecast_kernel(own_ref, near_ref, out_ref):
+    for i in each:
+        total = shift[i][:1] + shift[i][16:17] + mean[i][:1]
+        result = (root * x3[i] + total).astype(BF)
+        for s in range(count):
+            out_ref[s, i * LOCAL : (i + 1) * LOCAL] = result[s * LOCAL : (s + 1) * LOCAL]
+
+
+def forecast_kernel(in_ref, out_ref):
+    def unpacked(start):
+        blocks = [in_ref[position(p), start : start + LOCAL] for p in range(in_ref.shape[0])]
+        return [row.astype(F32) for row in swap_blocks(blocks, PATCH)]
+
     def by_field(rows):
         half = BAND // 2
         return [
@@ -269,7 +282,7 @@
             for field in range(FIELDS)
         ]
 
-    own, near = by_field(own_ref), by_field(unpacked(near_ref))
+    own, near = by_field(unpacked(0)), by_field(unpacked(LOCAL))
     fields = [n[BAND - FSTEPS :] + o + n[:FSTEPS] for o, n in zip(own, near)]
     done = forecast_rows(*fields)
     for field in range(FIELDS):
@@ -334,24 +347,25 @@
     near = near_rows(sample_collection, join_grid)
     rows = jnp.transpose(sample_collection.reshape(LOCAL, FIELDS * BAND, WIDTH), (1, 0, 2))
     region_shape = jax.ShapeDtypeStruct((count, 2 * LOCAL + 8, WIDTH), BF)
-    inner_shape = jax.ShapeDtypeStruct((count, LOCAL, WIDTH), BF)
     observations = (obs_values, obs_inverse_variance, obs_mask)
     region = exchange(call(pack_kernel, "forecast_pack", region_shape, rows, near.reshape(-1, WIDTH), *observations))
     members, points = count * LOCAL, 2 * WIDTH
+    patches = 2 if lax.axis_size("rows") == 2 else 1
     own_shapes = [
         jax.ShapeDtypeStruct((members, WIDTH), BF),
-        jax.ShapeDtypeStruct((members + 16, members), F32),
+        jax.ShapeDtypeStruct((members + 16, patches * members), F32),
         jax.ShapeDtypeStruct((8, WIDTH), F32),
     ]
     flops = 2 * members * members * points
     region_near = near_rows(region, join_region)
-    own = call(own_kernel, "own_half", own_shapes, me, region, flops=flops)
-    inner = exchange(call(analysis_kernel, "analysis", inner_shape, me, region_near, *own, flops=8 * flops))
-    inner_near = near_rows(inner, join_inner)
-    rows_shape = jax.ShapeDtypeStruct((FIELDS * BAND, LOCAL, WIDTH), F32)
-    inner = call(unpack_kernel, "unpack_own", rows_shape, inner)
+    own = call(functools.partial(own_kernel, patches), "own_half", own_shapes, me, region, flops=flops)
+    analysed_shape = jax.ShapeDtypeStruct((count, patches * LOCAL, WIDTH), BF)
+    kernel = functools.partial(analysis_kernel, patches)
+    inner = exchange(call(kernel, "analysis", analysed_shape, me, region_near, *own, flops=8 * flops))
+    if patches == 1:
+        inner = jnp.concatenate([inner, near_rows(inner, join_inner)], 1)
     out_shape = jax.ShapeDtypeStruct((LOCAL * FIELDS * BAND, WIDTH), F32)
-    cycled = call(forecast_kernel, "unpack_forecast", out_shape, inner, inner_near)
+    cycled = call(forecast_kernel, "unpack_forecast", out_shape, inner)
     return cycled.reshape(shape)
 
 

time: 31.7 us -> 31.8 us (level)
  blocking collectives: 23.7 us -> 24.8 us
  waiting for transfers between devices: 2.19 us -> 1.19 us
    all_to_all x2, blocking collectives: 23.7 us -> 24.8 us  [exchange(): lax.all_to_all(value, 'mem', split_axis=0, concat_axis=0, axis_index_grou...]
    ppermute x3 -> x2, waiting for transfers between devices: 2.19 us -> 1.19 us  [from_next(): lax.ppermute(value, 'rows', [((i + 1) % count, i) for i in range(count)])]
    pallas_call x5 -> x4, Pallas kernels: 4.08 us -> 4.13 us  [call(): pl.pallas_call(kernel, out_shape=out_shape, in_specs=[pl.BlockSpec(memory...]
  transfers between devices with their start and end apart: 3 -> 2, of which waited for: 3 -> 2; matrix products, arithmetic and copies ran while one was open for 3% -> 3% of each run, Pallas kernels for 2% -> 1%
where the time goes in v11:
time: 31.8 us; the launch traced here: 31.6 us
  blocking collectives  24.8 us (78%)
  Pallas kernels  4.13 us (13%)
  waiting for transfers between devices  1.19 us (4%)
  local copies, waits for them, and re-layouts  1 us (3%)
  starting transfers between devices  0.46 us (1%)
    all_to_all x2, blocking collectives, exchange(): lax.all_to_all(value, 'mem', split_axis=0, concat_axis=0, axis_index_grou...  24.8 us
    pallas_call x4, Pallas kernels, call(): pl.pallas_call(kernel, out_shape=out_shape, in_specs=[pl.BlockSpec(memory...  4.13 us
    ppermute x2, waiting for transfers between devices, from_next(): lax.ppermute(value, 'rows', [((i + 1) % count, i) for i in range(count)])  1.19 us
    unnamed x7, local copies, waits for them, and re-layouts  1 us
  transfers between devices with their start and end apart: 2, of which 2 were waited for; matrix products, arithmetic and copies ran while one was open for 3% of the time, Pallas kernels for 1%

profile of v11, /device:TPU:0, one launch (start us, length us, event | category | flops | bytes accessed | tf_op | source)
XLA Modules:
  0.0 31.6 jit_solution(2367803721923445417)
XLA Ops:
  0.0 0.5 %collective-permute-start = (f32[16,2,8,128]{3,2,1,0:T(8,128)}, f32[16,2,8,128]{3,2,1,0:T(8,128)S(1)}, u32[]{:S(2)}, u32[]{:S(2)}) collective-permute-start(f32[16,2,8,128]{3,2,1,0:T(8,128)} %param.4), channel_id=1, source_target_pairs={{1,0},{0,1},{3,2},{2,3},{5,4},{4,5},{7,6},{6,7},{9,8},{8,9},{11,10... | collective-permute-start | bytes 393224 | tf_op jit(solution)/shard_map/ppermute | solution.py:295
  0.5 0.0 copy-start
  0.5 0.0 copy-start.1
  0.5 0.0 copy-start.2
  0.5 1.0 %copy.5 = f32[16,2,8,128]{3,0,2,1:T(8,128)S(1)} copy(f32[16,2,8,128]{3,2,1,0:T(8,128)} %param.4) | data formatting | bytes 262144 | tf_op args[0]
  1.5 0.2 collective-permute-done
  1.7 0.0 copy-done
  1.7 0.0 copy-done.1
  1.7 0.0 copy-done.2
  1.7 0.8 %forecast_pack.1 = bf16[16,40,128]{2,1,0:T(8,128)(2,1)S(1)} custom-call(f32[16,16,128]{2,1,0:T(8,128)S(1)} %bitcast.6, f32[256,128]{1,0:T(8,128)S(1)} %bitcast.7, f32[2,8,8]{2,1,0:T(8,128)S(1)} %copy-done, f32[2,8,8]{2,1,0:T(8,128)S(1)} %copy-done.1, s32[2,8,8]{2,1,0:T(8,128)S(1)} %copy-done.2), custom_call_target="tpu_custom_call" | custom-call | bytes 427520 | tf_op jit(solution)/shard_map/forecast_pack/pallas_call | solution.py:331
  2.5 14.1 %all_to_all.10.own_ref = bf16[16,40,128]{2,1,0:T(8,128)(2,1)S(1)} all-to-all(bf16[16,40,128]{2,1,0:T(8,128)(2,1)S(1)} %forecast_pack.1), channel_id=1, replica_groups={{30,14,22,6,28,12,20,4,26,10,18,2,24,8,16,0},{31,15,23,7,29,13,21,5,27,..., dimensions={0} | all-to-all | bytes 327680 | tf_op jit(solution)/shard_map/all_to_all | solution.py:325
  16.7 0.0 collective-permute-start.1
  16.7 0.4 %own_half.1 = (bf16[256,128]{1,0:T(8,128)(2,1)S(1)}, f32[272,512]{1,0:T(8,128)S(1)}, f32[8,128]{1,0:T(8,128)S(1)}) custom-call(s32[1]{0:T(128)} %bitcast.me_ref, bf16[16,40,128]{2,1,0:T(8,128)(2,1)S(1)} %all_to_all.10.own_ref), custom_call_target="tpu_custom_call" | custom-call | flops 33554432 | bytes 790532 | tf_op jit(solution)/shard_map/own_half/pallas_call | solution.py:331
  17.1 1.0 %collective-permute-done.1.near_ref = bf16[16,40,128]{2,1,0:T(8,128)(2,1)S(1)} collective-permute-done((bf16[16,40,128]{2,1,0:T(8,128)(2,1)S(1)}, bf16[16,40,128]{2,1,0:T(8,128)(2,1)S(1)}, u32[]{:S(2)}, u32[]{:S(2)}) %collective-permute-start.1) | collective-permute-done | bytes 163872 | tf_op jit(solution)/shard_map/ppermute | solution.py:295
  18.0 1.5 %analysis.1 = bf16[16,32,128]{2,1,0:T(8,128)(2,1)S(1)} custom-call(s32[1]{0:T(128)} %bitcast.me_ref, bf16[16,40,128]{2,1,0:T(8,128)(2,1)S(1)} %collective-permute-done.1.near_ref, bf16[256,128]{1,0:T(8,128)(2,1)S(1)} %get-tuple-element.8.inner_ref, f32[272,512]{1,0:T(8,128)S(1)} %get-tuple-element.9.sums_ref, f32[8,128]{1,0:T(8,128)S(1)} %get-tuple-element.10.mean_ref), custom_call_target="tpu_custom_call" | custom-call | flops 268435456 | bytes 921604 | tf_op jit(solution)/shard_map/analysis/pallas_call | solution.py:331
  19.6 10.7 %all_to_all.11.in_ref = bf16[16,32,128]{2,1,0:T(8,128)(2,1)S(1)} all-to-all(bf16[16,32,128]{2,1,0:T(8,128)(2,1)S(1)} %analysis.1), channel_id=1, replica_groups={{30,14,22,6,28,12,20,4,26,10,18,2,24,8,16,0},{31,15,23,7,29,13,21,5,27,..., dimensions={0} | all-to-all | bytes 262144 | tf_op jit(solution)/shard_map/all_to_all | solution.py:325
  30.3 1.4 %unpack_forecast.1 = f32[256,128]{1,0:T(8,128)} custom-call(bf16[16,32,128]{2,1,0:T(8,128)(2,1)S(1)} %all_to_all.11.in_ref), custom_call_target="tpu_custom_call" | custom-call | bytes 262144 | tf_op jit(solution)/shard_map/unpack_forecast/pallas_call | solution.py:331
Async XLA Ops:
  0.0 1.6 %collective-permute-start = (f32[16,2,8,128]{3,2,1,0:T(8,128)}, f32[16,2,8,128]{3,2,1,0:T(8,128)S(1)}, u32[]{:S(2)}, u32[]{:S(2)}) collective-permute-start(f32[16,2,8,128]{3,2,1,0:T(8,128)} %param.4), channel_id=1, source_target_pairs={{1,0},{0,1},{3,2},{2,3},{5,4},{4,5},{7,6},{6,7},{9,8},{8,9},{11,10... | collective-permute-start | bytes 393224 | tf_op jit(solution)/shard_map/ppermute | solution.py:295
  0.5 1.2 %copy-start = (f32[2,8,8]{2,1,0:T(8,128)S(1)}, f32[2,8,8]{2,1,0:T(8,128)}, u32[]{:S(2)}) copy-start(f32[2,8,8]{2,1,0:T(8,128)} %values_ref.1) | copy-start | bytes 1540
  0.5 1.2 %copy-start.1 = (f32[2,8,8]{2,1,0:T(8,128)S(1)}, f32[2,8,8]{2,1,0:T(8,128)}, u32[]{:S(2)}) copy-start(f32[2,8,8]{2,1,0:T(8,128)} %inverse_ref.1) | copy-start | bytes 1540
  0.5 1.2 %copy-start.2 = (s32[2,8,8]{2,1,0:T(8,128)S(1)}, s32[2,8,8]{2,1,0:T(8,128)}, u32[]{:S(2)}) copy-start(s32[2,8,8]{2,1,0:T(8,128)} %mask_ref.1) | copy-start | bytes 1540
  16.7 1.4 %collective-permute-start.1 = (bf16[16,40,128]{2,1,0:T(8,128)(2,1)S(1)}, bf16[16,40,128]{2,1,0:T(8,128)(2,1)S(1)}, u32[]{:S(2)}, u32[]{:S(2)}) collective-permute-start(bf16[16,40,128]{2,1,0:T(8,128)(2,1)S(1)} %all_to_all.10.own_ref), channel_id=1, source_target_pairs={{1,0},{0,1},{3,2},{2,3},{5,4},{4,5},{7,6},{6,7},{9,8},{8,9},{11,10... | collective-permute-start | bytes 491528 | tf_op jit(solution)/shard_map/ppermute | solution.py:295

commit v12 on v11

--- a/solution.py
+++ b/solution.py
@@ -26,6 +26,14 @@
 def position(place):
     low, high = place & 3, place >> 2
     return PLACES - 1 - (low * 4 + (high & 1) * 2 + (high >> 1))
+
+
+def back_position(place):
+    return PLACES - 1 - place
+
+
+def group(rule):
+    return sorted(range(PLACES), key=rule)
 
 
 def forecast_rows(u_rows, v_rows):
@@ -266,13 +274,13 @@
     for i in each:
         total = shift[i][:1] + shift[i][16:17] + mean[i][:1]
         result = (root * x3[i] + total).astype(BF)
-        for s in range(count):
-            out_ref[s, i * LOCAL : (i + 1) * LOCAL] = result[s * LOCAL : (s + 1) * LOCAL]
+        for s, place in enumerate(group(position)):
+            out_ref[back_position(place), i * LOCAL : (i + 1) * LOCAL] = result[s * LOCAL : (s + 1) * LOCAL]
 
 
 def forecast_kernel(in_ref, out_ref):
     def unpacked(start):
-        blocks = [in_ref[position(p), start : start + LOCAL] for p in range(in_ref.shape[0])]
+        blocks = [in_ref[back_position(p), start : start + LOCAL] for p in range(in_ref.shape[0])]
         return [row.astype(F32) for row in swap_blocks(blocks, PATCH)]
 
     def by_field(rows):
@@ -320,9 +328,8 @@
     return jnp.concatenate([after[..., : WIDTH // 2], before[..., WIDTH // 2 :]], 2)
 
 
-def exchange(value):
-    group = [sorted(range(lax.axis_size("mem")), key=position)]
-    return lax.all_to_all(value, "mem", split_axis=0, concat_axis=0, axis_index_groups=group, tiled=True)
+def exchange(value, rule):
+    return lax.all_to_all(value, "mem", split_axis=0, concat_axis=0, axis_index_groups=[group(rule)], tiled=True)
 
 
 def call(kernel, name, out_shape, *args, flops=0):
@@ -348,7 +355,8 @@
     rows = jnp.transpose(sample_collection.reshape(LOCAL, FIELDS * BAND, WIDTH), (1, 0, 2))
     region_shape = jax.ShapeDtypeStruct((count, 2 * LOCAL + 8, WIDTH), BF)
     observations = (obs_values, obs_inverse_variance, obs_mask)
-    region = exchange(call(pack_kernel, "forecast_pack", region_shape, rows, near.reshape(-1, WIDTH), *observations))
+    sending = call(pack_kernel, "forecast_pack", region_shape, rows, near.reshape(-1, WIDTH), *observations)
+    region = exchange(sending, position)
     members, points = count * LOCAL, 2 * WIDTH
     patches = 2 if lax.axis_size("rows") == 2 else 1
     own_shapes = [
@@ -361,7 +369,8 @@
     own = call(functools.partial(own_kernel, patches), "own_half", own_shapes, me, region, flops=flops)
     analysed_shape = jax.ShapeDtypeStruct((count, patches * LOCAL, WIDTH), BF)
     kernel = functools.partial(analysis_kernel, patches)
-    inner = exchange(call(kernel, "analysis", analysed_shape, me, region_near, *own, flops=8 * flops))
+    analysed = call(kernel, "analysis", analysed_shape, me, region_near, *own, flops=8 * flops)
+    inner = exchange(analysed, back_position)
     if patches == 1:
         inner = jnp.concatenate([inner, near_rows(inner, join_inner)], 1)
     out_shape = jax.ShapeDtypeStruct((LOCAL * FIELDS * BAND, WIDTH), F32)

time: 31.8 us -> 31.8 us (level)
  no operation moved by 1% of the time
where the time goes in v12:
time: 31.8 us; the launch traced here: 31.6 us
  blocking collectives  24.8 us (78%)
  Pallas kernels  4.13 us (13%)
  waiting for transfers between devices  1.19 us (4%)
  local copies, waits for them, and re-layouts  1 us (3%)
  starting transfers between devices  0.46 us (1%)
    all_to_all x2, blocking collectives, exchange(): lax.all_to_all(value, 'mem', split_axis=0, concat_axis=0, axis_index_grou...  24.8 us
    pallas_call x4, Pallas kernels, call(): pl.pallas_call(kernel, out_shape=out_shape, in_specs=[pl.BlockSpec(memory...  4.13 us
    ppermute x2, waiting for transfers between devices, from_next(): lax.ppermute(value, 'rows', [((i + 1) % count, i) for i in range(count)])  1.19 us
    unnamed x7, local copies, waits for them, and re-layouts  1 us
  transfers between devices with their start and end apart: 2, of which 2 were waited for; matrix products, arithmetic and copies ran while one was open for 3% of the time, Pallas kernels for 1%

profile of v12, /device:TPU:0, one launch (start us, length us, event | category | flops | bytes accessed | tf_op | source)
XLA Modules:
  0.0 31.6 jit_solution(64389486146443990)
XLA Ops:
  0.0 0.5 %collective-permute-start = (f32[16,2,8,128]{3,2,1,0:T(8,128)}, f32[16,2,8,128]{3,2,1,0:T(8,128)S(1)}, u32[]{:S(2)}, u32[]{:S(2)}) collective-permute-start(f32[16,2,8,128]{3,2,1,0:T(8,128)} %param.4), channel_id=1, source_target_pairs={{1,0},{0,1},{3,2},{2,3},{5,4},{4,5},{7,6},{6,7},{9,8},{8,9},{11,10... | collective-permute-start | bytes 393224 | tf_op jit(solution)/shard_map/ppermute | solution.py:303
  0.5 0.0 copy-start
  0.5 0.0 copy-start.1
  0.5 0.0 copy-start.2
  0.5 1.0 %copy.5 = f32[16,2,8,128]{3,0,2,1:T(8,128)S(1)} copy(f32[16,2,8,128]{3,2,1,0:T(8,128)} %param.4) | data formatting | bytes 262144 | tf_op args[0]
  1.5 0.2 collective-permute-done
  1.7 0.0 copy-done
  1.7 0.0 copy-done.1
  1.7 0.0 copy-done.2
  1.7 0.8 %forecast_pack.1 = bf16[16,40,128]{2,1,0:T(8,128)(2,1)S(1)} custom-call(f32[16,16,128]{2,1,0:T(8,128)S(1)} %bitcast.6, f32[256,128]{1,0:T(8,128)S(1)} %bitcast.7, f32[2,8,8]{2,1,0:T(8,128)S(1)} %copy-done, f32[2,8,8]{2,1,0:T(8,128)S(1)} %copy-done.1, s32[2,8,8]{2,1,0:T(8,128)S(1)} %copy-done.2), custom_call_target="tpu_custom_call" | custom-call | bytes 427520 | tf_op jit(solution)/shard_map/forecast_pack/pallas_call | solution.py:338
  2.5 14.1 %all_to_all.10.own_ref = bf16[16,40,128]{2,1,0:T(8,128)(2,1)S(1)} all-to-all(bf16[16,40,128]{2,1,0:T(8,128)(2,1)S(1)} %forecast_pack.1), channel_id=1, replica_groups={{30,14,22,6,28,12,20,4,26,10,18,2,24,8,16,0},{31,15,23,7,29,13,21,5,27,..., dimensions={0} | all-to-all | bytes 327680 | tf_op jit(solution)/shard_map/all_to_all | solution.py:332
  16.7 0.0 collective-permute-start.1
  16.7 0.4 %own_half.1 = (bf16[256,128]{1,0:T(8,128)(2,1)S(1)}, f32[272,512]{1,0:T(8,128)S(1)}, f32[8,128]{1,0:T(8,128)S(1)}) custom-call(s32[1]{0:T(128)} %bitcast.me_ref, bf16[16,40,128]{2,1,0:T(8,128)(2,1)S(1)} %all_to_all.10.own_ref), custom_call_target="tpu_custom_call" | custom-call | flops 33554432 | bytes 790532 | tf_op jit(solution)/shard_map/own_half/pallas_call | solution.py:338
  17.1 1.0 %collective-permute-done.1.near_ref = bf16[16,40,128]{2,1,0:T(8,128)(2,1)S(1)} collective-permute-done((bf16[16,40,128]{2,1,0:T(8,128)(2,1)S(1)}, bf16[16,40,128]{2,1,0:T(8,128)(2,1)S(1)}, u32[]{:S(2)}, u32[]{:S(2)}) %collective-permute-start.1) | collective-permute-done | bytes 163872 | tf_op jit(solution)/shard_map/ppermute | solution.py:303
  18.0 1.5 %analysis.1 = bf16[16,32,128]{2,1,0:T(8,128)(2,1)S(1)} custom-call(s32[1]{0:T(128)} %bitcast.me_ref, bf16[16,40,128]{2,1,0:T(8,128)(2,1)S(1)} %collective-permute-done.1.near_ref, bf16[256,128]{1,0:T(8,128)(2,1)S(1)} %get-tuple-element.8.inner_ref, f32[272,512]{1,0:T(8,128)S(1)} %get-tuple-element.9.sums_ref, f32[8,128]{1,0:T(8,128)S(1)} %get-tuple-element.10.mean_ref), custom_call_target="tpu_custom_call" | custom-call | flops 268435456 | bytes 921604 | tf_op jit(solution)/shard_map/analysis/pallas_call | solution.py:338
  19.6 10.7 %all_to_all.11.in_ref = bf16[16,32,128]{2,1,0:T(8,128)(2,1)S(1)} all-to-all(bf16[16,32,128]{2,1,0:T(8,128)(2,1)S(1)} %analysis.1), channel_id=1, replica_groups={{30,28,26,24,22,20,18,16,14,12,10,8,6,4,2,0},{31,29,27,25,23,21,19,17,1..., dimensions={0} | all-to-all | bytes 262144 | tf_op jit(solution)/shard_map/all_to_all | solution.py:332
  30.3 1.4 %unpack_forecast.1 = f32[256,128]{1,0:T(8,128)} custom-call(bf16[16,32,128]{2,1,0:T(8,128)(2,1)S(1)} %all_to_all.11.in_ref), custom_call_target="tpu_custom_call" | custom-call | bytes 262144 | tf_op jit(solution)/shard_map/unpack_forecast/pallas_call | solution.py:338
Async XLA Ops:
  0.0 1.6 %collective-permute-start = (f32[16,2,8,128]{3,2,1,0:T(8,128)}, f32[16,2,8,128]{3,2,1,0:T(8,128)S(1)}, u32[]{:S(2)}, u32[]{:S(2)}) collective-permute-start(f32[16,2,8,128]{3,2,1,0:T(8,128)} %param.4), channel_id=1, source_target_pairs={{1,0},{0,1},{3,2},{2,3},{5,4},{4,5},{7,6},{6,7},{9,8},{8,9},{11,10... | collective-permute-start | bytes 393224 | tf_op jit(solution)/shard_map/ppermute | solution.py:303
  0.5 1.2 %copy-start = (f32[2,8,8]{2,1,0:T(8,128)S(1)}, f32[2,8,8]{2,1,0:T(8,128)}, u32[]{:S(2)}) copy-start(f32[2,8,8]{2,1,0:T(8,128)} %values_ref.1) | copy-start | bytes 1540
  0.5 1.2 %copy-start.1 = (f32[2,8,8]{2,1,0:T(8,128)S(1)}, f32[2,8,8]{2,1,0:T(8,128)}, u32[]{:S(2)}) copy-start(f32[2,8,8]{2,1,0:T(8,128)} %inverse_ref.1) | copy-start | bytes 1540
  0.5 1.2 %copy-start.2 = (s32[2,8,8]{2,1,0:T(8,128)S(1)}, s32[2,8,8]{2,1,0:T(8,128)}, u32[]{:S(2)}) copy-start(s32[2,8,8]{2,1,0:T(8,128)} %mask_ref.1) | copy-start | bytes 1540
  16.7 1.4 %collective-permute-start.1 = (bf16[16,40,128]{2,1,0:T(8,128)(2,1)S(1)}, bf16[16,40,128]{2,1,0:T(8,128)(2,1)S(1)}, u32[]{:S(2)}, u32[]{:S(2)}) collective-permute-start(bf16[16,40,128]{2,1,0:T(8,128)(2,1)S(1)} %all_to_all.10.own_ref), channel_id=1, source_target_pairs={{1,0},{0,1},{3,2},{2,3},{5,4},{4,5},{7,6},{6,7},{9,8},{8,9},{11,10... | collective-permute-start | bytes 491528 | tf_op jit(solution)/shard_map/ppermute | solution.py:303

commit v13 on v11

--- a/solution.py
+++ b/solution.py
@@ -41,20 +41,24 @@
     return u_rows, v_rows
 
 
-def swap_blocks(parts, size):
+def swap_blocks(parts, size, most):
     count = len(parts)
-    lane = lax.broadcasted_iota(jnp.int32, parts[0].shape, 1) // size
+    block = lax.broadcasted_iota(jnp.int32, parts[0].shape, 1) // size
     stride = 1
     while stride < count:
-        upper = (lane & stride) != 0
-        new = list(parts)
+        base = min(most, count // stride)
+        here = [(block // stride) % base == digit for digit in range(base)]
+        new = []
         for j in range(count):
-            if j & stride == 0:
-                a, b = parts[j], parts[j + stride]
-                new[j] = jnp.where(upper, pltpu.roll(b, stride * size, 1), a)
-                new[j + stride] = jnp.where(upper, b, pltpu.roll(a, WIDTH - stride * size, 1))
+            own = (j // stride) % base
+            value = parts[j]
+            for digit in range(base):
+                if digit != own:
+                    move = (digit - own) * stride
+                    value = jnp.where(here[digit], pltpu.roll(parts[j + move], (move * size) % WIDTH, 1), value)
+            new.append(value)
         parts = new
-        stride *= 2
+        stride *= base
     return parts
 
 
@@ -118,14 +122,14 @@
     for j in range(8):
         part = wide[start + j * 8 : start + j * 8 + 8]
         means.append(jnp.where(is_mean, part[:, :WIDTH], pltpu.roll(part[:, WIDTH:], 2, 0)))
-    means = swap_blocks(means, REGION)
+    means = swap_blocks(means, REGION, 2)
     for side in range(2):
         for half in range(2):
             parts = [
                 wide[(half * 8 + j) * LOCAL : (half * 8 + j + 1) * LOCAL, side * WIDTH : (side + 1) * WIDTH].astype(BF)
                 for j in range(8)
             ]
-            parts = swap_blocks(parts, REGION)
+            parts = swap_blocks(parts, REGION, 2)
             for i in range(8):
                 out_ref[position(side * 8 + i), half * LOCAL : (half + 1) * LOCAL] = parts[i]
         for i in range(8):
@@ -273,7 +277,7 @@
 def forecast_kernel(in_ref, out_ref):
     def unpacked(start):
         blocks = [in_ref[position(p), start : start + LOCAL] for p in range(in_ref.shape[0])]
-        return [row.astype(F32) for row in swap_blocks(blocks, PATCH)]
+        return [row.astype(F32) for row in swap_blocks(blocks, PATCH, 4)]
 
     def by_field(rows):
         half = BAND // 2

time: 31.8 us -> 31.9 us (level)
  no operation moved by 1% of the time
where the time goes in v13:
time: 31.9 us; the launch traced here: 31.7 us
  blocking collectives  24.8 us (78%)
  Pallas kernels  4.19 us (13%)
  waiting for transfers between devices  1.18 us (4%)
  local copies, waits for them, and re-layouts  1 us (3%)
  starting transfers between devices  0.46 us (1%)
    all_to_all x2, blocking collectives, exchange(): lax.all_to_all(value, 'mem', split_axis=0, concat_axis=0, axis_index_grou...  24.8 us
    pallas_call x4, Pallas kernels, call(): pl.pallas_call(kernel, out_shape=out_shape, in_specs=[pl.BlockSpec(memory...  4.19 us
    ppermute x2, waiting for transfers between devices, from_next(): lax.ppermute(value, 'rows', [((i + 1) % count, i) for i in range(count)])  1.18 us
    unnamed x7, local copies, waits for them, and re-layouts  1 us
  transfers between devices with their start and end apart: 2, of which 2 were waited for; matrix products, arithmetic and copies ran while one was open for 3% of the time, Pallas kernels for 1%

profile of v13, /device:TPU:0, one launch (start us, length us, event | category | flops | bytes accessed | tf_op | source)
XLA Modules:
  0.0 31.7 jit_solution(5631531501182476445)
XLA Ops:
  0.0 0.5 %collective-permute-start = (f32[16,2,8,128]{3,2,1,0:T(8,128)}, f32[16,2,8,128]{3,2,1,0:T(8,128)S(1)}, u32[]{:S(2)}, u32[]{:S(2)}) collective-permute-start(f32[16,2,8,128]{3,2,1,0:T(8,128)} %param.4), channel_id=1, source_target_pairs={{1,0},{0,1},{3,2},{2,3},{5,4},{4,5},{7,6},{6,7},{9,8},{8,9},{11,10... | collective-permute-start | bytes 393224 | tf_op jit(solution)/shard_map/ppermute | solution.py:299
  0.5 0.0 copy-start
  0.5 0.0 copy-start.1
  0.5 0.0 copy-start.2
  0.5 1.0 %copy.5 = f32[16,2,8,128]{3,0,2,1:T(8,128)S(1)} copy(f32[16,2,8,128]{3,2,1,0:T(8,128)} %param.4) | data formatting | bytes 262144 | tf_op args[0]
  1.5 0.2 collective-permute-done
  1.7 0.0 copy-done
  1.7 0.0 copy-done.1
  1.7 0.0 copy-done.2
  1.7 0.8 %forecast_pack.1 = bf16[16,40,128]{2,1,0:T(8,128)(2,1)S(1)} custom-call(f32[16,16,128]{2,1,0:T(8,128)S(1)} %bitcast.6, f32[256,128]{1,0:T(8,128)S(1)} %bitcast.7, f32[2,8,8]{2,1,0:T(8,128)S(1)} %copy-done, f32[2,8,8]{2,1,0:T(8,128)S(1)} %copy-done.1, s32[2,8,8]{2,1,0:T(8,128)S(1)} %copy-done.2), custom_call_target="tpu_custom_call" | custom-call | bytes 427520 | tf_op jit(solution)/shard_map/forecast_pack/pallas_call | solution.py:335
  2.5 14.1 %all_to_all.10.own_ref = bf16[16,40,128]{2,1,0:T(8,128)(2,1)S(1)} all-to-all(bf16[16,40,128]{2,1,0:T(8,128)(2,1)S(1)} %forecast_pack.1), channel_id=1, replica_groups={{30,14,22,6,28,12,20,4,26,10,18,2,24,8,16,0},{31,15,23,7,29,13,21,5,27,..., dimensions={0} | all-to-all | bytes 327680 | tf_op jit(solution)/shard_map/all_to_all | solution.py:329
  16.6 0.0 collective-permute-start.1
  16.7 0.4 %own_half.1 = (bf16[256,128]{1,0:T(8,128)(2,1)S(1)}, f32[272,512]{1,0:T(8,128)S(1)}, f32[8,128]{1,0:T(8,128)S(1)}) custom-call(s32[1]{0:T(128)} %bitcast.me_ref, bf16[16,40,128]{2,1,0:T(8,128)(2,1)S(1)} %all_to_all.10.own_ref), custom_call_target="tpu_custom_call" | custom-call | flops 33554432 | bytes 790532 | tf_op jit(solution)/shard_map/own_half/pallas_call | solution.py:335
  17.1 1.0 %collective-permute-done.1.near_ref = bf16[16,40,128]{2,1,0:T(8,128)(2,1)S(1)} collective-permute-done((bf16[16,40,128]{2,1,0:T(8,128)(2,1)S(1)}, bf16[16,40,128]{2,1,0:T(8,128)(2,1)S(1)}, u32[]{:S(2)}, u32[]{:S(2)}) %collective-permute-start.1) | collective-permute-done | bytes 163872 | tf_op jit(solution)/shard_map/ppermute | solution.py:299
  18.0 1.5 %analysis.1 = bf16[16,32,128]{2,1,0:T(8,128)(2,1)S(1)} custom-call(s32[1]{0:T(128)} %bitcast.me_ref, bf16[16,40,128]{2,1,0:T(8,128)(2,1)S(1)} %collective-permute-done.1.near_ref, bf16[256,128]{1,0:T(8,128)(2,1)S(1)} %get-tuple-element.8.inner_ref, f32[272,512]{1,0:T(8,128)S(1)} %get-tuple-element.9.sums_ref, f32[8,128]{1,0:T(8,128)S(1)} %get-tuple-element.10.mean_ref), custom_call_target="tpu_custom_call" | custom-call | flops 268435456 | bytes 921604 | tf_op jit(solution)/shard_map/analysis/pallas_call | solution.py:335
  19.6 10.7 %all_to_all.11.in_ref = bf16[16,32,128]{2,1,0:T(8,128)(2,1)S(1)} all-to-all(bf16[16,32,128]{2,1,0:T(8,128)(2,1)S(1)} %analysis.1), channel_id=1, replica_groups={{30,14,22,6,28,12,20,4,26,10,18,2,24,8,16,0},{31,15,23,7,29,13,21,5,27,..., dimensions={0} | all-to-all | bytes 262144 | tf_op jit(solution)/shard_map/all_to_all | solution.py:329
  30.3 1.4 %unpack_forecast.1 = f32[256,128]{1,0:T(8,128)} custom-call(bf16[16,32,128]{2,1,0:T(8,128)(2,1)S(1)} %all_to_all.11.in_ref), custom_call_target="tpu_custom_call" | custom-call | bytes 262144 | tf_op jit(solution)/shard_map/unpack_forecast/pallas_call | solution.py:335
Async XLA Ops:
  0.0 1.6 %collective-permute-start = (f32[16,2,8,128]{3,2,1,0:T(8,128)}, f32[16,2,8,128]{3,2,1,0:T(8,128)S(1)}, u32[]{:S(2)}, u32[]{:S(2)}) collective-permute-start(f32[16,2,8,128]{3,2,1,0:T(8,128)} %param.4), channel_id=1, source_target_pairs={{1,0},{0,1},{3,2},{2,3},{5,4},{4,5},{7,6},{6,7},{9,8},{8,9},{11,10... | collective-permute-start | bytes 393224 | tf_op jit(solution)/shard_map/ppermute | solution.py:299
  0.5 1.2 %copy-start = (f32[2,8,8]{2,1,0:T(8,128)S(1)}, f32[2,8,8]{2,1,0:T(8,128)}, u32[]{:S(2)}) copy-start(f32[2,8,8]{2,1,0:T(8,128)} %values_ref.1) | copy-start | bytes 1540
  0.5 1.2 %copy-start.1 = (f32[2,8,8]{2,1,0:T(8,128)S(1)}, f32[2,8,8]{2,1,0:T(8,128)}, u32[]{:S(2)}) copy-start(f32[2,8,8]{2,1,0:T(8,128)} %inverse_ref.1) | copy-start | bytes 1540
  0.5 1.2 %copy-start.2 = (s32[2,8,8]{2,1,0:T(8,128)S(1)}, s32[2,8,8]{2,1,0:T(8,128)}, u32[]{:S(2)}) copy-start(s32[2,8,8]{2,1,0:T(8,128)} %mask_ref.1) | copy-start | bytes 1540
  16.6 1.4 %collective-permute-start.1 = (bf16[16,40,128]{2,1,0:T(8,128)(2,1)S(1)}, bf16[16,40,128]{2,1,0:T(8,128)(2,1)S(1)}, u32[]{:S(2)}, u32[]{:S(2)}) collective-permute-start(bf16[16,40,128]{2,1,0:T(8,128)(2,1)S(1)} %all_to_all.10.own_ref), channel_id=1, source_target_pairs={{1,0},{0,1},{3,2},{2,3},{5,4},{4,5},{7,6},{6,7},{9,8},{8,9},{11,10... | collective-permute-start | bytes 491528 | tf_op jit(solution)/shard_map/ppermute | solution.py:299

commit v14 on v11

--- a/solution.py
+++ b/solution.py
@@ -23,9 +23,14 @@
 F32 = jnp.float32
 
 
-def position(place):
-    low, high = place & 3, place >> 2
-    return PLACES - 1 - (low * 4 + (high & 1) * 2 + (high >> 1))
+GOING = (15, 7, 11, 6, 10, 5, 9, 4, 8, 3, 2, 1, 14, 13, 12, 0)
+BACK = (15, 7, 11, 3, 14, 6, 10, 2, 13, 5, 9, 1, 12, 4, 8, 0)
+
+
+def position(place, order=GOING):
+    if isinstance(place, int):
+        return order.index(place)
+    return functools.reduce(lambda kept, k: jnp.where(place == order[k], k, kept), range(1, PLACES), 0)
 
 
 def forecast_rows(u_rows, v_rows):
@@ -266,13 +271,13 @@
     for i in each:
         total = shift[i][:1] + shift[i][16:17] + mean[i][:1]
         result = (root * x3[i] + total).astype(BF)
-        for s in range(count):
-            out_ref[s, i * LOCAL : (i + 1) * LOCAL] = result[s * LOCAL : (s + 1) * LOCAL]
+        for s, place in enumerate(GOING):
+            out_ref[position(place, BACK), i * LOCAL : (i + 1) * LOCAL] = result[s * LOCAL : (s + 1) * LOCAL]
 
 
 def forecast_kernel(in_ref, out_ref):
     def unpacked(start):
-        blocks = [in_ref[position(p), start : start + LOCAL] for p in range(in_ref.shape[0])]
+        blocks = [in_ref[position(p, BACK), start : start + LOCAL] for p in range(in_ref.shape[0])]
         return [row.astype(F32) for row in swap_blocks(blocks, PATCH)]
 
     def by_field(rows):
@@ -320,9 +325,8 @@
     return jnp.concatenate([after[..., : WIDTH // 2], before[..., WIDTH // 2 :]], 2)
 
 
-def exchange(value):
-    group = [sorted(range(lax.axis_size("mem")), key=position)]
-    return lax.all_to_all(value, "mem", split_axis=0, concat_axis=0, axis_index_groups=group, tiled=True)
+def exchange(value, order):
+    return lax.all_to_all(value, "mem", split_axis=0, concat_axis=0, axis_index_groups=[list(order)], tiled=True)
 
 
 def call(kernel, name, out_shape, *args, flops=0):
@@ -348,7 +352,8 @@
     rows = jnp.transpose(sample_collection.reshape(LOCAL, FIELDS * BAND, WIDTH), (1, 0, 2))
     region_shape = jax.ShapeDtypeStruct((count, 2 * LOCAL + 8, WIDTH), BF)
     observations = (obs_values, obs_inverse_variance, obs_mask)
-    region = exchange(call(pack_kernel, "forecast_pack", region_shape, rows, near.reshape(-1, WIDTH), *observations))
+    sending = call(pack_kernel, "forecast_pack", region_shape, rows, near.reshape(-1, WIDTH), *observations)
+    region = exchange(sending, GOING)
     members, points = count * LOCAL, 2 * WIDTH
     patches = 2 if lax.axis_size("rows") == 2 else 1
     own_shapes = [
@@ -361,7 +366,8 @@
     own = call(functools.partial(own_kernel, patches), "own_half", own_shapes, me, region, flops=flops)
     analysed_shape = jax.ShapeDtypeStruct((count, patches * LOCAL, WIDTH), BF)
     kernel = functools.partial(analysis_kernel, patches)
-    inner = exchange(call(kernel, "analysis", analysed_shape, me, region_near, *own, flops=8 * flops))
+    analysed = call(kernel, "analysis", analysed_shape, me, region_near, *own, flops=8 * flops)
+    inner = exchange(analysed, BACK)
     if patches == 1:
         inner = jnp.concatenate([inner, near_rows(inner, join_inner)], 1)
     out_shape = jax.ShapeDtypeStruct((LOCAL * FIELDS * BAND, WIDTH), F32)

time: 31.8 us -> 31.9 us (level)
  no operation moved by 1% of the time
where the time goes in v14:
time: 31.9 us; the launch traced here: 31.7 us
  blocking collectives  24.9 us (78%)
  Pallas kernels  4.15 us (13%)
  waiting for transfers between devices  1.17 us (4%)
  local copies, waits for them, and re-layouts  1 us (3%)
  starting transfers between devices  0.46 us (1%)
    all_to_all x2, blocking collectives, exchange(): lax.all_to_all(value, 'mem', split_axis=0, concat_axis=0, axis_index_grou...  24.9 us
    pallas_call x4, Pallas kernels, call(): pl.pallas_call(kernel, out_shape=out_shape, in_specs=[pl.BlockSpec(memory...  4.15 us
    ppermute x2, waiting for transfers between devices, from_next(): lax.ppermute(value, 'rows', [((i + 1) % count, i) for i in range(count)])  1.17 us
    unnamed x7, local copies, waits for them, and re-layouts  1 us
  transfers between devices with their start and end apart: 2, of which 2 were waited for; matrix products, arithmetic and copies ran while one was open for 3% of the time, Pallas kernels for 1%

profile of v14, /device:TPU:0, one launch (start us, length us, event | category | flops | bytes accessed | tf_op | source)
XLA Modules:
  0.0 31.7 jit_solution(701948712629672531)
XLA Ops:
  0.0 0.5 %collective-permute-start = (f32[16,2,8,128]{3,2,1,0:T(8,128)}, f32[16,2,8,128]{3,2,1,0:T(8,128)S(1)}, u32[]{:S(2)}, u32[]{:S(2)}) collective-permute-start(f32[16,2,8,128]{3,2,1,0:T(8,128)} %param.4), channel_id=1, source_target_pairs={{1,0},{0,1},{3,2},{2,3},{5,4},{4,5},{7,6},{6,7},{9,8},{8,9},{11,10... | collective-permute-start | bytes 393224 | tf_op jit(solution)/shard_map/ppermute | solution.py:300
  0.5 0.0 copy-start
  0.5 0.0 copy-start.1
  0.5 0.0 copy-start.2
  0.5 1.0 %copy.5 = f32[16,2,8,128]{3,0,2,1:T(8,128)S(1)} copy(f32[16,2,8,128]{3,2,1,0:T(8,128)} %param.4) | data formatting | bytes 262144 | tf_op args[0]
  1.5 0.2 collective-permute-done
  1.7 0.0 copy-done
  1.7 0.0 copy-done.1
  1.7 0.0 copy-done.2
  1.7 0.8 %forecast_pack.1 = bf16[16,40,128]{2,1,0:T(8,128)(2,1)S(1)} custom-call(f32[16,16,128]{2,1,0:T(8,128)S(1)} %bitcast.6, f32[256,128]{1,0:T(8,128)S(1)} %bitcast.7, f32[2,8,8]{2,1,0:T(8,128)S(1)} %copy-done, f32[2,8,8]{2,1,0:T(8,128)S(1)} %copy-done.1, s32[2,8,8]{2,1,0:T(8,128)S(1)} %copy-done.2), custom_call_target="tpu_custom_call" | custom-call | bytes 427520 | tf_op jit(solution)/shard_map/forecast_pack/pallas_call | solution.py:335
  2.5 14.2 %all_to_all.10.own_ref = bf16[16,40,128]{2,1,0:T(8,128)(2,1)S(1)} all-to-all(bf16[16,40,128]{2,1,0:T(8,128)(2,1)S(1)} %forecast_pack.1), channel_id=1, replica_groups={{30,14,22,12,20,10,18,8,16,6,4,2,28,26,24,0},{31,15,23,13,21,11,19,9,17..., dimensions={0} | all-to-all | bytes 327680 | tf_op jit(solution)/shard_map/all_to_all | solution.py:329
  16.7 0.0 collective-permute-start.1
  16.7 0.4 %own_half.1 = (bf16[256,128]{1,0:T(8,128)(2,1)S(1)}, f32[272,512]{1,0:T(8,128)S(1)}, f32[8,128]{1,0:T(8,128)S(1)}) custom-call(s32[1]{0:T(128)} %bitcast.me_ref, bf16[16,40,128]{2,1,0:T(8,128)(2,1)S(1)} %all_to_all.10.own_ref), custom_call_target="tpu_custom_call" | custom-call | flops 33554432 | bytes 790532 | tf_op jit(solution)/shard_map/own_half/pallas_call | solution.py:335
  17.1 1.0 %collective-permute-done.1.near_ref = bf16[16,40,128]{2,1,0:T(8,128)(2,1)S(1)} collective-permute-done((bf16[16,40,128]{2,1,0:T(8,128)(2,1)S(1)}, bf16[16,40,128]{2,1,0:T(8,128)(2,1)S(1)}, u32[]{:S(2)}, u32[]{:S(2)}) %collective-permute-start.1) | collective-permute-done | bytes 163872 | tf_op jit(solution)/shard_map/ppermute | solution.py:300
  18.1 1.5 %analysis.1 = bf16[16,32,128]{2,1,0:T(8,128)(2,1)S(1)} custom-call(s32[1]{0:T(128)} %bitcast.me_ref, bf16[16,40,128]{2,1,0:T(8,128)(2,1)S(1)} %collective-permute-done.1.near_ref, bf16[256,128]{1,0:T(8,128)(2,1)S(1)} %get-tuple-element.8.inner_ref, f32[272,512]{1,0:T(8,128)S(1)} %get-tuple-element.9.sums_ref, f32[8,128]{1,0:T(8,128)S(1)} %get-tuple-element.10.mean_ref), custom_call_target="tpu_custom_call" | custom-call | flops 268435456 | bytes 921604 | tf_op jit(solution)/shard_map/analysis/pallas_call | solution.py:335
  19.6 10.8 %all_to_all.11.in_ref = bf16[16,32,128]{2,1,0:T(8,128)(2,1)S(1)} all-to-all(bf16[16,32,128]{2,1,0:T(8,128)(2,1)S(1)} %analysis.1), channel_id=1, replica_groups={{30,14,22,6,28,12,20,4,26,10,18,2,24,8,16,0},{31,15,23,7,29,13,21,5,27,..., dimensions={0} | all-to-all | bytes 262144 | tf_op jit(solution)/shard_map/all_to_all | solution.py:329
  30.4 1.4 %unpack_forecast.1 = f32[256,128]{1,0:T(8,128)} custom-call(bf16[16,32,128]{2,1,0:T(8,128)(2,1)S(1)} %all_to_all.11.in_ref), custom_call_target="tpu_custom_call" | custom-call | bytes 262144 | tf_op jit(solution)/shard_map/unpack_forecast/pallas_call | solution.py:335
Async XLA Ops:
  0.0 1.6 %collective-permute-start = (f32[16,2,8,128]{3,2,1,0:T(8,128)}, f32[16,2,8,128]{3,2,1,0:T(8,128)S(1)}, u32[]{:S(2)}, u32[]{:S(2)}) collective-permute-start(f32[16,2,8,128]{3,2,1,0:T(8,128)} %param.4), channel_id=1, source_target_pairs={{1,0},{0,1},{3,2},{2,3},{5,4},{4,5},{7,6},{6,7},{9,8},{8,9},{11,10... | collective-permute-start | bytes 393224 | tf_op jit(solution)/shard_map/ppermute | solution.py:300
  0.5 1.2 %copy-start = (f32[2,8,8]{2,1,0:T(8,128)S(1)}, f32[2,8,8]{2,1,0:T(8,128)}, u32[]{:S(2)}) copy-start(f32[2,8,8]{2,1,0:T(8,128)} %values_ref.1) | copy-start | bytes 1540
  0.5 1.2 %copy-start.1 = (f32[2,8,8]{2,1,0:T(8,128)S(1)}, f32[2,8,8]{2,1,0:T(8,128)}, u32[]{:S(2)}) copy-start(f32[2,8,8]{2,1,0:T(8,128)} %inverse_ref.1) | copy-start | bytes 1540
  0.5 1.2 %copy-start.2 = (s32[2,8,8]{2,1,0:T(8,128)S(1)}, s32[2,8,8]{2,1,0:T(8,128)}, u32[]{:S(2)}) copy-start(s32[2,8,8]{2,1,0:T(8,128)} %mask_ref.1) | copy-start | bytes 1540
  16.7 1.4 %collective-permute-start.1 = (bf16[16,40,128]{2,1,0:T(8,128)(2,1)S(1)}, bf16[16,40,128]{2,1,0:T(8,128)(2,1)S(1)}, u32[]{:S(2)}, u32[]{:S(2)}) collective-permute-start(bf16[16,40,128]{2,1,0:T(8,128)(2,1)S(1)} %all_to_all.10.own_ref), channel_id=1, source_target_pairs={{1,0},{0,1},{3,2},{2,3},{5,4},{4,5},{7,6},{6,7},{9,8},{8,9},{11,10... | collective-permute-start | bytes 491528 | tf_op jit(solution)/shard_map/ppermute | solution.py:300

commit v15 on v14

--- a/solution.py
+++ b/solution.py
@@ -23,8 +23,8 @@
 F32 = jnp.float32
 
 
-GOING = (15, 7, 11, 6, 10, 5, 9, 4, 8, 3, 2, 1, 14, 13, 12, 0)
-BACK = (15, 7, 11, 3, 14, 6, 10, 2, 13, 5, 9, 1, 12, 4, 8, 0)
+GOING = (15, 7, 11, 3, 14, 6, 10, 2, 13, 5, 9, 1, 12, 4, 8, 0)
+BACK = (1, 2, 3, 4, 5, 6, 7, 8, 9, 10, 11, 12, 13, 14, 15, 0)
 
 
 def position(place, order=GOING):

time: 31.9 us -> 33.7 us (1.056)
  blocking collectives: 24.9 us -> 26.7 us
    all_to_all x2, blocking collectives: 24.9 us -> 26.7 us  [exchange(): lax.all_to_all(value, 'mem', split_axis=0, concat_axis=0, axis_index_grou...]
where the time goes in v15:
time: 33.7 us; the launch traced here: 33.5 us
  blocking collectives  26.7 us (79%)
  Pallas kernels  4.15 us (12%)
  waiting for transfers between devices  1.17 us (3%)
  local copies, waits for them, and re-layouts  1 us (3%)
  starting transfers between devices  0.46 us (1%)
    all_to_all x2, blocking collectives, exchange(): lax.all_to_all(value, 'mem', split_axis=0, concat_axis=0, axis_index_grou...  26.7 us
    pallas_call x4, Pallas kernels, call(): pl.pallas_call(kernel, out_shape=out_shape, in_specs=[pl.BlockSpec(memory...  4.15 us
    ppermute x2, waiting for transfers between devices, from_next(): lax.ppermute(value, 'rows', [((i + 1) % count, i) for i in range(count)])  1.17 us
    unnamed x7, local copies, waits for them, and re-layouts  1 us
  transfers between devices with their start and end apart: 2, of which 2 were waited for; matrix products, arithmetic and copies ran while one was open for 3% of the time, Pallas kernels for 1%

profile of v15, /device:TPU:0, one launch (start us, length us, event | category | flops | bytes accessed | tf_op | source)
XLA Modules:
  0.0 33.5 jit_solution(1181910791551145071)
XLA Ops:
  0.0 0.5 %collective-permute-start = (f32[16,2,8,128]{3,2,1,0:T(8,128)}, f32[16,2,8,128]{3,2,1,0:T(8,128)S(1)}, u32[]{:S(2)}, u32[]{:S(2)}) collective-permute-start(f32[16,2,8,128]{3,2,1,0:T(8,128)} %param.4), channel_id=1, source_target_pairs={{1,0},{0,1},{3,2},{2,3},{5,4},{4,5},{7,6},{6,7},{9,8},{8,9},{11,10... | collective-permute-start | bytes 393224 | tf_op jit(solution)/shard_map/ppermute | solution.py:300
  0.5 0.0 copy-start
  0.5 0.0 copy-start.1
  0.5 0.0 copy-start.2
  0.5 1.0 %copy.5 = f32[16,2,8,128]{3,0,2,1:T(8,128)S(1)} copy(f32[16,2,8,128]{3,2,1,0:T(8,128)} %param.4) | data formatting | bytes 262144 | tf_op args[0]
  1.5 0.2 collective-permute-done
  1.7 0.0 copy-done
  1.7 0.0 copy-done.1
  1.7 0.0 copy-done.2
  1.7 0.8 %forecast_pack.1 = bf16[16,40,128]{2,1,0:T(8,128)(2,1)S(1)} custom-call(f32[16,16,128]{2,1,0:T(8,128)S(1)} %bitcast.6, f32[256,128]{1,0:T(8,128)S(1)} %bitcast.7, f32[2,8,8]{2,1,0:T(8,128)S(1)} %copy-done, f32[2,8,8]{2,1,0:T(8,128)S(1)} %copy-done.1, s32[2,8,8]{2,1,0:T(8,128)S(1)} %copy-done.2), custom_call_target="tpu_custom_call" | custom-call | bytes 427520 | tf_op jit(solution)/shard_map/forecast_pack/pallas_call | solution.py:335
  2.5 14.1 %all_to_all.10.own_ref = bf16[16,40,128]{2,1,0:T(8,128)(2,1)S(1)} all-to-all(bf16[16,40,128]{2,1,0:T(8,128)(2,1)S(1)} %forecast_pack.1), channel_id=1, replica_groups={{30,14,22,6,28,12,20,4,26,10,18,2,24,8,16,0},{31,15,23,7,29,13,21,5,27,..., dimensions={0} | all-to-all | bytes 327680 | tf_op jit(solution)/shard_map/all_to_all | solution.py:329
  16.7 0.0 collective-permute-start.1
  16.7 0.4 %own_half.1 = (bf16[256,128]{1,0:T(8,128)(2,1)S(1)}, f32[272,512]{1,0:T(8,128)S(1)}, f32[8,128]{1,0:T(8,128)S(1)}) custom-call(s32[1]{0:T(128)} %bitcast.me_ref, bf16[16,40,128]{2,1,0:T(8,128)(2,1)S(1)} %all_to_all.10.own_ref), custom_call_target="tpu_custom_call" | custom-call | flops 33554432 | bytes 790532 | tf_op jit(solution)/shard_map/own_half/pallas_call | solution.py:335
  17.1 1.0 %collective-permute-done.1.near_ref = bf16[16,40,128]{2,1,0:T(8,128)(2,1)S(1)} collective-permute-done((bf16[16,40,128]{2,1,0:T(8,128)(2,1)S(1)}, bf16[16,40,128]{2,1,0:T(8,128)(2,1)S(1)}, u32[]{:S(2)}, u32[]{:S(2)}) %collective-permute-start.1) | collective-permute-done | bytes 163872 | tf_op jit(solution)/shard_map/ppermute | solution.py:300
  18.0 1.5 %analysis.1 = bf16[16,32,128]{2,1,0:T(8,128)(2,1)S(1)} custom-call(s32[1]{0:T(128)} %bitcast.me_ref, bf16[16,40,128]{2,1,0:T(8,128)(2,1)S(1)} %collective-permute-done.1.near_ref, bf16[256,128]{1,0:T(8,128)(2,1)S(1)} %get-tuple-element.8.inner_ref, f32[272,512]{1,0:T(8,128)S(1)} %get-tuple-element.9.sums_ref, f32[8,128]{1,0:T(8,128)S(1)} %get-tuple-element.10.mean_ref), custom_call_target="tpu_custom_call" | custom-call | flops 268435456 | bytes 921604 | tf_op jit(solution)/shard_map/analysis/pallas_call | solution.py:335
  19.6 12.5 %all_to_all.11.in_ref = bf16[16,32,128]{2,1,0:T(8,128)(2,1)S(1)} all-to-all(bf16[16,32,128]{2,1,0:T(8,128)(2,1)S(1)} %analysis.1), channel_id=1, replica_groups={{2,4,6,8,10,12,14,16,18,20,22,24,26,28,30,0},{3,5,7,9,11,13,15,17,19,21..., dimensions={0} | all-to-all | bytes 262144 | tf_op jit(solution)/shard_map/all_to_all | solution.py:329
  32.1 1.4 %unpack_forecast.1 = f32[256,128]{1,0:T(8,128)} custom-call(bf16[16,32,128]{2,1,0:T(8,128)(2,1)S(1)} %all_to_all.11.in_ref), custom_call_target="tpu_custom_call" | custom-call | bytes 262144 | tf_op jit(solution)/shard_map/unpack_forecast/pallas_call | solution.py:335
Async XLA Ops:
  0.0 1.6 %collective-permute-start = (f32[16,2,8,128]{3,2,1,0:T(8,128)}, f32[16,2,8,128]{3,2,1,0:T(8,128)S(1)}, u32[]{:S(2)}, u32[]{:S(2)}) collective-permute-start(f32[16,2,8,128]{3,2,1,0:T(8,128)} %param.4), channel_id=1, source_target_pairs={{1,0},{0,1},{3,2},{2,3},{5,4},{4,5},{7,6},{6,7},{9,8},{8,9},{11,10... | collective-permute-start | bytes 393224 | tf_op jit(solution)/shard_map/ppermute | solution.py:300
  0.5 1.2 %copy-start = (f32[2,8,8]{2,1,0:T(8,128)S(1)}, f32[2,8,8]{2,1,0:T(8,128)}, u32[]{:S(2)}) copy-start(f32[2,8,8]{2,1,0:T(8,128)} %values_ref.1) | copy-start | bytes 1540
  0.5 1.2 %copy-start.1 = (f32[2,8,8]{2,1,0:T(8,128)S(1)}, f32[2,8,8]{2,1,0:T(8,128)}, u32[]{:S(2)}) copy-start(f32[2,8,8]{2,1,0:T(8,128)} %inverse_ref.1) | copy-start | bytes 1540
  0.5 1.2 %copy-start.2 = (s32[2,8,8]{2,1,0:T(8,128)S(1)}, s32[2,8,8]{2,1,0:T(8,128)}, u32[]{:S(2)}) copy-start(s32[2,8,8]{2,1,0:T(8,128)} %mask_ref.1) | copy-start | bytes 1540
  16.7 1.4 %collective-permute-start.1 = (bf16[16,40,128]{2,1,0:T(8,128)(2,1)S(1)}, bf16[16,40,128]{2,1,0:T(8,128)(2,1)S(1)}, u32[]{:S(2)}, u32[]{:S(2)}) collective-permute-start(bf16[16,40,128]{2,1,0:T(8,128)(2,1)S(1)} %all_to_all.10.own_ref), channel_id=1, source_target_pairs={{1,0},{0,1},{3,2},{2,3},{5,4},{4,5},{7,6},{6,7},{9,8},{8,9},{11,10... | collective-permute-start | bytes 491528 | tf_op jit(solution)/shard_map/ppermute | solution.py:300

commit v16 on v11

--- a/solution.py
+++ b/solution.py
@@ -28,17 +28,29 @@
     return PLACES - 1 - (low * 4 + (high & 1) * 2 + (high >> 1))
 
 
-def forecast_rows(u_rows, v_rows):
-    for _ in range(FSTEPS):
-        new_u, new_v = [], []
+def advance(u_rows, v_rows, i):
+    cu, cv = CADV * u_rows[i], CADV * v_rows[i]
+    stepped = []
+    for rows in (u_rows, v_rows):
+        along_x = pltpu.roll(rows[i], WIDTH - 1, 1) - pltpu.roll(rows[i], 1, 1)
+        along_y = rows[i + 1] - rows[i - 1]
+        stepped.append(rows[i] - (cu * along_x + cv * along_y))
+    return stepped
+
+
+def forecast_rows(u_rows, v_rows, known=None):
+    for step in range(1, FSTEPS + 1):
+        stepped = []
         for i in range(1, len(u_rows) - 1):
-            cu, cv = CADV * u_rows[i], CADV * v_rows[i]
-            for rows, new in ((u_rows, new_u), (v_rows, new_v)):
-                along_x = pltpu.roll(rows[i], WIDTH - 1, 1) - pltpu.roll(rows[i], 1, 1)
-                along_y = rows[i + 1] - rows[i - 1]
-                new.append(rows[i] - (cu * along_x + cv * along_y))
-        u_rows, v_rows = new_u, new_v
+            row = i - 1 + step - FSTEPS
+            given = known(step, row) if known is not None and step <= row < BAND - step else None
+            stepped.append(given if given is not None else advance(u_rows, v_rows, i))
+        u_rows, v_rows = [u for u, _ in stepped], [v for _, v in stepped]
     return u_rows, v_rows
+
+
+def inner_steps():
+    return [(step, row) for step in range(1, FSTEPS) for row in range(step, BAND - step)]
 
 
 def swap_blocks(parts, size):
@@ -82,8 +94,26 @@
     return jnp.dot(gather, wide, preferred_element_type=F32)
 
 
-def pack_kernel(rows_ref, near_ref, values_ref, inverse_ref, mask_ref, out_ref):
+def inner_kernel(rows_ref, values_ref, inverse_ref, mask_ref, out_ref, obs_ref):
+    obs_ref[...] = observation_rows(values_ref, inverse_ref, mask_ref)
+    u_rows, v_rows = ([rows_ref[field * BAND + r] for r in range(BAND)] for field in range(FIELDS))
+    kept = 0
+    for _ in range(1, FSTEPS):
+        stepped = [advance(u_rows, v_rows, i) for i in range(1, len(u_rows) - 1)]
+        u_rows, v_rows = [u for u, _ in stepped], [v for _, v in stepped]
+        for row in stepped:
+            for value in row:
+                out_ref[kept] = value
+                kept += 1
+
+
+def pack_kernel(rows_ref, inner_ref, obs_ref, near_ref, out_ref):
     points = FIELDS * BAND
+    places = inner_steps()
+
+    def known(step, row):
+        first = FIELDS * places.index((step, row))
+        return [inner_ref[first + field] for field in range(FIELDS)]
 
     def near(field, index):
         return near_ref[pl.ds(field * BAND + index, LOCAL, stride=points), :]
@@ -94,7 +124,7 @@
         own = [rows_ref[field * BAND + r] for r in range(BAND)]
         after = [near(field, r) for r in range(FSTEPS)]
         fields.append(before + own + after)
-    done = forecast_rows(*fields)
+    done = forecast_rows(*fields, known)
     half_rows = BAND // 2
     index = lax.broadcasted_iota(jnp.int32, (8, WIDTH), 0)
     values, means = [], [jnp.zeros((8, WIDTH), F32)] * (FIELDS * half_rows)
@@ -111,7 +141,7 @@
     wanted = ((lane // REGION) * PATCH + lane % REGION + (WIDTH - RADIUS)) % WIDTH
     widen = (column == wanted).astype(F32).astype(BF)
     wide = jnp.dot(rows, widen, preferred_element_type=F32)
-    obs = observation_rows(values_ref, inverse_ref, mask_ref)
+    obs = obs_ref[...]
     start = len(values) * LOCAL
     is_mean = index & 2 == 0
     means = []
@@ -347,8 +377,10 @@
     near = near_rows(sample_collection, join_grid)
     rows = jnp.transpose(sample_collection.reshape(LOCAL, FIELDS * BAND, WIDTH), (1, 0, 2))
     region_shape = jax.ShapeDtypeStruct((count, 2 * LOCAL + 8, WIDTH), BF)
-    observations = (obs_values, obs_inverse_variance, obs_mask)
-    region = exchange(call(pack_kernel, "forecast_pack", region_shape, rows, near.reshape(-1, WIDTH), *observations))
+    kept = FIELDS * len(inner_steps())
+    inner_shapes = [jax.ShapeDtypeStruct((kept, LOCAL, WIDTH), F32), jax.ShapeDtypeStruct((8, WIDTH), F32)]
+    inner = call(inner_kernel, "inner_rows", inner_shapes, rows, obs_values, obs_inverse_variance, obs_mask)
+    region = exchange(call(pack_kernel, "forecast_pack", region_shape, rows, *inner, near.reshape(-1, WIDTH)))
     members, points = count * LOCAL, 2 * WIDTH
     patches = 2 if lax.axis_size("rows") == 2 else 1
     own_shapes = [

time: 31.8 us -> 31.8 us (level)
    pallas_call x4 -> x5, Pallas kernels: 4.13 us -> 4.25 us  [call(): pl.pallas_call(kernel, out_shape=out_shape, in_specs=[pl.BlockSpec(memory...]
  transfers between devices with their start and end apart: 2 -> 2, of which waited for: 2 -> 1; matrix products, arithmetic and copies ran while one was open for 3% -> 3% of each run, Pallas kernels for 1% -> 2%
where the time goes in v16:
time: 31.8 us; the launch traced here: 31.6 us
  blocking collectives  24.8 us (78%)
  Pallas kernels  4.25 us (13%)
  waiting for transfers between devices  0.99 us (3%)
  local copies, waits for them, and re-layouts  0.96 us (3%)
  starting transfers between devices  0.52 us (2%)
    all_to_all x2, blocking collectives, exchange(): lax.all_to_all(value, 'mem', split_axis=0, concat_axis=0, axis_index_grou...  24.8 us
    pallas_call x5, Pallas kernels, call(): pl.pallas_call(kernel, out_shape=out_shape, in_specs=[pl.BlockSpec(memory...  4.25 us
    ppermute x2, waiting for transfers between devices, from_next(): lax.ppermute(value, 'rows', [((i + 1) % count, i) for i in range(count)])  0.99 us
    unnamed x7, local copies, waits for them, and re-layouts  0.96 us
  transfers between devices with their start and end apart: 2, of which 1 were waited for; matrix products, arithmetic and copies ran while one was open for 3% of the time, Pallas kernels for 2%

profile of v16, /device:TPU:0, one launch (start us, length us, event | category | flops | bytes accessed | tf_op | source)
XLA Modules:
  0.0 31.6 jit_solution(18169999852710601735)
XLA Ops:
  0.0 0.0 copy-start.2
  0.0 0.0 copy-start.1
  0.0 0.0 copy-start
  0.0 0.5 %collective-permute-start = (f32[16,2,8,128]{3,2,1,0:T(8,128)}, f32[16,2,8,128]{3,2,1,0:T(8,128)S(1)}, u32[]{:S(2)}, u32[]{:S(2)}) collective-permute-start(f32[16,2,8,128]{3,2,1,0:T(8,128)} %param.4), channel_id=1, source_target_pairs={{1,0},{0,1},{3,2},{2,3},{5,4},{4,5},{7,6},{6,7},{9,8},{8,9},{11,10... | collective-permute-start | bytes 393224 | tf_op jit(solution)/shard_map/ppermute | solution.py:325
  0.5 0.9 %copy.5 = f32[16,2,8,128]{3,0,2,1:T(8,128)S(1)} copy(f32[16,2,8,128]{3,2,1,0:T(8,128)} %param.4) | data formatting | bytes 262144 | tf_op args[0]
  1.5 0.0 copy-done.2
  1.5 0.0 copy-done.1
  1.5 0.0 copy-done
  1.5 0.2 inner_rows.1
  1.8 0.0 collective-permute-done
  1.8 0.7 %forecast_pack.1 = bf16[16,40,128]{2,1,0:T(8,128)(2,1)S(1)} custom-call(f32[16,16,128]{2,1,0:T(8,128)S(1)} %bitcast.7, f32[24,16,128]{2,1,0:T(8,128)S(1)} %get-tuple-element.10.inner_ref, f32[8,128]{1,0:T(8,128)S(1)} %get-tuple-element.11.obs_ref, f32[256,128]{1,0:T(8,128)S(1)} %bitcast.8), custom_call_target="tpu_custom_call" | custom-call | bytes 626688 | tf_op jit(solution)/shard_map/forecast_pack/pallas_call | solution.py:361
  2.5 14.1 %all_to_all.10.own_ref = bf16[16,40,128]{2,1,0:T(8,128)(2,1)S(1)} all-to-all(bf16[16,40,128]{2,1,0:T(8,128)(2,1)S(1)} %forecast_pack.1), channel_id=1, replica_groups={{30,14,22,6,28,12,20,4,26,10,18,2,24,8,16,0},{31,15,23,7,29,13,21,5,27,..., dimensions={0} | all-to-all | bytes 327680 | tf_op jit(solution)/shard_map/all_to_all | solution.py:355
  16.6 0.0 collective-permute-start.1
  16.7 0.4 %own_half.1 = (bf16[256,128]{1,0:T(8,128)(2,1)S(1)}, f32[272,512]{1,0:T(8,128)S(1)}, f32[8,128]{1,0:T(8,128)S(1)}) custom-call(s32[1]{0:T(128)} %bitcast.me_ref, bf16[16,40,128]{2,1,0:T(8,128)(2,1)S(1)} %all_to_all.10.own_ref), custom_call_target="tpu_custom_call" | custom-call | flops 33554432 | bytes 790532 | tf_op jit(solution)/shard_map/own_half/pallas_call | solution.py:361
  17.1 1.0 %collective-permute-done.1.near_ref = bf16[16,40,128]{2,1,0:T(8,128)(2,1)S(1)} collective-permute-done((bf16[16,40,128]{2,1,0:T(8,128)(2,1)S(1)}, bf16[16,40,128]{2,1,0:T(8,128)(2,1)S(1)}, u32[]{:S(2)}, u32[]{:S(2)}) %collective-permute-start.1) | collective-permute-done | bytes 163872 | tf_op jit(solution)/shard_map/ppermute | solution.py:325
  18.0 1.5 %analysis.1 = bf16[16,32,128]{2,1,0:T(8,128)(2,1)S(1)} custom-call(s32[1]{0:T(128)} %bitcast.me_ref, bf16[16,40,128]{2,1,0:T(8,128)(2,1)S(1)} %collective-permute-done.1.near_ref, bf16[256,128]{1,0:T(8,128)(2,1)S(1)} %get-tuple-element.12.inner_ref, f32[272,512]{1,0:T(8,128)S(1)} %get-tuple-element.13.sums_ref, f32[8,128]{1,0:T(8,128)S(1)} %get-tuple-element.14.mean_ref), custom_call_target="tpu_custom_call" | custom-call | flops 268435456 | bytes 921604 | tf_op jit(solution)/shard_map/analysis/pallas_call | solution.py:361
  19.6 10.7 %all_to_all.11.in_ref = bf16[16,32,128]{2,1,0:T(8,128)(2,1)S(1)} all-to-all(bf16[16,32,128]{2,1,0:T(8,128)(2,1)S(1)} %analysis.1), channel_id=1, replica_groups={{30,14,22,6,28,12,20,4,26,10,18,2,24,8,16,0},{31,15,23,7,29,13,21,5,27,..., dimensions={0} | all-to-all | bytes 262144 | tf_op jit(solution)/shard_map/all_to_all | solution.py:355
  30.3 1.4 %unpack_forecast.1 = f32[256,128]{1,0:T(8,128)} custom-call(bf16[16,32,128]{2,1,0:T(8,128)(2,1)S(1)} %all_to_all.11.in_ref), custom_call_target="tpu_custom_call" | custom-call | bytes 262144 | tf_op jit(solution)/shard_map/unpack_forecast/pallas_call | solution.py:361
Async XLA Ops:
  0.0 1.5 %copy-start.2 = (s32[2,8,8]{2,1,0:T(8,128)S(1)}, s32[2,8,8]{2,1,0:T(8,128)}, u32[]{:S(2)}) copy-start(s32[2,8,8]{2,1,0:T(8,128)} %mask_ref.1) | copy-start | bytes 1540
  0.0 1.5 %copy-start.1 = (f32[2,8,8]{2,1,0:T(8,128)S(1)}, f32[2,8,8]{2,1,0:T(8,128)}, u32[]{:S(2)}) copy-start(f32[2,8,8]{2,1,0:T(8,128)} %inverse_ref.1) | copy-start | bytes 1540
  0.0 1.5 %copy-start = (f32[2,8,8]{2,1,0:T(8,128)S(1)}, f32[2,8,8]{2,1,0:T(8,128)}, u32[]{:S(2)}) copy-start(f32[2,8,8]{2,1,0:T(8,128)} %values_ref.1) | copy-start | bytes 1540
  0.0 1.7 %collective-permute-start = (f32[16,2,8,128]{3,2,1,0:T(8,128)}, f32[16,2,8,128]{3,2,1,0:T(8,128)S(1)}, u32[]{:S(2)}, u32[]{:S(2)}) collective-permute-start(f32[16,2,8,128]{3,2,1,0:T(8,128)} %param.4), channel_id=1, source_target_pairs={{1,0},{0,1},{3,2},{2,3},{5,4},{4,5},{7,6},{6,7},{9,8},{8,9},{11,10... | collective-permute-start | bytes 393224 | tf_op jit(solution)/shard_map/ppermute | solution.py:325
  16.6 1.4 %collective-permute-start.1 = (bf16[16,40,128]{2,1,0:T(8,128)(2,1)S(1)}, bf16[16,40,128]{2,1,0:T(8,128)(2,1)S(1)}, u32[]{:S(2)}, u32[]{:S(2)}) collective-permute-start(bf16[16,40,128]{2,1,0:T(8,128)(2,1)S(1)} %all_to_all.10.own_ref), channel_id=1, source_target_pairs={{1,0},{0,1},{3,2},{2,3},{5,4},{4,5},{7,6},{6,7},{9,8},{8,9},{11,10... | collective-permute-start | bytes 491528 | tf_op jit(solution)/shard_map/ppermute | solution.py:325

commit v17 on v10

--- a/solution.py
+++ b/solution.py
@@ -28,17 +28,29 @@
     return PLACES - 1 - (low * 4 + (high & 1) * 2 + (high >> 1))
 
 
-def forecast_rows(u_rows, v_rows):
-    for _ in range(FSTEPS):
-        new_u, new_v = [], []
+def advance(u_rows, v_rows, i):
+    cu, cv = CADV * u_rows[i], CADV * v_rows[i]
+    stepped = []
+    for rows in (u_rows, v_rows):
+        along_x = pltpu.roll(rows[i], WIDTH - 1, 1) - pltpu.roll(rows[i], 1, 1)
+        along_y = rows[i + 1] - rows[i - 1]
+        stepped.append(rows[i] - (cu * along_x + cv * along_y))
+    return stepped
+
+
+def forecast_rows(u_rows, v_rows, known=None):
+    for step in range(1, FSTEPS + 1):
+        stepped = []
         for i in range(1, len(u_rows) - 1):
-            cu, cv = CADV * u_rows[i], CADV * v_rows[i]
-            for rows, new in ((u_rows, new_u), (v_rows, new_v)):
-                along_x = pltpu.roll(rows[i], WIDTH - 1, 1) - pltpu.roll(rows[i], 1, 1)
-                along_y = rows[i + 1] - rows[i - 1]
-                new.append(rows[i] - (cu * along_x + cv * along_y))
-        u_rows, v_rows = new_u, new_v
+            row = i - 1 + step - FSTEPS
+            given = known(step, row) if known is not None and step <= row < BAND - step else None
+            stepped.append(given if given is not None else advance(u_rows, v_rows, i))
+        u_rows, v_rows = [u for u, _ in stepped], [v for _, v in stepped]
     return u_rows, v_rows
+
+
+def inner_steps():
+    return [(step, row) for step in range(1, FSTEPS) for row in range(step, BAND - step)]
 
 
 def swap_blocks(parts, size):
@@ -82,7 +94,33 @@
     return jnp.dot(gather, wide, preferred_element_type=F32)
 
 
-def pack_kernel(rows_ref, near_ref, values_ref, inverse_ref, mask_ref, out_ref):
+def advance_inner(u_rows, v_rows, out_ref):
+    kept = 0
+    for _ in range(1, FSTEPS):
+        stepped = [advance(u_rows, v_rows, i) for i in range(1, len(u_rows) - 1)]
+        u_rows, v_rows = [u for u, _ in stepped], [v for _, v in stepped]
+        for row in stepped:
+            for value in row:
+                out_ref[kept] = value
+                kept += 1
+
+
+def kept_rows(inner_ref):
+    places = inner_steps()
+
+    def known(step, row):
+        first = FIELDS * places.index((step, row))
+        return [inner_ref[first + field] for field in range(FIELDS)]
+
+    return known
+
+
+def inner_kernel(rows_ref, values_ref, inverse_ref, mask_ref, out_ref, obs_ref):
+    obs_ref[...] = observation_rows(values_ref, inverse_ref, mask_ref)
+    advance_inner(*([rows_ref[field * BAND + r] for r in range(BAND)] for field in range(FIELDS)), out_ref)
+
+
+def pack_kernel(rows_ref, inner_ref, obs_ref, near_ref, out_ref):
     points = FIELDS * BAND
 
     def near(field, index):
@@ -94,7 +132,7 @@
         own = [rows_ref[field * BAND + r] for r in range(BAND)]
         after = [near(field, r) for r in range(FSTEPS)]
         fields.append(before + own + after)
-    done = forecast_rows(*fields)
+    done = forecast_rows(*fields, kept_rows(inner_ref))
     half_rows = BAND // 2
     index = lax.broadcasted_iota(jnp.int32, (8, WIDTH), 0)
     values, means = [], [jnp.zeros((8, WIDTH), F32)] * (FIELDS * half_rows)
@@ -111,7 +149,7 @@
     wanted = ((lane // REGION) * PATCH + lane % REGION + (WIDTH - RADIUS)) % WIDTH
     widen = (column == wanted).astype(F32).astype(BF)
     wide = jnp.dot(rows, widen, preferred_element_type=F32)
-    obs = observation_rows(values_ref, inverse_ref, mask_ref)
+    obs = obs_ref[...]
     start = len(values) * LOCAL
     is_mean = index & 2 == 0
     means = []
@@ -256,22 +294,22 @@
     return [row.astype(F32) for row in swap_blocks([ref[position(p)] for p in range(ref.shape[0])], PATCH)]
 
 
-def unpack_kernel(in_ref, out_ref):
-    for i, row in enumerate(unpacked(in_ref)):
-        out_ref[i] = row
-
-
-def forecast_kernel(own_ref, near_ref, out_ref):
-    def by_field(rows):
-        half = BAND // 2
-        return [
-            [rows[h * FIELDS * half + field * half + r] for h in range(2) for r in range(half)]
-            for field in range(FIELDS)
-        ]
-
+def by_field(rows):
+    half = BAND // 2
+    return [[rows[h * FIELDS * half + field * half + r] for h in range(2) for r in range(half)] for field in range(FIELDS)]
+
+
+def unpack_kernel(in_ref, rows_ref, inner_ref):
+    rows = unpacked(in_ref)
+    for i, row in enumerate(rows):
+        rows_ref[i] = row
+    advance_inner(*by_field(rows), inner_ref)
+
+
+def forecast_kernel(own_ref, inner_ref, near_ref, out_ref):
     own, near = by_field(own_ref), by_field(unpacked(near_ref))
     fields = [n[BAND - FSTEPS :] + o + n[:FSTEPS] for o, n in zip(own, near)]
-    done = forecast_rows(*fields)
+    done = forecast_rows(*fields, kept_rows(inner_ref))
     for field in range(FIELDS):
         for r in range(BAND):
             out_ref[pl.ds(field * BAND + r, LOCAL, stride=FIELDS * BAND), :] = done[field][r]
@@ -337,8 +375,11 @@
     rows = jnp.transpose(sample_collection.reshape(LOCAL, FIELDS * BAND, WIDTH), (1, 0, 2))
     region_shape = jax.ShapeDtypeStruct((count, 2 * LOCAL + 8, WIDTH), BF)
     inner_shape = jax.ShapeDtypeStruct((count, LOCAL, WIDTH), BF)
-    observations = (obs_values, obs_inverse_variance, obs_mask)
-    region = exchange(call(pack_kernel, "forecast_pack", region_shape, rows, near.reshape(-1, WIDTH), *observations))
+    rows_shape = jax.ShapeDtypeStruct((FIELDS * BAND, LOCAL, WIDTH), F32)
+    kept_shape = jax.ShapeDtypeStruct((FIELDS * len(inner_steps()), LOCAL, WIDTH), F32)
+    first = [kept_shape, jax.ShapeDtypeStruct((8, WIDTH), F32)]
+    kept = call(inner_kernel, "inner_rows", first, rows, obs_values, obs_inverse_variance, obs_mask)
+    region = exchange(call(pack_kernel, "forecast_pack", region_shape, rows, *kept, near.reshape(-1, WIDTH)))
     members, points = count * LOCAL, 2 * WIDTH
     own_shapes = [
         jax.ShapeDtypeStruct((members, WIDTH), BF),
@@ -350,10 +391,9 @@
     own = call(own_kernel, "own_half", own_shapes, me, region, flops=flops)
     inner = exchange(call(analysis_kernel, "analysis", inner_shape, me, region_near, *own, flops=8 * flops))
     inner_near = near_rows(inner, join_inner)
-    rows_shape = jax.ShapeDtypeStruct((FIELDS * BAND, LOCAL, WIDTH), F32)
-    inner = call(unpack_kernel, "unpack_own", rows_shape, inner)
+    own_rows = call(unpack_kernel, "unpack_own", [rows_shape, kept_shape], inner)
     out_shape = jax.ShapeDtypeStruct((LOCAL * FIELDS * BAND, WIDTH), F32)
-    cycled = call(forecast_kernel, "unpack_forecast", out_shape, inner, inner_near)
+    cycled = call(forecast_kernel, "unpack_forecast", out_shape, *own_rows, inner_near)
     return cycled.reshape(shape)
 
 

time: 31.7 us -> 31.7 us (level)
  waiting for transfers between devices: 2.19 us -> 1.76 us
  Pallas kernels: 4.08 us -> 4.41 us
    ppermute x3, waiting for transfers between devices: 2.19 us -> 1.76 us  [from_next(): lax.ppermute(value, 'rows', [((i + 1) % count, i) for i in range(count)])]
    pallas_call x5 -> x6, Pallas kernels: 4.08 us -> 4.41 us  [call(): pl.pallas_call(kernel, out_shape=out_shape, in_specs=[pl.BlockSpec(memory...]
  transfers between devices with their start and end apart: 3 -> 3, of which waited for: 3 -> 2; matrix products, arithmetic and copies ran while one was open for 3% -> 3% of each run, Pallas kernels for 2% -> 4%
where the time goes in v17:
time: 31.7 us; the launch traced here: 31.5 us
  blocking collectives  23.7 us (75%)
  Pallas kernels  4.41 us (14%)
  waiting for transfers between devices  1.76 us (6%)
  local copies, waits for them, and re-layouts  0.96 us (3%)
  starting transfers between devices  0.53 us (2%)
    all_to_all x2, blocking collectives, exchange(): lax.all_to_all(value, ('mem', 'rows'), split_axis=0, concat_axis=0, axis_...  23.7 us
    pallas_call x6, Pallas kernels, call(): pl.pallas_call(kernel, out_shape=out_shape, in_specs=[pl.BlockSpec(memory...  4.41 us
    ppermute x3, waiting for transfers between devices, from_next(): lax.ppermute(value, 'rows', [((i + 1) % count, i) for i in range(count)])  1.76 us
    unnamed x7, local copies, waits for them, and re-layouts  0.96 us
  transfers between devices with their start and end apart: 3, of which 2 were waited for; matrix products, arithmetic and copies ran while one was open for 3% of the time, Pallas kernels for 4%

profile of v17, /device:TPU:0, one launch (start us, length us, event | category | flops | bytes accessed | tf_op | source)
XLA Modules:
  0.0 31.5 jit_solution(16180566245028058225)
XLA Ops:
  0.0 0.0 copy-start.2
  0.0 0.0 copy-start.1
  0.0 0.0 copy-start
  0.0 0.5 %collective-permute-start = (f32[16,2,8,128]{3,2,1,0:T(8,128)}, f32[16,2,8,128]{3,2,1,0:T(8,128)S(1)}, u32[]{:S(2)}, u32[]{:S(2)}) collective-permute-start(f32[16,2,8,128]{3,2,1,0:T(8,128)} %param.4), channel_id=1, source_target_pairs={{1,0},{0,1},{3,2},{2,3},{5,4},{4,5},{7,6},{6,7},{9,8},{8,9},{11,10... | collective-permute-start | bytes 393224 | tf_op jit(solution)/shard_map/ppermute | solution.py:320
  0.5 0.9 %copy.5 = f32[16,2,8,128]{3,0,2,1:T(8,128)S(1)} copy(f32[16,2,8,128]{3,2,1,0:T(8,128)} %param.4) | data formatting | bytes 262144 | tf_op args[0]
  1.5 0.0 copy-done.2
  1.5 0.0 copy-done.1
  1.5 0.0 copy-done
  1.5 0.2 inner_rows.1
  1.8 0.0 collective-permute-done
  1.8 0.7 %forecast_pack.1 = bf16[16,40,128]{2,1,0:T(8,128)(2,1)S(1)} custom-call(f32[16,16,128]{2,1,0:T(8,128)S(1)} %bitcast.7, f32[24,16,128]{2,1,0:T(8,128)S(1)} %get-tuple-element.12.inner_ref, f32[8,128]{1,0:T(8,128)S(1)} %get-tuple-element.13.obs_ref, f32[256,128]{1,0:T(8,128)S(1)} %bitcast.8), custom_call_target="tpu_custom_call" | custom-call | bytes 626688 | tf_op jit(solution)/shard_map/forecast_pack/pallas_call | solution.py:358
  2.5 14.1 %all_to_all.10.own_ref = bf16[16,40,128]{2,1,0:T(8,128)(2,1)S(1)} all-to-all(bf16[16,40,128]{2,1,0:T(8,128)(2,1)S(1)} %forecast_pack.1), channel_id=1, replica_groups={{31,15,23,7,29,13,21,5,27,11,19,3,25,9,17,1},{30,14,22,6,28,12,20,4,26,..., dimensions={0} | all-to-all | bytes 327680 | tf_op jit(solution)/shard_map/all_to_all | solution.py:352
  16.6 0.0 collective-permute-start.1
  16.7 0.3 %own_half.1 = (bf16[256,128]{1,0:T(8,128)(2,1)S(1)}, f32[272,256]{1,0:T(8,128)S(1)}, f32[8,128]{1,0:T(8,128)S(1)}) custom-call(s32[1]{0:T(128)} %bitcast.me_ref, bf16[16,40,128]{2,1,0:T(8,128)(2,1)S(1)} %all_to_all.10.own_ref), custom_call_target="tpu_custom_call" | custom-call | flops 33554432 | bytes 512004 | tf_op jit(solution)/shard_map/own_half/pallas_call | solution.py:358
  17.0 1.1 %collective-permute-done.1.near_ref = bf16[16,40,128]{2,1,0:T(8,128)(2,1)S(1)} collective-permute-done((bf16[16,40,128]{2,1,0:T(8,128)(2,1)S(1)}, bf16[16,40,128]{2,1,0:T(8,128)(2,1)S(1)}, u32[]{:S(2)}, u32[]{:S(2)}) %collective-permute-start.1) | collective-permute-done | bytes 163872 | tf_op jit(solution)/shard_map/ppermute | solution.py:320
  18.0 1.3 %analysis.1 = bf16[16,16,128]{2,1,0:T(8,128)(2,1)S(1)} custom-call(s32[1]{0:T(128)} %bitcast.me_ref, bf16[16,40,128]{2,1,0:T(8,128)(2,1)S(1)} %collective-permute-done.1.near_ref, bf16[256,128]{1,0:T(8,128)(2,1)S(1)} %get-tuple-element.14.inner_ref, f32[272,256]{1,0:T(8,128)S(1)} %get-tuple-element.15.sums_ref, f32[8,128]{1,0:T(8,128)S(1)} %get-tuple-element.16.mean_ref), custom_call_target="tpu_custom_call" | custom-call | flops 268435456 | bytes 577540 | tf_op jit(solution)/shard_map/analysis/pallas_call | solution.py:358
  19.4 9.6 %all_to_all.11.in_ref = bf16[16,16,128]{2,1,0:T(8,128)(2,1)S(1)} all-to-all(bf16[16,16,128]{2,1,0:T(8,128)(2,1)S(1)} %analysis.1), channel_id=1, replica_groups={{31,15,23,7,29,13,21,5,27,11,19,3,25,9,17,1},{30,14,22,6,28,12,20,4,26,..., dimensions={0} | all-to-all | bytes 131072 | tf_op jit(solution)/shard_map/all_to_all | solution.py:352
  29.0 0.0 collective-permute-start.2
  29.0 0.5 %unpack_own.1 = (f32[16,16,128]{2,1,0:T(8,128)S(1)}, f32[24,16,128]{2,1,0:T(8,128)S(1)}) custom-call(bf16[16,16,128]{2,1,0:T(8,128)(2,1)S(1)} %all_to_all.11.in_ref), custom_call_target="tpu_custom_call" | custom-call | bytes 393216 | tf_op jit(solution)/shard_map/unpack_own/pallas_call | solution.py:358
  29.5 0.7 %collective-permute-done.2.near_ref = bf16[16,16,128]{2,1,0:T(8,128)(2,1)S(1)} collective-permute-done((bf16[16,16,128]{2,1,0:T(8,128)(2,1)S(1)}, bf16[16,16,128]{2,1,0:T(8,128)(2,1)S(1)}, u32[]{:S(2)}, u32[]{:S(2)}) %collective-permute-start.2) | collective-permute-done | bytes 65568 | tf_op jit(solution)/shard_map/ppermute | solution.py:320
  30.2 1.2 %unpack_forecast.1 = f32[256,128]{1,0:T(8,128)} custom-call(f32[16,16,128]{2,1,0:T(8,128)S(1)} %get-tuple-element.17.own_ref, f32[24,16,128]{2,1,0:T(8,128)S(1)} %get-tuple-element.18.inner_ref, bf16[16,16,128]{2,1,0:T(8,128)(2,1)S(1)} %collective-permute-done.2.near_ref), custom_call_target="tpu_custom_call" | custom-call | bytes 524288 | tf_op jit(solution)/shard_map/unpack_forecast/pallas_call | solution.py:358
Async XLA Ops:
  0.0 1.5 %copy-start.2 = (s32[2,8,8]{2,1,0:T(8,128)S(1)}, s32[2,8,8]{2,1,0:T(8,128)}, u32[]{:S(2)}) copy-start(s32[2,8,8]{2,1,0:T(8,128)} %mask_ref.1) | copy-start | bytes 1540
  0.0 1.5 %copy-start.1 = (f32[2,8,8]{2,1,0:T(8,128)S(1)}, f32[2,8,8]{2,1,0:T(8,128)}, u32[]{:S(2)}) copy-start(f32[2,8,8]{2,1,0:T(8,128)} %inverse_ref.1) | copy-start | bytes 1540
  0.0 1.5 %copy-start = (f32[2,8,8]{2,1,0:T(8,128)S(1)}, f32[2,8,8]{2,1,0:T(8,128)}, u32[]{:S(2)}) copy-start(f32[2,8,8]{2,1,0:T(8,128)} %values_ref.1) | copy-start | bytes 1540
  0.0 1.7 %collective-permute-start = (f32[16,2,8,128]{3,2,1,0:T(8,128)}, f32[16,2,8,128]{3,2,1,0:T(8,128)S(1)}, u32[]{:S(2)}, u32[]{:S(2)}) collective-permute-start(f32[16,2,8,128]{3,2,1,0:T(8,128)} %param.4), channel_id=1, source_target_pairs={{1,0},{0,1},{3,2},{2,3},{5,4},{4,5},{7,6},{6,7},{9,8},{8,9},{11,10... | collective-permute-start | bytes 393224 | tf_op jit(solution)/shard_map/ppermute | solution.py:320
  16.6 1.4 %collective-permute-start.1 = (bf16[16,40,128]{2,1,0:T(8,128)(2,1)S(1)}, bf16[16,40,128]{2,1,0:T(8,128)(2,1)S(1)}, u32[]{:S(2)}, u32[]{:S(2)}) collective-permute-start(bf16[16,40,128]{2,1,0:T(8,128)(2,1)S(1)} %all_to_all.10.own_ref), channel_id=1, source_target_pairs={{1,0},{0,1},{3,2},{2,3},{5,4},{4,5},{7,6},{6,7},{9,8},{8,9},{11,10... | collective-permute-start | bytes 491528 | tf_op jit(solution)/shard_map/ppermute | solution.py:320
  29.0 1.3 %collective-permute-start.2 = (bf16[16,16,128]{2,1,0:T(8,128)(2,1)S(1)}, bf16[16,16,128]{2,1,0:T(8,128)(2,1)S(1)}, u32[]{:S(2)}, u32[]{:S(2)}) collective-permute-start(bf16[16,16,128]{2,1,0:T(8,128)(2,1)S(1)} %all_to_all.11.in_ref), channel_id=1, source_target_pairs={{1,0},{0,1},{3,2},{2,3},{5,4},{4,5},{7,6},{6,7},{9,8},{8,9},{11,10... | collective-permute-start | bytes 196616 | tf_op jit(solution)/shard_map/ppermute | solution.py:320

commit v18 on v17

--- a/solution.py
+++ b/solution.py
@@ -23,9 +23,13 @@
 F32 = jnp.float32
 
 
+ORDER = (15, 7, 3, 10, 14, 6, 2, 9, 13, 5, 1, 8, 12, 4, 0, 11)
+
+
 def position(place):
-    low, high = place & 3, place >> 2
-    return PLACES - 1 - (low * 4 + (high & 1) * 2 + (high >> 1))
+    if isinstance(place, int):
+        return ORDER.index(place)
+    return functools.reduce(lambda kept, k: jnp.where(place == ORDER[k], k, kept), range(1, PLACES), 0)
 
 
 def advance(u_rows, v_rows, i):
@@ -346,10 +350,7 @@
 
 
 def exchange(value):
-    bands = lax.axis_size("rows")
-    places = sorted(range(lax.axis_size("mem")), key=position)
-    groups = [[place * bands + band for place in places] for band in reversed(range(bands))]
-    return lax.all_to_all(value, ("mem", "rows"), split_axis=0, concat_axis=0, axis_index_groups=groups, tiled=True)
+    return lax.all_to_all(value, "mem", split_axis=0, concat_axis=0, axis_index_groups=[list(ORDER)], tiled=True)
 
 
 def call(kernel, name, out_shape, *args, flops=0):

time: 31.7 us -> 31.8 us (level)
  no operation moved by 1% of the time
where the time goes in v18:
time: 31.8 us; the launch traced here: 31.6 us
  blocking collectives  23.8 us (75%)
  Pallas kernels  4.44 us (14%)
  waiting for transfers between devices  1.75 us (6%)
  local copies, waits for them, and re-layouts  0.96 us (3%)
  starting transfers between devices  0.53 us (2%)
    all_to_all x2, blocking collectives, exchange(): lax.all_to_all(value, 'mem', split_axis=0, concat_axis=0, axis_index_grou...  23.8 us
    pallas_call x6, Pallas kernels, call(): pl.pallas_call(kernel, out_shape=out_shape, in_specs=[pl.BlockSpec(memory...  4.44 us
    ppermute x3, waiting for transfers between devices, from_next(): lax.ppermute(value, 'rows', [((i + 1) % count, i) for i in range(count)])  1.75 us
    unnamed x7, local copies, waits for them, and re-layouts  0.96 us
  transfers between devices with their start and end apart: 3, of which 2 were waited for; matrix products, arithmetic and copies ran while one was open for 3% of the time, Pallas kernels for 4%

profile of v18, /device:TPU:0, one launch (start us, length us, event | category | flops | bytes accessed | tf_op | source)
XLA Modules:
  0.0 31.6 jit_solution(7956751178219778827)
XLA Ops:
  0.0 0.0 copy-start.2
  0.0 0.0 copy-start.1
  0.0 0.0 copy-start
  0.0 0.5 %collective-permute-start = (f32[16,2,8,128]{3,2,1,0:T(8,128)}, f32[16,2,8,128]{3,2,1,0:T(8,128)S(1)}, u32[]{:S(2)}, u32[]{:S(2)}) collective-permute-start(f32[16,2,8,128]{3,2,1,0:T(8,128)} %param.4), channel_id=1, source_target_pairs={{1,0},{0,1},{3,2},{2,3},{5,4},{4,5},{7,6},{6,7},{9,8},{8,9},{11,10... | collective-permute-start | bytes 393224 | tf_op jit(solution)/shard_map/ppermute | solution.py:324
  0.5 0.9 %copy.5 = f32[16,2,8,128]{3,0,2,1:T(8,128)S(1)} copy(f32[16,2,8,128]{3,2,1,0:T(8,128)} %param.4) | data formatting | bytes 262144 | tf_op args[0]
  1.5 0.0 copy-done.2
  1.5 0.0 copy-done.1
  1.5 0.0 copy-done
  1.5 0.2 inner_rows.1
  1.8 0.0 collective-permute-done
  1.8 0.7 %forecast_pack.1 = bf16[16,40,128]{2,1,0:T(8,128)(2,1)S(1)} custom-call(f32[16,16,128]{2,1,0:T(8,128)S(1)} %bitcast.7, f32[24,16,128]{2,1,0:T(8,128)S(1)} %get-tuple-element.12.inner_ref, f32[8,128]{1,0:T(8,128)S(1)} %get-tuple-element.13.obs_ref, f32[256,128]{1,0:T(8,128)S(1)} %bitcast.8), custom_call_target="tpu_custom_call" | custom-call | bytes 626688 | tf_op jit(solution)/shard_map/forecast_pack/pallas_call | solution.py:359
  2.5 14.0 %all_to_all.10.own_ref = bf16[16,40,128]{2,1,0:T(8,128)(2,1)S(1)} all-to-all(bf16[16,40,128]{2,1,0:T(8,128)(2,1)S(1)} %forecast_pack.1), channel_id=1, replica_groups={{30,14,6,20,28,12,4,18,26,10,2,16,24,8,0,22},{31,15,7,21,29,13,5,19,27,..., dimensions={0} | all-to-all | bytes 327680 | tf_op jit(solution)/shard_map/all_to_all | solution.py:353
  16.6 0.0 collective-permute-start.1
  16.6 0.3 %own_half.1 = (bf16[256,128]{1,0:T(8,128)(2,1)S(1)}, f32[272,256]{1,0:T(8,128)S(1)}, f32[8,128]{1,0:T(8,128)S(1)}) custom-call(s32[1]{0:T(128)} %bitcast.me_ref, bf16[16,40,128]{2,1,0:T(8,128)(2,1)S(1)} %all_to_all.10.own_ref), custom_call_target="tpu_custom_call" | custom-call | flops 33554432 | bytes 512004 | tf_op jit(solution)/shard_map/own_half/pallas_call | solution.py:359
  16.9 1.0 %collective-permute-done.1.near_ref = bf16[16,40,128]{2,1,0:T(8,128)(2,1)S(1)} collective-permute-done((bf16[16,40,128]{2,1,0:T(8,128)(2,1)S(1)}, bf16[16,40,128]{2,1,0:T(8,128)(2,1)S(1)}, u32[]{:S(2)}, u32[]{:S(2)}) %collective-permute-start.1) | collective-permute-done | bytes 163872 | tf_op jit(solution)/shard_map/ppermute | solution.py:324
  17.9 1.3 %analysis.1 = bf16[16,16,128]{2,1,0:T(8,128)(2,1)S(1)} custom-call(s32[1]{0:T(128)} %bitcast.me_ref, bf16[16,40,128]{2,1,0:T(8,128)(2,1)S(1)} %collective-permute-done.1.near_ref, bf16[256,128]{1,0:T(8,128)(2,1)S(1)} %get-tuple-element.14.inner_ref, f32[272,256]{1,0:T(8,128)S(1)} %get-tuple-element.15.sums_ref, f32[8,128]{1,0:T(8,128)S(1)} %get-tuple-element.16.mean_ref), custom_call_target="tpu_custom_call" | custom-call | flops 268435456 | bytes 577540 | tf_op jit(solution)/shard_map/analysis/pallas_call | solution.py:359
  19.3 9.8 %all_to_all.11.in_ref = bf16[16,16,128]{2,1,0:T(8,128)(2,1)S(1)} all-to-all(bf16[16,16,128]{2,1,0:T(8,128)(2,1)S(1)} %analysis.1), channel_id=1, replica_groups={{30,14,6,20,28,12,4,18,26,10,2,16,24,8,0,22},{31,15,7,21,29,13,5,19,27,..., dimensions={0} | all-to-all | bytes 131072 | tf_op jit(solution)/shard_map/all_to_all | solution.py:353
  29.1 0.0 collective-permute-start.2
  29.1 0.5 %unpack_own.1 = (f32[16,16,128]{2,1,0:T(8,128)S(1)}, f32[24,16,128]{2,1,0:T(8,128)S(1)}) custom-call(bf16[16,16,128]{2,1,0:T(8,128)(2,1)S(1)} %all_to_all.11.in_ref), custom_call_target="tpu_custom_call" | custom-call | bytes 393216 | tf_op jit(solution)/shard_map/unpack_own/pallas_call | solution.py:359
  29.6 0.7 %collective-permute-done.2.near_ref = bf16[16,16,128]{2,1,0:T(8,128)(2,1)S(1)} collective-permute-done((bf16[16,16,128]{2,1,0:T(8,128)(2,1)S(1)}, bf16[16,16,128]{2,1,0:T(8,128)(2,1)S(1)}, u32[]{:S(2)}, u32[]{:S(2)}) %collective-permute-start.2) | collective-permute-done | bytes 65568 | tf_op jit(solution)/shard_map/ppermute | solution.py:324
  30.4 1.2 %unpack_forecast.1 = f32[256,128]{1,0:T(8,128)} custom-call(f32[16,16,128]{2,1,0:T(8,128)S(1)} %get-tuple-element.17.own_ref, f32[24,16,128]{2,1,0:T(8,128)S(1)} %get-tuple-element.18.inner_ref, bf16[16,16,128]{2,1,0:T(8,128)(2,1)S(1)} %collective-permute-done.2.near_ref), custom_call_target="tpu_custom_call" | custom-call | bytes 524288 | tf_op jit(solution)/shard_map/unpack_forecast/pallas_call | solution.py:359
Async XLA Ops:
  0.0 1.5 %copy-start.2 = (s32[2,8,8]{2,1,0:T(8,128)S(1)}, s32[2,8,8]{2,1,0:T(8,128)}, u32[]{:S(2)}) copy-start(s32[2,8,8]{2,1,0:T(8,128)} %mask_ref.1) | copy-start | bytes 1540
  0.0 1.5 %copy-start.1 = (f32[2,8,8]{2,1,0:T(8,128)S(1)}, f32[2,8,8]{2,1,0:T(8,128)}, u32[]{:S(2)}) copy-start(f32[2,8,8]{2,1,0:T(8,128)} %inverse_ref.1) | copy-start | bytes 1540
  0.0 1.5 %copy-start = (f32[2,8,8]{2,1,0:T(8,128)S(1)}, f32[2,8,8]{2,1,0:T(8,128)}, u32[]{:S(2)}) copy-start(f32[2,8,8]{2,1,0:T(8,128)} %values_ref.1) | copy-start | bytes 1540
  0.0 1.7 %collective-permute-start = (f32[16,2,8,128]{3,2,1,0:T(8,128)}, f32[16,2,8,128]{3,2,1,0:T(8,128)S(1)}, u32[]{:S(2)}, u32[]{:S(2)}) collective-permute-start(f32[16,2,8,128]{3,2,1,0:T(8,128)} %param.4), channel_id=1, source_target_pairs={{1,0},{0,1},{3,2},{2,3},{5,4},{4,5},{7,6},{6,7},{9,8},{8,9},{11,10... | collective-permute-start | bytes 393224 | tf_op jit(solution)/shard_map/ppermute | solution.py:324
  16.6 1.4 %collective-permute-start.1 = (bf16[16,40,128]{2,1,0:T(8,128)(2,1)S(1)}, bf16[16,40,128]{2,1,0:T(8,128)(2,1)S(1)}, u32[]{:S(2)}, u32[]{:S(2)}) collective-permute-start(bf16[16,40,128]{2,1,0:T(8,128)(2,1)S(1)} %all_to_all.10.own_ref), channel_id=1, source_target_pairs={{1,0},{0,1},{3,2},{2,3},{5,4},{4,5},{7,6},{6,7},{9,8},{8,9},{11,10... | collective-permute-start | bytes 491528 | tf_op jit(solution)/shard_map/ppermute | solution.py:324
  29.1 1.3 %collective-permute-start.2 = (bf16[16,16,128]{2,1,0:T(8,128)(2,1)S(1)}, bf16[16,16,128]{2,1,0:T(8,128)(2,1)S(1)}, u32[]{:S(2)}, u32[]{:S(2)}) collective-permute-start(bf16[16,16,128]{2,1,0:T(8,128)(2,1)S(1)} %all_to_all.11.in_ref), channel_id=1, source_target_pairs={{1,0},{0,1},{3,2},{2,3},{5,4},{4,5},{7,6},{6,7},{9,8},{8,9},{11,10... | collective-permute-start | bytes 196616 | tf_op jit(solution)/shard_map/ppermute | solution.py:324

commit v19 on v18

--- a/solution.py
+++ b/solution.py
@@ -23,7 +23,7 @@
 F32 = jnp.float32
 
 
-ORDER = (15, 7, 3, 10, 14, 6, 2, 9, 13, 5, 1, 8, 12, 4, 0, 11)
+ORDER = (15, 11, 7, 3, 14, 10, 6, 2, 13, 9, 5, 1, 12, 8, 4, 0)
 
 
 def position(place):

time: 31.8 us -> 32 us (level)
  no operation moved by 1% of the time
where the time goes in v19:
time: 32 us; the launch traced here: 31.8 us
  blocking collectives  24 us (75%)
  Pallas kernels  4.44 us (14%)
  waiting for transfers between devices  1.75 us (5%)
  local copies, waits for them, and re-layouts  0.96 us (3%)
  starting transfers between devices  0.53 us (2%)
    all_to_all x2, blocking collectives, exchange(): lax.all_to_all(value, 'mem', split_axis=0, concat_axis=0, axis_index_grou...  24 us
    pallas_call x6, Pallas kernels, call(): pl.pallas_call(kernel, out_shape=out_shape, in_specs=[pl.BlockSpec(memory...  4.44 us
    ppermute x3, waiting for transfers between devices, from_next(): lax.ppermute(value, 'rows', [((i + 1) % count, i) for i in range(count)])  1.75 us
    unnamed x7, local copies, waits for them, and re-layouts  0.96 us
  transfers between devices with their start and end apart: 3, of which 2 were waited for; matrix products, arithmetic and copies ran while one was open for 3% of the time, Pallas kernels for 4%

profile of v19, /device:TPU:0, one launch (start us, length us, event | category | flops | bytes accessed | tf_op | source)
XLA Modules:
  0.0 31.8 jit_solution(15237495981720692573)
XLA Ops:
  0.0 0.0 copy-start.2
  0.0 0.0 copy-start.1
  0.0 0.0 copy-start
  0.0 0.5 %collective-permute-start = (f32[16,2,8,128]{3,2,1,0:T(8,128)}, f32[16,2,8,128]{3,2,1,0:T(8,128)S(1)}, u32[]{:S(2)}, u32[]{:S(2)}) collective-permute-start(f32[16,2,8,128]{3,2,1,0:T(8,128)} %param.4), channel_id=1, source_target_pairs={{1,0},{0,1},{3,2},{2,3},{5,4},{4,5},{7,6},{6,7},{9,8},{8,9},{11,10... | collective-permute-start | bytes 393224 | tf_op jit(solution)/shard_map/ppermute | solution.py:324
  0.5 0.9 %copy.5 = f32[16,2,8,128]{3,0,2,1:T(8,128)S(1)} copy(f32[16,2,8,128]{3,2,1,0:T(8,128)} %param.4) | data formatting | bytes 262144 | tf_op args[0]
  1.5 0.0 copy-done.2
  1.5 0.0 copy-done.1
  1.5 0.0 copy-done
  1.5 0.2 inner_rows.1
  1.8 0.0 collective-permute-done
  1.8 0.7 %forecast_pack.1 = bf16[16,40,128]{2,1,0:T(8,128)(2,1)S(1)} custom-call(f32[16,16,128]{2,1,0:T(8,128)S(1)} %bitcast.7, f32[24,16,128]{2,1,0:T(8,128)S(1)} %get-tuple-element.12.inner_ref, f32[8,128]{1,0:T(8,128)S(1)} %get-tuple-element.13.obs_ref, f32[256,128]{1,0:T(8,128)S(1)} %bitcast.8), custom_call_target="tpu_custom_call" | custom-call | bytes 626688 | tf_op jit(solution)/shard_map/forecast_pack/pallas_call | solution.py:359
  2.5 14.3 %all_to_all.10.own_ref = bf16[16,40,128]{2,1,0:T(8,128)(2,1)S(1)} all-to-all(bf16[16,40,128]{2,1,0:T(8,128)(2,1)S(1)} %forecast_pack.1), channel_id=1, replica_groups={{30,22,14,6,28,20,12,4,26,18,10,2,24,16,8,0},{31,23,15,7,29,21,13,5,27,..., dimensions={0} | all-to-all | bytes 327680 | tf_op jit(solution)/shard_map/all_to_all | solution.py:353
  16.8 0.0 collective-permute-start.1
  16.8 0.4 %own_half.1 = (bf16[256,128]{1,0:T(8,128)(2,1)S(1)}, f32[272,256]{1,0:T(8,128)S(1)}, f32[8,128]{1,0:T(8,128)S(1)}) custom-call(s32[1]{0:T(128)} %bitcast.me_ref, bf16[16,40,128]{2,1,0:T(8,128)(2,1)S(1)} %all_to_all.10.own_ref), custom_call_target="tpu_custom_call" | custom-call | flops 33554432 | bytes 512004 | tf_op jit(solution)/shard_map/own_half/pallas_call | solution.py:359
  17.2 1.0 %collective-permute-done.1.near_ref = bf16[16,40,128]{2,1,0:T(8,128)(2,1)S(1)} collective-permute-done((bf16[16,40,128]{2,1,0:T(8,128)(2,1)S(1)}, bf16[16,40,128]{2,1,0:T(8,128)(2,1)S(1)}, u32[]{:S(2)}, u32[]{:S(2)}) %collective-permute-start.1) | collective-permute-done | bytes 163872 | tf_op jit(solution)/shard_map/ppermute | solution.py:324
  18.2 1.3 %analysis.1 = bf16[16,16,128]{2,1,0:T(8,128)(2,1)S(1)} custom-call(s32[1]{0:T(128)} %bitcast.me_ref, bf16[16,40,128]{2,1,0:T(8,128)(2,1)S(1)} %collective-permute-done.1.near_ref, bf16[256,128]{1,0:T(8,128)(2,1)S(1)} %get-tuple-element.14.inner_ref, f32[272,256]{1,0:T(8,128)S(1)} %get-tuple-element.15.sums_ref, f32[8,128]{1,0:T(8,128)S(1)} %get-tuple-element.16.mean_ref), custom_call_target="tpu_custom_call" | custom-call | flops 268435456 | bytes 577540 | tf_op jit(solution)/shard_map/analysis/pallas_call | solution.py:359
  19.6 9.7 %all_to_all.11.in_ref = bf16[16,16,128]{2,1,0:T(8,128)(2,1)S(1)} all-to-all(bf16[16,16,128]{2,1,0:T(8,128)(2,1)S(1)} %analysis.1), channel_id=1, replica_groups={{30,22,14,6,28,20,12,4,26,18,10,2,24,16,8,0},{31,23,15,7,29,21,13,5,27,..., dimensions={0} | all-to-all | bytes 131072 | tf_op jit(solution)/shard_map/all_to_all | solution.py:353
  29.3 0.0 collective-permute-start.2
  29.3 0.5 %unpack_own.1 = (f32[16,16,128]{2,1,0:T(8,128)S(1)}, f32[24,16,128]{2,1,0:T(8,128)S(1)}) custom-call(bf16[16,16,128]{2,1,0:T(8,128)(2,1)S(1)} %all_to_all.11.in_ref), custom_call_target="tpu_custom_call" | custom-call | bytes 393216 | tf_op jit(solution)/shard_map/unpack_own/pallas_call | solution.py:359
  29.8 0.7 %collective-permute-done.2.near_ref = bf16[16,16,128]{2,1,0:T(8,128)(2,1)S(1)} collective-permute-done((bf16[16,16,128]{2,1,0:T(8,128)(2,1)S(1)}, bf16[16,16,128]{2,1,0:T(8,128)(2,1)S(1)}, u32[]{:S(2)}, u32[]{:S(2)}) %collective-permute-start.2) | collective-permute-done | bytes 65568 | tf_op jit(solution)/shard_map/ppermute | solution.py:324
  30.5 1.2 %unpack_forecast.1 = f32[256,128]{1,0:T(8,128)} custom-call(f32[16,16,128]{2,1,0:T(8,128)S(1)} %get-tuple-element.17.own_ref, f32[24,16,128]{2,1,0:T(8,128)S(1)} %get-tuple-element.18.inner_ref, bf16[16,16,128]{2,1,0:T(8,128)(2,1)S(1)} %collective-permute-done.2.near_ref), custom_call_target="tpu_custom_call" | custom-call | bytes 524288 | tf_op jit(solution)/shard_map/unpack_forecast/pallas_call | solution.py:359
Async XLA Ops:
  0.0 1.5 %copy-start.2 = (s32[2,8,8]{2,1,0:T(8,128)S(1)}, s32[2,8,8]{2,1,0:T(8,128)}, u32[]{:S(2)}) copy-start(s32[2,8,8]{2,1,0:T(8,128)} %mask_ref.1) | copy-start | bytes 1540
  0.0 1.5 %copy-start.1 = (f32[2,8,8]{2,1,0:T(8,128)S(1)}, f32[2,8,8]{2,1,0:T(8,128)}, u32[]{:S(2)}) copy-start(f32[2,8,8]{2,1,0:T(8,128)} %inverse_ref.1) | copy-start | bytes 1540
  0.0 1.5 %copy-start = (f32[2,8,8]{2,1,0:T(8,128)S(1)}, f32[2,8,8]{2,1,0:T(8,128)}, u32[]{:S(2)}) copy-start(f32[2,8,8]{2,1,0:T(8,128)} %values_ref.1) | copy-start | bytes 1540
  0.0 1.7 %collective-permute-start = (f32[16,2,8,128]{3,2,1,0:T(8,128)}, f32[16,2,8,128]{3,2,1,0:T(8,128)S(1)}, u32[]{:S(2)}, u32[]{:S(2)}) collective-permute-start(f32[16,2,8,128]{3,2,1,0:T(8,128)} %param.4), channel_id=1, source_target_pairs={{1,0},{0,1},{3,2},{2,3},{5,4},{4,5},{7,6},{6,7},{9,8},{8,9},{11,10... | collective-permute-start | bytes 393224 | tf_op jit(solution)/shard_map/ppermute | solution.py:324
  16.8 1.4 %collective-permute-start.1 = (bf16[16,40,128]{2,1,0:T(8,128)(2,1)S(1)}, bf16[16,40,128]{2,1,0:T(8,128)(2,1)S(1)}, u32[]{:S(2)}, u32[]{:S(2)}) collective-permute-start(bf16[16,40,128]{2,1,0:T(8,128)(2,1)S(1)} %all_to_all.10.own_ref), channel_id=1, source_target_pairs={{1,0},{0,1},{3,2},{2,3},{5,4},{4,5},{7,6},{6,7},{9,8},{8,9},{11,10... | collective-permute-start | bytes 491528 | tf_op jit(solution)/shard_map/ppermute | solution.py:324
  29.3 1.3 %collective-permute-start.2 = (bf16[16,16,128]{2,1,0:T(8,128)(2,1)S(1)}, bf16[16,16,128]{2,1,0:T(8,128)(2,1)S(1)}, u32[]{:S(2)}, u32[]{:S(2)}) collective-permute-start(bf16[16,16,128]{2,1,0:T(8,128)(2,1)S(1)} %all_to_all.11.in_ref), channel_id=1, source_target_pairs={{1,0},{0,1},{3,2},{2,3},{5,4},{4,5},{7,6},{6,7},{9,8},{8,9},{11,10... | collective-permute-start | bytes 196616 | tf_op jit(solution)/shard_map/ppermute | solution.py:324

commit v20 on v17

--- a/solution.py
+++ b/solution.py
@@ -53,20 +53,24 @@
     return [(step, row) for step in range(1, FSTEPS) for row in range(step, BAND - step)]
 
 
-def swap_blocks(parts, size):
+def swap_blocks(parts, size, most):
     count = len(parts)
-    lane = lax.broadcasted_iota(jnp.int32, parts[0].shape, 1) // size
+    block = lax.broadcasted_iota(jnp.int32, parts[0].shape, 1) // size
     stride = 1
     while stride < count:
-        upper = (lane & stride) != 0
-        new = list(parts)
+        base = min(most, count // stride)
+        here = [(block // stride) % base == digit for digit in range(base)]
+        new = []
         for j in range(count):
-            if j & stride == 0:
-                a, b = parts[j], parts[j + stride]
-                new[j] = jnp.where(upper, pltpu.roll(b, stride * size, 1), a)
-                new[j + stride] = jnp.where(upper, b, pltpu.roll(a, WIDTH - stride * size, 1))
+            own = (j // stride) % base
+            value = parts[j]
+            for digit in range(base):
+                if digit != own:
+                    move = (digit - own) * stride
+                    value = jnp.where(here[digit], pltpu.roll(parts[j + move], (move * size) % WIDTH, 1), value)
+            new.append(value)
         parts = new
-        stride *= 2
+        stride *= base
     return parts
 
 
@@ -156,14 +160,14 @@
     for j in range(8):
         part = wide[start + j * 8 : start + j * 8 + 8]
         means.append(jnp.where(is_mean, part[:, :WIDTH], pltpu.roll(part[:, WIDTH:], 2, 0)))
-    means = swap_blocks(means, REGION)
+    means = swap_blocks(means, REGION, 2)
     for side in range(2):
         for half in range(2):
             parts = [
                 wide[(half * 8 + j) * LOCAL : (half * 8 + j + 1) * LOCAL, side * WIDTH : (side + 1) * WIDTH].astype(BF)
                 for j in range(8)
             ]
-            parts = swap_blocks(parts, REGION)
+            parts = swap_blocks(parts, REGION, 2)
             for i in range(8):
                 out_ref[position(side * 8 + i), half * LOCAL : (half + 1) * LOCAL] = parts[i]
         for i in range(8):
@@ -290,24 +294,27 @@
         out_ref[s] = result[s * LOCAL : (s + 1) * LOCAL]
 
 
-def unpacked(ref):
-    return [row.astype(F32) for row in swap_blocks([ref[position(p)] for p in range(ref.shape[0])], PATCH)]
-
-
 def by_field(rows):
     half = BAND // 2
     return [[rows[h * FIELDS * half + field * half + r] for h in range(2) for r in range(half)] for field in range(FIELDS)]
 
 
-def unpack_kernel(in_ref, rows_ref, inner_ref):
-    rows = unpacked(in_ref)
-    for i, row in enumerate(rows):
+def unpack_kernel(in_ref, rows_ref):
+    blocks = [in_ref[position(p)] for p in range(in_ref.shape[0])]
+    for i, row in enumerate(swap_blocks(blocks, PATCH, 4)):
         rows_ref[i] = row
-    advance_inner(*by_field(rows), inner_ref)
+
+
+def read_rows(ref):
+    return by_field([ref[i].astype(F32) for i in range(ref.shape[0])])
+
+
+def inner_again_kernel(rows_ref, inner_ref):
+    advance_inner(*read_rows(rows_ref), inner_ref)
 
 
 def forecast_kernel(own_ref, inner_ref, near_ref, out_ref):
-    own, near = by_field(own_ref), by_field(unpacked(near_ref))
+    own, near = read_rows(own_ref), read_rows(near_ref)
     fields = [n[BAND - FSTEPS :] + o + n[:FSTEPS] for o, n in zip(own, near)]
     done = forecast_rows(*fields, kept_rows(inner_ref))
     for field in range(FIELDS):
@@ -342,7 +349,7 @@
 
 
 def join_inner(after, before):
-    return jnp.concatenate([after[..., : WIDTH // 2], before[..., WIDTH // 2 :]], 2)
+    return jnp.concatenate([after[: FIELDS * BAND // 2], before[FIELDS * BAND // 2 :]], 0)
 
 
 def exchange(value):
@@ -390,10 +397,11 @@
     region_near = near_rows(region, join_region)
     own = call(own_kernel, "own_half", own_shapes, me, region, flops=flops)
     inner = exchange(call(analysis_kernel, "analysis", inner_shape, me, region_near, *own, flops=8 * flops))
-    inner_near = near_rows(inner, join_inner)
-    own_rows = call(unpack_kernel, "unpack_own", [rows_shape, kept_shape], inner)
+    own_rows = call(unpack_kernel, "unpack_own", jax.ShapeDtypeStruct(rows_shape.shape, BF), inner)
+    rows_near = near_rows(own_rows, join_inner)
+    kept = call(inner_again_kernel, "inner_rows_again", kept_shape, own_rows)
     out_shape = jax.ShapeDtypeStruct((LOCAL * FIELDS * BAND, WIDTH), F32)
-    cycled = call(forecast_kernel, "unpack_forecast", out_shape, *own_rows, inner_near)
+    cycled = call(forecast_kernel, "unpack_forecast", out_shape, own_rows, kept, rows_near)
     return cycled.reshape(shape)
 
 

time: 31.7 us -> 31.7 us (level)
    pallas_call x6 -> x7, Pallas kernels: 4.41 us -> 4.11 us  [call(): pl.pallas_call(kernel, out_shape=out_shape, in_specs=[pl.BlockSpec(memory...]
  transfers between devices with their start and end apart: 3 -> 3, of which waited for: 2 -> 2; matrix products, arithmetic and copies ran while one was open for 3% -> 3% of each run, Pallas kernels for 4% -> 3%
where the time goes in v20:
time: 31.7 us; the launch traced here: 31.5 us
  blocking collectives  23.7 us (75%)
  Pallas kernels  4.11 us (13%)
  waiting for transfers between devices  2.06 us (6%)
  local copies, waits for them, and re-layouts  0.96 us (3%)
  starting transfers between devices  0.59 us (2%)
    all_to_all x2, blocking collectives, exchange(): lax.all_to_all(value, ('mem', 'rows'), split_axis=0, concat_axis=0, axis_...  23.7 us
    pallas_call x7, Pallas kernels, call(): pl.pallas_call(kernel, out_shape=out_shape, in_specs=[pl.BlockSpec(memory...  4.11 us
    ppermute x3, waiting for transfers between devices, from_next(): lax.ppermute(value, 'rows', [((i + 1) % count, i) for i in range(count)])  2.06 us
    unnamed x7, local copies, waits for them, and re-layouts  0.96 us
  transfers between devices with their start and end apart: 3, of which 2 were waited for; matrix products, arithmetic and copies ran while one was open for 3% of the time, Pallas kernels for 3%

profile of v20, /device:TPU:0, one launch (start us, length us, event | category | flops | bytes accessed | tf_op | source)
XLA Modules:
  0.0 31.5 jit_solution(16629870645259962858)
XLA Ops:
  0.0 0.0 copy-start.2
  0.0 0.0 copy-start.1
  0.0 0.0 copy-start
  0.0 0.5 %collective-permute-start = (f32[16,2,8,128]{3,2,1,0:T(8,128)}, f32[16,2,8,128]{3,2,1,0:T(8,128)S(1)}, u32[]{:S(2)}, u32[]{:S(2)}) collective-permute-start(f32[16,2,8,128]{3,2,1,0:T(8,128)} %param.4), channel_id=1, source_target_pairs={{1,0},{0,1},{3,2},{2,3},{5,4},{4,5},{7,6},{6,7},{9,8},{8,9},{11,10... | collective-permute-start | bytes 393224 | tf_op jit(solution)/shard_map/ppermute | solution.py:327
  0.5 0.9 %copy.5 = f32[16,2,8,128]{3,0,2,1:T(8,128)S(1)} copy(f32[16,2,8,128]{3,2,1,0:T(8,128)} %param.4) | data formatting | bytes 262144 | tf_op args[0]
  1.5 0.0 copy-done.2
  1.5 0.0 copy-done.1
  1.5 0.0 copy-done
  1.5 0.2 inner_rows.1
  1.8 0.0 collective-permute-done
  1.8 0.7 %forecast_pack.1 = bf16[16,40,128]{2,1,0:T(8,128)(2,1)S(1)} custom-call(f32[16,16,128]{2,1,0:T(8,128)S(1)} %bitcast.7, f32[24,16,128]{2,1,0:T(8,128)S(1)} %get-tuple-element.10.inner_ref, f32[8,128]{1,0:T(8,128)S(1)} %get-tuple-element.11.obs_ref, f32[256,128]{1,0:T(8,128)S(1)} %bitcast.8), custom_call_target="tpu_custom_call" | custom-call | bytes 626688 | tf_op jit(solution)/shard_map/forecast_pack/pallas_call | solution.py:365
  2.5 14.1 %all_to_all.10.own_ref = bf16[16,40,128]{2,1,0:T(8,128)(2,1)S(1)} all-to-all(bf16[16,40,128]{2,1,0:T(8,128)(2,1)S(1)} %forecast_pack.1), channel_id=1, replica_groups={{31,15,23,7,29,13,21,5,27,11,19,3,25,9,17,1},{30,14,22,6,28,12,20,4,26,..., dimensions={0} | all-to-all | bytes 327680 | tf_op jit(solution)/shard_map/all_to_all | solution.py:359
  16.6 0.0 collective-permute-start.1
  16.6 0.3 %own_half.1 = (bf16[256,128]{1,0:T(8,128)(2,1)S(1)}, f32[272,256]{1,0:T(8,128)S(1)}, f32[8,128]{1,0:T(8,128)S(1)}) custom-call(s32[1]{0:T(128)} %bitcast.me_ref, bf16[16,40,128]{2,1,0:T(8,128)(2,1)S(1)} %all_to_all.10.own_ref), custom_call_target="tpu_custom_call" | custom-call | flops 33554432 | bytes 512004 | tf_op jit(solution)/shard_map/own_half/pallas_call | solution.py:365
  17.0 1.1 %collective-permute-done.1.near_ref = bf16[16,40,128]{2,1,0:T(8,128)(2,1)S(1)} collective-permute-done((bf16[16,40,128]{2,1,0:T(8,128)(2,1)S(1)}, bf16[16,40,128]{2,1,0:T(8,128)(2,1)S(1)}, u32[]{:S(2)}, u32[]{:S(2)}) %collective-permute-start.1) | collective-permute-done | bytes 163872 | tf_op jit(solution)/shard_map/ppermute | solution.py:327
  18.0 1.3 %analysis.1 = bf16[16,16,128]{2,1,0:T(8,128)(2,1)S(1)} custom-call(s32[1]{0:T(128)} %bitcast.me_ref, bf16[16,40,128]{2,1,0:T(8,128)(2,1)S(1)} %collective-permute-done.1.near_ref, bf16[256,128]{1,0:T(8,128)(2,1)S(1)} %get-tuple-element.12.inner_ref, f32[272,256]{1,0:T(8,128)S(1)} %get-tuple-element.13.sums_ref, f32[8,128]{1,0:T(8,128)S(1)} %get-tuple-element.14.mean_ref), custom_call_target="tpu_custom_call" | custom-call | flops 268435456 | bytes 577540 | tf_op jit(solution)/shard_map/analysis/pallas_call | solution.py:365
  19.4 9.6 %all_to_all.11.in_ref = bf16[16,16,128]{2,1,0:T(8,128)(2,1)S(1)} all-to-all(bf16[16,16,128]{2,1,0:T(8,128)(2,1)S(1)} %analysis.1), channel_id=1, replica_groups={{31,15,23,7,29,13,21,5,27,11,19,3,25,9,17,1},{30,14,22,6,28,12,20,4,26,..., dimensions={0} | all-to-all | bytes 131072 | tf_op jit(solution)/shard_map/all_to_all | solution.py:359
  29.0 0.2 unpack_own.1.rows_ref.own_ref
  29.2 0.1 collective-permute-start.2
  29.3 0.2 inner_rows_again.1.inner_ref
  29.5 1.0 %collective-permute-done.2.near_ref = bf16[16,16,128]{2,1,0:T(8,128)(2,1)S(1)} collective-permute-done((bf16[16,16,128]{2,1,0:T(8,128)(2,1)S(1)}, bf16[16,16,128]{2,1,0:T(8,128)(2,1)S(1)}, u32[]{:S(2)}, u32[]{:S(2)}) %collective-permute-start.2) | collective-permute-done | bytes 65568 | tf_op jit(solution)/shard_map/ppermute | solution.py:327
  30.5 1.0 %unpack_forecast.1 = f32[256,128]{1,0:T(8,128)} custom-call(bf16[16,16,128]{2,1,0:T(8,128)(2,1)S(1)} %unpack_own.1.rows_ref.own_ref, f32[24,16,128]{2,1,0:T(8,128)S(1)} %inner_rows_again.1.inner_ref, bf16[16,16,128]{2,1,0:T(8,128)(2,1)S(1)} %collective-permute-done.2.near_ref), custom_call_target="tpu_custom_call" | custom-call | bytes 458752 | tf_op jit(solution)/shard_map/unpack_forecast/pallas_call | solution.py:365
Async XLA Ops:
  0.0 1.5 %copy-start.2 = (s32[2,8,8]{2,1,0:T(8,128)S(1)}, s32[2,8,8]{2,1,0:T(8,128)}, u32[]{:S(2)}) copy-start(s32[2,8,8]{2,1,0:T(8,128)} %mask_ref.1) | copy-start | bytes 1540
  0.0 1.5 %copy-start.1 = (f32[2,8,8]{2,1,0:T(8,128)S(1)}, f32[2,8,8]{2,1,0:T(8,128)}, u32[]{:S(2)}) copy-start(f32[2,8,8]{2,1,0:T(8,128)} %inverse_ref.1) | copy-start | bytes 1540
  0.0 1.5 %copy-start = (f32[2,8,8]{2,1,0:T(8,128)S(1)}, f32[2,8,8]{2,1,0:T(8,128)}, u32[]{:S(2)}) copy-start(f32[2,8,8]{2,1,0:T(8,128)} %values_ref.1) | copy-start | bytes 1540
  0.0 1.7 %collective-permute-start = (f32[16,2,8,128]{3,2,1,0:T(8,128)}, f32[16,2,8,128]{3,2,1,0:T(8,128)S(1)}, u32[]{:S(2)}, u32[]{:S(2)}) collective-permute-start(f32[16,2,8,128]{3,2,1,0:T(8,128)} %param.4), channel_id=1, source_target_pairs={{1,0},{0,1},{3,2},{2,3},{5,4},{4,5},{7,6},{6,7},{9,8},{8,9},{11,10... | collective-permute-start | bytes 393224 | tf_op jit(solution)/shard_map/ppermute | solution.py:327
  16.6 1.4 %collective-permute-start.1 = (bf16[16,40,128]{2,1,0:T(8,128)(2,1)S(1)}, bf16[16,40,128]{2,1,0:T(8,128)(2,1)S(1)}, u32[]{:S(2)}, u32[]{:S(2)}) collective-permute-start(bf16[16,40,128]{2,1,0:T(8,128)(2,1)S(1)} %all_to_all.10.own_ref), channel_id=1, source_target_pairs={{1,0},{0,1},{3,2},{2,3},{5,4},{4,5},{7,6},{6,7},{9,8},{8,9},{11,10... | collective-permute-start | bytes 491528 | tf_op jit(solution)/shard_map/ppermute | solution.py:327
  29.2 1.3 %collective-permute-start.2 = (bf16[16,16,128]{2,1,0:T(8,128)(2,1)S(1)}, bf16[16,16,128]{2,1,0:T(8,128)(2,1)S(1)}, u32[]{:S(2)}, u32[]{:S(2)}) collective-permute-start(bf16[16,16,128]{2,1,0:T(8,128)(2,1)S(1)} %unpack_own.1.rows_ref.own_ref), channel_id=1, source_target_pairs={{1,0},{0,1},{3,2},{2,3},{5,4},{4,5},{7,6},{6,7},{9,8},{8,9},{11,10... | collective-permute-start | bytes 196616 | tf_op jit(solution)/shard_map/ppermute | solution.py:327

commit v21 on v20

--- a/solution.py
+++ b/solution.py
@@ -203,7 +203,10 @@
     for half in range(2):
         base = half * 4
         means = [t[base : base + 1] + t[base + 1 : base + 2] for t in tails]
-        mean = functools.reduce(jnp.add, means) * (1.0 / count)
+        level = means
+        while len(level) > 1:
+            level = [a + b for a, b in zip(level[::2], level[1::2])]
+        mean = level[0] * (1.0 / count)
         deviation = []
         for s, own_mean in enumerate(means):
             value = ref[s, half * LOCAL : (half + 1) * LOCAL].astype(F32)
@@ -237,7 +240,10 @@
 
 def own_kernel(me_ref, own_ref, inner_ref, sums_ref, mean_ref):
     halves = halves_of(own_ref, me_ref[0])
-    deviation, sums_ref[...] = half_sums(halves, [jnp.zeros_like] * 2)
+    deviation, sums = half_sums(halves, [jnp.zeros_like] * 2)
+    row = lax.broadcasted_iota(jnp.int32, sums.shape, 0)
+    col = lax.broadcasted_iota(jnp.int32, sums.shape, 1)
+    sums_ref[...] = sums + jnp.where(row == col, sums.shape[1] - 1.0, 0.0)
     lane = lax.broadcasted_iota(jnp.int32, (2 * WIDTH, WIDTH), 0)
     target = lax.broadcasted_iota(jnp.int32, (2 * WIDTH, WIDTH), 1)
     narrow = (lane == (target // PATCH) * REGION + RADIUS + target % PATCH).astype(F32).astype(BF)
@@ -255,9 +261,8 @@
     members = count * LOCAL
     halves = halves_of(near_ref, me_ref[0])
     both = sums_ref[...] + half_sums(halves, [lambda r: r + 1, lambda r: RADIUS - r])[1]
-    row = lax.broadcasted_iota(jnp.int32, (members, members), 0)
-    col = lax.broadcasted_iota(jnp.int32, (members, members), 1)
-    system = both[:members] + jnp.where(row == col, members - 1.0, 0.0)
+    system = both[:members]
+
     def mul(a, b):
         return jnp.dot(a.astype(BF), b.astype(BF), preferred_element_type=F32)
 

time: 31.7 us -> 31.7 us (level)
  no operation moved by 1% of the time
where the time goes in v21:
time: 31.7 us; the launch traced here: 31.5 us
  blocking collectives  23.7 us (75%)
  Pallas kernels  4.11 us (13%)
  waiting for transfers between devices  2.05 us (6%)
  local copies, waits for them, and re-layouts  0.96 us (3%)
  starting transfers between devices  0.59 us (2%)
    all_to_all x2, blocking collectives, exchange(): lax.all_to_all(value, ('mem', 'rows'), split_axis=0, concat_axis=0, axis_...  23.7 us
    pallas_call x7, Pallas kernels, call(): pl.pallas_call(kernel, out_shape=out_shape, in_specs=[pl.BlockSpec(memory...  4.11 us
    ppermute x3, waiting for transfers between devices, from_next(): lax.ppermute(value, 'rows', [((i + 1) % count, i) for i in range(count)])  2.05 us
    unnamed x7, local copies, waits for them, and re-layouts  0.96 us
  transfers between devices with their start and end apart: 3, of which 2 were waited for; matrix products, arithmetic and copies ran while one was open for 3% of the time, Pallas kernels for 3%

profile of v21, /device:TPU:0, one launch (start us, length us, event | category | flops | bytes accessed | tf_op | source)
XLA Modules:
  0.0 31.5 jit_solution(5731092567380471206)
XLA Ops:
  0.0 0.0 copy-start.2
  0.0 0.0 copy-start.1
  0.0 0.0 copy-start
  0.0 0.5 %collective-permute-start = (f32[16,2,8,128]{3,2,1,0:T(8,128)}, f32[16,2,8,128]{3,2,1,0:T(8,128)S(1)}, u32[]{:S(2)}, u32[]{:S(2)}) collective-permute-start(f32[16,2,8,128]{3,2,1,0:T(8,128)} %param.4), channel_id=1, source_target_pairs={{1,0},{0,1},{3,2},{2,3},{5,4},{4,5},{7,6},{6,7},{9,8},{8,9},{11,10... | collective-permute-start | bytes 393224 | tf_op jit(solution)/shard_map/ppermute | solution.py:332
  0.5 0.9 %copy.5 = f32[16,2,8,128]{3,0,2,1:T(8,128)S(1)} copy(f32[16,2,8,128]{3,2,1,0:T(8,128)} %param.4) | data formatting | bytes 262144 | tf_op args[0]
  1.5 0.0 copy-done.2
  1.5 0.0 copy-done.1
  1.5 0.0 copy-done
  1.5 0.2 inner_rows.1
  1.8 0.0 collective-permute-done
  1.8 0.7 %forecast_pack.1 = bf16[16,40,128]{2,1,0:T(8,128)(2,1)S(1)} custom-call(f32[16,16,128]{2,1,0:T(8,128)S(1)} %bitcast.7, f32[24,16,128]{2,1,0:T(8,128)S(1)} %get-tuple-element.10.inner_ref, f32[8,128]{1,0:T(8,128)S(1)} %get-tuple-element.11.obs_ref, f32[256,128]{1,0:T(8,128)S(1)} %bitcast.8), custom_call_target="tpu_custom_call" | custom-call | bytes 626688 | tf_op jit(solution)/shard_map/forecast_pack/pallas_call | solution.py:370
  2.5 14.1 %all_to_all.10.own_ref = bf16[16,40,128]{2,1,0:T(8,128)(2,1)S(1)} all-to-all(bf16[16,40,128]{2,1,0:T(8,128)(2,1)S(1)} %forecast_pack.1), channel_id=1, replica_groups={{31,15,23,7,29,13,21,5,27,11,19,3,25,9,17,1},{30,14,22,6,28,12,20,4,26,..., dimensions={0} | all-to-all | bytes 327680 | tf_op jit(solution)/shard_map/all_to_all | solution.py:364
  16.6 0.0 collective-permute-start.1
  16.6 0.3 %own_half.1 = (bf16[256,128]{1,0:T(8,128)(2,1)S(1)}, f32[272,256]{1,0:T(8,128)S(1)}, f32[8,128]{1,0:T(8,128)S(1)}) custom-call(s32[1]{0:T(128)} %bitcast.me_ref, bf16[16,40,128]{2,1,0:T(8,128)(2,1)S(1)} %all_to_all.10.own_ref), custom_call_target="tpu_custom_call" | custom-call | flops 33554432 | bytes 512004 | tf_op jit(solution)/shard_map/own_half/pallas_call | solution.py:370
  17.0 1.0 %collective-permute-done.1.near_ref = bf16[16,40,128]{2,1,0:T(8,128)(2,1)S(1)} collective-permute-done((bf16[16,40,128]{2,1,0:T(8,128)(2,1)S(1)}, bf16[16,40,128]{2,1,0:T(8,128)(2,1)S(1)}, u32[]{:S(2)}, u32[]{:S(2)}) %collective-permute-start.1) | collective-permute-done | bytes 163872 | tf_op jit(solution)/shard_map/ppermute | solution.py:332
  18.0 1.3 %analysis.1 = bf16[16,16,128]{2,1,0:T(8,128)(2,1)S(1)} custom-call(s32[1]{0:T(128)} %bitcast.me_ref, bf16[16,40,128]{2,1,0:T(8,128)(2,1)S(1)} %collective-permute-done.1.near_ref, bf16[256,128]{1,0:T(8,128)(2,1)S(1)} %get-tuple-element.12.inner_ref, f32[272,256]{1,0:T(8,128)S(1)} %get-tuple-element.13.sums_ref, f32[8,128]{1,0:T(8,128)S(1)} %get-tuple-element.14.mean_ref), custom_call_target="tpu_custom_call" | custom-call | flops 268435456 | bytes 577540 | tf_op jit(solution)/shard_map/analysis/pallas_call | solution.py:370
  19.4 9.6 %all_to_all.11.in_ref = bf16[16,16,128]{2,1,0:T(8,128)(2,1)S(1)} all-to-all(bf16[16,16,128]{2,1,0:T(8,128)(2,1)S(1)} %analysis.1), channel_id=1, replica_groups={{31,15,23,7,29,13,21,5,27,11,19,3,25,9,17,1},{30,14,22,6,28,12,20,4,26,..., dimensions={0} | all-to-all | bytes 131072 | tf_op jit(solution)/shard_map/all_to_all | solution.py:364
  29.0 0.2 unpack_own.1.rows_ref.own_ref
  29.2 0.1 collective-permute-start.2
  29.3 0.2 inner_rows_again.1.inner_ref
  29.5 1.0 %collective-permute-done.2.near_ref = bf16[16,16,128]{2,1,0:T(8,128)(2,1)S(1)} collective-permute-done((bf16[16,16,128]{2,1,0:T(8,128)(2,1)S(1)}, bf16[16,16,128]{2,1,0:T(8,128)(2,1)S(1)}, u32[]{:S(2)}, u32[]{:S(2)}) %collective-permute-start.2) | collective-permute-done | bytes 65568 | tf_op jit(solution)/shard_map/ppermute | solution.py:332
  30.5 1.0 %unpack_forecast.1 = f32[256,128]{1,0:T(8,128)} custom-call(bf16[16,16,128]{2,1,0:T(8,128)(2,1)S(1)} %unpack_own.1.rows_ref.own_ref, f32[24,16,128]{2,1,0:T(8,128)S(1)} %inner_rows_again.1.inner_ref, bf16[16,16,128]{2,1,0:T(8,128)(2,1)S(1)} %collective-permute-done.2.near_ref), custom_call_target="tpu_custom_call" | custom-call | bytes 458752 | tf_op jit(solution)/shard_map/unpack_forecast/pallas_call | solution.py:370
Async XLA Ops:
  0.0 1.5 %copy-start.2 = (s32[2,8,8]{2,1,0:T(8,128)S(1)}, s32[2,8,8]{2,1,0:T(8,128)}, u32[]{:S(2)}) copy-start(s32[2,8,8]{2,1,0:T(8,128)} %mask_ref.1) | copy-start | bytes 1540
  0.0 1.5 %copy-start.1 = (f32[2,8,8]{2,1,0:T(8,128)S(1)}, f32[2,8,8]{2,1,0:T(8,128)}, u32[]{:S(2)}) copy-start(f32[2,8,8]{2,1,0:T(8,128)} %inverse_ref.1) | copy-start | bytes 1540
  0.0 1.5 %copy-start = (f32[2,8,8]{2,1,0:T(8,128)S(1)}, f32[2,8,8]{2,1,0:T(8,128)}, u32[]{:S(2)}) copy-start(f32[2,8,8]{2,1,0:T(8,128)} %values_ref.1) | copy-start | bytes 1540
  0.0 1.7 %collective-permute-start = (f32[16,2,8,128]{3,2,1,0:T(8,128)}, f32[16,2,8,128]{3,2,1,0:T(8,128)S(1)}, u32[]{:S(2)}, u32[]{:S(2)}) collective-permute-start(f32[16,2,8,128]{3,2,1,0:T(8,128)} %param.4), channel_id=1, source_target_pairs={{1,0},{0,1},{3,2},{2,3},{5,4},{4,5},{7,6},{6,7},{9,8},{8,9},{11,10... | collective-permute-start | bytes 393224 | tf_op jit(solution)/shard_map/ppermute | solution.py:332
  16.6 1.4 %collective-permute-start.1 = (bf16[16,40,128]{2,1,0:T(8,128)(2,1)S(1)}, bf16[16,40,128]{2,1,0:T(8,128)(2,1)S(1)}, u32[]{:S(2)}, u32[]{:S(2)}) collective-permute-start(bf16[16,40,128]{2,1,0:T(8,128)(2,1)S(1)} %all_to_all.10.own_ref), channel_id=1, source_target_pairs={{1,0},{0,1},{3,2},{2,3},{5,4},{4,5},{7,6},{6,7},{9,8},{8,9},{11,10... | collective-permute-start | bytes 491528 | tf_op jit(solution)/shard_map/ppermute | solution.py:332
  29.2 1.3 %collective-permute-start.2 = (bf16[16,16,128]{2,1,0:T(8,128)(2,1)S(1)}, bf16[16,16,128]{2,1,0:T(8,128)(2,1)S(1)}, u32[]{:S(2)}, u32[]{:S(2)}) collective-permute-start(bf16[16,16,128]{2,1,0:T(8,128)(2,1)S(1)} %unpack_own.1.rows_ref.own_ref), channel_id=1, source_target_pairs={{1,0},{0,1},{3,2},{2,3},{5,4},{4,5},{7,6},{6,7},{9,8},{8,9},{11,10... | collective-permute-start | bytes 196616 | tf_op jit(solution)/shard_map/ppermute | solution.py:332
